TPU v7x, 32 devices: a whole 2x2x4 slice. The times are simulated.
32 devices in a mesh: tile: 16 (over z, y, core), layer: 2 (over x).
Axes of the slice: x: 2, y: 2, z: 4, core: 2. Of those that a mesh axis runs over, the one named last changes fastest.
Arguments:
- class_index: int32 [2, 2, 256, 8192], P('layer', None, 'tile'), may hold values from 0 to 15
- class_conductance: float32 [2, 16], P('layer'), may hold values from 0.5 to 8
- loads: float32 [2, 256, 8192], P('layer', 'tile'), may hold values from -4 to 4
- start_volts: float32 [2, 256, 8192], P('layer', 'tile'), may hold values from 0.8 to 1
- via_cells: int32 [2, 131072], P('layer', 'tile'), may hold values from 0 to 15, as said below
- via_counts: int32 [2, 131072], P('layer', 'tile'), may hold values from 0 to 4
Outputs:
- volts: float32 [2, 256, 8192], P('layer', 'tile')
Inputs may be any that keep to these rules, and one draw needn't show every extreme that they name: `via_cells`: each slot names a row of its own strip; slot s sits in column s % 8192, so each column of a strip holds exactly one slot of each layer.
All inputs are finite; a program needn't handle non-finite values.
Results may differ from a plain program's by a relative error of at most 0.00002.
Values sent between devices are 32-bit elements; how exact they have to be, the bound alone decides.
No kernel may reach another device: no remote copies, remote signals or barrier semaphores. Data moves between devices by JAX's collectives and lax.ppermute only.
A program may use at most 64 MiB of HBM per device.

v0:
```python
import jax
import jax.numpy as jnp
from jax import lax
from jax.sharding import PartitionSpec as P

CLASSES = 16
OUTER = 2
SWEEPS = 3


VIA_UNIT = 2.0
LOWER_BOUND = 0.05
UPPER_BOUND = 2.0


def passed_along(block, axis, distance):
    devices = range(lax.axis_size(axis))
    route = [(i - distance, i) for i in devices if i - distance in devices]
    return lax.ppermute(block, axis, route)


def padded_2(shard, sides, width):
    for axis, dim in sides:
        peers, length = (lax.axis_size(axis), shard.shape[dim])
        up = [(i, (i + 1) % peers) for i in range(peers - 1)]
        down = [(j, i) for i, j in up]
        last = lax.slice_in_dim(shard, length - width, length, axis=dim)
        leading = lax.slice_in_dim(shard, 0, width, axis=dim)
        before = lax.ppermute(last, axis, up)
        after = lax.ppermute(leading, axis, down)
        shard = jnp.concatenate([before, shard, after], axis=dim)
    return shard


def chebyshev_terms(count):
    centre_value = 0.5 * (UPPER_BOUND + LOWER_BOUND)
    half_width = 0.5 * (UPPER_BOUND - LOWER_BOUND)
    sigma = centre_value / half_width
    rho_last = 1.0 / sigma
    terms = [(0.0, 1.0 / centre_value)]
    for index in range(1, count):
        rho_next = 1.0 / (2.0 * sigma - rho_last)
        terms.append((rho_next * rho_last, 2.0 * rho_next / half_width))
        rho_last = rho_next
    return terms


def lookup(class_codes, class_table):
    result = jnp.zeros(class_codes.shape, jnp.float32)
    for code in range(CLASSES):
        result = result + jnp.where(class_codes == code, class_table[code], jnp.float32(0.0))
    return result


def neighbours(padded, vertical_links, across):
    span = padded.shape[0]
    centre_cells = padded[1 : span - 1]
    vertical = (
        vertical_links[0 : span - 2] * padded[0 : span - 2]
        + vertical_links[1 : span - 1] * padded[2:span]
    )
    right_flow = jnp.pad(centre_cells[:, 1:], ((0, 0), (0, 1))) * across
    left_flow = jnp.pad(centre_cells[:, :-1] * across[:, :-1], ((0, 0), (1, 0)))
    return vertical + right_flow + left_flow


def relax_sweep(padded, vertical_links, across, right_side, inverse_diag, previous, factors):
    centre_cells = padded[1:-1]
    residual = (
        inverse_diag * (right_side + neighbours(padded, vertical_links, across)) - centre_cells
    )
    if previous is None:
        update = factors[1] * residual
    else:
        update = factors[0] * previous + factors[1] * residual
    return (centre_cells + update, update)


def pick_rows(field, marks):
    return jnp.sum(jnp.where(marks, field, jnp.float32(0.0)), axis=0)


def local(class_index, class_conductance, loads, start_volts, via_cells, via_counts):
    row_count = loads.shape[1]
    col_count = loads.shape[2]
    conductance = lookup(class_index[0], class_conductance[0])
    col_ids = lax.broadcasted_iota(jnp.int32, (row_count, col_count), 1)
    local_rows = lax.broadcasted_iota(jnp.int32, (row_count, col_count), 0)
    row_ids = local_rows + lax.axis_index("tile") * row_count
    across = jnp.where(col_ids < col_count - 1, conductance[0], jnp.float32(0.0))
    downward = jnp.where(
        row_ids < lax.axis_size("tile") * row_count - 1, conductance[1], jnp.float32(0.0)
    )
    upper_links = passed_along(downward[row_count - 1 :], "tile", 1)
    vertical_links = jnp.concatenate([upper_links, downward], axis=0)
    own_cells = via_cells[0]
    own_counts = via_counts[0]
    lower_cells, lower_counts = passed_along((own_cells, own_counts), "layer", 1)
    own_weight = VIA_UNIT * own_counts.astype(jnp.float32)
    lower_weight = VIA_UNIT * lower_counts.astype(jnp.float32)
    own_marks = local_rows == own_cells[None, :]
    lower_marks = local_rows == lower_cells[None, :]
    zero_value = jnp.float32(0.0)
    via_diag = jnp.where(own_marks, own_weight[None, :], zero_value) + jnp.where(
        lower_marks, lower_weight[None, :], zero_value
    )
    diagonal = (
        across
        + jnp.pad(across[:, :-1], ((0, 0), (1, 0)))
        + vertical_links[:-1]
        + vertical_links[1:]
        + via_diag
    )
    inverse_diag = 1.0 / diagonal
    on_top_layer = lax.axis_index("layer") == lax.axis_size("layer") - 1
    factors = chebyshev_terms(SWEEPS)
    volts = start_volts[0]
    for outer_index in range(OUTER):
        from_below = passed_along(pick_rows(volts, own_marks), "layer", 1)
        from_above = passed_along(pick_rows(volts, lower_marks), "layer", -1)
        from_above = jnp.where(on_top_layer, jnp.float32(1.0), from_above)
        source = jnp.where(own_marks, (own_weight * from_above)[None, :], zero_value) + jnp.where(
            lower_marks, (lower_weight * from_below)[None, :], zero_value
        )
        right_side = source - loads[0]
        update = None
        for sweep_index in range(SWEEPS):
            padded = padded_2(volts, (("tile", 0),), 1)
            volts, update = relax_sweep(
                padded,
                vertical_links,
                across,
                right_side,
                inverse_diag,
                update,
                factors[sweep_index],
            )
    return volts[None]


def solution(mesh):
    placed = (
        P("layer", None, "tile", None),
        P("layer", None),
        P("layer", "tile", None),
        P("layer", "tile", None),
        P("layer", "tile"),
        P("layer", "tile"),
    )
    return jax.shard_map(
        local, mesh=mesh, in_specs=placed, out_specs=P("layer", "tile", None), check_vma=False
    )
```

profile of v0, /device:TPU:5, one launch (start us, length us, event | category | flops | bytes accessed | tf_op | source)
XLA Modules:
  0.0 93.1 jit_solution(16443223584024976029)
XLA Ops:
  0.0 3.1 %collective-permute-start.1 = (s32[8192]{0:T(1024)}, s32[8192]{0:T(1024)S(1)}, u32[]{:S(2)}, u32[]{:S(2)}) collective-permute-start(s32[8192]{0:T(1024)} %bitcast.64), channel_id=1, source_target_pairs={{0,1},{2,3},{4,5},{6,7},{8,9},{10,11},{12,13},{14,15},{16,17},{18,... | collective-permute-start | bytes 98312 | tf_op jit(solution)/shard_map/ppermute | solution.py:19
  3.1 1.3 %collective-permute-start.2 = (s32[8192]{0:T(1024)}, s32[8192]{0:T(1024)S(1)}, u32[]{:S(2)}, u32[]{:S(2)}) collective-permute-start(s32[8192]{0:T(1024)} %bitcast.78), channel_id=1, source_target_pairs={{0,1},{2,3},{4,5},{6,7},{8,9},{10,11},{12,13},{14,15},{16,17},{18,... | collective-permute-start | bytes 98312 | tf_op jit(solution)/shard_map/ppermute | solution.py:19
  4.4 1.7 %slice_bitcast_fusion.3 = (f32[1,8192]{1,0:T(1,128)}, f32[1,8192]{1,0:T(1,128)S(1)}) fusion(f32[1,16,8192]{2,1,0:T(8,128)} %param.9), kind=kLoop, calls=%fused_computation.101 | loop fusion | bytes 131072 | tf_op jit(solution)/shard_map/slice | solution.py:27
  6.1 4.0 %collective-permute-start.5 = (f32[1,8192]{1,0:T(1,128)}, f32[1,8192]{1,0:T(1,128)S(1)}, u32[]{:S(2)}, u32[]{:S(2)}) collective-permute-start(f32[1,8192]{1,0:T(1,128)} %get-tuple-element.43), channel_id=1, source_target_pairs={{0,2},{2,4},{4,6},{6,8},{8,10},{10,12},{12,14},{14,16},{16,18},{18... | collective-permute-start | bytes 98312 | tf_op jit(solution)/shard_map/ppermute | solution.py:29
  10.1 1.9 %collective-permute-start.6 = (f32[1,8192]{1,0:T(1,128)S(1)}, f32[1,8192]{1,0:T(1,128)S(1)}, u32[]{:S(2)}, u32[]{:S(2)}) collective-permute-start(f32[1,8192]{1,0:T(1,128)S(1)} %get-tuple-element.44), channel_id=1, source_target_pairs={{2,0},{4,2},{6,4},{8,6},{10,8},{12,10},{14,12},{16,14},{18,16},{20... | collective-permute-start | bytes 98312 | tf_op jit(solution)/shard_map/ppermute | solution.py:30
  12.0 0.0 copy-start.4
  12.1 0.6 copy-done.4
  12.7 0.7 fusion.85
  13.4 12.7 %bitcast_add_fusion = f32[2,16,8192]{2,1,0:T(8,128)S(1)} fusion(s32[1,2,16,8192]{3,2,1,0:T(8,128)} %param.6, f32[]{:T(128)} %bitcast.17, f32[]{:T(128)} %bitcast.15, f32[]{:T(128)} %bitcast.14, f32[]{:T(128)} %bitcast.13, f32[]{:T(128)} %bitcast.12, f32[]{:T(128)} %bitcast.11, f32[]{:T(128)} %bitcast.10, f32[]{:T(128)} %bitcast.9, f32[]{:T(128)} %bitcast.8, ...), kind=kLoop, calls=%fused_computation | loop fusion | flops 12320768 | bytes 2097216 | tf_op jit(solution)/shard_map/add | solution.py:51
  26.0 0.0 copy-start
  26.1 0.1 fusion.63
  26.2 4.5 %collective-permute-start = (f32[1,8192]{1,0:T(1,128)S(1)}, f32[1,8192]{1,0:T(1,128)S(1)}, u32[]{:S(2)}, u32[]{:S(2)}) collective-permute-start(f32[1,8192]{1,0:T(1,128)S(1)} %slice.279), channel_id=1, source_target_pairs={{0,2},{2,4},{4,6},{6,8},{8,10},{10,12},{12,14},{14,16},{16,18},{18... | collective-permute-start | bytes 98312 | tf_op jit(solution)/shard_map/ppermute | solution.py:19
  30.8 0.0 copy-done
  30.8 0.0 copy-start.2
  30.8 1.0 %fusion.84 = (f32[16,8191]{1,0:T(8,128)S(1)}, f32[16,8191]{1,0:T(8,128)S(1)}, f32[16,8191]{1,0:T(8,128)}) fusion(f32[16,8192]{1,0:T(8,128)S(1)} %get-tuple-element.19, f32[16,8192]{1,0:T(8,128)S(1)} %bitcast.62), kind=kLoop, calls=%fused_computation.120 | loop fusion | flops 131056 | bytes 3145344 | tf_op jit(solution)/shard_map/slice | solution.py:109
  31.8 0.0 collective-permute-done.1
  31.8 0.0 copy-done.2
  31.8 0.2 select_reduce_fusion.3
  32.0 1.9 %collective-permute-start.4 = (f32[8192]{0:T(1024)S(1)}, f32[8192]{0:T(1024)}, u32[]{:S(2)}, u32[]{:S(2)}) collective-permute-start(f32[8192]{0:T(1024)S(1)} %get-tuple-element.8), channel_id=1, source_target_pairs={{0,1},{2,3},{4,5},{6,7},{8,9},{10,11},{12,13},{14,15},{16,17},{18,... | collective-permute-start | bytes 98312 | tf_op jit(solution)/shard_map/ppermute | solution.py:19
  33.9 0.0 copy-done.3
  34.0 0.0 collective-permute-done.2
  34.0 1.3 %collective-permute-start.3 = (f32[8192]{0:T(1024)S(1)}, f32[8192]{0:T(1024)S(1)}, u32[]{:S(2)}, u32[]{:S(2)}) collective-permute-start(f32[8192]{0:T(1024)S(1)} %get-tuple-element.7), channel_id=1, source_target_pairs={{1,0},{3,2},{5,4},{7,6},{9,8},{11,10},{13,12},{15,14},{17,16},{19,... | collective-permute-start | bytes 98312 | tf_op jit(solution)/shard_map/ppermute | solution.py:19
  35.3 0.0 collective-permute-done.4
  35.3 0.8 convert_multiply_fusion.1
  36.1 2.6 %collective-permute-done.3 = f32[8192]{0:T(1024)S(1)} collective-permute-done((f32[8192]{0:T(1024)S(1)}, f32[8192]{0:T(1024)S(1)}, u32[]{:S(2)}, u32[]{:S(2)}) %collective-permute-start.3) | collective-permute-done | bytes 32800 | tf_op jit(solution)/shard_map/ppermute | solution.py:19
  38.7 0.0 collective-permute-done.5
  38.7 0.0 collective-permute-done.6
  38.7 0.0 collective-permute-done
  38.7 0.0 copy-done.1
  38.7 1.7 %multiply_add_fusion.1 = (f32[16,8192]{1,0:T(8,128)S(1)}, f32[16,8192]{1,0:T(8,128)S(1)}) fusion(f32[1,16,8192]{2,1,0:T(8,128)S(1)} %copy-done, f32[16,8192]{1,0:T(8,128)S(1)} %bitcast.63, f32[16,8191]{1,0:T(8,128)S(1)} %get-tuple-element.41, f32[16,8192]{1,0:T(8,128)S(1)} %get-tuple-element.19, f32[16,8191]{1,0:T(8,128)} %get-tuple-element.42, ...), kind=kLoop, calls=%fused_computation.92 | loop fusion | flops 3670016 | bytes 5537600 | tf_op jit(solution)/shard_map/add | solution.py:76
  40.5 3.2 %collective-permute-start.7 = (f32[1,8192]{1,0:T(1,128)S(1)}, f32[1,8192]{1,0:T(1,128)S(1)}, u32[]{:S(2)}, u32[]{:S(2)}) collective-permute-start(f32[1,8192]{1,0:T(1,128)S(1)} %get-tuple-element.36), channel_id=1, source_target_pairs={{0,2},{2,4},{4,6},{6,8},{8,10},{10,12},{12,14},{14,16},{16,18},{18... | collective-permute-start | bytes 98312 | tf_op jit(solution)/shard_map/ppermute | solution.py:29
  43.7 1.9 %collective-permute-start.8 = (f32[1,8192]{1,0:T(1,128)S(1)}, f32[1,8192]{1,0:T(1,128)S(1)}, u32[]{:S(2)}, u32[]{:S(2)}) collective-permute-start(f32[1,8192]{1,0:T(1,128)S(1)} %get-tuple-element.37), channel_id=1, source_target_pairs={{2,0},{4,2},{6,4},{8,6},{10,8},{12,10},{14,12},{16,14},{18,16},{20... | collective-permute-start | bytes 98312 | tf_op jit(solution)/shard_map/ppermute | solution.py:30
  45.6 0.2 fusion.83
  45.8 0.0 collective-permute-done.7
  45.8 4.0 %collective-permute-done.8 = f32[1,8192]{1,0:T(1,128)S(1)} collective-permute-done((f32[1,8192]{1,0:T(1,128)S(1)}, f32[1,8192]{1,0:T(1,128)S(1)}, u32[]{:S(2)}, u32[]{:S(2)}) %collective-permute-start.8) | collective-permute-done | bytes 32800 | tf_op jit(solution)/shard_map/ppermute | solution.py:30
  49.8 0.8 fusion.66
  50.6 1.9 %collective-permute-start.9 = (f32[1,8192]{1,0:T(1,128)S(1)}, f32[1,8192]{1,0:T(1,128)S(1)}, u32[]{:S(2)}, u32[]{:S(2)}) collective-permute-start(f32[1,8192]{1,0:T(1,128)S(1)} %get-tuple-element.32), channel_id=1, source_target_pairs={{0,2},{2,4},{4,6},{6,8},{8,10},{10,12},{12,14},{14,16},{16,18},{18... | collective-permute-start | bytes 98312 | tf_op jit(solution)/shard_map/ppermute | solution.py:29
  52.6 2.4 %collective-permute-start.10 = (f32[1,8192]{1,0:T(1,128)S(1)}, f32[1,8192]{1,0:T(1,128)S(1)}, u32[]{:S(2)}, u32[]{:S(2)}) collective-permute-start(f32[1,8192]{1,0:T(1,128)S(1)} %get-tuple-element.33), channel_id=1, source_target_pairs={{2,0},{4,2},{6,4},{8,6},{10,8},{12,10},{14,12},{16,14},{18,16},{20... | collective-permute-start | bytes 98312 | tf_op jit(solution)/shard_map/ppermute | solution.py:30
  55.0 0.2 fusion.81
  55.2 0.0 collective-permute-done.9
  55.2 3.5 %collective-permute-done.10 = f32[1,8192]{1,0:T(1,128)S(1)} collective-permute-done((f32[1,8192]{1,0:T(1,128)S(1)}, f32[1,8192]{1,0:T(1,128)S(1)}, u32[]{:S(2)}, u32[]{:S(2)}) %collective-permute-start.10) | collective-permute-done | bytes 32800 | tf_op jit(solution)/shard_map/ppermute | solution.py:30
  58.7 0.9 select_reduce_fusion.1
  59.6 1.3 %collective-permute-start.11 = (f32[8192]{0:T(1024)S(1)}, f32[8192]{0:T(1024)S(1)}, u32[]{:S(2)}, u32[]{:S(2)}) collective-permute-start(f32[8192]{0:T(1024)S(1)} %get-tuple-element.5), channel_id=1, source_target_pairs={{1,0},{3,2},{5,4},{7,6},{9,8},{11,10},{13,12},{15,14},{17,16},{19,... | collective-permute-start | bytes 98312 | tf_op jit(solution)/shard_map/ppermute | solution.py:19
  60.9 0.2 fusion.79
  61.2 4.0 %collective-permute-start.12 = (f32[8192]{0:T(1024)S(1)}, f32[8192]{0:T(1024)S(1)}, u32[]{:S(2)}, u32[]{:S(2)}) collective-permute-start(f32[8192]{0:T(1024)S(1)} %get-tuple-element.6), channel_id=1, source_target_pairs={{0,1},{2,3},{4,5},{6,7},{8,9},{10,11},{12,13},{14,15},{16,17},{18,... | collective-permute-start | bytes 98312 | tf_op jit(solution)/shard_map/ppermute | solution.py:19
  65.2 2.5 %collective-permute-start.13 = (f32[1,8192]{1,0:T(1,128)S(1)}, f32[1,8192]{1,0:T(1,128)S(1)}, u32[]{:S(2)}, u32[]{:S(2)}) collective-permute-start(f32[1,8192]{1,0:T(1,128)S(1)} %get-tuple-element.28), channel_id=1, source_target_pairs={{0,2},{2,4},{4,6},{6,8},{8,10},{10,12},{12,14},{14,16},{16,18},{18... | collective-permute-start | bytes 98312 | tf_op jit(solution)/shard_map/ppermute | solution.py:29
  67.7 1.9 %collective-permute-start.14 = (f32[1,8192]{1,0:T(1,128)S(1)}, f32[1,8192]{1,0:T(1,128)S(1)}, u32[]{:S(2)}, u32[]{:S(2)}) collective-permute-start(f32[1,8192]{1,0:T(1,128)S(1)} %get-tuple-element.29), channel_id=1, source_target_pairs={{2,0},{4,2},{6,4},{8,6},{10,8},{12,10},{14,12},{16,14},{18,16},{20... | collective-permute-start | bytes 98312 | tf_op jit(solution)/shard_map/ppermute | solution.py:30
  69.6 0.0 collective-permute-done.11
  69.6 0.0 collective-permute-done.12
  69.7 0.0 collective-permute-done.13
  69.7 4.1 %collective-permute-done.14 = f32[1,8192]{1,0:T(1,128)S(1)} collective-permute-done((f32[1,8192]{1,0:T(1,128)S(1)}, f32[1,8192]{1,0:T(1,128)S(1)}, u32[]{:S(2)}, u32[]{:S(2)}) %collective-permute-start.14) | collective-permute-done | bytes 32800 | tf_op jit(solution)/shard_map/ppermute | solution.py:30
  73.8 0.7 multiply_add_fusion
  74.6 1.9 %collective-permute-start.15 = (f32[1,8192]{1,0:T(1,128)S(1)}, f32[1,8192]{1,0:T(1,128)S(1)}, u32[]{:S(2)}, u32[]{:S(2)}) collective-permute-start(f32[1,8192]{1,0:T(1,128)S(1)} %get-tuple-element.24), channel_id=1, source_target_pairs={{0,2},{2,4},{4,6},{6,8},{8,10},{10,12},{12,14},{14,16},{16,18},{18... | collective-permute-start | bytes 98312 | tf_op jit(solution)/shard_map/ppermute | solution.py:29
  76.5 2.4 %collective-permute-start.16 = (f32[1,8192]{1,0:T(1,128)S(1)}, f32[1,8192]{1,0:T(1,128)S(1)}, u32[]{:S(2)}, u32[]{:S(2)}) collective-permute-start(f32[1,8192]{1,0:T(1,128)S(1)} %get-tuple-element.25), channel_id=1, source_target_pairs={{2,0},{4,2},{6,4},{8,6},{10,8},{12,10},{14,12},{16,14},{18,16},{20... | collective-permute-start | bytes 98312 | tf_op jit(solution)/shard_map/ppermute | solution.py:30
  78.9 0.2 fusion.77
  79.1 0.0 collective-permute-done.15
  79.1 3.5 %collective-permute-done.16 = f32[1,8192]{1,0:T(1,128)S(1)} collective-permute-done((f32[1,8192]{1,0:T(1,128)S(1)}, f32[1,8192]{1,0:T(1,128)S(1)}, u32[]{:S(2)}, u32[]{:S(2)}) %collective-permute-start.16) | collective-permute-done | bytes 32800 | tf_op jit(solution)/shard_map/ppermute | solution.py:30
  82.6 0.8 fusion.65
  83.5 1.9 %collective-permute-start.17 = (f32[1,8192]{1,0:T(1,128)S(1)}, f32[1,8192]{1,0:T(1,128)S(1)}, u32[]{:S(2)}, u32[]{:S(2)}) collective-permute-start(f32[1,8192]{1,0:T(1,128)S(1)} %get-tuple-element.22), channel_id=1, source_target_pairs={{0,2},{2,4},{4,6},{6,8},{8,10},{10,12},{12,14},{14,16},{16,18},{18... | collective-permute-start | bytes 98312 | tf_op jit(solution)/shard_map/ppermute | solution.py:29
  85.4 2.4 %collective-permute-start.18 = (f32[1,8192]{1,0:T(1,128)S(1)}, f32[1,8192]{1,0:T(1,128)S(1)}, u32[]{:S(2)}, u32[]{:S(2)}) collective-permute-start(f32[1,8192]{1,0:T(1,128)S(1)} %get-tuple-element.23), channel_id=1, source_target_pairs={{2,0},{4,2},{6,4},{8,6},{10,8},{12,10},{14,12},{16,14},{18,16},{20... | collective-permute-start | bytes 98312 | tf_op jit(solution)/shard_map/ppermute | solution.py:30
  87.8 0.2 fusion.74
  88.0 0.0 collective-permute-done.17
  88.0 3.5 %collective-permute-done.18 = f32[1,8192]{1,0:T(1,128)S(1)} collective-permute-done((f32[1,8192]{1,0:T(1,128)S(1)}, f32[1,8192]{1,0:T(1,128)S(1)}, u32[]{:S(2)}, u32[]{:S(2)}) %collective-permute-start.18) | collective-permute-done | bytes 32800 | tf_op jit(solution)/shard_map/ppermute | solution.py:30
  91.5 1.5 %fusion.10 = f32[1,16,8192]{2,1,0:T(8,128)} fusion(f32[16,8192]{1,0:T(8,128)S(1)} %get-tuple-element.9, f32[16,8192]{1,0:T(8,128)S(1)} %get-tuple-element.18, f32[1,8192]{1,0:T(1,128)S(1)} %collective-permute-done.18, f32[1,8192]{1,0:T(1,128)S(1)} %collective-permute-done.17, f32[1,8192]{1,0:T(1,128)S(1)} %collective-permute-done, ...), kind=kLoop, calls=%fused_computation.13 | loop fusion | flops 3932160 | bytes 5013312 | tf_op jit(solution)/shard_map/broadcast_in_dim | solution.py:138
  (14 shorter events, 0.3 us)
Async XLA Ops:
  0.0 31.8 %collective-permute-start.1 = (s32[8192]{0:T(1024)}, s32[8192]{0:T(1024)S(1)}, u32[]{:S(2)}, u32[]{:S(2)}) collective-permute-start(s32[8192]{0:T(1024)} %bitcast.64), channel_id=1, source_target_pairs={{0,1},{2,3},{4,5},{6,7},{8,9},{10,11},{12,13},{14,15},{16,17},{18,... | collective-permute-start | bytes 98312 | tf_op jit(solution)/shard_map/ppermute | solution.py:19
  3.1 30.9 %collective-permute-start.2 = (s32[8192]{0:T(1024)}, s32[8192]{0:T(1024)S(1)}, u32[]{:S(2)}, u32[]{:S(2)}) collective-permute-start(s32[8192]{0:T(1024)} %bitcast.78), channel_id=1, source_target_pairs={{0,1},{2,3},{4,5},{6,7},{8,9},{10,11},{12,13},{14,15},{16,17},{18,... | collective-permute-start | bytes 98312 | tf_op jit(solution)/shard_map/ppermute | solution.py:19
  6.1 32.6 %collective-permute-start.5 = (f32[1,8192]{1,0:T(1,128)}, f32[1,8192]{1,0:T(1,128)S(1)}, u32[]{:S(2)}, u32[]{:S(2)}) collective-permute-start(f32[1,8192]{1,0:T(1,128)} %get-tuple-element.43), channel_id=1, source_target_pairs={{0,2},{2,4},{4,6},{6,8},{8,10},{10,12},{12,14},{14,16},{16,18},{18... | collective-permute-start | bytes 98312 | tf_op jit(solution)/shard_map/ppermute | solution.py:29
  10.1 28.6 %collective-permute-start.6 = (f32[1,8192]{1,0:T(1,128)S(1)}, f32[1,8192]{1,0:T(1,128)S(1)}, u32[]{:S(2)}, u32[]{:S(2)}) collective-permute-start(f32[1,8192]{1,0:T(1,128)S(1)} %get-tuple-element.44), channel_id=1, source_target_pairs={{2,0},{4,2},{6,4},{8,6},{10,8},{12,10},{14,12},{16,14},{18,16},{20... | collective-permute-start | bytes 98312 | tf_op jit(solution)/shard_map/ppermute | solution.py:30
  12.0 0.7 copy-start.4
  26.0 4.7 %copy-start = (f32[1,16,8192]{2,1,0:T(8,128)S(1)}, f32[1,16,8192]{2,1,0:T(8,128)}, u32[]{:S(2)}) copy-start(f32[1,16,8192]{2,1,0:T(8,128)} %param.9) | copy-start | bytes 1572868
  26.2 12.5 %collective-permute-start = (f32[1,8192]{1,0:T(1,128)S(1)}, f32[1,8192]{1,0:T(1,128)S(1)}, u32[]{:S(2)}, u32[]{:S(2)}) collective-permute-start(f32[1,8192]{1,0:T(1,128)S(1)} %slice.279), channel_id=1, source_target_pairs={{0,2},{2,4},{4,6},{6,8},{8,10},{10,12},{12,14},{14,16},{16,18},{18... | collective-permute-start | bytes 98312 | tf_op jit(solution)/shard_map/ppermute | solution.py:19
  30.8 1.0 %copy-start.2 = (s32[1,8192]{1,0:T(1,128)S(1)}, s32[1,8192]{1,0:T(1,128)}, u32[]{:S(2)}) copy-start(s32[1,8192]{1,0:T(1,128)} %param.10) | copy-start | bytes 98308
  31.8 2.2 %copy-start.3 = (s32[1,8192]{1,0:T(1,128)S(1)}, s32[1,8192]{1,0:T(1,128)}, u32[]{:S(2)}) copy-start(s32[1,8192]{1,0:T(1,128)} %param.11) | copy-start | bytes 98308
  31.8 6.9 %copy-start.1 = (f32[1,16,8192]{2,1,0:T(8,128)S(1)}, f32[1,16,8192]{2,1,0:T(8,128)}, u32[]{:S(2)}) copy-start(f32[1,16,8192]{2,1,0:T(8,128)} %param.8) | copy-start | bytes 1572868
  32.0 3.2 %collective-permute-start.4 = (f32[8192]{0:T(1024)S(1)}, f32[8192]{0:T(1024)}, u32[]{:S(2)}, u32[]{:S(2)}) collective-permute-start(f32[8192]{0:T(1024)S(1)} %get-tuple-element.8), channel_id=1, source_target_pairs={{0,1},{2,3},{4,5},{6,7},{8,9},{10,11},{12,13},{14,15},{16,17},{18,... | collective-permute-start | bytes 98312 | tf_op jit(solution)/shard_map/ppermute | solution.py:19
  34.0 4.7 %collective-permute-start.3 = (f32[8192]{0:T(1024)S(1)}, f32[8192]{0:T(1024)S(1)}, u32[]{:S(2)}, u32[]{:S(2)}) collective-permute-start(f32[8192]{0:T(1024)S(1)} %get-tuple-element.7), channel_id=1, source_target_pairs={{1,0},{3,2},{5,4},{7,6},{9,8},{11,10},{13,12},{15,14},{17,16},{19,... | collective-permute-start | bytes 98312 | tf_op jit(solution)/shard_map/ppermute | solution.py:19
  40.5 5.3 %collective-permute-start.7 = (f32[1,8192]{1,0:T(1,128)S(1)}, f32[1,8192]{1,0:T(1,128)S(1)}, u32[]{:S(2)}, u32[]{:S(2)}) collective-permute-start(f32[1,8192]{1,0:T(1,128)S(1)} %get-tuple-element.36), channel_id=1, source_target_pairs={{0,2},{2,4},{4,6},{6,8},{8,10},{10,12},{12,14},{14,16},{16,18},{18... | collective-permute-start | bytes 98312 | tf_op jit(solution)/shard_map/ppermute | solution.py:29
  43.7 6.1 %collective-permute-start.8 = (f32[1,8192]{1,0:T(1,128)S(1)}, f32[1,8192]{1,0:T(1,128)S(1)}, u32[]{:S(2)}, u32[]{:S(2)}) collective-permute-start(f32[1,8192]{1,0:T(1,128)S(1)} %get-tuple-element.37), channel_id=1, source_target_pairs={{2,0},{4,2},{6,4},{8,6},{10,8},{12,10},{14,12},{16,14},{18,16},{20... | collective-permute-start | bytes 98312 | tf_op jit(solution)/shard_map/ppermute | solution.py:30
  50.6 4.5 %collective-permute-start.9 = (f32[1,8192]{1,0:T(1,128)S(1)}, f32[1,8192]{1,0:T(1,128)S(1)}, u32[]{:S(2)}, u32[]{:S(2)}) collective-permute-start(f32[1,8192]{1,0:T(1,128)S(1)} %get-tuple-element.32), channel_id=1, source_target_pairs={{0,2},{2,4},{4,6},{6,8},{8,10},{10,12},{12,14},{14,16},{16,18},{18... | collective-permute-start | bytes 98312 | tf_op jit(solution)/shard_map/ppermute | solution.py:29
  52.6 6.1 %collective-permute-start.10 = (f32[1,8192]{1,0:T(1,128)S(1)}, f32[1,8192]{1,0:T(1,128)S(1)}, u32[]{:S(2)}, u32[]{:S(2)}) collective-permute-start(f32[1,8192]{1,0:T(1,128)S(1)} %get-tuple-element.33), channel_id=1, source_target_pairs={{2,0},{4,2},{6,4},{8,6},{10,8},{12,10},{14,12},{16,14},{18,16},{20... | collective-permute-start | bytes 98312 | tf_op jit(solution)/shard_map/ppermute | solution.py:30
  59.6 10.0 %collective-permute-start.11 = (f32[8192]{0:T(1024)S(1)}, f32[8192]{0:T(1024)S(1)}, u32[]{:S(2)}, u32[]{:S(2)}) collective-permute-start(f32[8192]{0:T(1024)S(1)} %get-tuple-element.5), channel_id=1, source_target_pairs={{1,0},{3,2},{5,4},{7,6},{9,8},{11,10},{13,12},{15,14},{17,16},{19,... | collective-permute-start | bytes 98312 | tf_op jit(solution)/shard_map/ppermute | solution.py:19
  61.2 8.4 %collective-permute-start.12 = (f32[8192]{0:T(1024)S(1)}, f32[8192]{0:T(1024)S(1)}, u32[]{:S(2)}, u32[]{:S(2)}) collective-permute-start(f32[8192]{0:T(1024)S(1)} %get-tuple-element.6), channel_id=1, source_target_pairs={{0,1},{2,3},{4,5},{6,7},{8,9},{10,11},{12,13},{14,15},{16,17},{18,... | collective-permute-start | bytes 98312 | tf_op jit(solution)/shard_map/ppermute | solution.py:19
  65.2 4.5 %collective-permute-start.13 = (f32[1,8192]{1,0:T(1,128)S(1)}, f32[1,8192]{1,0:T(1,128)S(1)}, u32[]{:S(2)}, u32[]{:S(2)}) collective-permute-start(f32[1,8192]{1,0:T(1,128)S(1)} %get-tuple-element.28), channel_id=1, source_target_pairs={{0,2},{2,4},{4,6},{6,8},{8,10},{10,12},{12,14},{14,16},{16,18},{18... | collective-permute-start | bytes 98312 | tf_op jit(solution)/shard_map/ppermute | solution.py:29
  67.7 6.1 %collective-permute-start.14 = (f32[1,8192]{1,0:T(1,128)S(1)}, f32[1,8192]{1,0:T(1,128)S(1)}, u32[]{:S(2)}, u32[]{:S(2)}) collective-permute-start(f32[1,8192]{1,0:T(1,128)S(1)} %get-tuple-element.29), channel_id=1, source_target_pairs={{2,0},{4,2},{6,4},{8,6},{10,8},{12,10},{14,12},{16,14},{18,16},{20... | collective-permute-start | bytes 98312 | tf_op jit(solution)/shard_map/ppermute | solution.py:30
  74.6 4.5 %collective-permute-start.15 = (f32[1,8192]{1,0:T(1,128)S(1)}, f32[1,8192]{1,0:T(1,128)S(1)}, u32[]{:S(2)}, u32[]{:S(2)}) collective-permute-start(f32[1,8192]{1,0:T(1,128)S(1)} %get-tuple-element.24), channel_id=1, source_target_pairs={{0,2},{2,4},{4,6},{6,8},{8,10},{10,12},{12,14},{14,16},{16,18},{18... | collective-permute-start | bytes 98312 | tf_op jit(solution)/shard_map/ppermute | solution.py:29
  76.5 6.1 %collective-permute-start.16 = (f32[1,8192]{1,0:T(1,128)S(1)}, f32[1,8192]{1,0:T(1,128)S(1)}, u32[]{:S(2)}, u32[]{:S(2)}) collective-permute-start(f32[1,8192]{1,0:T(1,128)S(1)} %get-tuple-element.25), channel_id=1, source_target_pairs={{2,0},{4,2},{6,4},{8,6},{10,8},{12,10},{14,12},{16,14},{18,16},{20... | collective-permute-start | bytes 98312 | tf_op jit(solution)/shard_map/ppermute | solution.py:30
  83.5 4.5 %collective-permute-start.17 = (f32[1,8192]{1,0:T(1,128)S(1)}, f32[1,8192]{1,0:T(1,128)S(1)}, u32[]{:S(2)}, u32[]{:S(2)}) collective-permute-start(f32[1,8192]{1,0:T(1,128)S(1)} %get-tuple-element.22), channel_id=1, source_target_pairs={{0,2},{2,4},{4,6},{6,8},{8,10},{10,12},{12,14},{14,16},{16,18},{18... | collective-permute-start | bytes 98312 | tf_op jit(solution)/shard_map/ppermute | solution.py:29
  85.4 6.1 %collective-permute-start.18 = (f32[1,8192]{1,0:T(1,128)S(1)}, f32[1,8192]{1,0:T(1,128)S(1)}, u32[]{:S(2)}, u32[]{:S(2)}) collective-permute-start(f32[1,8192]{1,0:T(1,128)S(1)} %get-tuple-element.23), channel_id=1, source_target_pairs={{2,0},{4,2},{6,4},{8,6},{10,8},{12,10},{14,12},{16,14},{18,16},{20... | collective-permute-start | bytes 98312 | tf_op jit(solution)/shard_map/ppermute | solution.py:30
where the time goes:
time: 94 us; the launch traced here: 93.1 us
  starting transfers between devices  45.8 us (49%)
  other arithmetic  22.4 us (24%)
  waiting for transfers between devices  21.3 us (23%)
  local copies, waits for them, and re-layouts  3.3 us (4%)
    ppermute x6, waiting for transfers between devices, padded_2(): after = lax.ppermute(leading, axis, down)  18.7 us
    ppermute x7, starting transfers between devices, passed_along(): return lax.ppermute(block, axis, route)  17.4 us
    ppermute x6, starting transfers between devices, padded_2(): before = lax.ppermute(last, axis, up)  15.4 us
    ppermute x6, starting transfers between devices, padded_2(): after = lax.ppermute(leading, axis, down)  13 us
    add x1, other arithmetic, lookup(): result + jnp.where(class_codes == code, class_table[code], jnp.float32(0.0))  12.7 us
    add x4, other arithmetic, relax_sweep(): return (centre_cells + update, update)  4.03 us
    ppermute x7, waiting for transfers between devices, passed_along(): return lax.ppermute(block, axis, route)  2.6 us
    slice x6, local copies, waits for them, and re-layouts, padded_2(): last = lax.slice_in_dim(shard, length - width, length, axis=dim)  1.92 us
  transfers between devices with their start and end apart: 19, of which 6 were waited for; matrix products, arithmetic and copies ran while one was open for 20% of the time, Pallas kernels for 0%

commit v1 on v0

v1 whole, which is shorter than its diff:
```python
import functools

import jax
import jax.numpy as jnp
from jax import lax
from jax.experimental import pallas as pl
from jax.experimental.pallas import tpu as pltpu
from jax.sharding import PartitionSpec as P

OUTER = 2
SWEEPS = 3
VIA_UNIT = 2.0
LOWER_BOUND = 0.05
UPPER_BOUND = 2.0
LANES = 128


def chebyshev_terms(count):
    centre_value = 0.5 * (UPPER_BOUND + LOWER_BOUND)
    half_width = 0.5 * (UPPER_BOUND - LOWER_BOUND)
    sigma = centre_value / half_width
    rho_last = 1.0 / sigma
    terms = [(0.0, 1.0 / centre_value)]
    for index in range(1, count):
        rho_next = 1.0 / (2.0 * sigma - rho_last)
        terms.append((rho_next * rho_last, 2.0 * rho_next / half_width))
        rho_last = rho_next
    return terms


FACTORS = chebyshev_terms(SWEEPS)


def column_right(row):
    lane = lax.broadcasted_iota(jnp.int32, row.shape, 1)
    turned = pltpu.roll(row, LANES - 1, 1)
    return jnp.where(lane == LANES - 1, pltpu.roll(turned, row.shape[0] - 1, 0), turned)


def column_left(row):
    lane = lax.broadcasted_iota(jnp.int32, row.shape, 1)
    turned = pltpu.roll(row, 1, 1)
    return jnp.where(lane == 0, pltpu.roll(turned, 1, 0), turned)


def beside(x, across):
    return across * column_right(x) + column_left(across * x)


def place():
    return lax.axis_index("tile"), lax.axis_index("layer")


def marked(cells, row, value):
    return jnp.where(cells == row, value, 0.0)


def pick(x_ref, cells, rows):
    total = jnp.zeros(cells.shape, jnp.float32)
    for row in range(rows):
        total = total + marked(cells, row, x_ref[row])
    return total


def weight_of(counts):
    return VIA_UNIT * counts.astype(jnp.float32)


def unpack_kernel(index_ref, table_ref, loads_ref, volts_ref, across_ref, down_ref, loads_out, x_ref):
    rows, cols = loads_ref.shape
    lines = cols // LANES
    tile, _ = place()
    last_tile = tile == lax.axis_size("tile") - 1
    table = jnp.broadcast_to(table_ref[...], (8, LANES))
    lane = lax.broadcasted_iota(jnp.int32, (8, LANES), 1)
    sub = lax.broadcasted_iota(jnp.int32, (8, LANES), 0)
    for top in range(0, rows, 8):
        part = pl.ds(top, 8)
        for line in range(lines):
            here = pl.ds(line * LANES, LANES)
            across = jnp.take_along_axis(table, index_ref[0, part, here], axis=1, mode="promise_in_bounds")
            if line == lines - 1:
                across = jnp.where(lane == LANES - 1, 0.0, across)
            across_ref[part, line, :] = across
            down = jnp.take_along_axis(table, index_ref[1, part, here], axis=1, mode="promise_in_bounds")
            if top + 8 == rows:
                down = jnp.where((sub == 7) & last_tile, 0.0, down)
            down_ref[part, line, :] = down
            loads_out[part, line, :] = loads_ref[part, here]
            x_ref[part, line, :] = volts_ref[part, here]


def links_kernel(single, rows, x_ref, own_ref, count_ref, low_ref, *out_refs):
    _, layer = place()
    own, low = own_ref[...], low_ref[...]
    weight = weight_of(count_ref[...])
    if single:
        out_refs[0][0] = pick(x_ref, jnp.where(layer == 0, own, low), rows)
        out_refs[0][1] = weight
    else:
        out_refs[0][0] = pick(x_ref, own, rows)
        out_refs[0][1] = weight
        out_refs[1][0] = pick(x_ref, low, rows)


def via_terms(own_ref, count_ref, low_ref, low_weight, from_above, from_below):
    _, layer = place()
    on_top = layer == lax.axis_size("layer") - 1
    own_weight = weight_of(count_ref[...])
    low_weight = jnp.where(layer == 0, 0.0, low_weight)
    own_source = own_weight * jnp.where(on_top, 1.0, from_above)
    low_source = low_weight * from_below
    own, low = own_ref[...], low_ref[...]

    def via(row):
        return marked(own, row, own_weight) + marked(low, row, low_weight)

    def source(row):
        return marked(own, row, own_source) + marked(low, row, low_source)

    return via, source


def send_by_parity(first_ref, second_ref, slot, top, bottom):
    tile, _ = place()
    even = lax.rem(tile, 2) == 0
    first_ref[slot] = jnp.where(even, bottom, top)
    second_ref[slot] = jnp.where(even, top, bottom)


def taken_by_parity(first_ref, second_ref, slot):
    tile, _ = place()
    even = lax.rem(tile, 2) == 0
    first, second = first_ref[slot], second_ref[slot]
    return jnp.where(even, second, first), jnp.where(even, first, second)


def edge_one(x_ref, across_ref, down_ref, row, right_side, inverse):
    x = x_ref[row]
    flow = beside(x, across_ref[row]) + down_ref[row] * x_ref[row + 1] + down_ref[row - 1] * x_ref[row - 1]
    return x + FACTORS[0][1] * (inverse * (right_side + flow) - x)


def edges(x_ref, across_ref, down_ref, right_side, inverse_1, inverse_n, rows):
    top_side, bottom_side = right_side(0), right_side(rows - 1)
    below_top = down_ref[0]
    above_bottom = down_ref[rows - 2]
    top_1 = edge_one(x_ref, across_ref, down_ref, 1, right_side(1), inverse_1)
    bottom_1 = edge_one(x_ref, across_ref, down_ref, rows - 2, right_side(rows - 2), inverse_n)
    return (
        (x_ref[0], x_ref[rows - 1]),
        (top_side + below_top * x_ref[1], bottom_side + above_bottom * x_ref[rows - 2]),
        (top_side + below_top * top_1, bottom_side + above_bottom * bottom_1),
    )


def first_edges_kernel(
    rows, x_ref, across_ref, down_ref, loads_ref, own_ref, count_ref, low_ref, above_ref, below_ref, first_ref, second_ref
):
    via, source = via_terms(own_ref, count_ref, low_ref, below_ref[1], above_ref[0], below_ref[0])

    def right_side(row):
        return source(row) - loads_ref[row]

    def diagonal(row, links):
        across = across_ref[row]
        total = across + column_left(across)
        for link in links:
            total = total + down_ref[link]
        return total + via(row)

    values = edges(
        x_ref,
        across_ref,
        down_ref,
        right_side,
        1.0 / diagonal(1, (0, 1)),
        1.0 / diagonal(rows - 2, (rows - 3, rows - 2)),
        rows,
    )
    for slot, (top, bottom) in enumerate(values):
        send_by_parity(first_ref, second_ref, slot, top, bottom)
    send_by_parity(first_ref, second_ref, 3, diagonal(0, (0,)), diagonal(rows - 1, (rows - 2,)))
    send_by_parity(first_ref, second_ref, 4, across_ref[0], across_ref[rows - 1])
    send_by_parity(first_ref, second_ref, 5, down_ref[0], down_ref[rows - 1])


def next_edges_kernel(
    rows,
    x_ref,
    across_ref,
    down_ref,
    loads_ref,
    inverse_ref,
    own_ref,
    count_ref,
    low_ref,
    weight_ref,
    above_ref,
    below_ref,
    first_ref,
    second_ref,
):
    _, source = via_terms(own_ref, count_ref, low_ref, weight_ref[1], above_ref[0], below_ref[0])

    def right_side(row):
        return source(row) - loads_ref[row]

    values = edges(x_ref, across_ref, down_ref, right_side, inverse_ref[2], inverse_ref[rows - 1], rows)
    for slot, (top, bottom) in enumerate(values):
        send_by_parity(first_ref, second_ref, slot, top, bottom)


def step_body(x_ref, across_ref, down_ref, side_ref, inverse_ref, halo, even_ref, odd_ref, update_ref, write, rows):
    (top_x, top_q, top_across, link), (low_x, low_q, low_across) = halo
    low_link = down_ref[rows - 1]

    def fill(row, carry):
        even_ref[row + 1] = x_ref[row]
        return carry

    even_ref[0] = top_x
    even_ref[rows + 1] = low_x
    lax.fori_loop(0, rows, fill, 0)
    up_ref = down_ref
    buffers = [even_ref, odd_ref, even_ref, odd_ref]
    for sweep in range(SWEEPS):
        source, target = buffers[sweep], buffers[sweep + 1]
        keep, gain = FACTORS[sweep]
        last = sweep == SWEEPS - 1

        def relax(at, flow, side):
            x = source[at]
            update = gain * (inverse_ref[at] * (side + flow) - x)
            if sweep > 0:
                update = update + keep * update_ref[at]
            if not last:
                update_ref[at] = update
            return x + update

        if not last:
            flow = beside(source[0], top_across) + link * source[1]
            target[0] = relax(0, flow, top_q[sweep])
            flow = beside(source[rows + 1], low_across) + low_link * source[rows]
            target[rows + 1] = relax(rows + 1, flow, low_q[sweep])

        def one_row(row, above):
            flow = beside(source[row + 1], across_ref[row])
            flow = flow + down_ref[row] * source[row + 2] + above * source[row]
            value = relax(row + 1, flow, side_ref[row])
            if last:
                write(row, value)
            else:
                target[row + 1] = value

        one_row(0, link)

        def body(row, carry):
            one_row(row, up_ref[row - 1])
            return carry

        lax.fori_loop(1, rows, body, 0)


def first_step_kernel(
    single,
    rows,
    x_ref,
    across_ref,
    down_ref,
    loads_ref,
    own_ref,
    count_ref,
    low_ref,
    above_ref,
    below_ref,
    first_ref,
    second_ref,
    next_ref,
    inverse_ref,
    halo_ref,
    *rest,
):
    sends, (side_ref, even_ref, odd_ref, update_ref) = rest[:-4], rest[-4:]
    tile, layer = place()
    via, source = via_terms(own_ref, count_ref, low_ref, below_ref[1], above_ref[0], below_ref[0])
    top_x, low_x = taken_by_parity(first_ref, second_ref, 0)
    top_q0, low_q0 = taken_by_parity(first_ref, second_ref, 1)
    top_q1, low_q1 = taken_by_parity(first_ref, second_ref, 2)
    top_diag, low_diag = taken_by_parity(first_ref, second_ref, 3)
    top_across, low_across = taken_by_parity(first_ref, second_ref, 4)
    link, _ = taken_by_parity(first_ref, second_ref, 5)
    link = jnp.where(tile == 0, 0.0, link)
    halo_ref[0] = top_across
    halo_ref[1] = low_across
    halo_ref[2] = link
    inverse_ref[0] = 1.0 / (top_diag + link)
    inverse_ref[rows + 1] = 1.0 / (low_diag + down_ref[rows - 1])

    def setup(row, above):
        across = across_ref[row]
        diagonal = across + column_left(across) + down_ref[row] + above + via(row)
        inverse_ref[row + 1] = 1.0 / diagonal
        side_ref[row] = source(row) - loads_ref[row]

    setup(0, link)

    def body(row, carry):
        setup(row, down_ref[row - 1])
        return carry

    lax.fori_loop(1, rows, body, 0)

    def write(row, value):
        next_ref[row] = value

    halo = (top_x, (top_q0, top_q1), top_across, link), (low_x, (low_q0, low_q1), low_across)
    step_body(x_ref, across_ref, down_ref, side_ref, inverse_ref, halo, even_ref, odd_ref, update_ref, write, rows)
    own, low = own_ref[...], low_ref[...]
    if single:
        sends[0][0] = pick(next_ref, jnp.where(layer == 0, own, low), rows)
    else:
        sends[0][0] = pick(next_ref, own, rows)
        sends[1][0] = pick(next_ref, low, rows)


def last_step_kernel(
    rows,
    x_ref,
    across_ref,
    down_ref,
    loads_ref,
    inverse_ref,
    halo_ref,
    own_ref,
    count_ref,
    low_ref,
    weight_ref,
    above_ref,
    below_ref,
    first_ref,
    second_ref,
    out_ref,
    side_ref,
    even_ref,
    odd_ref,
    update_ref,
    last_ref,
):
    _, source = via_terms(own_ref, count_ref, low_ref, weight_ref[1], above_ref[0], below_ref[0])
    top_x, low_x = taken_by_parity(first_ref, second_ref, 0)
    top_q0, low_q0 = taken_by_parity(first_ref, second_ref, 1)
    top_q1, low_q1 = taken_by_parity(first_ref, second_ref, 2)

    def body(row, carry):
        side_ref[row] = source(row) - loads_ref[row]
        return carry

    lax.fori_loop(0, rows, body, 0)

    def write(row, value):
        last_ref[row] = value

    halo = (top_x, (top_q0, top_q1), halo_ref[0], halo_ref[2]), (low_x, (low_q0, low_q1), halo_ref[1])
    step_body(x_ref, across_ref, down_ref, side_ref, inverse_ref, halo, even_ref, odd_ref, update_ref, write, rows)
    for top in range(0, rows, 8):
        for line in range(out_ref.shape[1] // LANES):
            out_ref[pl.ds(top, 8), pl.ds(line * LANES, LANES)] = last_ref[pl.ds(top, 8), line, :]


def call(kernel, name, outs, scratch, *args):
    spec = pl.BlockSpec(memory_space=pltpu.VMEM)
    return pl.pallas_call(
        kernel,
        out_shape=[jax.ShapeDtypeStruct(shape, jnp.float32) for shape in outs],
        in_specs=[spec] * len(args),
        out_specs=[spec] * len(outs),
        scratch_shapes=[pltpu.VMEM(shape, jnp.float32) for shape in scratch],
        compiler_params=pltpu.CompilerParams(vmem_limit_bytes=40 * 1024 * 1024),
        name=name,
    )(*args)


def routes(tiles, layers):
    def at(tile, layer):
        return tile * layers + layer % layers

    everywhere = [(tile, layer) for tile in range(tiles) for layer in range(layers)]
    up = [(at(t, l), at(t, l + 1)) for t, l in everywhere]
    down = [(at(t, l), at(t, l - 1)) for t, l in everywhere]
    first, second = [], []
    for t, l in everywhere:
        first.append((at(t, l), at(t ^ 1, l)))
        beyond = t + 1 if t % 2 else t - 1
        if 0 <= beyond < tiles:
            second.append((at(t, l), at(beyond, l)))
        else:
            second.append((at(t, l), at(t, l + 1)))
    return up, down, first, second


def local(class_index, class_conductance, loads, start_volts, via_cells, via_counts):
    rows, cols = loads.shape[1:]
    lines = cols // LANES
    tiles, layers = lax.axis_size("tile"), lax.axis_size("layer")
    up, down, first, second = routes(tiles, layers)
    single = layers == 2
    move = functools.partial(lax.ppermute, axis_name=("tile", "layer"))
    field = (rows, lines, LANES)
    padded = (rows + 2, lines, LANES)

    def rows_of(count):
        return (count, lines, LANES)

    def between_layers(sends):
        if single:
            got = move(sends[0], perm=up)
            return got, got
        return move(sends[1], perm=down), move(sends[0], perm=up)

    own = via_cells.reshape(lines, LANES)
    counts = via_counts.reshape(lines, LANES)
    low = move(own, perm=up)
    table = jnp.pad(class_conductance, ((0, 0), (0, LANES - class_conductance.shape[1])))
    across, downward, load, x = call(
        unpack_kernel, "unpack", [field] * 4, [], class_index[0], table, loads[0], start_volts[0]
    )
    sends = call(
        functools.partial(links_kernel, single, rows),
        "links",
        [rows_of(2)] if single else [rows_of(2), rows_of(1)],
        [],
        x,
        own,
        counts,
        low,
    )
    above, below = between_layers(sends)
    weights = below
    sent = call(
        functools.partial(first_edges_kernel, rows),
        "first_edges",
        [rows_of(6)] * 2,
        [],
        *(x, across, downward, load, own, counts, low, above, below),
    )
    got = [move(sent[0], perm=first), move(sent[1], perm=second)]
    x, inverse, halo, *sends = call(
        functools.partial(first_step_kernel, single, rows),
        "first_step",
        [field, padded, rows_of(3)] + ([rows_of(1)] if single else [rows_of(1)] * 2),
        [field, padded, padded, padded],
        *(x, across, downward, load, own, counts, low, above, below, *got),
    )
    above, below = between_layers(sends)
    sent = call(
        functools.partial(next_edges_kernel, rows),
        "next_edges",
        [rows_of(3)] * 2,
        [],
        *(x, across, downward, load, inverse, own, counts, low, weights, above, below),
    )
    got = [move(sent[0], perm=first), move(sent[1], perm=second)]
    (volts,) = call(
        functools.partial(last_step_kernel, rows),
        "last_step",
        [(rows, cols)],
        [field, padded, padded, padded, field],
        *(x, across, downward, load, inverse, halo, own, counts, low, weights, above, below, *got),
    )
    return volts[None]


def solution(mesh):
    placed = (
        P("layer", None, "tile", None),
        P("layer", None),
        P("layer", "tile", None),
        P("layer", "tile", None),
        P("layer", "tile"),
        P("layer", "tile"),
    )
    return jax.shard_map(
        local, mesh=mesh, in_specs=placed, out_specs=P("layer", "tile", None), check_vma=False
    )
```

time: 94 us -> 41.2 us (0.44)
  starting transfers between devices: 45.8 us -> 8.53 us
  other arithmetic: 22.4 us -> 0 us
  Pallas kernels: 0 us -> 14.8 us
  waiting for transfers between devices: 21.3 us -> 14.3 us
    ppermute x19 -> x7, starting transfers between devices: 45.8 us -> 8.53 us  [the longest x4 6.17 us: local(): got = [move(sent[0], perm=first), move(sent[1], perm=second)]]
    add x5 -> x0, other arithmetic: 16.7 us -> none  [the longest x1 12.7 us: lookup(): result + jnp.where(class_codes == code, class_table[code], jnp.float32(0.0))]
    pallas_call x0 -> x6, Pallas kernels: none -> 14.8 us  [call(): pl.pallas_call(kernel, out_shape=[jax.ShapeDtypeStruct(shape, jnp.float32...]
    ppermute x19 -> x7, waiting for transfers between devices: 21.3 us -> 14.3 us  [the longest x4 9.43 us: local(): got = [move(sent[0], perm=first), move(sent[1], perm=second)]]
    unnamed x10 -> x12, local copies, waits for them, and re-layouts: 0.66 us -> 3.31 us
    slice x8 -> x0, local copies, waits for them, and re-layouts: 2.64 us -> none  [the longest x6 1.92 us: padded_2(): last = lax.slice_in_dim(shard, length - width, length, axis=dim)]
    slice x6 -> x0, other arithmetic: 2.01 us -> none  [the longest x5 1.01 us: neighbours(): right_flow = jnp.pad(centre_cells[:, 1:], ((0, 0), (0, 1))) * across]
    broadcast_in_dim x1 -> x0, other arithmetic: 1.55 us -> none  [local(): return volts[None]]
  transfers between devices with their start and end apart: 19 -> 7, of which waited for: 6 -> 5; matrix products, arithmetic and copies ran while one was open for 20% -> 0% of each run, Pallas kernels for 0% -> 4%
where the time goes in v1:
time: 41.2 us; the launch traced here: 41 us
  Pallas kernels  14.8 us (36%)
  waiting for transfers between devices  14.3 us (35%)
  starting transfers between devices  8.53 us (21%)
  local copies, waits for them, and re-layouts  3.32 us (8%)
    pallas_call x6, Pallas kernels, call(): pl.pallas_call(kernel, out_shape=[jax.ShapeDtypeStruct(shape, jnp.float32...  14.8 us
    ppermute x4, waiting for transfers between devices, local(): got = [move(sent[0], perm=first), move(sent[1], perm=second)]  9.43 us
    ppermute x4, starting transfers between devices, local(): got = [move(sent[0], perm=first), move(sent[1], perm=second)]  6.17 us
    ppermute x2, waiting for transfers between devices, between_layers(): got = move(sends[0], perm=up)  4.86 us
    unnamed x12, local copies, waits for them, and re-layouts  3.31 us
    ppermute x1, starting transfers between devices, local(): low = move(own, perm=up)  1.21 us
    ppermute x2, starting transfers between devices, between_layers(): got = move(sends[0], perm=up)  1.15 us
  transfers between devices with their start and end apart: 7, of which 5 were waited for; matrix products, arithmetic and copies ran while one was open for 0% of the time, Pallas kernels for 4%

profile of v1, /device:TPU:5, one launch (start us, length us, event | category | flops | bytes accessed | tf_op | source)
XLA Modules:
  0.0 41.0 jit_solution(14620572700350746430)
XLA Ops:
  0.0 0.0 copy-start.5
  0.0 1.2 %collective-permute-start = (s32[64,128]{1,0:T(8,128)}, s32[64,128]{1,0:T(8,128)S(1)}, u32[]{:S(2)}, u32[]{:S(2)}) collective-permute-start(s32[64,128]{1,0:T(8,128)} %bitcast.7), channel_id=1, source_target_pairs={{0,1},{1,0},{2,3},{3,2},{4,5},{5,4},{6,7},{7,6},{8,9},{9,8},{10,11... | collective-permute-start | bytes 98312 | tf_op jit(solution)/shard_map/ppermute | solution.py:423
  1.2 0.0 copy-done.5
  1.2 0.0 copy-start
  1.2 1.2 %copy-done = s32[1,2,16,8192]{3,2,1,0:T(8,128)S(1)} copy-done((s32[1,2,16,8192]{3,2,1,0:T(8,128)S(1)}, s32[1,2,16,8192]{3,2,1,0:T(8,128)}, u32[]{:S(2)}) %copy-start) | copy-done | bytes 1048600
  2.4 0.0 copy-start.3
  2.5 1.0 %copy-done.3 = f32[1,16,8192]{2,1,0:T(8,128)S(1)} copy-done((f32[1,16,8192]{2,1,0:T(8,128)S(1)}, f32[1,16,8192]{2,1,0:T(8,128)}, u32[]{:S(2)}) %copy-start.3) | copy-done | bytes 524312
  3.5 0.0 copy-start.4
  3.5 1.0 %copy-done.4 = f32[1,16,8192]{2,1,0:T(8,128)S(1)} copy-done((f32[1,16,8192]{2,1,0:T(8,128)S(1)}, f32[1,16,8192]{2,1,0:T(8,128)}, u32[]{:S(2)}) %copy-start.4) | copy-done | bytes 524312
  4.5 0.0 copy-start.1
  4.5 0.0 copy-start.2
  4.5 1.6 %unpack.1 = (f32[16,64,128]{2,1,0:T(8,128)S(1)}, f32[16,64,128]{2,1,0:T(8,128)S(1)}, f32[16,64,128]{2,1,0:T(8,128)S(1)}, f32[16,64,128]{2,1,0:T(8,128)S(1)}) custom-call(s32[2,16,8192]{2,1,0:T(8,128)S(1)} %bitcast.6, f32[1,128]{1,0:T(1,128)S(1)} %pad.4.table_ref, f32[16,8192]{1,0:T(8,128)S(1)} %bitcast.18, f32[16,8192]{1,0:T(8,128)S(1)} %bitcast.19), custom_call_target="tpu_custom_call" | custom-call | tf_op jit(solution)/shard_map/unpack/pallas_call | solution.py:373
  6.2 0.0 collective-permute-done.low_ref
  6.2 0.0 copy-done.1
  6.2 0.0 copy-done.2
  6.2 0.1 links.1
  6.3 0.7 %collective-permute-start.1 = (f32[2,64,128]{2,1,0:T(8,128)S(1)}, f32[2,64,128]{2,1,0:T(8,128)S(1)}, u32[]{:S(2)}, u32[]{:S(2)}) collective-permute-start(f32[2,64,128]{2,1,0:T(8,128)S(1)} %links.1), channel_id=1, source_target_pairs={{0,1},{1,0},{2,3},{3,2},{4,5},{5,4},{6,7},{7,6},{8,9},{9,8},{10,11... | collective-permute-start | bytes 196616 | tf_op jit(solution)/shard_map/ppermute | solution.py:417
  7.0 2.5 %collective-permute-done.1.above_ref.below_ref.weight_ref = f32[2,64,128]{2,1,0:T(8,128)S(1)} collective-permute-done((f32[2,64,128]{2,1,0:T(8,128)S(1)}, f32[2,64,128]{2,1,0:T(8,128)S(1)}, u32[]{:S(2)}, u32[]{:S(2)}) %collective-permute-start.1) | collective-permute-done | bytes 65568 | tf_op jit(solution)/shard_map/ppermute | solution.py:417
  9.5 0.2 first_edges.1
  9.7 2.2 %collective-permute-start.2 = (f32[6,64,128]{2,1,0:T(8,128)S(1)}, f32[6,64,128]{2,1,0:T(8,128)S(1)}, u32[]{:S(2)}, u32[]{:S(2)}) collective-permute-start(f32[6,64,128]{2,1,0:T(8,128)S(1)} %get-tuple-element.21), channel_id=1, source_target_pairs={{0,2},{1,3},{2,0},{3,1},{4,6},{5,7},{6,4},{7,5},{8,10},{9,11},{10,... | collective-permute-start | bytes 589832 | tf_op jit(solution)/shard_map/ppermute | solution.py:447
  11.8 1.2 %collective-permute-start.3 = (f32[6,64,128]{2,1,0:T(8,128)S(1)}, f32[6,64,128]{2,1,0:T(8,128)S(1)}, u32[]{:S(2)}, u32[]{:S(2)}) collective-permute-start(f32[6,64,128]{2,1,0:T(8,128)S(1)} %get-tuple-element.22), channel_id=1, source_target_pairs={{0,1},{1,0},{2,4},{3,5},{4,2},{5,3},{6,8},{7,9},{8,6},{9,7},{10,12... | collective-permute-start | bytes 589832 | tf_op jit(solution)/shard_map/ppermute | solution.py:447
  13.0 0.0 collective-permute-done.2.first_ref
  13.0 4.9 %collective-permute-done.3.second_ref = f32[6,64,128]{2,1,0:T(8,128)S(1)} collective-permute-done((f32[6,64,128]{2,1,0:T(8,128)S(1)}, f32[6,64,128]{2,1,0:T(8,128)S(1)}, u32[]{:S(2)}, u32[]{:S(2)}) %collective-permute-start.3) | collective-permute-done | bytes 196640 | tf_op jit(solution)/shard_map/ppermute | solution.py:447
  17.9 6.5 %first_step.1 = (f32[16,64,128]{2,1,0:T(8,128)S(1)}, f32[18,64,128]{2,1,0:T(8,128)S(1)}, f32[3,64,128]{2,1,0:T(8,128)S(1)}, f32[1,64,128]{2,1,0:T(8,128)S(1)}) custom-call(f32[16,64,128]{2,1,0:T(8,128)S(1)} %get-tuple-element.17.x_ref, f32[16,64,128]{2,1,0:T(8,128)S(1)} %get-tuple-element.18.across_ref, f32[16,64,128]{2,1,0:T(8,128)S(1)} %get-tuple-element.19.down_ref, ...), custom_call_target="tpu_custom_call" | custom-call | tf_op jit(solution)/shard_map/first_step/pallas_call | solution.py:373
  24.4 0.4 %collective-permute-start.4 = (f32[1,64,128]{2,1,0:T(8,128)S(1)}, f32[1,64,128]{2,1,0:T(8,128)S(1)}, u32[]{:S(2)}, u32[]{:S(2)}) collective-permute-start(f32[1,64,128]{2,1,0:T(8,128)S(1)} %get-tuple-element.26), channel_id=1, source_target_pairs={{0,1},{1,0},{2,3},{3,2},{4,5},{5,4},{6,7},{7,6},{8,9},{9,8},{10,11... | collective-permute-start | bytes 98312 | tf_op jit(solution)/shard_map/ppermute | solution.py:417
  24.9 2.4 %collective-permute-done.4.above_ref.below_ref = f32[1,64,128]{2,1,0:T(8,128)S(1)} collective-permute-done((f32[1,64,128]{2,1,0:T(8,128)S(1)}, f32[1,64,128]{2,1,0:T(8,128)S(1)}, u32[]{:S(2)}, u32[]{:S(2)}) %collective-permute-start.4) | collective-permute-done | bytes 32800 | tf_op jit(solution)/shard_map/ppermute | solution.py:417
  27.3 0.1 next_edges.1
  27.4 2.4 %collective-permute-start.5 = (f32[3,64,128]{2,1,0:T(8,128)S(1)}, f32[3,64,128]{2,1,0:T(8,128)S(1)}, u32[]{:S(2)}, u32[]{:S(2)}) collective-permute-start(f32[3,64,128]{2,1,0:T(8,128)S(1)} %get-tuple-element.27), channel_id=1, source_target_pairs={{0,2},{1,3},{2,0},{3,1},{4,6},{5,7},{6,4},{7,5},{8,10},{9,11},{10,... | collective-permute-start | bytes 294920 | tf_op jit(solution)/shard_map/ppermute | solution.py:463
  29.8 0.4 collective-permute-start.6
  30.2 0.5 %collective-permute-done.5.first_ref = f32[3,64,128]{2,1,0:T(8,128)S(1)} collective-permute-done((f32[3,64,128]{2,1,0:T(8,128)S(1)}, f32[3,64,128]{2,1,0:T(8,128)S(1)}, u32[]{:S(2)}, u32[]{:S(2)}) %collective-permute-start.5) | collective-permute-done | bytes 98336 | tf_op jit(solution)/shard_map/ppermute | solution.py:463
  30.7 4.0 %collective-permute-done.6.second_ref = f32[3,64,128]{2,1,0:T(8,128)S(1)} collective-permute-done((f32[3,64,128]{2,1,0:T(8,128)S(1)}, f32[3,64,128]{2,1,0:T(8,128)S(1)}, u32[]{:S(2)}, u32[]{:S(2)}) %collective-permute-start.6) | collective-permute-done | bytes 98336 | tf_op jit(solution)/shard_map/ppermute | solution.py:463
  34.7 6.2 %last_step.1 = f32[16,8192]{1,0:T(8,128)} custom-call(f32[16,64,128]{2,1,0:T(8,128)S(1)} %get-tuple-element.23.x_ref, f32[16,64,128]{2,1,0:T(8,128)S(1)} %get-tuple-element.18.across_ref, f32[16,64,128]{2,1,0:T(8,128)S(1)} %get-tuple-element.19.down_ref, f32[16,64,128]{2,1,0:T(8,128)S(1)} %get-tuple-element.20.loads_ref, ...), custom_call_target="tpu_custom_call" | custom-call | tf_op jit(solution)/shard_map/last_step/pallas_call | solution.py:373
  (1 shorter events, 0.0 us)
Async XLA Ops:
  0.0 1.2 %copy-start.5 = (f32[1,16]{1,0:T(1,128)S(1)}, f32[1,16]{1,0:T(1,128)}, u32[]{:S(2)}) copy-start(f32[1,16]{1,0:T(1,128)} %param.7) | copy-start | bytes 196
  0.0 6.2 %collective-permute-start = (s32[64,128]{1,0:T(8,128)}, s32[64,128]{1,0:T(8,128)S(1)}, u32[]{:S(2)}, u32[]{:S(2)}) collective-permute-start(s32[64,128]{1,0:T(8,128)} %bitcast.7), channel_id=1, source_target_pairs={{0,1},{1,0},{2,3},{3,2},{4,5},{5,4},{6,7},{7,6},{8,9},{9,8},{10,11... | collective-permute-start | bytes 98312 | tf_op jit(solution)/shard_map/ppermute | solution.py:423
  1.2 1.2 %copy-start = (s32[1,2,16,8192]{3,2,1,0:T(8,128)S(1)}, s32[1,2,16,8192]{3,2,1,0:T(8,128)}, u32[]{:S(2)}) copy-start(s32[1,2,16,8192]{3,2,1,0:T(8,128)} %param.6) | copy-start | bytes 3145732
  2.4 1.0 %copy-start.3 = (f32[1,16,8192]{2,1,0:T(8,128)S(1)}, f32[1,16,8192]{2,1,0:T(8,128)}, u32[]{:S(2)}) copy-start(f32[1,16,8192]{2,1,0:T(8,128)} %param.8) | copy-start | bytes 1572868
  3.5 1.0 %copy-start.4 = (f32[1,16,8192]{2,1,0:T(8,128)S(1)}, f32[1,16,8192]{2,1,0:T(8,128)}, u32[]{:S(2)}) copy-start(f32[1,16,8192]{2,1,0:T(8,128)} %param.9) | copy-start | bytes 1572868
  4.5 1.7 %copy-start.1 = (s32[1,8192]{1,0:T(1,128)S(1)}, s32[1,8192]{1,0:T(1,128)}, u32[]{:S(2)}) copy-start(s32[1,8192]{1,0:T(1,128)} %param.10) | copy-start | bytes 98308
  4.5 1.7 %copy-start.2 = (s32[1,8192]{1,0:T(1,128)S(1)}, s32[1,8192]{1,0:T(1,128)}, u32[]{:S(2)}) copy-start(s32[1,8192]{1,0:T(1,128)} %param.11) | copy-start | bytes 98308
  6.3 3.2 %collective-permute-start.1 = (f32[2,64,128]{2,1,0:T(8,128)S(1)}, f32[2,64,128]{2,1,0:T(8,128)S(1)}, u32[]{:S(2)}, u32[]{:S(2)}) collective-permute-start(f32[2,64,128]{2,1,0:T(8,128)S(1)} %links.1), channel_id=1, source_target_pairs={{0,1},{1,0},{2,3},{3,2},{4,5},{5,4},{6,7},{7,6},{8,9},{9,8},{10,11... | collective-permute-start | bytes 196616 | tf_op jit(solution)/shard_map/ppermute | solution.py:417
  9.7 3.4 %collective-permute-start.2 = (f32[6,64,128]{2,1,0:T(8,128)S(1)}, f32[6,64,128]{2,1,0:T(8,128)S(1)}, u32[]{:S(2)}, u32[]{:S(2)}) collective-permute-start(f32[6,64,128]{2,1,0:T(8,128)S(1)} %get-tuple-element.21), channel_id=1, source_target_pairs={{0,2},{1,3},{2,0},{3,1},{4,6},{5,7},{6,4},{7,5},{8,10},{9,11},{10,... | collective-permute-start | bytes 589832 | tf_op jit(solution)/shard_map/ppermute | solution.py:447
  11.8 6.1 %collective-permute-start.3 = (f32[6,64,128]{2,1,0:T(8,128)S(1)}, f32[6,64,128]{2,1,0:T(8,128)S(1)}, u32[]{:S(2)}, u32[]{:S(2)}) collective-permute-start(f32[6,64,128]{2,1,0:T(8,128)S(1)} %get-tuple-element.22), channel_id=1, source_target_pairs={{0,1},{1,0},{2,4},{3,5},{4,2},{5,3},{6,8},{7,9},{8,6},{9,7},{10,12... | collective-permute-start | bytes 589832 | tf_op jit(solution)/shard_map/ppermute | solution.py:447
  24.4 2.8 %collective-permute-start.4 = (f32[1,64,128]{2,1,0:T(8,128)S(1)}, f32[1,64,128]{2,1,0:T(8,128)S(1)}, u32[]{:S(2)}, u32[]{:S(2)}) collective-permute-start(f32[1,64,128]{2,1,0:T(8,128)S(1)} %get-tuple-element.26), channel_id=1, source_target_pairs={{0,1},{1,0},{2,3},{3,2},{4,5},{5,4},{6,7},{7,6},{8,9},{9,8},{10,11... | collective-permute-start | bytes 98312 | tf_op jit(solution)/shard_map/ppermute | solution.py:417
  27.4 3.3 %collective-permute-start.5 = (f32[3,64,128]{2,1,0:T(8,128)S(1)}, f32[3,64,128]{2,1,0:T(8,128)S(1)}, u32[]{:S(2)}, u32[]{:S(2)}) collective-permute-start(f32[3,64,128]{2,1,0:T(8,128)S(1)} %get-tuple-element.27), channel_id=1, source_target_pairs={{0,2},{1,3},{2,0},{3,1},{4,6},{5,7},{6,4},{7,5},{8,10},{9,11},{10,... | collective-permute-start | bytes 294920 | tf_op jit(solution)/shard_map/ppermute | solution.py:463
  29.8 4.9 %collective-permute-start.6 = (f32[3,64,128]{2,1,0:T(8,128)S(1)}, f32[3,64,128]{2,1,0:T(8,128)S(1)}, u32[]{:S(2)}, u32[]{:S(2)}) collective-permute-start(f32[3,64,128]{2,1,0:T(8,128)S(1)} %get-tuple-element.28), channel_id=1, source_target_pairs={{0,1},{1,0},{2,4},{3,5},{4,2},{5,3},{6,8},{7,9},{8,6},{9,7},{10,12... | collective-permute-start | bytes 294920 | tf_op jit(solution)/shard_map/ppermute | solution.py:463

commit v2 on v1

v2 whole, which is shorter than its diff:
```python
import functools

import jax
import jax.numpy as jnp
from jax import lax
from jax.experimental import pallas as pl
from jax.experimental.pallas import tpu as pltpu
from jax.sharding import PartitionSpec as P

OUTER = 2
SWEEPS = 3
VIA_UNIT = 2.0
LOWER_BOUND = 0.05
UPPER_BOUND = 2.0
LANES = 128


def chebyshev_terms(count):
    centre_value = 0.5 * (UPPER_BOUND + LOWER_BOUND)
    half_width = 0.5 * (UPPER_BOUND - LOWER_BOUND)
    sigma = centre_value / half_width
    rho_last = 1.0 / sigma
    terms = [(0.0, 1.0 / centre_value)]
    for index in range(1, count):
        rho_next = 1.0 / (2.0 * sigma - rho_last)
        terms.append((rho_next * rho_last, 2.0 * rho_next / half_width))
        rho_last = rho_next
    return terms


FACTORS = chebyshev_terms(SWEEPS)


def column_right(row):
    lane = lax.broadcasted_iota(jnp.int32, row.shape, 1)
    turned = pltpu.roll(row, LANES - 1, 1)
    return jnp.where(lane == LANES - 1, pltpu.roll(turned, row.shape[0] - 1, 0), turned)


def column_left(row):
    lane = lax.broadcasted_iota(jnp.int32, row.shape, 1)
    turned = pltpu.roll(row, 1, 1)
    return jnp.where(lane == 0, pltpu.roll(turned, 1, 0), turned)


def beside(x, across):
    return across * column_right(x) + column_left(across * x)


def place():
    return lax.axis_index("tile"), lax.axis_index("layer")


def marked(cells, row, value):
    return jnp.where(cells == row, value, 0.0)


def pick(x_ref, cells, rows):
    total = jnp.zeros(cells.shape, jnp.float32)
    for row in range(rows):
        total = total + marked(cells, row, x_ref[row])
    return total


def weight_of(counts):
    return VIA_UNIT * counts.astype(jnp.float32)


def copies(pairs, sems):
    made = []
    for index, (source, target) in enumerate(pairs):
        copy = pltpu.make_async_copy(source, target, sems.at[index])
        copy.start()
        made.append(copy)
    return made


def chunks_of(cols, count):
    width = cols // count
    return [(first, width) for first in range(0, cols, width)]


def unpack_volts_kernel(count, volts_ref, x_ref, held, sems):
    rows, cols = held.shape
    chunks = chunks_of(cols, count)
    arriving = copies([(volts_ref.at[0, :, pl.ds(*c)], held.at[:, pl.ds(*c)]) for c in chunks], sems)
    for (first, width), copy in zip(chunks, arriving):
        copy.wait()
        for top in range(0, rows, 8):
            for start in range(first, first + width, LANES):
                x_ref[pl.ds(top, 8), start // LANES, :] = held[pl.ds(top, 8), pl.ds(start, LANES)]


def unpack_kernel(
    count, index_ref, table_ref, loads_ref, after_ref, across_ref, down_ref, loads_out, index_held, loads_held, sems
):
    rows, cols = loads_held.shape
    tile, _ = place()
    last_tile = tile == lax.axis_size("tile") - 1
    chunks = chunks_of(cols, count)
    pairs = []
    for c in chunks:
        pairs.append((index_ref.at[0, :, :, pl.ds(*c)], index_held.at[:, :, pl.ds(*c)]))
        pairs.append((loads_ref.at[0, :, pl.ds(*c)], loads_held.at[:, pl.ds(*c)]))
    arriving = copies(pairs, sems)
    table = jnp.broadcast_to(table_ref[...], (8, LANES))
    lane = lax.broadcasted_iota(jnp.int32, (8, LANES), 1)
    sub = lax.broadcasted_iota(jnp.int32, (8, LANES), 0)
    for number, (first, width) in enumerate(chunks):
        arriving[2 * number].wait()
        arriving[2 * number + 1].wait()
        for top in range(0, rows, 8):
            part = pl.ds(top, 8)
            for start in range(first, first + width, LANES):
                here, line = pl.ds(start, LANES), start // LANES
                across = jnp.take_along_axis(table, index_held[0, part, here], axis=1, mode="promise_in_bounds")
                if start + LANES == cols:
                    across = jnp.where(lane == LANES - 1, 0.0, across)
                across_ref[part, line, :] = across
                down = jnp.take_along_axis(table, index_held[1, part, here], axis=1, mode="promise_in_bounds")
                if top + 8 == rows:
                    down = jnp.where((sub == 7) & last_tile, 0.0, down)
                down_ref[part, line, :] = down
                loads_out[part, line, :] = loads_held[part, here]


def links_kernel(single, rows, x_ref, own_ref, count_ref, low_ref, *out_refs):
    for out_ref, cells in zip(out_refs, chosen(single, own_ref[...], low_ref[...])):
        out_ref[0] = pick(x_ref, cells, rows)
    out_refs[0][1] = weight_of(count_ref[...])


def via_terms(own_ref, count_ref, low_ref, low_weight, from_above, from_below):
    _, layer = place()
    on_top = layer == lax.axis_size("layer") - 1
    own_weight = weight_of(count_ref[...])
    low_weight = jnp.where(layer == 0, 0.0, low_weight)
    own_source = own_weight * jnp.where(on_top, 1.0, from_above)
    low_source = low_weight * from_below
    own, low = own_ref[...], low_ref[...]

    def via(row):
        return marked(own, row, own_weight) + marked(low, row, low_weight)

    def source(row):
        return marked(own, row, own_source) + marked(low, row, low_source)

    return via, source


def send_by_parity(first_ref, second_ref, slot, top, bottom):
    tile, _ = place()
    even = lax.rem(tile, 2) == 0
    first_ref[slot] = jnp.where(even, bottom, top)
    second_ref[slot] = jnp.where(even, top, bottom)


def taken_by_parity(first_ref, second_ref, slot):
    tile, _ = place()
    even = lax.rem(tile, 2) == 0
    first, second = first_ref[slot], second_ref[slot]
    return jnp.where(even, second, first), jnp.where(even, first, second)


def edge_one(x_ref, across_ref, down_ref, row, right_side, inverse):
    x = x_ref[row]
    flow = beside(x, across_ref[row]) + down_ref[row] * x_ref[row + 1] + down_ref[row - 1] * x_ref[row - 1]
    return x + FACTORS[0][1] * (inverse * (right_side + flow) - x)


def edges(x_ref, across_ref, down_ref, right_side, inverse_1, inverse_n, rows):
    top_side, bottom_side = right_side(0), right_side(rows - 1)
    below_top = down_ref[0]
    above_bottom = down_ref[rows - 2]
    top_1 = edge_one(x_ref, across_ref, down_ref, 1, right_side(1), inverse_1)
    bottom_1 = edge_one(x_ref, across_ref, down_ref, rows - 2, right_side(rows - 2), inverse_n)
    return (
        (x_ref[0], x_ref[rows - 1]),
        (top_side + below_top * x_ref[1], bottom_side + above_bottom * x_ref[rows - 2]),
        (top_side + below_top * top_1, bottom_side + above_bottom * bottom_1),
    )


def first_edges_kernel(
    rows, x_ref, across_ref, down_ref, loads_ref, own_ref, count_ref, low_ref, above_ref, below_ref, first_ref, second_ref
):
    via, source = via_terms(own_ref, count_ref, low_ref, below_ref[1], above_ref[0], below_ref[0])

    def right_side(row):
        return source(row) - loads_ref[row]

    def diagonal(row, links):
        across = across_ref[row]
        total = across + column_left(across)
        for link in links:
            total = total + down_ref[link]
        return total + via(row)

    values = edges(
        x_ref,
        across_ref,
        down_ref,
        right_side,
        1.0 / diagonal(1, (0, 1)),
        1.0 / diagonal(rows - 2, (rows - 3, rows - 2)),
        rows,
    )
    for slot, (top, bottom) in enumerate(values):
        send_by_parity(first_ref, second_ref, slot, top, bottom)
    send_by_parity(first_ref, second_ref, 3, diagonal(0, (0,)), diagonal(rows - 1, (rows - 2,)))
    send_by_parity(first_ref, second_ref, 4, across_ref[0], across_ref[rows - 1])
    send_by_parity(first_ref, second_ref, 5, down_ref[0], down_ref[rows - 1])


def next_edges_kernel(
    rows,
    x_ref,
    across_ref,
    down_ref,
    loads_ref,
    inverse_ref,
    own_ref,
    count_ref,
    low_ref,
    weight_ref,
    above_ref,
    below_ref,
    first_ref,
    second_ref,
):
    _, source = via_terms(own_ref, count_ref, low_ref, weight_ref[1], above_ref[0], below_ref[0])

    def right_side(row):
        return source(row) - loads_ref[row]

    values = edges(x_ref, across_ref, down_ref, right_side, inverse_ref[1], inverse_ref[rows - 2], rows)
    for slot, (top, bottom) in enumerate(values):
        send_by_parity(first_ref, second_ref, slot, top, bottom)


def relaxed(x, flow, side, inverse, previous, sweep):
    keep, gain = FACTORS[sweep]
    update = gain * (inverse * (side + flow) - x)
    if sweep > 0:
        update = update + keep * previous
    return x + update, update


def chosen(single, own, low):
    _, layer = place()
    return [jnp.where(layer == 0, own, low)] if single else [own, low]


def inner_rows(rows, x_ref, across_ref, down_ref, side_ref, inverse_ref, work, update_ref, core_ref, keep_ref):
    sources = [x_ref, *work]
    targets = [*work, core_ref]
    for sweep in range(SWEEPS):
        source, target = sources[sweep], targets[sweep]
        for row in range(sweep + 1, rows - 1 - sweep):
            x = source[row]
            flow = beside(x, across_ref[row]) + down_ref[row] * source[row + 1] + down_ref[row - 1] * source[row - 1]
            previous = update_ref[row] if sweep > 0 else None
            value, update = relaxed(x, flow, side_ref[row], inverse_ref[row], previous, sweep)
            target[row] = value
            if sweep < SWEEPS - 1:
                update_ref[row] = update
                for side, depth in ((0, row), (1, rows - 1 - row)):
                    slot = 3 * (2 * sweep + side)
                    if depth == sweep + 1:
                        keep_ref[slot] = value
                        keep_ref[slot + 2] = update
                    if depth == sweep + 2:
                        keep_ref[slot + 1] = value


def outer_rows(side, rows, halo, link, inverse_edge, x_ref, across_ref, down_ref, side_ref, inverse, keep_ref):
    edge_x, edge_q, edge_across = halo

    def row_of(depth):
        return depth if side == 0 else rows - 1 - depth

    def link_out(depth):
        if depth == 0:
            return link
        return down_ref[depth - 1] if side == 0 else down_ref[rows - 1 - depth]

    def link_in(depth):
        return down_ref[depth] if side == 0 else down_ref[rows - 2 - depth]

    values = {-1: edge_x}
    updates = {}
    for depth in range(SWEEPS + 1):
        values[depth] = x_ref[row_of(depth)]
    for sweep in range(SWEEPS):
        found, changed = {}, {}
        if sweep < SWEEPS - 1:
            flow = beside(edge_value := values[-1], edge_across) + link * values[0]
            found[-1], changed[-1] = relaxed(
                edge_value, flow, edge_q[sweep], inverse_edge, updates.get(-1), sweep
            )
        for depth in range(sweep + 1):
            row = row_of(depth)
            x = values[depth]
            flow = beside(x, across_ref[row]) + link_out(depth) * values[depth - 1] + link_in(depth) * values[depth + 1]
            found[depth], changed[depth] = relaxed(
                x, flow, side_ref[row], inverse(row), updates.get(depth), sweep
            )
        if sweep < SWEEPS - 1:
            slot = 3 * (2 * sweep + side)
            found[sweep + 1] = keep_ref[slot]
            changed[sweep + 1] = keep_ref[slot + 2]
            found[sweep + 2] = keep_ref[slot + 1]
        values, updates = found, changed
    return {row_of(depth): value for depth, value in values.items()}


KEPT = 6 * (SWEEPS - 1)


def first_inner_kernel(
    single,
    rows,
    x_ref,
    across_ref,
    down_ref,
    loads_ref,
    own_ref,
    count_ref,
    low_ref,
    above_ref,
    below_ref,
    after_ref,
    core_ref,
    side_ref,
    inverse_ref,
    keep_ref,
    picked_ref,
    *scratch,
):
    via, source = via_terms(own_ref, count_ref, low_ref, below_ref[1], above_ref[0], below_ref[0])
    for row in range(rows):
        side_ref[row] = source(row) - loads_ref[row]
        across = across_ref[row]
        diagonal = across + column_left(across) + down_ref[row] + via(row)
        if row > 0:
            diagonal = diagonal + down_ref[row - 1]
            inverse_ref[row] = 1.0 / diagonal
        else:
            inverse_ref[row] = diagonal
    inner_rows(
        rows, x_ref, across_ref, down_ref, side_ref, inverse_ref, scratch[:-1], scratch[-1], core_ref, keep_ref
    )
    for index, cells in enumerate(chosen(single, own_ref[...], low_ref[...])):
        total = jnp.zeros(cells.shape, jnp.float32)
        for row in range(SWEEPS, rows - SWEEPS):
            total = total + marked(cells, row, core_ref[row])
        picked_ref[index] = total


def first_outer_kernel(
    single,
    rows,
    x_ref,
    across_ref,
    down_ref,
    side_ref,
    inverse_ref,
    keep_ref,
    picked_ref,
    own_ref,
    low_ref,
    first_ref,
    second_ref,
    core_ref,
    next_ref,
    halo_ref,
    *sends,
):
    tile, _ = place()
    top_x, low_x = taken_by_parity(first_ref, second_ref, 0)
    top_q0, low_q0 = taken_by_parity(first_ref, second_ref, 1)
    top_q1, low_q1 = taken_by_parity(first_ref, second_ref, 2)
    top_diag, low_diag = taken_by_parity(first_ref, second_ref, 3)
    top_across, low_across = taken_by_parity(first_ref, second_ref, 4)
    link, _ = taken_by_parity(first_ref, second_ref, 5)
    link = jnp.where(tile == 0, 0.0, link)
    low_link = down_ref[rows - 1]
    top_inverse = 1.0 / (top_diag + link)
    low_inverse = 1.0 / (low_diag + low_link)
    inverse_0 = 1.0 / (inverse_ref[0] + link)
    for slot, value in enumerate((top_across, low_across, link, top_inverse, low_inverse, inverse_0)):
        halo_ref[slot] = value

    def inverse(row):
        return inverse_0 if row == 0 else inverse_ref[row]

    shared = (x_ref, across_ref, down_ref, side_ref, inverse, keep_ref)
    outer = outer_rows(0, rows, (top_x, (top_q0, top_q1), top_across), link, top_inverse, *shared)
    outer.update(
        outer_rows(1, rows, (low_x, (low_q0, low_q1), low_across), low_link, low_inverse, *shared)
    )
    for row, value in outer.items():
        next_ref[row] = value
    for index, cells in enumerate(chosen(single, own_ref[...], low_ref[...])):
        total = picked_ref[index]
        for row, value in outer.items():
            total = total + marked(cells, row, value)
        sends[index][0] = total


def last_inner_kernel(
    rows,
    x_ref,
    across_ref,
    down_ref,
    loads_ref,
    inverse_ref,
    own_ref,
    count_ref,
    low_ref,
    weight_ref,
    above_ref,
    below_ref,
    after_ref,
    core_ref,
    side_ref,
    keep_ref,
    *scratch,
):
    _, source = via_terms(own_ref, count_ref, low_ref, weight_ref[1], above_ref[0], below_ref[0])
    for row in range(rows):
        side_ref[row] = source(row) - loads_ref[row]
    inner_rows(
        rows, x_ref, across_ref, down_ref, side_ref, inverse_ref, scratch[:-1], scratch[-1], core_ref, keep_ref
    )


def last_outer_kernel(
    count,
    rows,
    x_ref,
    across_ref,
    down_ref,
    side_ref,
    inverse_ref,
    keep_ref,
    halo_ref,
    first_ref,
    second_ref,
    core_ref,
    out_ref,
    next_ref,
    held,
    sems,
):
    top_x, low_x = taken_by_parity(first_ref, second_ref, 0)
    top_q0, low_q0 = taken_by_parity(first_ref, second_ref, 1)
    top_q1, low_q1 = taken_by_parity(first_ref, second_ref, 2)

    def inverse(row):
        return halo_ref[5] if row == 0 else inverse_ref[row]

    shared = (x_ref, across_ref, down_ref, side_ref, inverse, keep_ref)
    outer = outer_rows(0, rows, (top_x, (top_q0, top_q1), halo_ref[0]), halo_ref[2], halo_ref[3], *shared)
    outer.update(
        outer_rows(1, rows, (low_x, (low_q0, low_q1), halo_ref[1]), down_ref[rows - 1], halo_ref[4], *shared)
    )
    for row, value in outer.items():
        next_ref[row] = value
    leaving = []
    for number, (first, width) in enumerate(chunks_of(held.shape[1], count)):
        for top in range(0, rows, 8):
            for start in range(first, first + width, LANES):
                held[pl.ds(top, 8), pl.ds(start, LANES)] = next_ref[pl.ds(top, 8), start // LANES, :]
        part = pl.ds(first, width)
        copy = pltpu.make_async_copy(held.at[:, part], out_ref.at[:, part], sems.at[number])
        copy.start()
        leaving.append(copy)
    for copy in leaving:
        copy.wait()


def call(kernel, name, ins, outs, scratch=(), aliases=None):
    spaces = {"vmem": pltpu.VMEM, "hbm": pltpu.HBM, "any": pl.ANY}
    return pl.pallas_call(
        kernel,
        out_shape=[jax.ShapeDtypeStruct(shape, jnp.float32) for _, shape in outs],
        in_specs=[pl.BlockSpec(memory_space=spaces[space]) for space, _ in ins],
        out_specs=[pl.BlockSpec(memory_space=spaces[space]) for space, _ in outs],
        scratch_shapes=list(scratch),
        input_output_aliases=aliases or {},
        compiler_params=pltpu.CompilerParams(vmem_limit_bytes=40 * 1024 * 1024),
        name=name,
    )(*(array for _, array in ins))


def routes(tiles, layers):
    def at(tile, layer):
        return tile * layers + layer % layers

    everywhere = [(tile, layer) for tile in range(tiles) for layer in range(layers)]
    up = [(at(t, l), at(t, l + 1)) for t, l in everywhere]
    down = [(at(t, l), at(t, l - 1)) for t, l in everywhere]
    first, second = [], []
    for t, l in everywhere:
        first.append((at(t, l), at(t ^ 1, l)))
        beyond = t + 1 if t % 2 else t - 1
        if 0 <= beyond < tiles:
            second.append((at(t, l), at(beyond, l)))
        else:
            second.append((at(t, l), at(t, l + 1)))
    return up, down, first, second


CHUNKS = 4


def local(class_index, class_conductance, loads, start_volts, via_cells, via_counts):
    rows, cols = loads.shape[1:]
    lines = cols // LANES
    tiles, layers = lax.axis_size("tile"), lax.axis_size("layer")
    up, down, first, second = routes(tiles, layers)
    single = layers == 2
    move = functools.partial(lax.ppermute, axis_name=("tile", "layer"))

    def rows_of(count):
        return (count, lines, LANES)

    def held(shape, kind=jnp.float32):
        return pltpu.VMEM(shape, kind)

    def flags(count):
        return pltpu.SemaphoreType.DMA((count,))

    def vmem(*arrays):
        return [("vmem", array) for array in arrays]

    def between_layers(sends):
        if single:
            got = move(sends[0], perm=up)
            return got, got
        return move(sends[1], perm=down), move(sends[0], perm=up)

    def beside_tile(sent):
        return move(sent[0], perm=first), move(sent[1], perm=second)

    field = ("vmem", rows_of(rows))
    work = [held(rows_of(rows))] * SWEEPS
    pick_count = 1 if single else 2
    picks = [("vmem", rows_of(1))] * pick_count

    own = via_cells.reshape(lines, LANES)
    counts = via_counts.reshape(lines, LANES)
    low = move(own, perm=up)
    table = jnp.pad(class_conductance, ((0, 0), (0, LANES - class_conductance.shape[1])))
    (x,) = call(
        functools.partial(unpack_volts_kernel, CHUNKS),
        "unpack_volts",
        [("hbm", start_volts)],
        [field],
        [held((rows, cols)), flags(CHUNKS)],
    )
    sends = call(
        functools.partial(links_kernel, single, rows),
        "links",
        vmem(x, own, counts, low),
        [("vmem", rows_of(2))] if single else [("vmem", rows_of(2)), ("vmem", rows_of(1))],
    )
    above, below = between_layers(sends)
    weights = below
    across, downward, load = call(
        functools.partial(unpack_kernel, CHUNKS),
        "unpack",
        [("hbm", class_index), ("vmem", table), ("hbm", loads), ("any", sends[0])],
        [field] * 3,
        [held((2, rows, cols), jnp.int32), held((rows, cols)), flags(2 * CHUNKS)],
    )
    vias = (own, counts, low)
    sent = call(
        functools.partial(first_edges_kernel, rows),
        "first_edges",
        vmem(x, across, downward, load, *vias, above, below),
        [("vmem", rows_of(6))] * 2,
    )
    got = beside_tile(sent)
    core, side, inverse, keep, picked = call(
        functools.partial(first_inner_kernel, single, rows),
        "first_inner",
        vmem(x, across, downward, load, *vias, above, below) + [("any", sent[1])],
        [field, field, field, ("vmem", rows_of(KEPT)), ("vmem", rows_of(pick_count))],
        work,
    )
    x, halo, *sends = call(
        functools.partial(first_outer_kernel, single, rows),
        "first_outer",
        vmem(x, across, downward, side, inverse, keep, picked, own, low, *got, core),
        [field, ("vmem", rows_of(6))] + picks,
        aliases={11: 0},
    )
    above, below = between_layers(sends)
    sent = call(
        functools.partial(next_edges_kernel, rows),
        "next_edges",
        vmem(x, across, downward, load, inverse, *vias, weights, above, below),
        [("vmem", rows_of(3))] * 2,
    )
    got = beside_tile(sent)
    core, side, keep = call(
        functools.partial(last_inner_kernel, rows),
        "last_inner",
        vmem(x, across, downward, load, inverse, *vias, weights, above, below) + [("any", sent[1])],
        [field, field, ("vmem", rows_of(KEPT))],
        work,
    )
    volts, _ = call(
        functools.partial(last_outer_kernel, CHUNKS, rows),
        "last_outer",
        vmem(x, across, downward, side, inverse, keep, halo, *got, core),
        [("hbm", (rows, cols)), field],
        [held((rows, cols)), flags(CHUNKS)],
        aliases={9: 1},
    )
    return volts[None]


def solution(mesh):
    placed = (
        P("layer", None, "tile", None),
        P("layer", None),
        P("layer", "tile", None),
        P("layer", "tile", None),
        P("layer", "tile"),
        P("layer", "tile"),
    )
    return jax.shard_map(
        local, mesh=mesh, in_specs=placed, out_specs=P("layer", "tile", None), check_vma=False
    )
```

time: 41.2 us -> 28.3 us (0.69)
  Pallas kernels: 14.8 us -> 7.21 us
  waiting for transfers between devices: 14.3 us -> 8.93 us
  starting transfers between devices: 8.53 us -> 10.9 us
  local copies, waits for them, and re-layouts: 3.32 us -> 1.07 us
    pallas_call x6 -> x9, Pallas kernels: 14.8 us -> 7.21 us  [call(): pl.pallas_call(kernel, out_shape=[jax.ShapeDtypeStruct(shape, jnp.float32...]
    ppermute x2, waiting for transfers between devices: 4.86 us -> 1.58 us  [between_layers(): got = move(sends[0], perm=up)]
    unnamed x12, local copies, waits for them, and re-layouts: 3.31 us -> 1.06 us
    ppermute x4, waiting for transfers between devices: 9.43 us -> 7.31 us  [beside_tile(): return (move(sent[0], perm=first), move(sent[1], perm=second))]
    ppermute x2, starting transfers between devices: 1.15 us -> 2.55 us  [between_layers(): got = move(sends[0], perm=up)]
    ppermute x4, starting transfers between devices: 6.17 us -> 7.04 us  [beside_tile(): return (move(sent[0], perm=first), move(sent[1], perm=second))]
  transfers between devices with their start and end apart: 7 -> 7, of which waited for: 5 -> 3; matrix products, arithmetic and copies ran while one was open for 0% -> 0% of each run, Pallas kernels for 4% -> 16%
where the time goes in v2:
time: 28.3 us; the launch traced here: 28.2 us
  starting transfers between devices  10.9 us (39%)
  waiting for transfers between devices  8.93 us (32%)
  Pallas kernels  7.21 us (25%)
  local copies, waits for them, and re-layouts  1.07 us (4%)
    ppermute x4, waiting for transfers between devices, beside_tile(): return (move(sent[0], perm=first), move(sent[1], perm=second))  7.31 us
    pallas_call x9, Pallas kernels, call(): pl.pallas_call(kernel, out_shape=[jax.ShapeDtypeStruct(shape, jnp.float32...  7.21 us
    ppermute x4, starting transfers between devices, beside_tile(): return (move(sent[0], perm=first), move(sent[1], perm=second))  7.04 us
    ppermute x2, starting transfers between devices, between_layers(): got = move(sends[0], perm=up)  2.55 us
    ppermute x2, waiting for transfers between devices, between_layers(): got = move(sends[0], perm=up)  1.58 us
    ppermute x1, starting transfers between devices, local(): low = move(own, perm=up)  1.28 us
    unnamed x12, local copies, waits for them, and re-layouts  1.06 us
  transfers between devices with their start and end apart: 7, of which 3 were waited for; matrix products, arithmetic and copies ran while one was open for 0% of the time, Pallas kernels for 16%

profile of v2, /device:TPU:5, one launch (start us, length us, event | category | flops | bytes accessed | tf_op | source)
XLA Modules:
  0.0 28.2 jit_solution(16296659589694927068)
XLA Ops:
  0.0 0.0 copy-start.2
  0.0 0.0 copy-start
  0.0 0.0 copy-start.1
  0.0 1.3 %collective-permute-start = (s32[64,128]{1,0:T(8,128)}, s32[64,128]{1,0:T(8,128)S(1)}, u32[]{:S(2)}, u32[]{:S(2)}) collective-permute-start(s32[64,128]{1,0:T(8,128)} %bitcast.3), channel_id=1, source_target_pairs={{0,1},{1,0},{2,3},{3,2},{4,5},{5,4},{6,7},{7,6},{8,9},{9,8},{10,11... | collective-permute-start | bytes 98312 | tf_op jit(solution)/shard_map/ppermute | solution.py:554
  1.3 0.0 copy-start.3
  1.3 1.0 %copy-done.3 = f32[1,16,8192]{2,1,0:T(8,128)S(1)} copy-done((f32[1,16,8192]{2,1,0:T(8,128)S(1)}, f32[1,16,8192]{2,1,0:T(8,128)}, u32[]{:S(2)}) %copy-start.3) | copy-done | bytes 524312
  2.3 0.7 %unpack_volts.1.x_ref = f32[16,64,128]{2,1,0:T(8,128)S(1)} custom-call(f32[1,16,8192]{2,1,0:T(8,128)S(1)} %copy-done.3), custom_call_target="tpu_custom_call" | custom-call | tf_op jit(solution)/shard_map/unpack_volts/pallas_call | solution.py:485
  3.0 0.0 copy-start.4
  3.0 0.0 collective-permute-done.low_ref
  3.1 0.0 copy-done.2
  3.1 0.0 copy-done
  3.1 0.0 copy-start.5
  3.1 0.1 links.1.after_ref
  3.1 1.3 %collective-permute-start.1 = (f32[2,64,128]{2,1,0:T(8,128)S(1)}, f32[2,64,128]{2,1,0:T(8,128)S(1)}, u32[]{:S(2)}, u32[]{:S(2)}) collective-permute-start(f32[2,64,128]{2,1,0:T(8,128)S(1)} %links.1.after_ref), channel_id=1, source_target_pairs={{0,1},{1,0},{2,3},{3,2},{4,5},{5,4},{6,7},{7,6},{8,9},{9,8},{10,11... | collective-permute-start | bytes 196616 | tf_op jit(solution)/shard_map/ppermute | solution.py:540
  4.4 0.0 copy-done.5
  4.4 0.0 copy-done.1
  4.4 0.0 copy-done.4
  4.4 1.8 %unpack.1 = (f32[16,64,128]{2,1,0:T(8,128)S(1)}, f32[16,64,128]{2,1,0:T(8,128)S(1)}, f32[16,64,128]{2,1,0:T(8,128)S(1)}) custom-call(s32[1,2,16,8192]{3,2,1,0:T(8,128)S(1)} %copy-done.1, f32[1,128]{1,0:T(1,128)S(1)} %pad.4.table_ref, f32[1,16,8192]{2,1,0:T(8,128)S(1)} %copy-done.4, f32[2,64,128]{2,1,0:T(8,128)S(1)} %links.1.after_ref), custom_call_target="tpu_custom_call" | custom-call | tf_op jit(solution)/shard_map/unpack/pallas_call | solution.py:485
  6.3 0.0 collective-permute-done.1.above_ref.below_ref.weight_ref
  6.3 0.2 first_edges.1
  6.5 3.0 %collective-permute-start.2 = (f32[6,64,128]{2,1,0:T(8,128)S(1)}, f32[6,64,128]{2,1,0:T(8,128)S(1)}, u32[]{:S(2)}, u32[]{:S(2)}) collective-permute-start(f32[6,64,128]{2,1,0:T(8,128)S(1)} %get-tuple-element.32), channel_id=1, source_target_pairs={{0,2},{1,3},{2,0},{3,1},{4,6},{5,7},{6,4},{7,5},{8,10},{9,11},{10,... | collective-permute-start | bytes 589832 | tf_op jit(solution)/shard_map/ppermute | solution.py:545
  9.5 1.2 %collective-permute-start.3 = (f32[6,64,128]{2,1,0:T(8,128)S(1)}, f32[6,64,128]{2,1,0:T(8,128)S(1)}, u32[]{:S(2)}, u32[]{:S(2)}) collective-permute-start(f32[6,64,128]{2,1,0:T(8,128)S(1)} %get-tuple-element.27.after_ref), channel_id=1, source_target_pairs={{0,1},{1,0},{2,4},{3,5},{4,2},{5,3},{6,8},{7,9},{8,6},{9,7},{10,12... | collective-permute-start | bytes 589832 | tf_op jit(solution)/shard_map/ppermute | solution.py:545
  10.7 1.2 %first_inner.1 = (f32[16,64,128]{2,1,0:T(8,128)S(1)}, f32[16,64,128]{2,1,0:T(8,128)S(1)}, f32[16,64,128]{2,1,0:T(8,128)S(1)}, f32[12,64,128]{2,1,0:T(8,128)S(1)}, f32[1,64,128]{2,1,0:T(8,128)S(1)}) custom-call(f32[16,64,128]{2,1,0:T(8,128)S(1)} %unpack_volts.1.x_ref, f32[16,64,128]{2,1,0:T(8,128)S(1)} %get-tuple-element.24.across_ref, ...), custom_call_target="tpu_custom_call" | custom-call | tf_op jit(solution)/shard_map/first_inner/pallas_call | solution.py:485
  11.9 0.0 collective-permute-done.2.first_ref
  11.9 3.7 %collective-permute-done.3.second_ref = f32[6,64,128]{2,1,0:T(8,128)S(1)} collective-permute-done((f32[6,64,128]{2,1,0:T(8,128)S(1)}, f32[6,64,128]{2,1,0:T(8,128)S(1)}, u32[]{:S(2)}, u32[]{:S(2)}) %collective-permute-start.3) | collective-permute-done | bytes 196640 | tf_op jit(solution)/shard_map/ppermute | solution.py:545
  15.6 0.6 %first_outer.1 = (f32[16,64,128]{2,1,0:T(8,128)S(1)}, f32[6,64,128]{2,1,0:T(8,128)S(1)}, f32[1,64,128]{2,1,0:T(8,128)S(1)}) custom-call(f32[16,64,128]{2,1,0:T(8,128)S(1)} %unpack_volts.1.x_ref, f32[16,64,128]{2,1,0:T(8,128)S(1)} %get-tuple-element.24.across_ref, f32[16,64,128]{2,1,0:T(8,128)S(1)} %get-tuple-element.25.down_ref, ...), custom_call_target="tpu_custom_call", output_to_operand_aliasing={{0}: (11, {})} | custom-call | tf_op jit(solution)/shard_map/first_outer/pallas_call | solution.py:485
  16.3 1.3 %collective-permute-start.4 = (f32[1,64,128]{2,1,0:T(8,128)S(1)}, f32[1,64,128]{2,1,0:T(8,128)S(1)}, u32[]{:S(2)}, u32[]{:S(2)}) collective-permute-start(f32[1,64,128]{2,1,0:T(8,128)S(1)} %get-tuple-element.35), channel_id=1, source_target_pairs={{0,1},{1,0},{2,3},{3,2},{4,5},{5,4},{6,7},{7,6},{8,9},{9,8},{10,11... | collective-permute-start | bytes 98312 | tf_op jit(solution)/shard_map/ppermute | solution.py:540
  17.5 1.6 %collective-permute-done.4.above_ref.below_ref = f32[1,64,128]{2,1,0:T(8,128)S(1)} collective-permute-done((f32[1,64,128]{2,1,0:T(8,128)S(1)}, f32[1,64,128]{2,1,0:T(8,128)S(1)}, u32[]{:S(2)}, u32[]{:S(2)}) %collective-permute-start.4) | collective-permute-done | bytes 32800 | tf_op jit(solution)/shard_map/ppermute | solution.py:540
  19.1 0.1 next_edges.1
  19.2 2.4 %collective-permute-start.5 = (f32[3,64,128]{2,1,0:T(8,128)S(1)}, f32[3,64,128]{2,1,0:T(8,128)S(1)}, u32[]{:S(2)}, u32[]{:S(2)}) collective-permute-start(f32[3,64,128]{2,1,0:T(8,128)S(1)} %get-tuple-element.40), channel_id=1, source_target_pairs={{0,2},{1,3},{2,0},{3,1},{4,6},{5,7},{6,4},{7,5},{8,10},{9,11},{10,... | collective-permute-start | bytes 294920 | tf_op jit(solution)/shard_map/ppermute | solution.py:545
  21.6 0.4 %collective-permute-start.6 = (f32[3,64,128]{2,1,0:T(8,128)S(1)}, f32[3,64,128]{2,1,0:T(8,128)S(1)}, u32[]{:S(2)}, u32[]{:S(2)}) collective-permute-start(f32[3,64,128]{2,1,0:T(8,128)S(1)} %get-tuple-element.36.after_ref), channel_id=1, source_target_pairs={{0,1},{1,0},{2,4},{3,5},{4,2},{5,3},{6,8},{7,9},{8,6},{9,7},{10,12... | collective-permute-start | bytes 294920 | tf_op jit(solution)/shard_map/ppermute | solution.py:545
  22.0 0.9 %last_inner.1 = (f32[16,64,128]{2,1,0:T(8,128)S(1)}, f32[16,64,128]{2,1,0:T(8,128)S(1)}, f32[12,64,128]{2,1,0:T(8,128)S(1)}) custom-call(f32[16,64,128]{2,1,0:T(8,128)S(1)} %get-tuple-element.34.x_ref, f32[16,64,128]{2,1,0:T(8,128)S(1)} %get-tuple-element.24.across_ref, f32[16,64,128]{2,1,0:T(8,128)S(1)} %get-tuple-element.25.down_ref, ...), custom_call_target="tpu_custom_call" | custom-call | tf_op jit(solution)/shard_map/last_inner/pallas_call | solution.py:485
  23.0 0.0 collective-permute-done.5.first_ref
  23.0 3.6 %collective-permute-done.6.second_ref = f32[3,64,128]{2,1,0:T(8,128)S(1)} collective-permute-done((f32[3,64,128]{2,1,0:T(8,128)S(1)}, f32[3,64,128]{2,1,0:T(8,128)S(1)}, u32[]{:S(2)}, u32[]{:S(2)}) %collective-permute-start.6) | collective-permute-done | bytes 98336 | tf_op jit(solution)/shard_map/ppermute | solution.py:545
  26.6 1.6 %last_outer.1 = (f32[16,8192]{1,0:T(8,128)}, f32[16,64,128]{2,1,0:T(8,128)S(1)}) custom-call(f32[16,64,128]{2,1,0:T(8,128)S(1)} %get-tuple-element.34.x_ref, f32[16,64,128]{2,1,0:T(8,128)S(1)} %get-tuple-element.24.across_ref, f32[16,64,128]{2,1,0:T(8,128)S(1)} %get-tuple-element.25.down_ref, ...), custom_call_target="tpu_custom_call", output_to_operand_aliasing={{1}: (9, {})} | custom-call | tf_op jit(solution)/shard_map/last_outer/pallas_call | solution.py:485
  (1 shorter events, 0.0 us)
Async XLA Ops:
  0.0 3.1 %copy-start.2 = (s32[1,8192]{1,0:T(1,128)S(1)}, s32[1,8192]{1,0:T(1,128)}, u32[]{:S(2)}) copy-start(s32[1,8192]{1,0:T(1,128)} %param.11) | copy-start | bytes 98308
  0.0 3.1 %copy-start = (s32[1,8192]{1,0:T(1,128)S(1)}, s32[1,8192]{1,0:T(1,128)}, u32[]{:S(2)}) copy-start(s32[1,8192]{1,0:T(1,128)} %param.10) | copy-start | bytes 98308
  0.0 4.4 %copy-start.1 = (s32[1,2,16,8192]{3,2,1,0:T(8,128)S(1)}, s32[1,2,16,8192]{3,2,1,0:T(8,128)}, u32[]{:S(2)}) copy-start(s32[1,2,16,8192]{3,2,1,0:T(8,128)} %index_ref.1) | copy-start | bytes 3145732
  0.0 3.0 %collective-permute-start = (s32[64,128]{1,0:T(8,128)}, s32[64,128]{1,0:T(8,128)S(1)}, u32[]{:S(2)}, u32[]{:S(2)}) collective-permute-start(s32[64,128]{1,0:T(8,128)} %bitcast.3), channel_id=1, source_target_pairs={{0,1},{1,0},{2,3},{3,2},{4,5},{5,4},{6,7},{7,6},{8,9},{9,8},{10,11... | collective-permute-start | bytes 98312 | tf_op jit(solution)/shard_map/ppermute | solution.py:554
  1.3 1.0 %copy-start.3 = (f32[1,16,8192]{2,1,0:T(8,128)S(1)}, f32[1,16,8192]{2,1,0:T(8,128)}, u32[]{:S(2)}) copy-start(f32[1,16,8192]{2,1,0:T(8,128)} %volts_ref.1) | copy-start | bytes 1572868
  3.0 1.4 %copy-start.4 = (f32[1,16,8192]{2,1,0:T(8,128)S(1)}, f32[1,16,8192]{2,1,0:T(8,128)}, u32[]{:S(2)}) copy-start(f32[1,16,8192]{2,1,0:T(8,128)} %loads_ref.1) | copy-start | bytes 1572868
  3.1 1.4 %copy-start.5 = (f32[1,16]{1,0:T(1,128)S(1)}, f32[1,16]{1,0:T(1,128)}, u32[]{:S(2)}) copy-start(f32[1,16]{1,0:T(1,128)} %param.7) | copy-start | bytes 196
  3.1 3.2 %collective-permute-start.1 = (f32[2,64,128]{2,1,0:T(8,128)S(1)}, f32[2,64,128]{2,1,0:T(8,128)S(1)}, u32[]{:S(2)}, u32[]{:S(2)}) collective-permute-start(f32[2,64,128]{2,1,0:T(8,128)S(1)} %links.1.after_ref), channel_id=1, source_target_pairs={{0,1},{1,0},{2,3},{3,2},{4,5},{5,4},{6,7},{7,6},{8,9},{9,8},{10,11... | collective-permute-start | bytes 196616 | tf_op jit(solution)/shard_map/ppermute | solution.py:540
  6.5 5.4 %collective-permute-start.2 = (f32[6,64,128]{2,1,0:T(8,128)S(1)}, f32[6,64,128]{2,1,0:T(8,128)S(1)}, u32[]{:S(2)}, u32[]{:S(2)}) collective-permute-start(f32[6,64,128]{2,1,0:T(8,128)S(1)} %get-tuple-element.32), channel_id=1, source_target_pairs={{0,2},{1,3},{2,0},{3,1},{4,6},{5,7},{6,4},{7,5},{8,10},{9,11},{10,... | collective-permute-start | bytes 589832 | tf_op jit(solution)/shard_map/ppermute | solution.py:545
  9.5 6.1 %collective-permute-start.3 = (f32[6,64,128]{2,1,0:T(8,128)S(1)}, f32[6,64,128]{2,1,0:T(8,128)S(1)}, u32[]{:S(2)}, u32[]{:S(2)}) collective-permute-start(f32[6,64,128]{2,1,0:T(8,128)S(1)} %get-tuple-element.27.after_ref), channel_id=1, source_target_pairs={{0,1},{1,0},{2,4},{3,5},{4,2},{5,3},{6,8},{7,9},{8,6},{9,7},{10,12... | collective-permute-start | bytes 589832 | tf_op jit(solution)/shard_map/ppermute | solution.py:545
  16.3 2.8 %collective-permute-start.4 = (f32[1,64,128]{2,1,0:T(8,128)S(1)}, f32[1,64,128]{2,1,0:T(8,128)S(1)}, u32[]{:S(2)}, u32[]{:S(2)}) collective-permute-start(f32[1,64,128]{2,1,0:T(8,128)S(1)} %get-tuple-element.35), channel_id=1, source_target_pairs={{0,1},{1,0},{2,3},{3,2},{4,5},{5,4},{6,7},{7,6},{8,9},{9,8},{10,11... | collective-permute-start | bytes 98312 | tf_op jit(solution)/shard_map/ppermute | solution.py:540
  19.2 3.8 %collective-permute-start.5 = (f32[3,64,128]{2,1,0:T(8,128)S(1)}, f32[3,64,128]{2,1,0:T(8,128)S(1)}, u32[]{:S(2)}, u32[]{:S(2)}) collective-permute-start(f32[3,64,128]{2,1,0:T(8,128)S(1)} %get-tuple-element.40), channel_id=1, source_target_pairs={{0,2},{1,3},{2,0},{3,1},{4,6},{5,7},{6,4},{7,5},{8,10},{9,11},{10,... | collective-permute-start | bytes 294920 | tf_op jit(solution)/shard_map/ppermute | solution.py:545
  21.6 4.9 %collective-permute-start.6 = (f32[3,64,128]{2,1,0:T(8,128)S(1)}, f32[3,64,128]{2,1,0:T(8,128)S(1)}, u32[]{:S(2)}, u32[]{:S(2)}) collective-permute-start(f32[3,64,128]{2,1,0:T(8,128)S(1)} %get-tuple-element.36.after_ref), channel_id=1, source_target_pairs={{0,1},{1,0},{2,4},{3,5},{4,2},{5,3},{6,8},{7,9},{8,6},{9,7},{10,12... | collective-permute-start | bytes 294920 | tf_op jit(solution)/shard_map/ppermute | solution.py:545

commit v3 on v2

v3 whole, which is shorter than its diff:
```python
import functools

import jax
import jax.numpy as jnp
from jax import lax
from jax.experimental import pallas as pl
from jax.experimental.pallas import tpu as pltpu
from jax.sharding import PartitionSpec as P

OUTER = 2
SWEEPS = 3
VIA_UNIT = 2.0
LOWER_BOUND = 0.05
UPPER_BOUND = 2.0
LANES = 128
CHUNKS = 2


def chebyshev_terms(count):
    centre_value = 0.5 * (UPPER_BOUND + LOWER_BOUND)
    half_width = 0.5 * (UPPER_BOUND - LOWER_BOUND)
    sigma = centre_value / half_width
    rho_last = 1.0 / sigma
    terms = [(0.0, 1.0 / centre_value)]
    for index in range(1, count):
        rho_next = 1.0 / (2.0 * sigma - rho_last)
        terms.append((rho_next * rho_last, 2.0 * rho_next / half_width))
        rho_last = rho_next
    return terms


FACTORS = chebyshev_terms(SWEEPS)


def column_right(row):
    lane = lax.broadcasted_iota(jnp.int32, row.shape, 1)
    turned = pltpu.roll(row, LANES - 1, 1)
    return jnp.where(lane == LANES - 1, pltpu.roll(turned, row.shape[0] - 1, 0), turned)


def column_left(row):
    lane = lax.broadcasted_iota(jnp.int32, row.shape, 1)
    turned = pltpu.roll(row, 1, 1)
    return jnp.where(lane == 0, pltpu.roll(turned, 1, 0), turned)


def beside(x, across):
    return across * column_right(x) + column_left(across * x)


def place():
    return lax.axis_index("tile"), lax.axis_index("layer")


def marked(cells, row, value):
    return jnp.where(cells == row, value, 0.0)


def pick(x_ref, cells, rows):
    total = jnp.zeros(cells.shape, jnp.float32)
    for row in range(rows):
        total = total + marked(cells, row, x_ref[row])
    return total


def weight_of(counts):
    return VIA_UNIT * counts.astype(jnp.float32)


def chunks_of(cols, count):
    width = cols // count
    return [(first, width) for first in range(0, cols, width)]


def unpack_volts_kernel(volts_ref, x_ref):
    rows, cols = volts_ref.shape[1:]
    for top in range(0, rows, 8):
        for start in range(0, cols, LANES):
            x_ref[pl.ds(top, 8), start // LANES, :] = volts_ref[0, pl.ds(top, 8), pl.ds(start, LANES)]


def unpack_kernel(index_ref, table_ref, loads_ref, across_ref, down_ref, loads_out):
    rows, cols = loads_ref.shape[1:]
    tile, _ = place()
    last_tile = tile == lax.axis_size("tile") - 1
    table = jnp.broadcast_to(table_ref[...], (8, LANES))
    lane = lax.broadcasted_iota(jnp.int32, (8, LANES), 1)
    sub = lax.broadcasted_iota(jnp.int32, (8, LANES), 0)
    for top in range(0, rows, 8):
        part = pl.ds(top, 8)
        for start in range(0, cols, LANES):
            here, line = pl.ds(start, LANES), start // LANES
            across = jnp.take_along_axis(table, index_ref[0, 0, part, here], axis=1, mode="promise_in_bounds")
            if start + LANES == cols:
                across = jnp.where(lane == LANES - 1, 0.0, across)
            across_ref[part, line, :] = across
            down = jnp.take_along_axis(table, index_ref[0, 1, part, here], axis=1, mode="promise_in_bounds")
            if top + 8 == rows:
                down = jnp.where((sub == 7) & last_tile, 0.0, down)
            down_ref[part, line, :] = down
            loads_out[part, line, :] = loads_ref[0, part, here]


def links_kernel(single, rows, x_ref, own_ref, count_ref, low_ref, *out_refs):
    for out_ref, cells in zip(out_refs, chosen(single, own_ref[...], low_ref[...])):
        out_ref[0] = pick(x_ref, cells, rows)
    out_refs[0][1] = weight_of(count_ref[...])


def via_terms(own_ref, count_ref, low_ref, low_weight, from_above, from_below):
    _, layer = place()
    on_top = layer == lax.axis_size("layer") - 1
    own_weight = weight_of(count_ref[...])
    low_weight = jnp.where(layer == 0, 0.0, low_weight)
    fixed_source = jnp.where(on_top, own_weight, 0.0)
    own, low = own_ref[...], low_ref[...]

    def via(row):
        return marked(own, row, own_weight) + marked(low, row, low_weight)

    def fixed(row):
        return marked(own, row, fixed_source)

    if from_above is None:
        return via, fixed, None
    own_source = jnp.where(on_top, 0.0, own_weight * from_above)
    low_source = low_weight * from_below

    def moving(row):
        return marked(own, row, own_source) + marked(low, row, low_source)

    return via, fixed, moving


def send_by_parity(first_ref, second_ref, slot, top, bottom):
    tile, _ = place()
    even = lax.rem(tile, 2) == 0
    first_ref[slot] = jnp.where(even, bottom, top)
    second_ref[slot] = jnp.where(even, top, bottom)


def taken_by_parity(first_ref, second_ref, slot):
    tile, _ = place()
    even = lax.rem(tile, 2) == 0
    first, second = first_ref[slot], second_ref[slot]
    return jnp.where(even, second, first), jnp.where(even, first, second)


def edge_flow(x_ref, across_ref, down_ref, row):
    return beside(x_ref[row], across_ref[row]) + down_ref[row] * x_ref[row + 1] + down_ref[row - 1] * x_ref[row - 1]


def edge_ends(rows):
    return (0, 1, 0), (rows - 1, rows - 2, rows - 2)


def edges(x_ref, across_ref, down_ref, right_side, inverses, rows):
    found = []
    for (edge, within, link), inverse in zip(edge_ends(rows), inverses):
        x = x_ref[within]
        flow = edge_flow(x_ref, across_ref, down_ref, within)
        later = x + FACTORS[0][1] * (inverse * (right_side(within) + flow) - x)
        found.append((right_side(edge) + down_ref[link] * x, right_side(edge) + down_ref[link] * later))
    return tuple(zip(*found))


def still_edges_kernel(x_ref, across_ref, down_ref, after_ref, first_ref, second_ref):
    rows = x_ref.shape[0]
    for slot, ref in enumerate((x_ref, across_ref, down_ref)):
        send_by_parity(first_ref, second_ref, slot, ref[0], ref[rows - 1])


def first_edges_kernel(
    rows, x_ref, across_ref, down_ref, loads_ref, own_ref, count_ref, low_ref, above_ref, below_ref, first_ref, second_ref
):
    via, fixed, moving = via_terms(own_ref, count_ref, low_ref, below_ref[1], above_ref[0], below_ref[0])

    def right_side(row):
        return fixed(row) + moving(row) - loads_ref[row]

    def diagonal(row, links):
        across = across_ref[row]
        total = across + column_left(across)
        for link in links:
            total = total + down_ref[link]
        return total + via(row)

    inverses = 1.0 / diagonal(1, (0, 1)), 1.0 / diagonal(rows - 2, (rows - 3, rows - 2))
    for slot, pair in enumerate(edges(x_ref, across_ref, down_ref, right_side, inverses, rows)):
        send_by_parity(first_ref, second_ref, slot, *pair)
    send_by_parity(first_ref, second_ref, 2, diagonal(0, (0,)), diagonal(rows - 1, (rows - 2,)))


def next_early_kernel(
    single,
    rows,
    x_ref,
    across_ref,
    down_ref,
    loads_ref,
    inverse_ref,
    own_ref,
    count_ref,
    low_ref,
    weight_ref,
    after_ref,
    first_ref,
    second_ref,
    *factor_refs,
):
    _, layer = place()
    _, fixed, _ = via_terms(own_ref, count_ref, low_ref, weight_ref[1], None, None)

    def right_side(row):
        return fixed(row) - loads_ref[row]

    send_by_parity(first_ref, second_ref, 0, x_ref[0], x_ref[rows - 1])
    inverses = inverse_ref[1], inverse_ref[rows - 2]
    for slot, pair in enumerate(edges(x_ref, across_ref, down_ref, right_side, inverses, rows)):
        send_by_parity(first_ref, second_ref, 1 + slot, *pair)
    if single:
        cells = jnp.where(layer == 0, own_ref[...], low_ref[...])
        weight = jnp.where(layer == 0, weight_of(count_ref[...]), weight_ref[1])
        send_by_parity(first_ref, second_ref, 3, marked(cells, 0, 1.0), marked(cells, rows - 1, 1.0))
        factors = []
        for (edge, within, link), inverse in zip(edge_ends(rows), inverses):
            share = FACTORS[0][1] * inverse * down_ref[link]
            factors.append(marked(cells, edge, weight) + marked(cells, within, weight * share))
        send_by_parity(*factor_refs, 0, *factors)


def next_late_kernel(
    rows, down_ref, inverse_ref, own_ref, count_ref, low_ref, weight_ref, above_ref, below_ref, first_ref, second_ref
):
    _, _, moving = via_terms(own_ref, count_ref, low_ref, weight_ref[1], above_ref[0], below_ref[0])
    found = []
    for edge, within, link in edge_ends(rows):
        change = moving(edge)
        share = FACTORS[0][1] * inverse_ref[within] * down_ref[link]
        found.append((change, change + share * moving(within)))
    for slot, pair in enumerate(zip(*found)):
        send_by_parity(first_ref, second_ref, slot, *pair)


def next_late_single_kernel(first_factor_ref, second_factor_ref, volts_ref, first_ref, second_ref):
    first_ref[0] = first_factor_ref[0] * volts_ref[0]
    second_ref[0] = second_factor_ref[0] * volts_ref[0]


def relaxed(x, flow, side, inverse, previous, sweep):
    keep, gain = FACTORS[sweep]
    update = gain * (inverse * (side + flow) - x)
    if sweep > 0:
        update = update + keep * previous
    return x + update, update


def chosen(single, own, low):
    _, layer = place()
    return [jnp.where(layer == 0, own, low)] if single else [own, low]


def inner_rows(
    rows, outside, x_ref, across_ref, down_ref, side_ref, inverse_ref, work, update_ref, core_ref, keep_ref
):
    sources = [x_ref, *work]
    targets = [*work, core_ref]
    for sweep in range(SWEEPS):
        source, target = sources[sweep], targets[sweep]
        for row in range(sweep, rows - sweep):
            x = source[row]
            flow = beside(x, across_ref[row])
            if row == 0:
                flow = flow + outside[0]
            else:
                flow = flow + down_ref[row - 1] * source[row - 1]
            if row == rows - 1:
                flow = flow + outside[1]
            else:
                flow = flow + down_ref[row] * source[row + 1]
            previous = update_ref[row] if sweep > 0 else None
            value, update = relaxed(x, flow, side_ref[row], inverse_ref[row], previous, sweep)
            target[row] = value
            if sweep < SWEEPS - 1:
                update_ref[row] = update
                for side, depth in ((0, row), (1, rows - 1 - row)):
                    slot = 3 * (2 * sweep + side)
                    if depth == sweep:
                        keep_ref[slot] = value
                        keep_ref[slot + 2] = update
                    if depth == sweep + 1:
                        keep_ref[slot + 1] = value


def outer_rows(side, rows, halo, link, inverse_edge, x_ref, across_ref, down_ref, side_ref, inverse_ref, keep_ref):
    edge_x, edge_q, edge_across = halo

    def row_of(depth):
        return depth if side == 0 else rows - 1 - depth

    def link_out(depth):
        if depth == 0:
            return link
        return down_ref[depth - 1] if side == 0 else down_ref[rows - 1 - depth]

    def link_in(depth):
        return down_ref[depth] if side == 0 else down_ref[rows - 2 - depth]

    values = {-1: edge_x, 0: x_ref[row_of(0)]}
    updates = {}
    for sweep in range(SWEEPS):
        found, changed = {}, {}
        if sweep < SWEEPS - 1:
            x = values[-1]
            flow = beside(x, edge_across) + link * values[0]
            found[-1], changed[-1] = relaxed(x, flow, edge_q[sweep], inverse_edge, updates.get(-1), sweep)
        for depth in range(sweep):
            row = row_of(depth)
            x = values[depth]
            flow = beside(x, across_ref[row]) + link_out(depth) * values[depth - 1] + link_in(depth) * values[depth + 1]
            found[depth], changed[depth] = relaxed(x, flow, side_ref[row], inverse_ref[row], updates[depth], sweep)
        if sweep < SWEEPS - 1:
            slot = 3 * (2 * sweep + side)
            found[sweep] = keep_ref[slot]
            changed[sweep] = keep_ref[slot + 2]
            found[sweep + 1] = keep_ref[slot + 1]
        values, updates = found, changed
    return {row_of(depth): value for depth, value in values.items()}


KEPT = 6 * (SWEEPS - 1)


def first_inner_kernel(
    single,
    rows,
    x_ref,
    across_ref,
    down_ref,
    loads_ref,
    own_ref,
    count_ref,
    low_ref,
    above_ref,
    below_ref,
    first_ref,
    second_ref,
    after_ref,
    core_ref,
    side_ref,
    inverse_ref,
    keep_ref,
    halo_ref,
    picked_ref,
    *scratch,
):
    tile, _ = place()
    via, fixed, moving = via_terms(own_ref, count_ref, low_ref, below_ref[1], above_ref[0], below_ref[0])
    top_x, low_x = taken_by_parity(first_ref, second_ref, 0)
    top_across, low_across = taken_by_parity(first_ref, second_ref, 1)
    link, _ = taken_by_parity(first_ref, second_ref, 2)
    link = jnp.where(tile == 0, 0.0, link)
    for slot, value in enumerate((top_across, low_across, link, top_x, low_x)):
        halo_ref[slot] = value
    for row in range(rows):
        side_ref[row] = fixed(row) + moving(row) - loads_ref[row]
        across = across_ref[row]
        diagonal = across + column_left(across) + down_ref[row] + via(row)
        diagonal = diagonal + (down_ref[row - 1] if row > 0 else link)
        inverse_ref[row] = 1.0 / diagonal
    outside = link * top_x, down_ref[rows - 1] * low_x
    shared = (x_ref, across_ref, down_ref, side_ref, inverse_ref)
    inner_rows(rows, outside, *shared, scratch[:-1], scratch[-1], core_ref, keep_ref)
    for index, cells in enumerate(chosen(single, own_ref[...], low_ref[...])):
        total = jnp.zeros(cells.shape, jnp.float32)
        for row in range(SWEEPS - 1, rows - SWEEPS + 1):
            total = total + marked(cells, row, core_ref[row])
        picked_ref[index] = total


def first_outer_kernel(
    single,
    rows,
    x_ref,
    across_ref,
    down_ref,
    side_ref,
    inverse_ref,
    keep_ref,
    halo_ref,
    picked_ref,
    own_ref,
    low_ref,
    first_ref,
    second_ref,
    core_ref,
    next_ref,
    edge_ref,
    *sends,
):
    top_q0, low_q0 = taken_by_parity(first_ref, second_ref, 0)
    top_q1, low_q1 = taken_by_parity(first_ref, second_ref, 1)
    top_diag, low_diag = taken_by_parity(first_ref, second_ref, 2)
    link, low_link = halo_ref[2], down_ref[rows - 1]
    top_inverse = 1.0 / (top_diag + link)
    low_inverse = 1.0 / (low_diag + low_link)
    edge_ref[0] = top_inverse
    edge_ref[1] = low_inverse
    shared = (x_ref, across_ref, down_ref, side_ref, inverse_ref, keep_ref)
    outer = outer_rows(0, rows, (halo_ref[3], (top_q0, top_q1), halo_ref[0]), link, top_inverse, *shared)
    outer.update(
        outer_rows(1, rows, (halo_ref[4], (low_q0, low_q1), halo_ref[1]), low_link, low_inverse, *shared)
    )
    for row, value in outer.items():
        next_ref[row] = value
    for index, cells in enumerate(chosen(single, own_ref[...], low_ref[...])):
        total = picked_ref[index]
        for row, value in outer.items():
            total = total + marked(cells, row, value)
        sends[index][0] = total


def last_inner_kernel(
    rows,
    x_ref,
    across_ref,
    down_ref,
    loads_ref,
    inverse_ref,
    halo_ref,
    own_ref,
    count_ref,
    low_ref,
    weight_ref,
    above_ref,
    below_ref,
    first_ref,
    second_ref,
    after_ref,
    core_ref,
    side_ref,
    keep_ref,
    *scratch,
):
    _, fixed, moving = via_terms(own_ref, count_ref, low_ref, weight_ref[1], above_ref[0], below_ref[0])
    for row in range(rows):
        side_ref[row] = fixed(row) + moving(row) - loads_ref[row]
    top_x, low_x = taken_by_parity(first_ref, second_ref, 0)
    outside = halo_ref[2] * top_x, down_ref[rows - 1] * low_x
    shared = (x_ref, across_ref, down_ref, side_ref, inverse_ref)
    inner_rows(rows, outside, *shared, scratch[:-1], scratch[-1], core_ref, keep_ref)


def last_outer_kernel(
    single,
    rows,
    x_ref,
    across_ref,
    down_ref,
    side_ref,
    inverse_ref,
    keep_ref,
    halo_ref,
    edge_ref,
    early_first_ref,
    early_second_ref,
    first_ref,
    second_ref,
    core_ref,
    out_ref,
    next_ref,
    held,
    sems,
):
    early = [taken_by_parity(early_first_ref, early_second_ref, slot) for slot in range(4 if single else 3)]
    late = [taken_by_parity(first_ref, second_ref, slot) for slot in range(1 if single else 2)]
    leaving = []
    for side in range(2):
        if single:
            changes = early[3][side] * late[0][side], late[0][side]
        else:
            changes = late[0][side], late[1][side]
        sides = early[1][side] + changes[0], early[2][side] + changes[1]
        outer = outer_rows(
            side,
            rows,
            (early[0][side], sides, halo_ref[side]),
            halo_ref[2] if side == 0 else down_ref[rows - 1],
            edge_ref[side],
            *(x_ref, across_ref, down_ref, side_ref, inverse_ref, keep_ref),
        )
        for row, value in outer.items():
            next_ref[row] = value
        half = rows // 2
        for first, width in chunks_of(held.shape[1], CHUNKS):
            for top in range(side * half, side * half + half, 8):
                for start in range(first, first + width, LANES):
                    held[pl.ds(top, 8), pl.ds(start, LANES)] = next_ref[pl.ds(top, 8), start // LANES, :]
            part = pl.ds(side * half, half), pl.ds(first, width)
            copy = pltpu.make_async_copy(held.at[part], out_ref.at[part], sems.at[len(leaving)])
            copy.start()
            leaving.append(copy)
    for copy in leaving:
        copy.wait()


def call(kernel, name, ins, outs, scratch=(), aliases=None):
    spaces = {"vmem": pltpu.VMEM, "hbm": pltpu.HBM, "any": pl.ANY}
    return pl.pallas_call(
        kernel,
        out_shape=[jax.ShapeDtypeStruct(shape, jnp.float32) for _, shape in outs],
        in_specs=[pl.BlockSpec(memory_space=spaces[space]) for space, _ in ins],
        out_specs=[pl.BlockSpec(memory_space=spaces[space]) for space, _ in outs],
        scratch_shapes=list(scratch),
        input_output_aliases=aliases or {},
        compiler_params=pltpu.CompilerParams(vmem_limit_bytes=40 * 1024 * 1024),
        name=name,
    )(*(array for _, array in ins))


def routes(tiles, layers):
    def at(tile, layer):
        return tile * layers + layer % layers

    everywhere = [(tile, layer) for tile in range(tiles) for layer in range(layers)]
    up = [(at(t, l), at(t, l + 1)) for t, l in everywhere]
    down = [(at(t, l), at(t, l - 1)) for t, l in everywhere]
    first, second = [], []
    for t, l in everywhere:
        first.append((at(t, l), at(t ^ 1, l)))
        beyond = t + 1 if t % 2 else t - 1
        if 0 <= beyond < tiles:
            second.append((at(t, l), at(beyond, l)))
        else:
            second.append((at(t, l), at(t, l + 1)))
    return up, down, first, second


def local(class_index, class_conductance, loads, start_volts, via_cells, via_counts):
    rows, cols = loads.shape[1:]
    lines = cols // LANES
    tiles, layers = lax.axis_size("tile"), lax.axis_size("layer")
    up, down, first, second = routes(tiles, layers)
    single = layers == 2
    move = functools.partial(lax.ppermute, axis_name=("tile", "layer"))

    def rows_of(count):
        return (count, lines, LANES)

    def vmem(*arrays):
        return [("vmem", array) for array in arrays]

    def between_layers(sends):
        if single:
            got = move(sends[0], perm=up)
            return got, got
        return move(sends[1], perm=down), move(sends[0], perm=up)

    def beside_tile(sent):
        return move(sent[0], perm=first), move(sent[1], perm=second)

    field = ("vmem", rows_of(rows))
    work = [pltpu.VMEM(rows_of(rows), jnp.float32)] * SWEEPS
    pick_count = 1 if single else 2
    picks = [("vmem", rows_of(1))] * pick_count

    own = via_cells.reshape(lines, LANES)
    counts = via_counts.reshape(lines, LANES)
    low = move(own, perm=up)
    table = jnp.pad(class_conductance, ((0, 0), (0, LANES - class_conductance.shape[1])))
    across, downward, load = call(unpack_kernel, "unpack", vmem(class_index, table, loads), [field] * 3)
    (x,) = call(unpack_volts_kernel, "unpack_volts", vmem(start_volts), [field])
    vias = (own, counts, low)
    sends = call(
        functools.partial(links_kernel, single, rows),
        "links",
        vmem(x, own, counts, low),
        [("vmem", rows_of(2))] if single else [("vmem", rows_of(2)), ("vmem", rows_of(1))],
    )
    above, below = between_layers(sends)
    weights = below
    sent = call(
        still_edges_kernel,
        "still_edges",
        vmem(x, across, downward) + [("any", sends[0])],
        [("vmem", rows_of(3))] * 2,
    )
    early = beside_tile(sent)
    sent = call(
        functools.partial(first_edges_kernel, rows),
        "first_edges",
        vmem(x, across, downward, load, *vias, above, below),
        [("vmem", rows_of(3))] * 2,
    )
    got = beside_tile(sent)
    core, side, inverse, keep, halo, picked = call(
        functools.partial(first_inner_kernel, single, rows),
        "first_inner",
        vmem(x, across, downward, load, *vias, above, below, *early) + [("any", sent[1])],
        [field, field, field, ("vmem", rows_of(KEPT)), ("vmem", rows_of(5)), ("vmem", rows_of(pick_count))],
        work,
    )
    x, edge, *sends = call(
        functools.partial(first_outer_kernel, single, rows),
        "first_outer",
        vmem(x, across, downward, side, inverse, keep, halo, picked, own, low, *got, core),
        [field, ("vmem", rows_of(2))] + picks,
        aliases={12: 0},
    )
    above, below = between_layers(sends)
    early_rows, late_rows = (4, 1) if single else (3, 2)
    sent = call(
        functools.partial(next_early_kernel, single, rows),
        "next_early",
        vmem(x, across, downward, load, inverse, *vias, weights) + [("any", sends[0])],
        [("vmem", rows_of(early_rows))] * 2 + [("vmem", rows_of(1))] * (2 if single else 0),
    )
    early = beside_tile(sent[:2])
    if single:
        late = call(
            next_late_single_kernel,
            "next_late",
            vmem(*sent[2:], above),
            [("vmem", rows_of(late_rows))] * 2,
        )
    else:
        late = call(
            functools.partial(next_late_kernel, rows),
            "next_late",
            vmem(downward, inverse, *vias, weights, above, below),
            [("vmem", rows_of(late_rows))] * 2,
        )
    got = beside_tile(late)
    core, side, keep = call(
        functools.partial(last_inner_kernel, rows),
        "last_inner",
        vmem(x, across, downward, load, inverse, halo, *vias, weights, above, below, *early) + [("any", late[1])],
        [field, field, ("vmem", rows_of(KEPT))],
        work,
    )
    volts, _ = call(
        functools.partial(last_outer_kernel, single, rows),
        "last_outer",
        vmem(x, across, downward, side, inverse, keep, halo, edge, *early, *got, core),
        [("hbm", (rows, cols)), field],
        [pltpu.VMEM((rows, cols), jnp.float32), pltpu.SemaphoreType.DMA((2 * CHUNKS,))],
        aliases={12: 1},
    )
    return volts[None]


def solution(mesh):
    placed = (
        P("layer", None, "tile", None),
        P("layer", None),
        P("layer", "tile", None),
        P("layer", "tile", None),
        P("layer", "tile"),
        P("layer", "tile"),
    )
    return jax.shard_map(
        local, mesh=mesh, in_specs=placed, out_specs=P("layer", "tile", None), check_vma=False
    )
```

time: 28.3 us -> 27 us (0.954)
  the two profiles are of different devices: /device:TPU:5 before, /device:TPU:0 now
where the time goes in v3:
time: 27 us; the launch traced here: 26.9 us
  starting transfers between devices  11.9 us (44%)
  waiting for transfers between devices  7.87 us (29%)
  Pallas kernels  5.98 us (22%)
  local copies, waits for them, and re-layouts  1.07 us (4%)
    pallas_call x11, Pallas kernels, call(): pl.pallas_call(kernel, out_shape=[jax.ShapeDtypeStruct(shape, jnp.float32...  5.98 us
    ppermute x8, starting transfers between devices, beside_tile(): return (move(sent[0], perm=first), move(sent[1], perm=second))  5.91 us
    ppermute x2, waiting for transfers between devices, between_layers(): got = move(sends[0], perm=up)  3.79 us
    ppermute x8, waiting for transfers between devices, beside_tile(): return (move(sent[0], perm=first), move(sent[1], perm=second))  3.33 us
    ppermute x1, starting transfers between devices, local(): low = move(own, perm=up)  3.01 us
    ppermute x2, starting transfers between devices, between_layers(): got = move(sends[0], perm=up)  2.95 us
    unnamed x12, local copies, waits for them, and re-layouts  1.06 us
    ppermute x1, waiting for transfers between devices, local(): low = move(own, perm=up)  0.76 us
  transfers between devices with their start and end apart: 11, of which 6 were waited for; matrix products, arithmetic and copies ran while one was open for 0% of the time, Pallas kernels for 15%

profile of v3, /device:TPU:0, one launch (start us, length us, event | category | flops | bytes accessed | tf_op | source)
XLA Modules:
  0.0 26.9 jit_solution(9848841235849470402)
XLA Ops:
  0.0 0.0 copy-start.2
  0.0 0.0 copy-start
  0.0 0.0 copy-start.1
  0.0 3.0 %collective-permute-start = (s32[64,128]{1,0:T(8,128)}, s32[64,128]{1,0:T(8,128)S(1)}, u32[]{:S(2)}, u32[]{:S(2)}) collective-permute-start(s32[64,128]{1,0:T(8,128)} %bitcast.3), channel_id=1, source_target_pairs={{0,1},{1,0},{2,3},{3,2},{4,5},{5,4},{6,7},{7,6},{8,9},{9,8},{10,11... | collective-permute-start | bytes 98312 | tf_op jit(solution)/shard_map/ppermute | solution.py:569
  3.0 0.0 copy-start.3
  3.0 1.0 %copy-done.3 = f32[1,16,8192]{2,1,0:T(8,128)S(1)} copy-done((f32[1,16,8192]{2,1,0:T(8,128)S(1)}, f32[1,16,8192]{2,1,0:T(8,128)}, u32[]{:S(2)}) %copy-start.3) | copy-done | bytes 524312
  4.1 0.3 %unpack_volts.1.x_ref = f32[16,64,128]{2,1,0:T(8,128)S(1)} custom-call(f32[1,16,8192]{2,1,0:T(8,128)S(1)} %copy-done.3), custom_call_target="tpu_custom_call" | custom-call | tf_op jit(solution)/shard_map/unpack_volts/pallas_call | solution.py:509
  4.3 0.0 copy-start.4
  4.4 0.8 %collective-permute-done.low_ref = s32[64,128]{1,0:T(8,128)S(1)} collective-permute-done((s32[64,128]{1,0:T(8,128)}, s32[64,128]{1,0:T(8,128)S(1)}, u32[]{:S(2)}, u32[]{:S(2)}) %collective-permute-start) | collective-permute-done | bytes 32800 | tf_op jit(solution)/shard_map/ppermute | solution.py:569
  5.1 0.0 copy-done.2
  5.1 0.0 copy-done
  5.1 0.0 copy-start.5
  5.1 0.1 links.1.after_ref
  5.2 2.1 %collective-permute-start.1 = (f32[2,64,128]{2,1,0:T(8,128)S(1)}, f32[2,64,128]{2,1,0:T(8,128)S(1)}, u32[]{:S(2)}, u32[]{:S(2)}) collective-permute-start(f32[2,64,128]{2,1,0:T(8,128)S(1)} %links.1.after_ref), channel_id=1, source_target_pairs={{0,1},{1,0},{2,3},{3,2},{4,5},{5,4},{6,7},{7,6},{8,9},{9,8},{10,11... | collective-permute-start | bytes 196616 | tf_op jit(solution)/shard_map/ppermute | solution.py:555
  7.3 0.0 copy-done.5
  7.3 0.0 copy-done.1
  7.3 0.0 copy-done.4
  7.3 1.1 %unpack.1 = (f32[16,64,128]{2,1,0:T(8,128)S(1)}, f32[16,64,128]{2,1,0:T(8,128)S(1)}, f32[16,64,128]{2,1,0:T(8,128)S(1)}) custom-call(s32[1,2,16,8192]{3,2,1,0:T(8,128)S(1)} %copy-done.1, f32[1,128]{1,0:T(1,128)S(1)} %pad.4.table_ref, f32[1,16,8192]{2,1,0:T(8,128)S(1)} %copy-done.4), custom_call_target="tpu_custom_call" | custom-call | tf_op jit(solution)/shard_map/unpack/pallas_call | solution.py:509
  8.5 0.1 collective-permute-start.2
  8.6 0.6 %collective-permute-start.3 = (f32[3,64,128]{2,1,0:T(8,128)S(1)}, f32[3,64,128]{2,1,0:T(8,128)S(1)}, u32[]{:S(2)}, u32[]{:S(2)}) collective-permute-start(f32[3,64,128]{2,1,0:T(8,128)S(1)} %get-tuple-element.35), channel_id=1, source_target_pairs={{0,1},{1,0},{2,4},{3,5},{4,2},{5,3},{6,8},{7,9},{8,6},{9,7},{10,12... | collective-permute-start | bytes 294920 | tf_op jit(solution)/shard_map/ppermute | solution.py:560
  9.1 0.4 %collective-permute-done.1.above_ref.below_ref.weight_ref = f32[2,64,128]{2,1,0:T(8,128)S(1)} collective-permute-done((f32[2,64,128]{2,1,0:T(8,128)S(1)}, f32[2,64,128]{2,1,0:T(8,128)S(1)}, u32[]{:S(2)}, u32[]{:S(2)}) %collective-permute-start.1) | collective-permute-done | bytes 65568 | tf_op jit(solution)/shard_map/ppermute | solution.py:555
  9.5 0.2 first_edges.1
  9.7 0.8 %collective-permute-start.4 = (f32[3,64,128]{2,1,0:T(8,128)S(1)}, f32[3,64,128]{2,1,0:T(8,128)S(1)}, u32[]{:S(2)}, u32[]{:S(2)}) collective-permute-start(f32[3,64,128]{2,1,0:T(8,128)S(1)} %get-tuple-element.42), channel_id=1, source_target_pairs={{0,2},{1,3},{2,0},{3,1},{4,6},{5,7},{6,4},{7,5},{8,10},{9,11},{10,... | collective-permute-start | bytes 294920 | tf_op jit(solution)/shard_map/ppermute | solution.py:560
  10.5 1.4 %collective-permute-start.5 = (f32[3,64,128]{2,1,0:T(8,128)S(1)}, f32[3,64,128]{2,1,0:T(8,128)S(1)}, u32[]{:S(2)}, u32[]{:S(2)}) collective-permute-start(f32[3,64,128]{2,1,0:T(8,128)S(1)} %get-tuple-element.36.after_ref), channel_id=1, source_target_pairs={{0,1},{1,0},{2,4},{3,5},{4,2},{5,3},{6,8},{7,9},{8,6},{9,7},{10,12... | collective-permute-start | bytes 294920 | tf_op jit(solution)/shard_map/ppermute | solution.py:560
  11.9 0.0 collective-permute-done.2.first_ref
  11.9 1.4 %collective-permute-done.3.second_ref = f32[3,64,128]{2,1,0:T(8,128)S(1)} collective-permute-done((f32[3,64,128]{2,1,0:T(8,128)S(1)}, f32[3,64,128]{2,1,0:T(8,128)S(1)}, u32[]{:S(2)}, u32[]{:S(2)}) %collective-permute-start.3) | collective-permute-done | bytes 98336 | tf_op jit(solution)/shard_map/ppermute | solution.py:560
  13.2 1.3 %first_inner.1 = (f32[16,64,128]{2,1,0:T(8,128)S(1)}, f32[16,64,128]{2,1,0:T(8,128)S(1)}, f32[16,64,128]{2,1,0:T(8,128)S(1)}, f32[12,64,128]{2,1,0:T(8,128)S(1)}...) custom-call(f32[16,64,128]{2,1,0:T(8,128)S(1)} %unpack_volts.1.x_ref, ...), custom_call_target="tpu_custom_call" | custom-call | tf_op jit(solution)/shard_map/first_inner/pallas_call | solution.py:509
  14.6 0.0 collective-permute-done.4.first_ref
  14.6 0.5 %collective-permute-done.5.second_ref = f32[3,64,128]{2,1,0:T(8,128)S(1)} collective-permute-done((f32[3,64,128]{2,1,0:T(8,128)S(1)}, f32[3,64,128]{2,1,0:T(8,128)S(1)}, u32[]{:S(2)}, u32[]{:S(2)}) %collective-permute-start.5) | collective-permute-done | bytes 98336 | tf_op jit(solution)/shard_map/ppermute | solution.py:560
  15.1 0.3 %first_outer.1 = (f32[16,64,128]{2,1,0:T(8,128)S(1)}, f32[2,64,128]{2,1,0:T(8,128)S(1)}, f32[1,64,128]{2,1,0:T(8,128)S(1)}) custom-call(f32[16,64,128]{2,1,0:T(8,128)S(1)} %unpack_volts.1.x_ref, f32[16,64,128]{2,1,0:T(8,128)S(1)} %get-tuple-element.31.across_ref, f32[16,64,128]{2,1,0:T(8,128)S(1)} %get-tuple-element.32.down_ref, ...), custom_call_target="tpu_custom_call", output_to_operand_aliasing={{0}: (12, {})} | custom-call | tf_op jit(solution)/shard_map/first_outer/pallas_call | solution.py:509
  15.5 0.1 next_early.1
  15.6 0.4 %collective-permute-start.7 = (f32[4,64,128]{2,1,0:T(8,128)S(1)}, f32[4,64,128]{2,1,0:T(8,128)S(1)}, u32[]{:S(2)}, u32[]{:S(2)}) collective-permute-start(f32[4,64,128]{2,1,0:T(8,128)S(1)} %get-tuple-element.46), channel_id=1, source_target_pairs={{0,2},{1,3},{2,0},{3,1},{4,6},{5,7},{6,4},{7,5},{8,10},{9,11},{10,... | collective-permute-start | bytes 393224 | tf_op jit(solution)/shard_map/ppermute | solution.py:560
  16.0 1.2 %collective-permute-start.8 = (f32[4,64,128]{2,1,0:T(8,128)S(1)}, f32[4,64,128]{2,1,0:T(8,128)S(1)}, u32[]{:S(2)}, u32[]{:S(2)}) collective-permute-start(f32[4,64,128]{2,1,0:T(8,128)S(1)} %get-tuple-element.47), channel_id=1, source_target_pairs={{0,1},{1,0},{2,4},{3,5},{4,2},{5,3},{6,8},{7,9},{8,6},{9,7},{10,12... | collective-permute-start | bytes 393224 | tf_op jit(solution)/shard_map/ppermute | solution.py:560
  17.2 0.9 %collective-permute-start.6 = (f32[1,64,128]{2,1,0:T(8,128)S(1)}, f32[1,64,128]{2,1,0:T(8,128)S(1)}, u32[]{:S(2)}, u32[]{:S(2)}) collective-permute-start(f32[1,64,128]{2,1,0:T(8,128)S(1)} %get-tuple-element.45.after_ref), channel_id=1, source_target_pairs={{0,1},{1,0},{2,3},{3,2},{4,5},{5,4},{6,7},{7,6},{8,9},{9,8},{10,11... | collective-permute-start | bytes 98312 | tf_op jit(solution)/shard_map/ppermute | solution.py:555
  18.0 3.4 %collective-permute-done.6.volts_ref.above_ref.below_ref = f32[1,64,128]{2,1,0:T(8,128)S(1)} collective-permute-done((f32[1,64,128]{2,1,0:T(8,128)S(1)}, f32[1,64,128]{2,1,0:T(8,128)S(1)}, u32[]{:S(2)}, u32[]{:S(2)}) %collective-permute-start.6) | collective-permute-done | bytes 32800 | tf_op jit(solution)/shard_map/ppermute | solution.py:555
  21.4 0.2 collective-permute-start.9
  21.6 1.4 %collective-permute-start.10 = (f32[1,64,128]{2,1,0:T(8,128)S(1)}, f32[1,64,128]{2,1,0:T(8,128)S(1)}, u32[]{:S(2)}, u32[]{:S(2)}) collective-permute-start(f32[1,64,128]{2,1,0:T(8,128)S(1)} %get-tuple-element.50.after_ref), channel_id=1, source_target_pairs={{0,1},{1,0},{2,4},{3,5},{4,2},{5,3},{6,8},{7,9},{8,6},{9,7},{10,12... | collective-permute-start | bytes 98312 | tf_op jit(solution)/shard_map/ppermute | solution.py:560
  23.0 0.0 collective-permute-done.7.first_ref.early_first_ref
  23.0 0.0 collective-permute-done.8.second_ref.early_second_ref
  23.0 1.1 %last_inner.1 = (f32[16,64,128]{2,1,0:T(8,128)S(1)}, f32[16,64,128]{2,1,0:T(8,128)S(1)}, f32[12,64,128]{2,1,0:T(8,128)S(1)}) custom-call(f32[16,64,128]{2,1,0:T(8,128)S(1)} %get-tuple-element.44.x_ref, f32[16,64,128]{2,1,0:T(8,128)S(1)} %get-tuple-element.31.across_ref, f32[16,64,128]{2,1,0:T(8,128)S(1)} %get-tuple-element.32.down_ref, ...), custom_call_target="tpu_custom_call" | custom-call | tf_op jit(solution)/shard_map/last_inner/pallas_call | solution.py:509
  24.1 0.0 collective-permute-done.9.first_ref
  24.1 1.4 %collective-permute-done.10.second_ref = f32[1,64,128]{2,1,0:T(8,128)S(1)} collective-permute-done((f32[1,64,128]{2,1,0:T(8,128)S(1)}, f32[1,64,128]{2,1,0:T(8,128)S(1)}, u32[]{:S(2)}, u32[]{:S(2)}) %collective-permute-start.10) | collective-permute-done | bytes 32800 | tf_op jit(solution)/shard_map/ppermute | solution.py:560
  25.5 1.4 %last_outer.1 = (f32[16,8192]{1,0:T(8,128)}, f32[16,64,128]{2,1,0:T(8,128)S(1)}) custom-call(f32[16,64,128]{2,1,0:T(8,128)S(1)} %get-tuple-element.44.x_ref, f32[16,64,128]{2,1,0:T(8,128)S(1)} %get-tuple-element.31.across_ref, f32[16,64,128]{2,1,0:T(8,128)S(1)} %get-tuple-element.32.down_ref, ...), custom_call_target="tpu_custom_call", output_to_operand_aliasing={{1}: (12, {})} | custom-call | tf_op jit(solution)/shard_map/last_outer/pallas_call | solution.py:509
  (3 shorter events, 0.0 us)
Async XLA Ops:
  0.0 5.1 %copy-start.2 = (s32[1,8192]{1,0:T(1,128)S(1)}, s32[1,8192]{1,0:T(1,128)}, u32[]{:S(2)}) copy-start(s32[1,8192]{1,0:T(1,128)} %param.11) | copy-start | bytes 98308
  0.0 5.1 %copy-start = (s32[1,8192]{1,0:T(1,128)S(1)}, s32[1,8192]{1,0:T(1,128)}, u32[]{:S(2)}) copy-start(s32[1,8192]{1,0:T(1,128)} %param.10) | copy-start | bytes 98308
  0.0 7.3 %copy-start.1 = (s32[1,2,16,8192]{3,2,1,0:T(8,128)S(1)}, s32[1,2,16,8192]{3,2,1,0:T(8,128)}, u32[]{:S(2)}) copy-start(s32[1,2,16,8192]{3,2,1,0:T(8,128)} %index_ref.1) | copy-start | bytes 3145732
  0.0 5.1 %collective-permute-start = (s32[64,128]{1,0:T(8,128)}, s32[64,128]{1,0:T(8,128)S(1)}, u32[]{:S(2)}, u32[]{:S(2)}) collective-permute-start(s32[64,128]{1,0:T(8,128)} %bitcast.3), channel_id=1, source_target_pairs={{0,1},{1,0},{2,3},{3,2},{4,5},{5,4},{6,7},{7,6},{8,9},{9,8},{10,11... | collective-permute-start | bytes 98312 | tf_op jit(solution)/shard_map/ppermute | solution.py:569
  3.0 1.0 %copy-start.3 = (f32[1,16,8192]{2,1,0:T(8,128)S(1)}, f32[1,16,8192]{2,1,0:T(8,128)}, u32[]{:S(2)}) copy-start(f32[1,16,8192]{2,1,0:T(8,128)} %volts_ref.1) | copy-start | bytes 1572868
  4.3 3.0 %copy-start.4 = (f32[1,16,8192]{2,1,0:T(8,128)S(1)}, f32[1,16,8192]{2,1,0:T(8,128)}, u32[]{:S(2)}) copy-start(f32[1,16,8192]{2,1,0:T(8,128)} %loads_ref.1) | copy-start | bytes 1572868
  5.1 2.2 %copy-start.5 = (f32[1,16]{1,0:T(1,128)S(1)}, f32[1,16]{1,0:T(1,128)}, u32[]{:S(2)}) copy-start(f32[1,16]{1,0:T(1,128)} %param.7) | copy-start | bytes 196
  5.2 4.3 %collective-permute-start.1 = (f32[2,64,128]{2,1,0:T(8,128)S(1)}, f32[2,64,128]{2,1,0:T(8,128)S(1)}, u32[]{:S(2)}, u32[]{:S(2)}) collective-permute-start(f32[2,64,128]{2,1,0:T(8,128)S(1)} %links.1.after_ref), channel_id=1, source_target_pairs={{0,1},{1,0},{2,3},{3,2},{4,5},{5,4},{6,7},{7,6},{8,9},{9,8},{10,11... | collective-permute-start | bytes 196616 | tf_op jit(solution)/shard_map/ppermute | solution.py:555
  8.5 3.4 %collective-permute-start.2 = (f32[3,64,128]{2,1,0:T(8,128)S(1)}, f32[3,64,128]{2,1,0:T(8,128)S(1)}, u32[]{:S(2)}, u32[]{:S(2)}) collective-permute-start(f32[3,64,128]{2,1,0:T(8,128)S(1)} %get-tuple-element.34), channel_id=1, source_target_pairs={{0,2},{1,3},{2,0},{3,1},{4,6},{5,7},{6,4},{7,5},{8,10},{9,11},{10,... | collective-permute-start | bytes 294920 | tf_op jit(solution)/shard_map/ppermute | solution.py:560
  8.6 4.7 %collective-permute-start.3 = (f32[3,64,128]{2,1,0:T(8,128)S(1)}, f32[3,64,128]{2,1,0:T(8,128)S(1)}, u32[]{:S(2)}, u32[]{:S(2)}) collective-permute-start(f32[3,64,128]{2,1,0:T(8,128)S(1)} %get-tuple-element.35), channel_id=1, source_target_pairs={{0,1},{1,0},{2,4},{3,5},{4,2},{5,3},{6,8},{7,9},{8,6},{9,7},{10,12... | collective-permute-start | bytes 294920 | tf_op jit(solution)/shard_map/ppermute | solution.py:560
  9.7 4.9 %collective-permute-start.4 = (f32[3,64,128]{2,1,0:T(8,128)S(1)}, f32[3,64,128]{2,1,0:T(8,128)S(1)}, u32[]{:S(2)}, u32[]{:S(2)}) collective-permute-start(f32[3,64,128]{2,1,0:T(8,128)S(1)} %get-tuple-element.42), channel_id=1, source_target_pairs={{0,2},{1,3},{2,0},{3,1},{4,6},{5,7},{6,4},{7,5},{8,10},{9,11},{10,... | collective-permute-start | bytes 294920 | tf_op jit(solution)/shard_map/ppermute | solution.py:560
  10.5 4.6 %collective-permute-start.5 = (f32[3,64,128]{2,1,0:T(8,128)S(1)}, f32[3,64,128]{2,1,0:T(8,128)S(1)}, u32[]{:S(2)}, u32[]{:S(2)}) collective-permute-start(f32[3,64,128]{2,1,0:T(8,128)S(1)} %get-tuple-element.36.after_ref), channel_id=1, source_target_pairs={{0,1},{1,0},{2,4},{3,5},{4,2},{5,3},{6,8},{7,9},{8,6},{9,7},{10,12... | collective-permute-start | bytes 294920 | tf_op jit(solution)/shard_map/ppermute | solution.py:560
  15.6 7.4 %collective-permute-start.7 = (f32[4,64,128]{2,1,0:T(8,128)S(1)}, f32[4,64,128]{2,1,0:T(8,128)S(1)}, u32[]{:S(2)}, u32[]{:S(2)}) collective-permute-start(f32[4,64,128]{2,1,0:T(8,128)S(1)} %get-tuple-element.46), channel_id=1, source_target_pairs={{0,2},{1,3},{2,0},{3,1},{4,6},{5,7},{6,4},{7,5},{8,10},{9,11},{10,... | collective-permute-start | bytes 393224 | tf_op jit(solution)/shard_map/ppermute | solution.py:560
  16.0 7.0 %collective-permute-start.8 = (f32[4,64,128]{2,1,0:T(8,128)S(1)}, f32[4,64,128]{2,1,0:T(8,128)S(1)}, u32[]{:S(2)}, u32[]{:S(2)}) collective-permute-start(f32[4,64,128]{2,1,0:T(8,128)S(1)} %get-tuple-element.47), channel_id=1, source_target_pairs={{0,1},{1,0},{2,4},{3,5},{4,2},{5,3},{6,8},{7,9},{8,6},{9,7},{10,12... | collective-permute-start | bytes 393224 | tf_op jit(solution)/shard_map/ppermute | solution.py:560
  17.2 4.3 %collective-permute-start.6 = (f32[1,64,128]{2,1,0:T(8,128)S(1)}, f32[1,64,128]{2,1,0:T(8,128)S(1)}, u32[]{:S(2)}, u32[]{:S(2)}) collective-permute-start(f32[1,64,128]{2,1,0:T(8,128)S(1)} %get-tuple-element.45.after_ref), channel_id=1, source_target_pairs={{0,1},{1,0},{2,3},{3,2},{4,5},{5,4},{6,7},{7,6},{8,9},{9,8},{10,11... | collective-permute-start | bytes 98312 | tf_op jit(solution)/shard_map/ppermute | solution.py:555
  21.4 2.7 %collective-permute-start.9 = (f32[1,64,128]{2,1,0:T(8,128)S(1)}, f32[1,64,128]{2,1,0:T(8,128)S(1)}, u32[]{:S(2)}, u32[]{:S(2)}) collective-permute-start(f32[1,64,128]{2,1,0:T(8,128)S(1)} %get-tuple-element.54), channel_id=1, source_target_pairs={{0,2},{1,3},{2,0},{3,1},{4,6},{5,7},{6,4},{7,5},{8,10},{9,11},{10,... | collective-permute-start | bytes 98312 | tf_op jit(solution)/shard_map/ppermute | solution.py:560
  21.6 3.9 %collective-permute-start.10 = (f32[1,64,128]{2,1,0:T(8,128)S(1)}, f32[1,64,128]{2,1,0:T(8,128)S(1)}, u32[]{:S(2)}, u32[]{:S(2)}) collective-permute-start(f32[1,64,128]{2,1,0:T(8,128)S(1)} %get-tuple-element.50.after_ref), channel_id=1, source_target_pairs={{0,1},{1,0},{2,4},{3,5},{4,2},{5,3},{6,8},{7,9},{8,6},{9,7},{10,12... | collective-permute-start | bytes 98312 | tf_op jit(solution)/shard_map/ppermute | solution.py:560

commit v4 on v3

--- a/solution.py
+++ b/solution.py
@@ -72,15 +72,15 @@
     return [(first, width) for first in range(0, cols, width)]
 
 
-def unpack_volts_kernel(volts_ref, x_ref):
-    rows, cols = volts_ref.shape[1:]
+def unpack_field_kernel(field_ref, out_ref):
+    rows, cols = field_ref.shape[1:]
     for top in range(0, rows, 8):
         for start in range(0, cols, LANES):
-            x_ref[pl.ds(top, 8), start // LANES, :] = volts_ref[0, pl.ds(top, 8), pl.ds(start, LANES)]
-
-
-def unpack_kernel(index_ref, table_ref, loads_ref, across_ref, down_ref, loads_out):
-    rows, cols = loads_ref.shape[1:]
+            out_ref[pl.ds(top, 8), start // LANES, :] = field_ref[0, pl.ds(top, 8), pl.ds(start, LANES)]
+
+
+def unpack_index_kernel(index_ref, table_ref, across_ref, down_ref):
+    rows, cols = index_ref.shape[2:]
     tile, _ = place()
     last_tile = tile == lax.axis_size("tile") - 1
     table = jnp.broadcast_to(table_ref[...], (8, LANES))
@@ -98,10 +98,9 @@
             if top + 8 == rows:
                 down = jnp.where((sub == 7) & last_tile, 0.0, down)
             down_ref[part, line, :] = down
-            loads_out[part, line, :] = loads_ref[0, part, here]
-
-
-def links_kernel(single, rows, x_ref, own_ref, count_ref, low_ref, *out_refs):
+
+
+def links_kernel(single, rows, x_ref, own_ref, count_ref, low_ref, after_ref, *out_refs):
     for out_ref, cells in zip(out_refs, chosen(single, own_ref[...], low_ref[...])):
         out_ref[0] = pick(x_ref, cells, rows)
     out_refs[0][1] = weight_of(count_ref[...])
@@ -164,7 +163,7 @@
     return tuple(zip(*found))
 
 
-def still_edges_kernel(x_ref, across_ref, down_ref, after_ref, first_ref, second_ref):
+def still_edges_kernel(x_ref, across_ref, down_ref, first_ref, second_ref):
     rows = x_ref.shape[0]
     for slot, ref in enumerate((x_ref, across_ref, down_ref)):
         send_by_parity(first_ref, second_ref, slot, ref[0], ref[rows - 1])
@@ -504,7 +503,7 @@
         copy.wait()
 
 
-def call(kernel, name, ins, outs, scratch=(), aliases=None):
+def call(kernel, name, ins, outs, scratch=(), aliases=None, work=None):
     spaces = {"vmem": pltpu.VMEM, "hbm": pltpu.HBM, "any": pl.ANY}
     return pl.pallas_call(
         kernel,
@@ -514,6 +513,7 @@
         scratch_shapes=list(scratch),
         input_output_aliases=aliases or {},
         compiler_params=pltpu.CompilerParams(vmem_limit_bytes=40 * 1024 * 1024),
+        cost_estimate=work and pl.CostEstimate(flops=work, bytes_accessed=work, transcendentals=0),
         name=name,
     )(*(array for _, array in ins))
 
@@ -568,24 +568,20 @@
     counts = via_counts.reshape(lines, LANES)
     low = move(own, perm=up)
     table = jnp.pad(class_conductance, ((0, 0), (0, LANES - class_conductance.shape[1])))
-    across, downward, load = call(unpack_kernel, "unpack", vmem(class_index, table, loads), [field] * 3)
-    (x,) = call(unpack_volts_kernel, "unpack_volts", vmem(start_volts), [field])
+    across, downward = call(unpack_index_kernel, "unpack_index", vmem(class_index, table), [field] * 2)
+    (x,) = call(unpack_field_kernel, "unpack_volts", vmem(start_volts), [field])
+    still = call(still_edges_kernel, "still_edges", vmem(x, across, downward), [("vmem", rows_of(3))] * 2)
     vias = (own, counts, low)
     sends = call(
         functools.partial(links_kernel, single, rows),
         "links",
-        vmem(x, own, counts, low),
+        vmem(x, own, counts, low) + [("any", still[0])],
         [("vmem", rows_of(2))] if single else [("vmem", rows_of(2)), ("vmem", rows_of(1))],
     )
     above, below = between_layers(sends)
     weights = below
-    sent = call(
-        still_edges_kernel,
-        "still_edges",
-        vmem(x, across, downward) + [("any", sends[0])],
-        [("vmem", rows_of(3))] * 2,
-    )
-    early = beside_tile(sent)
+    (load,) = call(unpack_field_kernel, "unpack_loads", vmem(loads), [field])
+    early = beside_tile(still)
     sent = call(
         functools.partial(first_edges_kernel, rows),
         "first_edges",
@@ -622,6 +618,7 @@
             "next_late",
             vmem(*sent[2:], above),
             [("vmem", rows_of(late_rows))] * 2,
+            work=2 * 10**10,
         )
     else:
         late = call(
@@ -629,6 +626,7 @@
             "next_late",
             vmem(downward, inverse, *vias, weights, above, below),
             [("vmem", rows_of(late_rows))] * 2,
+            work=2 * 10**10,
         )
     got = beside_tile(late)
     core, side, keep = call(

time: 27 us -> 25.6 us (0.948)
  starting transfers between devices: 11.9 us -> 9.09 us
  local copies, waits for them, and re-layouts: 1.07 us -> 2.12 us
    ppermute x8, starting transfers between devices: 5.91 us -> 4.46 us  [beside_tile(): return (move(sent[0], perm=first), move(sent[1], perm=second))]
    ppermute x2, starting transfers between devices: 2.95 us -> 1.69 us  [between_layers(): got = move(sends[0], perm=up)]
    ppermute x8, waiting for transfers between devices: 3.33 us -> 4.51 us  [beside_tile(): return (move(sent[0], perm=first), move(sent[1], perm=second))]
    unnamed x12, local copies, waits for them, and re-layouts: 1.06 us -> 2.12 us
    ppermute x1, waiting for transfers between devices: 0.76 us -> 0.01 us  [local(): low = move(own, perm=up)]
    pallas_call x11 -> x12, Pallas kernels: 5.98 us -> 6 us  [call(): pl.pallas_call(kernel, out_shape=[jax.ShapeDtypeStruct(shape, jnp.float32...]
  transfers between devices with their start and end apart: 11 -> 11, of which waited for: 6 -> 5; matrix products, arithmetic and copies ran while one was open for 0% -> 0% of each run, Pallas kernels for 15% -> 17%
where the time goes in v4:
time: 25.6 us; the launch traced here: 25.4 us
  starting transfers between devices  9.09 us (36%)
  waiting for transfers between devices  8.07 us (32%)
  Pallas kernels  6 us (23%)
  local copies, waits for them, and re-layouts  2.12 us (8%)
    pallas_call x12, Pallas kernels, call(): pl.pallas_call(kernel, out_shape=[jax.ShapeDtypeStruct(shape, jnp.float32...  6 us
    ppermute x8, waiting for transfers between devices, beside_tile(): return (move(sent[0], perm=first), move(sent[1], perm=second))  4.51 us
    ppermute x8, starting transfers between devices, beside_tile(): return (move(sent[0], perm=first), move(sent[1], perm=second))  4.46 us
    ppermute x2, waiting for transfers between devices, between_layers(): got = move(sends[0], perm=up)  3.56 us
    ppermute x1, starting transfers between devices, local(): low = move(own, perm=up)  2.94 us
    unnamed x12, local copies, waits for them, and re-layouts  2.12 us
    ppermute x2, starting transfers between devices, between_layers(): got = move(sends[0], perm=up)  1.69 us
  transfers between devices with their start and end apart: 11, of which 5 were waited for; matrix products, arithmetic and copies ran while one was open for 0% of the time, Pallas kernels for 17%

profile of v4, /device:TPU:0, one launch (start us, length us, event | category | flops | bytes accessed | tf_op | source)
XLA Modules:
  0.0 25.4 jit_solution(8515654747477960071)
XLA Ops:
  0.0 0.0 copy-start.1
  0.0 2.9 %collective-permute-start = (s32[64,128]{1,0:T(8,128)}, s32[64,128]{1,0:T(8,128)S(1)}, u32[]{:S(2)}, u32[]{:S(2)}) collective-permute-start(s32[64,128]{1,0:T(8,128)} %bitcast.3), channel_id=1, source_target_pairs={{0,1},{1,0},{2,3},{3,2},{4,5},{5,4},{6,7},{7,6},{8,9},{9,8},{10,11... | collective-permute-start | bytes 98312 | tf_op jit(solution)/shard_map/ppermute | solution.py:569
  2.9 0.0 copy-start.3
  2.9 1.0 %copy-done.3 = f32[1,16,8192]{2,1,0:T(8,128)S(1)} copy-done((f32[1,16,8192]{2,1,0:T(8,128)S(1)}, f32[1,16,8192]{2,1,0:T(8,128)}, u32[]{:S(2)}) %copy-start.3) | copy-done | bytes 524312
  4.0 0.0 copy-start.5
  4.0 0.3 %unpack_volts.1.x_ref = f32[16,64,128]{2,1,0:T(8,128)S(1)} custom-call(f32[1,16,8192]{2,1,0:T(8,128)S(1)} %copy-done.3), custom_call_target="tpu_custom_call" | custom-call | tf_op jit(solution)/shard_map/unpack_volts/pallas_call | solution.py:508
  4.3 0.4 %copy-done.5 = f32[1,16]{1,0:T(1,128)S(1)} copy-done((f32[1,16]{1,0:T(1,128)S(1)}, f32[1,16]{1,0:T(1,128)}, u32[]{:S(2)}) %copy-start.5) | copy-done | bytes 88
  4.6 0.0 copy-done.1
  4.6 0.9 %unpack_index.1 = (f32[16,64,128]{2,1,0:T(8,128)S(1)}, f32[16,64,128]{2,1,0:T(8,128)S(1)}) custom-call(s32[1,2,16,8192]{3,2,1,0:T(8,128)S(1)} %copy-done.1, f32[1,128]{1,0:T(1,128)S(1)} %pad.4.table_ref), custom_call_target="tpu_custom_call" | custom-call | tf_op jit(solution)/shard_map/unpack_index/pallas_call | solution.py:508
  5.5 0.0 copy-start
  5.5 0.0 copy-start.2
  5.6 0.0 copy-start.4
  5.6 0.0 collective-permute-done.low_ref
  5.6 0.7 %copy-done = s32[1,8192]{1,0:T(1,128)S(1)} copy-done((s32[1,8192]{1,0:T(1,128)S(1)}, s32[1,8192]{1,0:T(1,128)}, u32[]{:S(2)}) %copy-start) | copy-done | bytes 32792
  6.3 0.0 copy-done.2
  6.3 0.1 links.1
  6.4 0.8 %collective-permute-start.1 = (f32[2,64,128]{2,1,0:T(8,128)S(1)}, f32[2,64,128]{2,1,0:T(8,128)S(1)}, u32[]{:S(2)}, u32[]{:S(2)}) collective-permute-start(f32[2,64,128]{2,1,0:T(8,128)S(1)} %links.1), channel_id=1, source_target_pairs={{0,1},{1,0},{2,3},{3,2},{4,5},{5,4},{6,7},{7,6},{8,9},{9,8},{10,11... | collective-permute-start | bytes 196616 | tf_op jit(solution)/shard_map/ppermute | solution.py:555
  7.2 0.0 collective-permute-start.2
  7.2 1.2 %collective-permute-start.3 = (f32[3,64,128]{2,1,0:T(8,128)S(1)}, f32[3,64,128]{2,1,0:T(8,128)S(1)}, u32[]{:S(2)}, u32[]{:S(2)}) collective-permute-start(f32[3,64,128]{2,1,0:T(8,128)S(1)} %get-tuple-element.33), channel_id=1, source_target_pairs={{0,1},{1,0},{2,4},{3,5},{4,2},{5,3},{6,8},{7,9},{8,6},{9,7},{10,12... | collective-permute-start | bytes 294920 | tf_op jit(solution)/shard_map/ppermute | solution.py:560
  8.5 0.0 copy-done.4
  8.5 0.3 %unpack_loads.1.loads_ref = f32[16,64,128]{2,1,0:T(8,128)S(1)} custom-call(f32[1,16,8192]{2,1,0:T(8,128)S(1)} %copy-done.4), custom_call_target="tpu_custom_call" | custom-call | tf_op jit(solution)/shard_map/unpack_loads/pallas_call | solution.py:508
  8.8 1.9 %collective-permute-done.1.above_ref.below_ref.weight_ref = f32[2,64,128]{2,1,0:T(8,128)S(1)} collective-permute-done((f32[2,64,128]{2,1,0:T(8,128)S(1)}, f32[2,64,128]{2,1,0:T(8,128)S(1)}, u32[]{:S(2)}, u32[]{:S(2)}) %collective-permute-start.1) | collective-permute-done | bytes 65568 | tf_op jit(solution)/shard_map/ppermute | solution.py:555
  10.7 0.2 first_edges.1
  10.9 0.1 collective-permute-start.4
  10.9 0.8 %collective-permute-start.5 = (f32[3,64,128]{2,1,0:T(8,128)S(1)}, f32[3,64,128]{2,1,0:T(8,128)S(1)}, u32[]{:S(2)}, u32[]{:S(2)}) collective-permute-start(f32[3,64,128]{2,1,0:T(8,128)S(1)} %get-tuple-element.34.after_ref), channel_id=1, source_target_pairs={{0,1},{1,0},{2,4},{3,5},{4,2},{5,3},{6,8},{7,9},{8,6},{9,7},{10,12... | collective-permute-start | bytes 294920 | tf_op jit(solution)/shard_map/ppermute | solution.py:560
  11.8 0.0 collective-permute-done.3.second_ref
  11.8 0.0 collective-permute-done.2.first_ref
  11.8 1.3 %first_inner.1 = (f32[16,64,128]{2,1,0:T(8,128)S(1)}, f32[16,64,128]{2,1,0:T(8,128)S(1)}, f32[16,64,128]{2,1,0:T(8,128)S(1)}, f32[12,64,128]{2,1,0:T(8,128)S(1)}...) custom-call(f32[16,64,128]{2,1,0:T(8,128)S(1)} %unpack_volts.1.x_ref, ...), custom_call_target="tpu_custom_call" | custom-call | tf_op jit(solution)/shard_map/first_inner/pallas_call | solution.py:508
  13.2 0.0 collective-permute-done.4.first_ref
  13.2 2.5 %collective-permute-done.5.second_ref = f32[3,64,128]{2,1,0:T(8,128)S(1)} collective-permute-done((f32[3,64,128]{2,1,0:T(8,128)S(1)}, f32[3,64,128]{2,1,0:T(8,128)S(1)}, u32[]{:S(2)}, u32[]{:S(2)}) %collective-permute-start.5) | collective-permute-done | bytes 98336 | tf_op jit(solution)/shard_map/ppermute | solution.py:560
  15.6 0.3 %first_outer.1 = (f32[16,64,128]{2,1,0:T(8,128)S(1)}, f32[2,64,128]{2,1,0:T(8,128)S(1)}, f32[1,64,128]{2,1,0:T(8,128)S(1)}) custom-call(f32[16,64,128]{2,1,0:T(8,128)S(1)} %unpack_volts.1.x_ref, f32[16,64,128]{2,1,0:T(8,128)S(1)} %get-tuple-element.30.across_ref, f32[16,64,128]{2,1,0:T(8,128)S(1)} %get-tuple-element.31.down_ref, ...), custom_call_target="tpu_custom_call", output_to_operand_aliasing={{0}: (12, {})} | custom-call | tf_op jit(solution)/shard_map/first_outer/pallas_call | solution.py:508
  16.0 0.8 %collective-permute-start.6 = (f32[1,64,128]{2,1,0:T(8,128)S(1)}, f32[1,64,128]{2,1,0:T(8,128)S(1)}, u32[]{:S(2)}, u32[]{:S(2)}) collective-permute-start(f32[1,64,128]{2,1,0:T(8,128)S(1)} %get-tuple-element.43.after_ref), channel_id=1, source_target_pairs={{0,1},{1,0},{2,3},{3,2},{4,5},{5,4},{6,7},{7,6},{8,9},{9,8},{10,11... | collective-permute-start | bytes 98312 | tf_op jit(solution)/shard_map/ppermute | solution.py:555
  16.8 0.1 next_early.1
  17.0 0.1 collective-permute-start.7
  17.0 1.3 %collective-permute-start.8 = (f32[4,64,128]{2,1,0:T(8,128)S(1)}, f32[4,64,128]{2,1,0:T(8,128)S(1)}, u32[]{:S(2)}, u32[]{:S(2)}) collective-permute-start(f32[4,64,128]{2,1,0:T(8,128)S(1)} %get-tuple-element.45), channel_id=1, source_target_pairs={{0,1},{1,0},{2,4},{3,5},{4,2},{5,3},{6,8},{7,9},{8,6},{9,7},{10,12... | collective-permute-start | bytes 393224 | tf_op jit(solution)/shard_map/ppermute | solution.py:560
  18.3 1.6 %collective-permute-done.6.volts_ref.above_ref.below_ref = f32[1,64,128]{2,1,0:T(8,128)S(1)} collective-permute-done((f32[1,64,128]{2,1,0:T(8,128)S(1)}, f32[1,64,128]{2,1,0:T(8,128)S(1)}, u32[]{:S(2)}, u32[]{:S(2)}) %collective-permute-start.6) | collective-permute-done | bytes 32800 | tf_op jit(solution)/shard_map/ppermute | solution.py:555
  20.0 0.1 collective-permute-start.9
  20.1 0.8 %collective-permute-start.10 = (f32[1,64,128]{2,1,0:T(8,128)S(1)}, f32[1,64,128]{2,1,0:T(8,128)S(1)}, u32[]{:S(2)}, u32[]{:S(2)}) collective-permute-start(f32[1,64,128]{2,1,0:T(8,128)S(1)} %get-tuple-element.48.after_ref), channel_id=1, source_target_pairs={{0,1},{1,0},{2,4},{3,5},{4,2},{5,3},{6,8},{7,9},{8,6},{9,7},{10,12... | collective-permute-start | bytes 98312 | tf_op jit(solution)/shard_map/ppermute | solution.py:560
  20.9 0.0 collective-permute-done.7.first_ref.early_first_ref
  20.9 1.2 %collective-permute-done.8.second_ref.early_second_ref = f32[4,64,128]{2,1,0:T(8,128)S(1)} collective-permute-done((f32[4,64,128]{2,1,0:T(8,128)S(1)}, f32[4,64,128]{2,1,0:T(8,128)S(1)}, u32[]{:S(2)}, u32[]{:S(2)}) %collective-permute-start.8) | collective-permute-done | bytes 131104 | tf_op jit(solution)/shard_map/ppermute | solution.py:560
  22.1 1.1 %last_inner.1 = (f32[16,64,128]{2,1,0:T(8,128)S(1)}, f32[16,64,128]{2,1,0:T(8,128)S(1)}, f32[12,64,128]{2,1,0:T(8,128)S(1)}) custom-call(f32[16,64,128]{2,1,0:T(8,128)S(1)} %get-tuple-element.42.x_ref, f32[16,64,128]{2,1,0:T(8,128)S(1)} %get-tuple-element.30.across_ref, f32[16,64,128]{2,1,0:T(8,128)S(1)} %get-tuple-element.31.down_ref, ...), custom_call_target="tpu_custom_call" | custom-call | tf_op jit(solution)/shard_map/last_inner/pallas_call | solution.py:508
  23.2 0.0 collective-permute-done.9.first_ref
  23.2 0.8 %collective-permute-done.10.second_ref = f32[1,64,128]{2,1,0:T(8,128)S(1)} collective-permute-done((f32[1,64,128]{2,1,0:T(8,128)S(1)}, f32[1,64,128]{2,1,0:T(8,128)S(1)}, u32[]{:S(2)}, u32[]{:S(2)}) %collective-permute-start.10) | collective-permute-done | bytes 32800 | tf_op jit(solution)/shard_map/ppermute | solution.py:560
  24.0 1.4 %last_outer.1 = (f32[16,8192]{1,0:T(8,128)}, f32[16,64,128]{2,1,0:T(8,128)S(1)}) custom-call(f32[16,64,128]{2,1,0:T(8,128)S(1)} %get-tuple-element.42.x_ref, f32[16,64,128]{2,1,0:T(8,128)S(1)} %get-tuple-element.30.across_ref, f32[16,64,128]{2,1,0:T(8,128)S(1)} %get-tuple-element.31.down_ref, ...), custom_call_target="tpu_custom_call", output_to_operand_aliasing={{1}: (12, {})} | custom-call | tf_op jit(solution)/shard_map/last_outer/pallas_call | solution.py:508
  (3 shorter events, 0.0 us)
Async XLA Ops:
  0.0 4.6 %copy-start.1 = (s32[1,2,16,8192]{3,2,1,0:T(8,128)S(1)}, s32[1,2,16,8192]{3,2,1,0:T(8,128)}, u32[]{:S(2)}) copy-start(s32[1,2,16,8192]{3,2,1,0:T(8,128)} %index_ref.1) | copy-start | bytes 3145732
  0.0 5.6 %collective-permute-start = (s32[64,128]{1,0:T(8,128)}, s32[64,128]{1,0:T(8,128)S(1)}, u32[]{:S(2)}, u32[]{:S(2)}) collective-permute-start(s32[64,128]{1,0:T(8,128)} %bitcast.3), channel_id=1, source_target_pairs={{0,1},{1,0},{2,3},{3,2},{4,5},{5,4},{6,7},{7,6},{8,9},{9,8},{10,11... | collective-permute-start | bytes 98312 | tf_op jit(solution)/shard_map/ppermute | solution.py:569
  2.9 1.0 %copy-start.3 = (f32[1,16,8192]{2,1,0:T(8,128)S(1)}, f32[1,16,8192]{2,1,0:T(8,128)}, u32[]{:S(2)}) copy-start(f32[1,16,8192]{2,1,0:T(8,128)} %field_ref.2) | copy-start | bytes 1572868
  4.0 0.7 %copy-start.5 = (f32[1,16]{1,0:T(1,128)S(1)}, f32[1,16]{1,0:T(1,128)}, u32[]{:S(2)}) copy-start(f32[1,16]{1,0:T(1,128)} %param.7) | copy-start | bytes 196
  5.5 0.8 %copy-start = (s32[1,8192]{1,0:T(1,128)S(1)}, s32[1,8192]{1,0:T(1,128)}, u32[]{:S(2)}) copy-start(s32[1,8192]{1,0:T(1,128)} %param.10) | copy-start | bytes 98308
  5.5 0.8 %copy-start.2 = (s32[1,8192]{1,0:T(1,128)S(1)}, s32[1,8192]{1,0:T(1,128)}, u32[]{:S(2)}) copy-start(s32[1,8192]{1,0:T(1,128)} %param.11) | copy-start | bytes 98308
  5.6 2.9 %copy-start.4 = (f32[1,16,8192]{2,1,0:T(8,128)S(1)}, f32[1,16,8192]{2,1,0:T(8,128)}, u32[]{:S(2)}) copy-start(f32[1,16,8192]{2,1,0:T(8,128)} %field_ref.3) | copy-start | bytes 1572868
  6.4 4.3 %collective-permute-start.1 = (f32[2,64,128]{2,1,0:T(8,128)S(1)}, f32[2,64,128]{2,1,0:T(8,128)S(1)}, u32[]{:S(2)}, u32[]{:S(2)}) collective-permute-start(f32[2,64,128]{2,1,0:T(8,128)S(1)} %links.1), channel_id=1, source_target_pairs={{0,1},{1,0},{2,3},{3,2},{4,5},{5,4},{6,7},{7,6},{8,9},{9,8},{10,11... | collective-permute-start | bytes 196616 | tf_op jit(solution)/shard_map/ppermute | solution.py:555
  7.2 4.6 %collective-permute-start.2 = (f32[3,64,128]{2,1,0:T(8,128)S(1)}, f32[3,64,128]{2,1,0:T(8,128)S(1)}, u32[]{:S(2)}, u32[]{:S(2)}) collective-permute-start(f32[3,64,128]{2,1,0:T(8,128)S(1)} %get-tuple-element.32.after_ref), channel_id=1, source_target_pairs={{0,2},{1,3},{2,0},{3,1},{4,6},{5,7},{6,4},{7,5},{8,10},{9,11},{10,... | collective-permute-start | bytes 294920 | tf_op jit(solution)/shard_map/ppermute | solution.py:560
  7.2 4.6 %collective-permute-start.3 = (f32[3,64,128]{2,1,0:T(8,128)S(1)}, f32[3,64,128]{2,1,0:T(8,128)S(1)}, u32[]{:S(2)}, u32[]{:S(2)}) collective-permute-start(f32[3,64,128]{2,1,0:T(8,128)S(1)} %get-tuple-element.33), channel_id=1, source_target_pairs={{0,1},{1,0},{2,4},{3,5},{4,2},{5,3},{6,8},{7,9},{8,6},{9,7},{10,12... | collective-permute-start | bytes 294920 | tf_op jit(solution)/shard_map/ppermute | solution.py:560
  10.9 2.3 %collective-permute-start.4 = (f32[3,64,128]{2,1,0:T(8,128)S(1)}, f32[3,64,128]{2,1,0:T(8,128)S(1)}, u32[]{:S(2)}, u32[]{:S(2)}) collective-permute-start(f32[3,64,128]{2,1,0:T(8,128)S(1)} %get-tuple-element.40), channel_id=1, source_target_pairs={{0,2},{1,3},{2,0},{3,1},{4,6},{5,7},{6,4},{7,5},{8,10},{9,11},{10,... | collective-permute-start | bytes 294920 | tf_op jit(solution)/shard_map/ppermute | solution.py:560
  10.9 4.7 %collective-permute-start.5 = (f32[3,64,128]{2,1,0:T(8,128)S(1)}, f32[3,64,128]{2,1,0:T(8,128)S(1)}, u32[]{:S(2)}, u32[]{:S(2)}) collective-permute-start(f32[3,64,128]{2,1,0:T(8,128)S(1)} %get-tuple-element.34.after_ref), channel_id=1, source_target_pairs={{0,1},{1,0},{2,4},{3,5},{4,2},{5,3},{6,8},{7,9},{8,6},{9,7},{10,12... | collective-permute-start | bytes 294920 | tf_op jit(solution)/shard_map/ppermute | solution.py:560
  16.0 4.0 %collective-permute-start.6 = (f32[1,64,128]{2,1,0:T(8,128)S(1)}, f32[1,64,128]{2,1,0:T(8,128)S(1)}, u32[]{:S(2)}, u32[]{:S(2)}) collective-permute-start(f32[1,64,128]{2,1,0:T(8,128)S(1)} %get-tuple-element.43.after_ref), channel_id=1, source_target_pairs={{0,1},{1,0},{2,3},{3,2},{4,5},{5,4},{6,7},{7,6},{8,9},{9,8},{10,11... | collective-permute-start | bytes 98312 | tf_op jit(solution)/shard_map/ppermute | solution.py:555
  17.0 3.9 %collective-permute-start.7 = (f32[4,64,128]{2,1,0:T(8,128)S(1)}, f32[4,64,128]{2,1,0:T(8,128)S(1)}, u32[]{:S(2)}, u32[]{:S(2)}) collective-permute-start(f32[4,64,128]{2,1,0:T(8,128)S(1)} %get-tuple-element.44), channel_id=1, source_target_pairs={{0,2},{1,3},{2,0},{3,1},{4,6},{5,7},{6,4},{7,5},{8,10},{9,11},{10,... | collective-permute-start | bytes 393224 | tf_op jit(solution)/shard_map/ppermute | solution.py:560
  17.0 5.0 %collective-permute-start.8 = (f32[4,64,128]{2,1,0:T(8,128)S(1)}, f32[4,64,128]{2,1,0:T(8,128)S(1)}, u32[]{:S(2)}, u32[]{:S(2)}) collective-permute-start(f32[4,64,128]{2,1,0:T(8,128)S(1)} %get-tuple-element.45), channel_id=1, source_target_pairs={{0,1},{1,0},{2,4},{3,5},{4,2},{5,3},{6,8},{7,9},{8,6},{9,7},{10,12... | collective-permute-start | bytes 393224 | tf_op jit(solution)/shard_map/ppermute | solution.py:560
  20.0 3.2 %collective-permute-start.9 = (f32[1,64,128]{2,1,0:T(8,128)S(1)}, f32[1,64,128]{2,1,0:T(8,128)S(1)}, u32[]{:S(2)}, u32[]{:S(2)}) collective-permute-start(f32[1,64,128]{2,1,0:T(8,128)S(1)} %get-tuple-element.52), channel_id=1, source_target_pairs={{0,2},{1,3},{2,0},{3,1},{4,6},{5,7},{6,4},{7,5},{8,10},{9,11},{10,... | collective-permute-start | bytes 98312 | tf_op jit(solution)/shard_map/ppermute | solution.py:560
  20.1 4.0 %collective-permute-start.10 = (f32[1,64,128]{2,1,0:T(8,128)S(1)}, f32[1,64,128]{2,1,0:T(8,128)S(1)}, u32[]{:S(2)}, u32[]{:S(2)}) collective-permute-start(f32[1,64,128]{2,1,0:T(8,128)S(1)} %get-tuple-element.48.after_ref), channel_id=1, source_target_pairs={{0,1},{1,0},{2,4},{3,5},{4,2},{5,3},{6,8},{7,9},{8,6},{9,7},{10,12... | collective-permute-start | bytes 98312 | tf_op jit(solution)/shard_map/ppermute | solution.py:560

commit v5 on v4

--- a/solution.py
+++ b/solution.py
@@ -61,10 +61,6 @@
     for row in range(rows):
         total = total + marked(cells, row, x_ref[row])
     return total
-
-
-def weight_of(counts):
-    return VIA_UNIT * counts.astype(jnp.float32)
 
 
 def chunks_of(cols, count):
@@ -100,16 +96,16 @@
             down_ref[part, line, :] = down
 
 
-def links_kernel(single, rows, x_ref, own_ref, count_ref, low_ref, after_ref, *out_refs):
+def links_kernel(single, rows, x_ref, own_ref, own_weight_ref, low_ref, after_ref, *out_refs):
     for out_ref, cells in zip(out_refs, chosen(single, own_ref[...], low_ref[...])):
         out_ref[0] = pick(x_ref, cells, rows)
-    out_refs[0][1] = weight_of(count_ref[...])
-
-
-def via_terms(own_ref, count_ref, low_ref, low_weight, from_above, from_below):
+    out_refs[0][1] = own_weight_ref[...]
+
+
+def via_terms(own_ref, own_weight_ref, low_ref, low_weight, from_above, from_below):
     _, layer = place()
     on_top = layer == lax.axis_size("layer") - 1
-    own_weight = weight_of(count_ref[...])
+    own_weight = own_weight_ref[...]
     low_weight = jnp.where(layer == 0, 0.0, low_weight)
     fixed_source = jnp.where(on_top, own_weight, 0.0)
     own, low = own_ref[...], low_ref[...]
@@ -163,16 +159,18 @@
     return tuple(zip(*found))
 
 
-def still_edges_kernel(x_ref, across_ref, down_ref, first_ref, second_ref):
+def still_edges_kernel(x_ref, across_ref, down_ref, own_ref, count_ref, first_ref, second_ref, cells_ref, weight_ref):
     rows = x_ref.shape[0]
+    cells_ref[...] = own_ref[...]
+    weight_ref[...] = VIA_UNIT * count_ref[...].astype(jnp.float32)
     for slot, ref in enumerate((x_ref, across_ref, down_ref)):
         send_by_parity(first_ref, second_ref, slot, ref[0], ref[rows - 1])
 
 
 def first_edges_kernel(
-    rows, x_ref, across_ref, down_ref, loads_ref, own_ref, count_ref, low_ref, above_ref, below_ref, first_ref, second_ref
-):
-    via, fixed, moving = via_terms(own_ref, count_ref, low_ref, below_ref[1], above_ref[0], below_ref[0])
+    rows, x_ref, across_ref, down_ref, loads_ref, own_ref, own_weight_ref, low_ref, above_ref, below_ref, first_ref, second_ref
+):
+    via, fixed, moving = via_terms(own_ref, own_weight_ref, low_ref, below_ref[1], above_ref[0], below_ref[0])
 
     def right_side(row):
         return fixed(row) + moving(row) - loads_ref[row]
@@ -199,7 +197,7 @@
     loads_ref,
     inverse_ref,
     own_ref,
-    count_ref,
+    own_weight_ref,
     low_ref,
     weight_ref,
     after_ref,
@@ -208,7 +206,7 @@
     *factor_refs,
 ):
     _, layer = place()
-    _, fixed, _ = via_terms(own_ref, count_ref, low_ref, weight_ref[1], None, None)
+    _, fixed, _ = via_terms(own_ref, own_weight_ref, low_ref, weight_ref[1], None, None)
 
     def right_side(row):
         return fixed(row) - loads_ref[row]
@@ -219,7 +217,7 @@
         send_by_parity(first_ref, second_ref, 1 + slot, *pair)
     if single:
         cells = jnp.where(layer == 0, own_ref[...], low_ref[...])
-        weight = jnp.where(layer == 0, weight_of(count_ref[...]), weight_ref[1])
+        weight = jnp.where(layer == 0, own_weight_ref[...], weight_ref[1])
         send_by_parity(first_ref, second_ref, 3, marked(cells, 0, 1.0), marked(cells, rows - 1, 1.0))
         factors = []
         for (edge, within, link), inverse in zip(edge_ends(rows), inverses):
@@ -229,9 +227,9 @@
 
 
 def next_late_kernel(
-    rows, down_ref, inverse_ref, own_ref, count_ref, low_ref, weight_ref, above_ref, below_ref, first_ref, second_ref
-):
-    _, _, moving = via_terms(own_ref, count_ref, low_ref, weight_ref[1], above_ref[0], below_ref[0])
+    rows, down_ref, inverse_ref, own_ref, own_weight_ref, low_ref, weight_ref, above_ref, below_ref, first_ref, second_ref
+):
+    _, _, moving = via_terms(own_ref, own_weight_ref, low_ref, weight_ref[1], above_ref[0], below_ref[0])
     found = []
     for edge, within, link in edge_ends(rows):
         change = moving(edge)
@@ -260,13 +258,13 @@
 
 
 def inner_rows(
-    rows, outside, x_ref, across_ref, down_ref, side_ref, inverse_ref, work, update_ref, core_ref, keep_ref
+    rows, reach, outside, x_ref, across_ref, down_ref, side_ref, inverse_ref, work, update_ref, core_ref, keep_ref
 ):
     sources = [x_ref, *work]
     targets = [*work, core_ref]
     for sweep in range(SWEEPS):
         source, target = sources[sweep], targets[sweep]
-        for row in range(sweep, rows - sweep):
+        for row in range(sweep + reach, rows - sweep - reach):
             x = source[row]
             flow = beside(x, across_ref[row])
             if row == 0:
@@ -284,14 +282,14 @@
                 update_ref[row] = update
                 for side, depth in ((0, row), (1, rows - 1 - row)):
                     slot = 3 * (2 * sweep + side)
-                    if depth == sweep:
+                    if depth == sweep + reach:
                         keep_ref[slot] = value
                         keep_ref[slot + 2] = update
-                    if depth == sweep + 1:
+                    if depth == sweep + reach + 1:
                         keep_ref[slot + 1] = value
 
 
-def outer_rows(side, rows, halo, link, inverse_edge, x_ref, across_ref, down_ref, side_ref, inverse_ref, keep_ref):
+def outer_rows(side, rows, reach, halo, link, inverse_edge, x_ref, across_ref, down_ref, side_ref, inverse_ref, keep_ref):
     edge_x, edge_q, edge_across = halo
 
     def row_of(depth):
@@ -305,7 +303,9 @@
     def link_in(depth):
         return down_ref[depth] if side == 0 else down_ref[rows - 2 - depth]
 
-    values = {-1: edge_x, 0: x_ref[row_of(0)]}
+    values = {-1: edge_x}
+    for depth in range(reach + 1):
+        values[depth] = x_ref[row_of(depth)]
     updates = {}
     for sweep in range(SWEEPS):
         found, changed = {}, {}
@@ -313,16 +313,16 @@
             x = values[-1]
             flow = beside(x, edge_across) + link * values[0]
             found[-1], changed[-1] = relaxed(x, flow, edge_q[sweep], inverse_edge, updates.get(-1), sweep)
-        for depth in range(sweep):
+        for depth in range(sweep + reach):
             row = row_of(depth)
             x = values[depth]
             flow = beside(x, across_ref[row]) + link_out(depth) * values[depth - 1] + link_in(depth) * values[depth + 1]
-            found[depth], changed[depth] = relaxed(x, flow, side_ref[row], inverse_ref[row], updates[depth], sweep)
+            found[depth], changed[depth] = relaxed(x, flow, side_ref[row], inverse_ref[row], updates.get(depth), sweep)
         if sweep < SWEEPS - 1:
             slot = 3 * (2 * sweep + side)
-            found[sweep] = keep_ref[slot]
-            changed[sweep] = keep_ref[slot + 2]
-            found[sweep + 1] = keep_ref[slot + 1]
+            found[sweep + reach] = keep_ref[slot]
+            changed[sweep + reach] = keep_ref[slot + 2]
+            found[sweep + reach + 1] = keep_ref[slot + 1]
         values, updates = found, changed
     return {row_of(depth): value for depth, value in values.items()}
 
@@ -338,7 +338,7 @@
     down_ref,
     loads_ref,
     own_ref,
-    count_ref,
+    own_weight_ref,
     low_ref,
     above_ref,
     below_ref,
@@ -354,7 +354,7 @@
     *scratch,
 ):
     tile, _ = place()
-    via, fixed, moving = via_terms(own_ref, count_ref, low_ref, below_ref[1], above_ref[0], below_ref[0])
+    via, fixed, moving = via_terms(own_ref, own_weight_ref, low_ref, below_ref[1], above_ref[0], below_ref[0])
     top_x, low_x = taken_by_parity(first_ref, second_ref, 0)
     top_across, low_across = taken_by_parity(first_ref, second_ref, 1)
     link, _ = taken_by_parity(first_ref, second_ref, 2)
@@ -369,7 +369,7 @@
         inverse_ref[row] = 1.0 / diagonal
     outside = link * top_x, down_ref[rows - 1] * low_x
     shared = (x_ref, across_ref, down_ref, side_ref, inverse_ref)
-    inner_rows(rows, outside, *shared, scratch[:-1], scratch[-1], core_ref, keep_ref)
+    inner_rows(rows, 0, outside, *shared, scratch[:-1], scratch[-1], core_ref, keep_ref)
     for index, cells in enumerate(chosen(single, own_ref[...], low_ref[...])):
         total = jnp.zeros(cells.shape, jnp.float32)
         for row in range(SWEEPS - 1, rows - SWEEPS + 1):
@@ -406,9 +406,9 @@
     edge_ref[0] = top_inverse
     edge_ref[1] = low_inverse
     shared = (x_ref, across_ref, down_ref, side_ref, inverse_ref, keep_ref)
-    outer = outer_rows(0, rows, (halo_ref[3], (top_q0, top_q1), halo_ref[0]), link, top_inverse, *shared)
+    outer = outer_rows(0, rows, 0, (halo_ref[3], (top_q0, top_q1), halo_ref[0]), link, top_inverse, *shared)
     outer.update(
-        outer_rows(1, rows, (halo_ref[4], (low_q0, low_q1), halo_ref[1]), low_link, low_inverse, *shared)
+        outer_rows(1, rows, 0, (halo_ref[4], (low_q0, low_q1), halo_ref[1]), low_link, low_inverse, *shared)
     )
     for row, value in outer.items():
         next_ref[row] = value
@@ -426,28 +426,23 @@
     down_ref,
     loads_ref,
     inverse_ref,
-    halo_ref,
     own_ref,
-    count_ref,
+    own_weight_ref,
     low_ref,
     weight_ref,
     above_ref,
     below_ref,
-    first_ref,
-    second_ref,
     after_ref,
     core_ref,
     side_ref,
     keep_ref,
     *scratch,
 ):
-    _, fixed, moving = via_terms(own_ref, count_ref, low_ref, weight_ref[1], above_ref[0], below_ref[0])
+    _, fixed, moving = via_terms(own_ref, own_weight_ref, low_ref, weight_ref[1], above_ref[0], below_ref[0])
     for row in range(rows):
         side_ref[row] = fixed(row) + moving(row) - loads_ref[row]
-    top_x, low_x = taken_by_parity(first_ref, second_ref, 0)
-    outside = halo_ref[2] * top_x, down_ref[rows - 1] * low_x
     shared = (x_ref, across_ref, down_ref, side_ref, inverse_ref)
-    inner_rows(rows, outside, *shared, scratch[:-1], scratch[-1], core_ref, keep_ref)
+    inner_rows(rows, 1, None, *shared, scratch[:-1], scratch[-1], core_ref, keep_ref)
 
 
 def last_outer_kernel(
@@ -483,6 +478,7 @@
         outer = outer_rows(
             side,
             rows,
+            1,
             (early[0][side], sides, halo_ref[side]),
             halo_ref[2] if side == 0 else down_ref[rows - 1],
             edge_ref[side],
@@ -507,9 +503,9 @@
     spaces = {"vmem": pltpu.VMEM, "hbm": pltpu.HBM, "any": pl.ANY}
     return pl.pallas_call(
         kernel,
-        out_shape=[jax.ShapeDtypeStruct(shape, jnp.float32) for _, shape in outs],
+        out_shape=[jax.ShapeDtypeStruct(shape, *(kind or [jnp.float32])) for _, shape, *kind in outs],
         in_specs=[pl.BlockSpec(memory_space=spaces[space]) for space, _ in ins],
-        out_specs=[pl.BlockSpec(memory_space=spaces[space]) for space, _ in outs],
+        out_specs=[pl.BlockSpec(memory_space=spaces[space]) for space, *_ in outs],
         scratch_shapes=list(scratch),
         input_output_aliases=aliases or {},
         compiler_params=pltpu.CompilerParams(vmem_limit_bytes=40 * 1024 * 1024),
@@ -557,25 +553,31 @@
         return move(sends[1], perm=down), move(sends[0], perm=up)
 
     def beside_tile(sent):
-        return move(sent[0], perm=first), move(sent[1], perm=second)
+        across_chips = move(sent[1], perm=second)
+        return move(sent[0], perm=first), across_chips
 
     field = ("vmem", rows_of(rows))
     work = [pltpu.VMEM(rows_of(rows), jnp.float32)] * SWEEPS
     pick_count = 1 if single else 2
     picks = [("vmem", rows_of(1))] * pick_count
 
-    own = via_cells.reshape(lines, LANES)
+    cells = via_cells.reshape(lines, LANES)
     counts = via_counts.reshape(lines, LANES)
-    low = move(own, perm=up)
+    low = move(cells, perm=up)
     table = jnp.pad(class_conductance, ((0, 0), (0, LANES - class_conductance.shape[1])))
     across, downward = call(unpack_index_kernel, "unpack_index", vmem(class_index, table), [field] * 2)
     (x,) = call(unpack_field_kernel, "unpack_volts", vmem(start_volts), [field])
-    still = call(still_edges_kernel, "still_edges", vmem(x, across, downward), [("vmem", rows_of(3))] * 2)
-    vias = (own, counts, low)
+    *still, own, own_weight = call(
+        still_edges_kernel,
+        "still_edges",
+        vmem(x, across, downward, cells, counts),
+        [("vmem", rows_of(3))] * 2 + [("vmem", cells.shape, cells.dtype), ("vmem", cells.shape)],
+    )
+    vias = (own, own_weight, low)
     sends = call(
         functools.partial(links_kernel, single, rows),
         "links",
-        vmem(x, own, counts, low) + [("any", still[0])],
+        vmem(x, *vias) + [("any", still[0])],
         [("vmem", rows_of(2))] if single else [("vmem", rows_of(2)), ("vmem", rows_of(1))],
     )
     above, below = between_layers(sends)
@@ -632,7 +634,7 @@
     core, side, keep = call(
         functools.partial(last_inner_kernel, rows),
         "last_inner",
-        vmem(x, across, downward, load, inverse, halo, *vias, weights, above, below, *early) + [("any", late[1])],
+        vmem(x, across, downward, load, inverse, *vias, weights, above, below) + [("any", late[1])],
         [field, field, ("vmem", rows_of(KEPT))],
         work,
     )

time: 25.6 us -> 25.1 us (0.980)
  starting transfers between devices: 9.09 us -> 10.4 us
  waiting for transfers between devices: 8.07 us -> 6.9 us
  local copies, waits for them, and re-layouts: 2.12 us -> 1.43 us
    ppermute x2, starting transfers between devices: 1.69 us -> 3.02 us  [between_layers(): got = move(sends[0], perm=up)]
    ppermute x9, waiting for transfers between devices: 4.51 us -> 3.34 us  [the longest x4 3.33 us: beside_tile(): across_chips = move(sent[1], perm=second)]
    unnamed x12, local copies, waits for them, and re-layouts: 2.12 us -> 1.42 us
  transfers between devices with their start and end apart: 11 -> 11, of which waited for: 5 -> 4; matrix products, arithmetic and copies ran while one was open for 0% -> 0% of each run, Pallas kernels for 17% -> 16%
where the time goes in v5:
time: 25.1 us; the launch traced here: 24.9 us
  starting transfers between devices  10.4 us (41%)
  waiting for transfers between devices  6.9 us (27%)
  Pallas kernels  6.03 us (24%)
  local copies, waits for them, and re-layouts  1.43 us (6%)
    pallas_call x12, Pallas kernels, call(): pl.pallas_call(kernel, out_shape=[jax.ShapeDtypeStruct(shape, *(kind or [...  6.03 us
    ppermute x4, starting transfers between devices, beside_tile(): across_chips = move(sent[1], perm=second)  4.25 us
    ppermute x2, waiting for transfers between devices, between_layers(): got = move(sends[0], perm=up)  3.56 us
    ppermute x4, waiting for transfers between devices, beside_tile(): across_chips = move(sent[1], perm=second)  3.33 us
    ppermute x2, starting transfers between devices, between_layers(): got = move(sends[0], perm=up)  3.02 us
    ppermute x1, starting transfers between devices, local(): low = move(cells, perm=up)  2.94 us
    unnamed x12, local copies, waits for them, and re-layouts  1.42 us
  transfers between devices with their start and end apart: 11, of which 4 were waited for; matrix products, arithmetic and copies ran while one was open for 0% of the time, Pallas kernels for 16%

profile of v5, /device:TPU:0, one launch (start us, length us, event | category | flops | bytes accessed | tf_op | source)
XLA Modules:
  0.0 24.9 jit_solution(13649138618331036325)
XLA Ops:
  0.0 0.0 copy-start
  0.0 2.9 %collective-permute-start = (s32[64,128]{1,0:T(8,128)}, s32[64,128]{1,0:T(8,128)S(1)}, u32[]{:S(2)}, u32[]{:S(2)}) collective-permute-start(s32[64,128]{1,0:T(8,128)} %bitcast.4), channel_id=1, source_target_pairs={{0,1},{1,0},{2,3},{3,2},{4,5},{5,4},{6,7},{7,6},{8,9},{9,8},{10,11... | collective-permute-start | bytes 98312 | tf_op jit(solution)/shard_map/ppermute | solution.py:566
  2.9 0.0 copy-start.1
  2.9 1.0 %copy-done.1 = f32[1,16,8192]{2,1,0:T(8,128)S(1)} copy-done((f32[1,16,8192]{2,1,0:T(8,128)S(1)}, f32[1,16,8192]{2,1,0:T(8,128)}, u32[]{:S(2)}) %copy-start.1) | copy-done | bytes 524312
  4.0 0.0 copy-start.5
  4.0 0.3 %unpack_volts.1.x_ref = f32[16,64,128]{2,1,0:T(8,128)S(1)} custom-call(f32[1,16,8192]{2,1,0:T(8,128)S(1)} %copy-done.1), custom_call_target="tpu_custom_call" | custom-call | tf_op jit(solution)/shard_map/unpack_volts/pallas_call | solution.py:504
  4.3 0.4 %copy-done.5 = f32[1,16]{1,0:T(1,128)S(1)} copy-done((f32[1,16]{1,0:T(1,128)S(1)}, f32[1,16]{1,0:T(1,128)}, u32[]{:S(2)}) %copy-start.5) | copy-done | bytes 88
  4.6 0.0 copy-done
  4.6 0.0 copy-start.3
  4.7 0.0 copy-start.4
  4.7 0.9 %unpack_index.1 = (f32[16,64,128]{2,1,0:T(8,128)S(1)}, f32[16,64,128]{2,1,0:T(8,128)S(1)}) custom-call(s32[1,2,16,8192]{3,2,1,0:T(8,128)S(1)} %copy-done, f32[1,128]{1,0:T(1,128)S(1)} %pad.4.table_ref), custom_call_target="tpu_custom_call" | custom-call | tf_op jit(solution)/shard_map/unpack_index/pallas_call | solution.py:504
  5.5 0.0 copy-done.3
  5.5 0.0 copy-done.4
  5.6 0.0 copy-start.2
  5.6 0.0 collective-permute-done.low_ref
  5.6 0.1 links.1
  5.7 1.5 %collective-permute-start.1 = (f32[2,64,128]{2,1,0:T(8,128)S(1)}, f32[2,64,128]{2,1,0:T(8,128)S(1)}, u32[]{:S(2)}, u32[]{:S(2)}) collective-permute-start(f32[2,64,128]{2,1,0:T(8,128)S(1)} %links.1), channel_id=1, source_target_pairs={{0,1},{1,0},{2,3},{3,2},{4,5},{5,4},{6,7},{7,6},{8,9},{9,8},{10,11... | collective-permute-start | bytes 196616 | tf_op jit(solution)/shard_map/ppermute | solution.py:551
  7.2 0.0 collective-permute-start.2
  7.2 0.6 %collective-permute-start.3 = (f32[3,64,128]{2,1,0:T(8,128)S(1)}, f32[3,64,128]{2,1,0:T(8,128)S(1)}, u32[]{:S(2)}, u32[]{:S(2)}) collective-permute-start(f32[3,64,128]{2,1,0:T(8,128)S(1)} %get-tuple-element.37), channel_id=1, source_target_pairs={{0,1},{1,0},{2,4},{3,5},{4,2},{5,3},{6,8},{7,9},{8,6},{9,7},{10,12... | collective-permute-start | bytes 294920 | tf_op jit(solution)/shard_map/ppermute | solution.py:556
  7.8 0.0 copy-done.2
  7.8 0.3 %unpack_loads.1.loads_ref = f32[16,64,128]{2,1,0:T(8,128)S(1)} custom-call(f32[1,16,8192]{2,1,0:T(8,128)S(1)} %copy-done.2), custom_call_target="tpu_custom_call" | custom-call | tf_op jit(solution)/shard_map/unpack_loads/pallas_call | solution.py:504
  8.1 1.9 %collective-permute-done.1.above_ref.below_ref.weight_ref = f32[2,64,128]{2,1,0:T(8,128)S(1)} collective-permute-done((f32[2,64,128]{2,1,0:T(8,128)S(1)}, f32[2,64,128]{2,1,0:T(8,128)S(1)}, u32[]{:S(2)}, u32[]{:S(2)}) %collective-permute-start.1) | collective-permute-done | bytes 65568 | tf_op jit(solution)/shard_map/ppermute | solution.py:551
  10.0 0.2 first_edges.1
  10.2 0.1 collective-permute-start.4
  10.3 1.5 %collective-permute-start.5 = (f32[3,64,128]{2,1,0:T(8,128)S(1)}, f32[3,64,128]{2,1,0:T(8,128)S(1)}, u32[]{:S(2)}, u32[]{:S(2)}) collective-permute-start(f32[3,64,128]{2,1,0:T(8,128)S(1)} %get-tuple-element.38.after_ref), channel_id=1, source_target_pairs={{0,1},{1,0},{2,4},{3,5},{4,2},{5,3},{6,8},{7,9},{8,6},{9,7},{10,12... | collective-permute-start | bytes 294920 | tf_op jit(solution)/shard_map/ppermute | solution.py:556
  11.8 0.0 collective-permute-done.3.second_ref
  11.8 0.0 collective-permute-done.2.first_ref
  11.8 1.3 %first_inner.1 = (f32[16,64,128]{2,1,0:T(8,128)S(1)}, f32[16,64,128]{2,1,0:T(8,128)S(1)}, f32[16,64,128]{2,1,0:T(8,128)S(1)}, f32[12,64,128]{2,1,0:T(8,128)S(1)}...) custom-call(f32[16,64,128]{2,1,0:T(8,128)S(1)} %unpack_volts.1.x_ref, ...), custom_call_target="tpu_custom_call" | custom-call | tf_op jit(solution)/shard_map/first_inner/pallas_call | solution.py:504
  13.2 0.0 collective-permute-done.4.first_ref
  13.2 1.8 %collective-permute-done.5.second_ref = f32[3,64,128]{2,1,0:T(8,128)S(1)} collective-permute-done((f32[3,64,128]{2,1,0:T(8,128)S(1)}, f32[3,64,128]{2,1,0:T(8,128)S(1)}, u32[]{:S(2)}, u32[]{:S(2)}) %collective-permute-start.5) | collective-permute-done | bytes 98336 | tf_op jit(solution)/shard_map/ppermute | solution.py:556
  15.0 0.3 %first_outer.1 = (f32[16,64,128]{2,1,0:T(8,128)S(1)}, f32[2,64,128]{2,1,0:T(8,128)S(1)}, f32[1,64,128]{2,1,0:T(8,128)S(1)}) custom-call(f32[16,64,128]{2,1,0:T(8,128)S(1)} %unpack_volts.1.x_ref, f32[16,64,128]{2,1,0:T(8,128)S(1)} %get-tuple-element.32.across_ref, f32[16,64,128]{2,1,0:T(8,128)S(1)} %get-tuple-element.33.down_ref, ...), custom_call_target="tpu_custom_call", output_to_operand_aliasing={{0}: (12, {})} | custom-call | tf_op jit(solution)/shard_map/first_outer/pallas_call | solution.py:504
  15.3 1.5 %collective-permute-start.6 = (f32[1,64,128]{2,1,0:T(8,128)S(1)}, f32[1,64,128]{2,1,0:T(8,128)S(1)}, u32[]{:S(2)}, u32[]{:S(2)}) collective-permute-start(f32[1,64,128]{2,1,0:T(8,128)S(1)} %get-tuple-element.47.after_ref), channel_id=1, source_target_pairs={{0,1},{1,0},{2,3},{3,2},{4,5},{5,4},{6,7},{7,6},{8,9},{9,8},{10,11... | collective-permute-start | bytes 98312 | tf_op jit(solution)/shard_map/ppermute | solution.py:551
  16.8 0.1 next_early.1
  16.9 0.1 collective-permute-start.7
  17.0 0.6 %collective-permute-start.8 = (f32[4,64,128]{2,1,0:T(8,128)S(1)}, f32[4,64,128]{2,1,0:T(8,128)S(1)}, u32[]{:S(2)}, u32[]{:S(2)}) collective-permute-start(f32[4,64,128]{2,1,0:T(8,128)S(1)} %get-tuple-element.55), channel_id=1, source_target_pairs={{0,1},{1,0},{2,4},{3,5},{4,2},{5,3},{6,8},{7,9},{8,6},{9,7},{10,12... | collective-permute-start | bytes 393224 | tf_op jit(solution)/shard_map/ppermute | solution.py:556
  17.7 1.6 %collective-permute-done.6.volts_ref.above_ref.below_ref = f32[1,64,128]{2,1,0:T(8,128)S(1)} collective-permute-done((f32[1,64,128]{2,1,0:T(8,128)S(1)}, f32[1,64,128]{2,1,0:T(8,128)S(1)}, u32[]{:S(2)}, u32[]{:S(2)}) %collective-permute-start.6) | collective-permute-done | bytes 32800 | tf_op jit(solution)/shard_map/ppermute | solution.py:551
  19.3 0.1 collective-permute-start.9
  19.4 1.5 %collective-permute-start.10 = (f32[1,64,128]{2,1,0:T(8,128)S(1)}, f32[1,64,128]{2,1,0:T(8,128)S(1)}, u32[]{:S(2)}, u32[]{:S(2)}) collective-permute-start(f32[1,64,128]{2,1,0:T(8,128)S(1)} %get-tuple-element.50.after_ref), channel_id=1, source_target_pairs={{0,1},{1,0},{2,4},{3,5},{4,2},{5,3},{6,8},{7,9},{8,6},{9,7},{10,12... | collective-permute-start | bytes 98312 | tf_op jit(solution)/shard_map/ppermute | solution.py:556
  20.9 1.0 %last_inner.1 = (f32[16,64,128]{2,1,0:T(8,128)S(1)}, f32[16,64,128]{2,1,0:T(8,128)S(1)}, f32[12,64,128]{2,1,0:T(8,128)S(1)}) custom-call(f32[16,64,128]{2,1,0:T(8,128)S(1)} %get-tuple-element.46.x_ref, f32[16,64,128]{2,1,0:T(8,128)S(1)} %get-tuple-element.32.across_ref, f32[16,64,128]{2,1,0:T(8,128)S(1)} %get-tuple-element.33.down_ref, ...), custom_call_target="tpu_custom_call" | custom-call | tf_op jit(solution)/shard_map/last_inner/pallas_call | solution.py:504
  21.9 0.0 collective-permute-done.9.first_ref
  21.9 1.5 %collective-permute-done.10.second_ref = f32[1,64,128]{2,1,0:T(8,128)S(1)} collective-permute-done((f32[1,64,128]{2,1,0:T(8,128)S(1)}, f32[1,64,128]{2,1,0:T(8,128)S(1)}, u32[]{:S(2)}, u32[]{:S(2)}) %collective-permute-start.10) | collective-permute-done | bytes 32800 | tf_op jit(solution)/shard_map/ppermute | solution.py:556
  23.4 0.0 collective-permute-done.7.early_first_ref
  23.4 0.0 collective-permute-done.8.early_second_ref
  23.4 1.6 %last_outer.1 = (f32[16,8192]{1,0:T(8,128)}, f32[16,64,128]{2,1,0:T(8,128)S(1)}) custom-call(f32[16,64,128]{2,1,0:T(8,128)S(1)} %get-tuple-element.46.x_ref, f32[16,64,128]{2,1,0:T(8,128)S(1)} %get-tuple-element.32.across_ref, f32[16,64,128]{2,1,0:T(8,128)S(1)} %get-tuple-element.33.down_ref, ...), custom_call_target="tpu_custom_call", output_to_operand_aliasing={{1}: (12, {})} | custom-call | tf_op jit(solution)/shard_map/last_outer/pallas_call | solution.py:504
  (3 shorter events, 0.0 us)
Async XLA Ops:
  0.0 4.6 %copy-start = (s32[1,2,16,8192]{3,2,1,0:T(8,128)S(1)}, s32[1,2,16,8192]{3,2,1,0:T(8,128)}, u32[]{:S(2)}) copy-start(s32[1,2,16,8192]{3,2,1,0:T(8,128)} %index_ref.1) | copy-start | bytes 3145732
  0.0 5.6 %collective-permute-start = (s32[64,128]{1,0:T(8,128)}, s32[64,128]{1,0:T(8,128)S(1)}, u32[]{:S(2)}, u32[]{:S(2)}) collective-permute-start(s32[64,128]{1,0:T(8,128)} %bitcast.4), channel_id=1, source_target_pairs={{0,1},{1,0},{2,3},{3,2},{4,5},{5,4},{6,7},{7,6},{8,9},{9,8},{10,11... | collective-permute-start | bytes 98312 | tf_op jit(solution)/shard_map/ppermute | solution.py:566
  2.9 1.0 %copy-start.1 = (f32[1,16,8192]{2,1,0:T(8,128)S(1)}, f32[1,16,8192]{2,1,0:T(8,128)}, u32[]{:S(2)}) copy-start(f32[1,16,8192]{2,1,0:T(8,128)} %field_ref.2) | copy-start | bytes 1572868
  4.0 0.7 %copy-start.5 = (f32[1,16]{1,0:T(1,128)S(1)}, f32[1,16]{1,0:T(1,128)}, u32[]{:S(2)}) copy-start(f32[1,16]{1,0:T(1,128)} %param.7) | copy-start | bytes 196
  4.6 0.9 %copy-start.3 = (s32[1,8192]{1,0:T(1,128)S(1)}, s32[1,8192]{1,0:T(1,128)}, u32[]{:S(2)}) copy-start(s32[1,8192]{1,0:T(1,128)} %param.11) | copy-start | bytes 98308
  4.7 0.9 %copy-start.4 = (s32[1,8192]{1,0:T(1,128)S(1)}, s32[1,8192]{1,0:T(1,128)}, u32[]{:S(2)}) copy-start(s32[1,8192]{1,0:T(1,128)} %param.10) | copy-start | bytes 98308
  5.6 2.2 %copy-start.2 = (f32[1,16,8192]{2,1,0:T(8,128)S(1)}, f32[1,16,8192]{2,1,0:T(8,128)}, u32[]{:S(2)}) copy-start(f32[1,16,8192]{2,1,0:T(8,128)} %field_ref.3) | copy-start | bytes 1572868
  5.7 4.3 %collective-permute-start.1 = (f32[2,64,128]{2,1,0:T(8,128)S(1)}, f32[2,64,128]{2,1,0:T(8,128)S(1)}, u32[]{:S(2)}, u32[]{:S(2)}) collective-permute-start(f32[2,64,128]{2,1,0:T(8,128)S(1)} %links.1), channel_id=1, source_target_pairs={{0,1},{1,0},{2,3},{3,2},{4,5},{5,4},{6,7},{7,6},{8,9},{9,8},{10,11... | collective-permute-start | bytes 196616 | tf_op jit(solution)/shard_map/ppermute | solution.py:551
  7.2 4.6 %collective-permute-start.2 = (f32[3,64,128]{2,1,0:T(8,128)S(1)}, f32[3,64,128]{2,1,0:T(8,128)S(1)}, u32[]{:S(2)}, u32[]{:S(2)}) collective-permute-start(f32[3,64,128]{2,1,0:T(8,128)S(1)} %get-tuple-element.36.after_ref), channel_id=1, source_target_pairs={{0,2},{1,3},{2,0},{3,1},{4,6},{5,7},{6,4},{7,5},{8,10},{9,11},{10,... | collective-permute-start | bytes 294920 | tf_op jit(solution)/shard_map/ppermute | solution.py:557
  7.2 4.6 %collective-permute-start.3 = (f32[3,64,128]{2,1,0:T(8,128)S(1)}, f32[3,64,128]{2,1,0:T(8,128)S(1)}, u32[]{:S(2)}, u32[]{:S(2)}) collective-permute-start(f32[3,64,128]{2,1,0:T(8,128)S(1)} %get-tuple-element.37), channel_id=1, source_target_pairs={{0,1},{1,0},{2,4},{3,5},{4,2},{5,3},{6,8},{7,9},{8,6},{9,7},{10,12... | collective-permute-start | bytes 294920 | tf_op jit(solution)/shard_map/ppermute | solution.py:556
  10.2 3.0 %collective-permute-start.4 = (f32[3,64,128]{2,1,0:T(8,128)S(1)}, f32[3,64,128]{2,1,0:T(8,128)S(1)}, u32[]{:S(2)}, u32[]{:S(2)}) collective-permute-start(f32[3,64,128]{2,1,0:T(8,128)S(1)} %get-tuple-element.44), channel_id=1, source_target_pairs={{0,2},{1,3},{2,0},{3,1},{4,6},{5,7},{6,4},{7,5},{8,10},{9,11},{10,... | collective-permute-start | bytes 294920 | tf_op jit(solution)/shard_map/ppermute | solution.py:557
  10.3 4.7 %collective-permute-start.5 = (f32[3,64,128]{2,1,0:T(8,128)S(1)}, f32[3,64,128]{2,1,0:T(8,128)S(1)}, u32[]{:S(2)}, u32[]{:S(2)}) collective-permute-start(f32[3,64,128]{2,1,0:T(8,128)S(1)} %get-tuple-element.38.after_ref), channel_id=1, source_target_pairs={{0,1},{1,0},{2,4},{3,5},{4,2},{5,3},{6,8},{7,9},{8,6},{9,7},{10,12... | collective-permute-start | bytes 294920 | tf_op jit(solution)/shard_map/ppermute | solution.py:556
  15.3 4.0 %collective-permute-start.6 = (f32[1,64,128]{2,1,0:T(8,128)S(1)}, f32[1,64,128]{2,1,0:T(8,128)S(1)}, u32[]{:S(2)}, u32[]{:S(2)}) collective-permute-start(f32[1,64,128]{2,1,0:T(8,128)S(1)} %get-tuple-element.47.after_ref), channel_id=1, source_target_pairs={{0,1},{1,0},{2,3},{3,2},{4,5},{5,4},{6,7},{7,6},{8,9},{9,8},{10,11... | collective-permute-start | bytes 98312 | tf_op jit(solution)/shard_map/ppermute | solution.py:551
  16.9 6.4 %collective-permute-start.7 = (f32[4,64,128]{2,1,0:T(8,128)S(1)}, f32[4,64,128]{2,1,0:T(8,128)S(1)}, u32[]{:S(2)}, u32[]{:S(2)}) collective-permute-start(f32[4,64,128]{2,1,0:T(8,128)S(1)} %get-tuple-element.54), channel_id=1, source_target_pairs={{0,2},{1,3},{2,0},{3,1},{4,6},{5,7},{6,4},{7,5},{8,10},{9,11},{10,... | collective-permute-start | bytes 393224 | tf_op jit(solution)/shard_map/ppermute | solution.py:557
  17.0 6.3 %collective-permute-start.8 = (f32[4,64,128]{2,1,0:T(8,128)S(1)}, f32[4,64,128]{2,1,0:T(8,128)S(1)}, u32[]{:S(2)}, u32[]{:S(2)}) collective-permute-start(f32[4,64,128]{2,1,0:T(8,128)S(1)} %get-tuple-element.55), channel_id=1, source_target_pairs={{0,1},{1,0},{2,4},{3,5},{4,2},{5,3},{6,8},{7,9},{8,6},{9,7},{10,12... | collective-permute-start | bytes 393224 | tf_op jit(solution)/shard_map/ppermute | solution.py:556
  19.3 2.6 %collective-permute-start.9 = (f32[1,64,128]{2,1,0:T(8,128)S(1)}, f32[1,64,128]{2,1,0:T(8,128)S(1)}, u32[]{:S(2)}, u32[]{:S(2)}) collective-permute-start(f32[1,64,128]{2,1,0:T(8,128)S(1)} %get-tuple-element.56), channel_id=1, source_target_pairs={{0,2},{1,3},{2,0},{3,1},{4,6},{5,7},{6,4},{7,5},{8,10},{9,11},{10,... | collective-permute-start | bytes 98312 | tf_op jit(solution)/shard_map/ppermute | solution.py:557
  19.4 4.0 %collective-permute-start.10 = (f32[1,64,128]{2,1,0:T(8,128)S(1)}, f32[1,64,128]{2,1,0:T(8,128)S(1)}, u32[]{:S(2)}, u32[]{:S(2)}) collective-permute-start(f32[1,64,128]{2,1,0:T(8,128)S(1)} %get-tuple-element.50.after_ref), channel_id=1, source_target_pairs={{0,1},{1,0},{2,4},{3,5},{4,2},{5,3},{6,8},{7,9},{8,6},{9,7},{10,12... | collective-permute-start | bytes 98312 | tf_op jit(solution)/shard_map/ppermute | solution.py:556

commit v6 on v5

--- a/solution.py
+++ b/solution.py
@@ -14,6 +14,7 @@
 UPPER_BOUND = 2.0
 LANES = 128
 CHUNKS = 2
+FILL = 8
 
 
 def chebyshev_terms(count):
@@ -96,12 +97,6 @@
             down_ref[part, line, :] = down
 
 
-def links_kernel(single, rows, x_ref, own_ref, own_weight_ref, low_ref, after_ref, *out_refs):
-    for out_ref, cells in zip(out_refs, chosen(single, own_ref[...], low_ref[...])):
-        out_ref[0] = pick(x_ref, cells, rows)
-    out_refs[0][1] = own_weight_ref[...]
-
-
 def via_terms(own_ref, own_weight_ref, low_ref, low_weight, from_above, from_below):
     _, layer = place()
     on_top = layer == lax.axis_size("layer") - 1
@@ -130,14 +125,20 @@
 def send_by_parity(first_ref, second_ref, slot, top, bottom):
     tile, _ = place()
     even = lax.rem(tile, 2) == 0
-    first_ref[slot] = jnp.where(even, bottom, top)
-    second_ref[slot] = jnp.where(even, top, bottom)
-
-
-def taken_by_parity(first_ref, second_ref, slot):
+    part = pl.ds(slot * top.shape[0], top.shape[0])
+    first_ref[part] = jnp.where(even, bottom, top)
+    second_ref[part] = jnp.where(even, top, bottom)
+    lengths = first_ref.shape[0], second_ref.shape[0]
+    if slot == 0:
+        longer = first_ref if lengths[0] > lengths[1] else second_ref
+        longer[pl.ds(min(lengths), FILL)] = jnp.zeros((FILL, LANES), jnp.float32)
+
+
+def taken_by_parity(first_ref, second_ref, slot, lines):
     tile, _ = place()
     even = lax.rem(tile, 2) == 0
-    first, second = first_ref[slot], second_ref[slot]
+    part = pl.ds(slot * lines, lines)
+    first, second = first_ref[part], second_ref[part]
     return jnp.where(even, second, first), jnp.where(even, first, second)
 
 
@@ -159,12 +160,22 @@
     return tuple(zip(*found))
 
 
-def still_edges_kernel(x_ref, across_ref, down_ref, own_ref, count_ref, first_ref, second_ref, cells_ref, weight_ref):
+def links_kernel(
+    single, x_ref, across_ref, down_ref, own_ref, count_ref, low_ref, first_ref, second_ref, weight_ref, cells_ref, *sends
+):
     rows = x_ref.shape[0]
-    cells_ref[...] = own_ref[...]
-    weight_ref[...] = VIA_UNIT * count_ref[...].astype(jnp.float32)
+    own, low = own_ref[...], low_ref[...]
+    weight = VIA_UNIT * count_ref[...].astype(jnp.float32)
+    cells_ref[...] = own
+    weight_ref[...] = weight
+    links = chosen(single, own, low)
+    for send_ref, cells in zip(sends, links):
+        send_ref[0] = pick(x_ref, cells, rows)
+    sends[0][1] = weight
     for slot, ref in enumerate((x_ref, across_ref, down_ref)):
         send_by_parity(first_ref, second_ref, slot, ref[0], ref[rows - 1])
+    if single:
+        send_by_parity(first_ref, second_ref, 3, marked(links[0], 0, 1.0), marked(links[0], rows - 1, 1.0))
 
 
 def first_edges_kernel(
@@ -218,12 +229,12 @@
     if single:
         cells = jnp.where(layer == 0, own_ref[...], low_ref[...])
         weight = jnp.where(layer == 0, own_weight_ref[...], weight_ref[1])
-        send_by_parity(first_ref, second_ref, 3, marked(cells, 0, 1.0), marked(cells, rows - 1, 1.0))
         factors = []
         for (edge, within, link), inverse in zip(edge_ends(rows), inverses):
             share = FACTORS[0][1] * inverse * down_ref[link]
             factors.append(marked(cells, edge, weight) + marked(cells, within, weight * share))
-        send_by_parity(*factor_refs, 0, *factors)
+        for ref, factor in zip(factor_refs, factors):
+            ref[...] = factor
 
 
 def next_late_kernel(
@@ -239,9 +250,9 @@
         send_by_parity(first_ref, second_ref, slot, *pair)
 
 
-def next_late_single_kernel(first_factor_ref, second_factor_ref, volts_ref, first_ref, second_ref):
-    first_ref[0] = first_factor_ref[0] * volts_ref[0]
-    second_ref[0] = second_factor_ref[0] * volts_ref[0]
+def next_late_single_kernel(top_ref, bottom_ref, volts_ref, first_ref, second_ref):
+    volts = volts_ref[0]
+    send_by_parity(first_ref, second_ref, 0, top_ref[...] * volts, bottom_ref[...] * volts)
 
 
 def relaxed(x, flow, side, inverse, previous, sweep):
@@ -355,11 +366,14 @@
 ):
     tile, _ = place()
     via, fixed, moving = via_terms(own_ref, own_weight_ref, low_ref, below_ref[1], above_ref[0], below_ref[0])
-    top_x, low_x = taken_by_parity(first_ref, second_ref, 0)
-    top_across, low_across = taken_by_parity(first_ref, second_ref, 1)
-    link, _ = taken_by_parity(first_ref, second_ref, 2)
+    top_x, low_x = taken_by_parity(first_ref, second_ref, 0, x_ref.shape[1])
+    top_across, low_across = taken_by_parity(first_ref, second_ref, 1, x_ref.shape[1])
+    link, _ = taken_by_parity(first_ref, second_ref, 2, x_ref.shape[1])
     link = jnp.where(tile == 0, 0.0, link)
-    for slot, value in enumerate((top_across, low_across, link, top_x, low_x)):
+    held = [top_across, low_across, link, top_x, low_x]
+    if single:
+        held.extend(taken_by_parity(first_ref, second_ref, 3, x_ref.shape[1]))
+    for slot, value in enumerate(held):
         halo_ref[slot] = value
     for row in range(rows):
         side_ref[row] = fixed(row) + moving(row) - loads_ref[row]
@@ -397,9 +411,9 @@
     edge_ref,
     *sends,
 ):
-    top_q0, low_q0 = taken_by_parity(first_ref, second_ref, 0)
-    top_q1, low_q1 = taken_by_parity(first_ref, second_ref, 1)
-    top_diag, low_diag = taken_by_parity(first_ref, second_ref, 2)
+    top_q0, low_q0 = taken_by_parity(first_ref, second_ref, 0, x_ref.shape[1])
+    top_q1, low_q1 = taken_by_parity(first_ref, second_ref, 1, x_ref.shape[1])
+    top_diag, low_diag = taken_by_parity(first_ref, second_ref, 2, x_ref.shape[1])
     link, low_link = halo_ref[2], down_ref[rows - 1]
     top_inverse = 1.0 / (top_diag + link)
     low_inverse = 1.0 / (low_diag + low_link)
@@ -466,12 +480,13 @@
     held,
     sems,
 ):
-    early = [taken_by_parity(early_first_ref, early_second_ref, slot) for slot in range(4 if single else 3)]
-    late = [taken_by_parity(first_ref, second_ref, slot) for slot in range(1 if single else 2)]
+    lines = x_ref.shape[1]
+    early = [taken_by_parity(early_first_ref, early_second_ref, slot, lines) for slot in range(3)]
+    late = [taken_by_parity(first_ref, second_ref, slot, lines) for slot in range(1 if single else 2)]
     leaving = []
     for side in range(2):
         if single:
-            changes = early[3][side] * late[0][side], late[0][side]
+            changes = halo_ref[5 + side] * late[0][side], late[0][side]
         else:
             changes = late[0][side], late[1][side]
         sides = early[1][side] + changes[0], early[2][side] + changes[1]
@@ -543,6 +558,9 @@
     def rows_of(count):
         return (count, lines, LANES)
 
+    def messages(count, longer):
+        return [("vmem", (count * lines + (FILL if longer == side else 0), LANES)) for side in range(2)]
+
     def vmem(*arrays):
         return [("vmem", array) for array in arrays]
 
@@ -567,35 +585,32 @@
     table = jnp.pad(class_conductance, ((0, 0), (0, LANES - class_conductance.shape[1])))
     across, downward = call(unpack_index_kernel, "unpack_index", vmem(class_index, table), [field] * 2)
     (x,) = call(unpack_field_kernel, "unpack_volts", vmem(start_volts), [field])
-    *still, own, own_weight = call(
-        still_edges_kernel,
-        "still_edges",
-        vmem(x, across, downward, cells, counts),
-        [("vmem", rows_of(3))] * 2 + [("vmem", cells.shape, cells.dtype), ("vmem", cells.shape)],
+    first_sent, second_sent, own_weight, own, *sends = call(
+        functools.partial(links_kernel, single),
+        "links",
+        vmem(x, across, downward, cells, counts, low),
+        messages(4 if single else 3, 0)
+        + [("vmem", cells.shape), ("vmem", cells.shape, cells.dtype), ("vmem", rows_of(2))]
+        + ([] if single else [("vmem", rows_of(1))]),
     )
     vias = (own, own_weight, low)
-    sends = call(
-        functools.partial(links_kernel, single, rows),
-        "links",
-        vmem(x, *vias) + [("any", still[0])],
-        [("vmem", rows_of(2))] if single else [("vmem", rows_of(2)), ("vmem", rows_of(1))],
-    )
     above, below = between_layers(sends)
     weights = below
     (load,) = call(unpack_field_kernel, "unpack_loads", vmem(loads), [field])
-    early = beside_tile(still)
+    early = beside_tile((first_sent, second_sent))
     sent = call(
         functools.partial(first_edges_kernel, rows),
         "first_edges",
         vmem(x, across, downward, load, *vias, above, below),
-        [("vmem", rows_of(3))] * 2,
+        messages(3, 1),
+        work=2 * 10**10,
     )
     got = beside_tile(sent)
     core, side, inverse, keep, halo, picked = call(
         functools.partial(first_inner_kernel, single, rows),
         "first_inner",
         vmem(x, across, downward, load, *vias, above, below, *early) + [("any", sent[1])],
-        [field, field, field, ("vmem", rows_of(KEPT)), ("vmem", rows_of(5)), ("vmem", rows_of(pick_count))],
+        [field, field, field, ("vmem", rows_of(KEPT)), ("vmem", rows_of(7 if single else 5)), ("vmem", rows_of(pick_count))],
         work,
     )
     x, edge, *sends = call(
@@ -606,12 +621,11 @@
         aliases={12: 0},
     )
     above, below = between_layers(sends)
-    early_rows, late_rows = (4, 1) if single else (3, 2)
     sent = call(
         functools.partial(next_early_kernel, single, rows),
         "next_early",
         vmem(x, across, downward, load, inverse, *vias, weights) + [("any", sends[0])],
-        [("vmem", rows_of(early_rows))] * 2 + [("vmem", rows_of(1))] * (2 if single else 0),
+        messages(3, 0) + [("vmem", cells.shape)] * (2 if single else 0),
     )
     early = beside_tile(sent[:2])
     if single:
@@ -619,7 +633,7 @@
             next_late_single_kernel,
             "next_late",
             vmem(*sent[2:], above),
-            [("vmem", rows_of(late_rows))] * 2,
+            messages(1, 1),
             work=2 * 10**10,
         )
     else:
@@ -627,7 +641,7 @@
             functools.partial(next_late_kernel, rows),
             "next_late",
             vmem(downward, inverse, *vias, weights, above, below),
-            [("vmem", rows_of(late_rows))] * 2,
+            messages(2, 1),
             work=2 * 10**10,
         )
     got = beside_tile(late)

time: 25.1 us -> 25.1 us (level)
  waiting for transfers between devices: 6.9 us -> 2.84 us
  starting transfers between devices: 10.4 us -> 14 us
  Pallas kernels: 6.03 us -> 6.55 us
    ppermute x4, starting transfers between devices: 0.22 us -> 3.32 us  [beside_tile(): return (move(sent[0], perm=first), across_chips)]
    ppermute x2, waiting for transfers between devices: 3.56 us -> 0.83 us  [between_layers(): got = move(sends[0], perm=up)]
    ppermute x4, waiting for transfers between devices: 3.33 us -> 1.99 us  [beside_tile(): across_chips = move(sent[1], perm=second)]
    pallas_call x12 -> x11, Pallas kernels: 6.03 us -> 6.55 us  [call(): pl.pallas_call(kernel, out_shape=[jax.ShapeDtypeStruct(shape, *(kind or [...]
    ppermute x4, starting transfers between devices: 4.25 us -> 4.67 us  [beside_tile(): across_chips = move(sent[1], perm=second)]
  transfers between devices with their start and end apart: 11 -> 11, of which waited for: 4 -> 5; matrix products, arithmetic and copies ran while one was open for 0% -> 0% of each run, Pallas kernels for 16% -> 18%
where the time goes in v6:
time: 25.1 us; the launch traced here: 25 us
  starting transfers between devices  14 us (56%)
  Pallas kernels  6.55 us (26%)
  waiting for transfers between devices  2.84 us (11%)
  local copies, waits for them, and re-layouts  1.43 us (6%)
    pallas_call x11, Pallas kernels, call(): pl.pallas_call(kernel, out_shape=[jax.ShapeDtypeStruct(shape, *(kind or [...  6.55 us
    ppermute x4, starting transfers between devices, beside_tile(): across_chips = move(sent[1], perm=second)  4.67 us
    ppermute x4, starting transfers between devices, beside_tile(): return (move(sent[0], perm=first), across_chips)  3.32 us
    ppermute x2, starting transfers between devices, between_layers(): got = move(sends[0], perm=up)  3.11 us
    ppermute x1, starting transfers between devices, local(): low = move(cells, perm=up)  2.94 us
    ppermute x4, waiting for transfers between devices, beside_tile(): across_chips = move(sent[1], perm=second)  1.99 us
    unnamed x12, local copies, waits for them, and re-layouts  1.42 us
    ppermute x2, waiting for transfers between devices, between_layers(): got = move(sends[0], perm=up)  0.83 us
  transfers between devices with their start and end apart: 11, of which 5 were waited for; matrix products, arithmetic and copies ran while one was open for 0% of the time, Pallas kernels for 18%

profile of v6, /device:TPU:0, one launch (start us, length us, event | category | flops | bytes accessed | tf_op | source)
XLA Modules:
  0.0 25.0 jit_solution(2380127341434506486)
XLA Ops:
  0.0 0.0 copy-start
  0.0 2.9 %collective-permute-start = (s32[64,128]{1,0:T(8,128)}, s32[64,128]{1,0:T(8,128)S(1)}, u32[]{:S(2)}, u32[]{:S(2)}) collective-permute-start(s32[64,128]{1,0:T(8,128)} %bitcast.3), channel_id=1, source_target_pairs={{0,1},{1,0},{2,3},{3,2},{4,5},{5,4},{6,7},{7,6},{8,9},{9,8},{10,11... | collective-permute-start | bytes 98312 | tf_op jit(solution)/shard_map/ppermute | solution.py:584
  2.9 0.0 copy-start.1
  2.9 1.0 %copy-done.1 = f32[1,16,8192]{2,1,0:T(8,128)S(1)} copy-done((f32[1,16,8192]{2,1,0:T(8,128)S(1)}, f32[1,16,8192]{2,1,0:T(8,128)}, u32[]{:S(2)}) %copy-start.1) | copy-done | bytes 524312
  4.0 0.0 copy-start.5
  4.0 0.3 %unpack_volts.1.x_ref = f32[16,64,128]{2,1,0:T(8,128)S(1)} custom-call(f32[1,16,8192]{2,1,0:T(8,128)S(1)} %copy-done.1), custom_call_target="tpu_custom_call" | custom-call | tf_op jit(solution)/shard_map/unpack_volts/pallas_call | solution.py:519
  4.3 0.4 %copy-done.5 = f32[1,16]{1,0:T(1,128)S(1)} copy-done((f32[1,16]{1,0:T(1,128)S(1)}, f32[1,16]{1,0:T(1,128)}, u32[]{:S(2)}) %copy-start.5) | copy-done | bytes 88
  4.6 0.0 copy-done
  4.6 0.0 copy-start.3
  4.7 0.0 copy-start.4
  4.7 0.9 %unpack_index.1 = (f32[16,64,128]{2,1,0:T(8,128)S(1)}, f32[16,64,128]{2,1,0:T(8,128)S(1)}) custom-call(s32[1,2,16,8192]{3,2,1,0:T(8,128)S(1)} %copy-done, f32[1,128]{1,0:T(1,128)S(1)} %pad.4.table_ref), custom_call_target="tpu_custom_call" | custom-call | tf_op jit(solution)/shard_map/unpack_index/pallas_call | solution.py:519
  5.5 0.0 collective-permute-done.low_ref
  5.5 0.0 copy-done.3
  5.6 0.0 copy-done.4
  5.6 0.0 copy-start.2
  5.6 0.1 links.1
  5.7 1.6 %collective-permute-start.1 = (f32[2,64,128]{2,1,0:T(8,128)S(1)}, f32[2,64,128]{2,1,0:T(8,128)S(1)}, u32[]{:S(2)}, u32[]{:S(2)}) collective-permute-start(f32[2,64,128]{2,1,0:T(8,128)S(1)} %get-tuple-element.37), channel_id=1, source_target_pairs={{0,1},{1,0},{2,3},{3,2},{4,5},{5,4},{6,7},{7,6},{8,9},{9,8},{10,11... | collective-permute-start | bytes 196616 | tf_op jit(solution)/shard_map/ppermute | solution.py:569
  7.2 0.0 copy-done.2
  7.2 0.3 %unpack_loads.1.loads_ref = f32[16,64,128]{2,1,0:T(8,128)S(1)} custom-call(f32[1,16,8192]{2,1,0:T(8,128)S(1)} %copy-done.2), custom_call_target="tpu_custom_call" | custom-call | tf_op jit(solution)/shard_map/unpack_loads/pallas_call | solution.py:519
  7.5 1.0 %collective-permute-start.3 = (f32[256,128]{1,0:T(8,128)S(1)}, f32[256,128]{1,0:T(8,128)S(1)}, u32[]{:S(2)}, u32[]{:S(2)}) collective-permute-start(f32[256,128]{1,0:T(8,128)S(1)} %get-tuple-element.39), channel_id=1, source_target_pairs={{0,1},{1,0},{2,4},{3,5},{4,2},{5,3},{6,8},{7,9},{8,6},{9,7},{10,12... | collective-permute-start | bytes 393224 | tf_op jit(solution)/shard_map/ppermute | solution.py:574
  8.5 0.7 %collective-permute-start.2 = (f32[264,128]{1,0:T(8,128)S(1)}, f32[264,128]{1,0:T(8,128)S(1)}, u32[]{:S(2)}, u32[]{:S(2)}) collective-permute-start(f32[264,128]{1,0:T(8,128)S(1)} %get-tuple-element.38), channel_id=1, source_target_pairs={{0,2},{1,3},{2,0},{3,1},{4,6},{5,7},{6,4},{7,5},{8,10},{9,11},{10,... | collective-permute-start | bytes 405512 | tf_op jit(solution)/shard_map/ppermute | solution.py:575
  9.2 0.8 %collective-permute-done.1.above_ref.below_ref.weight_ref = f32[2,64,128]{2,1,0:T(8,128)S(1)} collective-permute-done((f32[2,64,128]{2,1,0:T(8,128)S(1)}, f32[2,64,128]{2,1,0:T(8,128)S(1)}, u32[]{:S(2)}, u32[]{:S(2)}) %collective-permute-start.1) | collective-permute-done | bytes 65568 | tf_op jit(solution)/shard_map/ppermute | solution.py:569
  10.0 0.2 first_edges.1
  10.2 1.6 %collective-permute-start.5 = (f32[200,128]{1,0:T(8,128)S(1)}, f32[200,128]{1,0:T(8,128)S(1)}, u32[]{:S(2)}, u32[]{:S(2)}) collective-permute-start(f32[200,128]{1,0:T(8,128)S(1)} %get-tuple-element.40.after_ref), channel_id=1, source_target_pairs={{0,1},{1,0},{2,4},{3,5},{4,2},{5,3},{6,8},{7,9},{8,6},{9,7},{10,12... | collective-permute-start | bytes 307208 | tf_op jit(solution)/shard_map/ppermute | solution.py:574
  11.7 0.1 collective-permute-start.4
  11.9 0.7 %collective-permute-done.3.second_ref = f32[256,128]{1,0:T(8,128)S(1)} collective-permute-done((f32[256,128]{1,0:T(8,128)S(1)}, f32[256,128]{1,0:T(8,128)S(1)}, u32[]{:S(2)}, u32[]{:S(2)}) %collective-permute-start.3) | collective-permute-done | bytes 131104 | tf_op jit(solution)/shard_map/ppermute | solution.py:574
  12.6 0.0 collective-permute-done.2.first_ref
  12.6 1.5 %first_inner.1 = (f32[16,64,128]{2,1,0:T(8,128)S(1)}, f32[16,64,128]{2,1,0:T(8,128)S(1)}, f32[16,64,128]{2,1,0:T(8,128)S(1)}, f32[12,64,128]{2,1,0:T(8,128)S(1)}...) custom-call(f32[16,64,128]{2,1,0:T(8,128)S(1)} %unpack_volts.1.x_ref, ...), custom_call_target="tpu_custom_call" | custom-call | tf_op jit(solution)/shard_map/first_inner/pallas_call | solution.py:519
  14.1 0.0 collective-permute-done.4.first_ref
  14.1 0.8 %collective-permute-done.5.second_ref = f32[200,128]{1,0:T(8,128)S(1)} collective-permute-done((f32[200,128]{1,0:T(8,128)S(1)}, f32[200,128]{1,0:T(8,128)S(1)}, u32[]{:S(2)}, u32[]{:S(2)}) %collective-permute-start.5) | collective-permute-done | bytes 102432 | tf_op jit(solution)/shard_map/ppermute | solution.py:574
  14.9 0.4 %first_outer.1 = (f32[16,64,128]{2,1,0:T(8,128)S(1)}, f32[2,64,128]{2,1,0:T(8,128)S(1)}, f32[1,64,128]{2,1,0:T(8,128)S(1)}) custom-call(f32[16,64,128]{2,1,0:T(8,128)S(1)} %unpack_volts.1.x_ref, f32[16,64,128]{2,1,0:T(8,128)S(1)} %get-tuple-element.33.across_ref, f32[16,64,128]{2,1,0:T(8,128)S(1)} %get-tuple-element.34.down_ref, ...), custom_call_target="tpu_custom_call", output_to_operand_aliasing={{0}: (12, {})} | custom-call | tf_op jit(solution)/shard_map/first_outer/pallas_call | solution.py:519
  15.3 1.6 %collective-permute-start.6 = (f32[1,64,128]{2,1,0:T(8,128)S(1)}, f32[1,64,128]{2,1,0:T(8,128)S(1)}, u32[]{:S(2)}, u32[]{:S(2)}) collective-permute-start(f32[1,64,128]{2,1,0:T(8,128)S(1)} %get-tuple-element.49.after_ref), channel_id=1, source_target_pairs={{0,1},{1,0},{2,3},{3,2},{4,5},{5,4},{6,7},{7,6},{8,9},{9,8},{10,11... | collective-permute-start | bytes 98312 | tf_op jit(solution)/shard_map/ppermute | solution.py:569
  16.9 0.1 next_early.1
  17.0 0.6 %collective-permute-start.8 = (f32[192,128]{1,0:T(8,128)S(1)}, f32[192,128]{1,0:T(8,128)S(1)}, u32[]{:S(2)}, u32[]{:S(2)}) collective-permute-start(f32[192,128]{1,0:T(8,128)S(1)} %get-tuple-element.57), channel_id=1, source_target_pairs={{0,1},{1,0},{2,4},{3,5},{4,2},{5,3},{6,8},{7,9},{8,6},{9,7},{10,12... | collective-permute-start | bytes 294920 | tf_op jit(solution)/shard_map/ppermute | solution.py:574
  17.6 1.6 %collective-permute-start.7 = (f32[200,128]{1,0:T(8,128)S(1)}, f32[200,128]{1,0:T(8,128)S(1)}, u32[]{:S(2)}, u32[]{:S(2)}) collective-permute-start(f32[200,128]{1,0:T(8,128)S(1)} %get-tuple-element.56), channel_id=1, source_target_pairs={{0,2},{1,3},{2,0},{3,1},{4,6},{5,7},{6,4},{7,5},{8,10},{9,11},{10,... | collective-permute-start | bytes 307208 | tf_op jit(solution)/shard_map/ppermute | solution.py:575
  19.2 0.1 collective-permute-done.6.volts_ref.above_ref.below_ref
  19.3 1.6 %collective-permute-start.10 = (f32[72,128]{1,0:T(8,128)S(1)}, f32[72,128]{1,0:T(8,128)S(1)}, u32[]{:S(2)}, u32[]{:S(2)}) collective-permute-start(f32[72,128]{1,0:T(8,128)S(1)} %get-tuple-element.52.after_ref), channel_id=1, source_target_pairs={{0,1},{1,0},{2,4},{3,5},{4,2},{5,3},{6,8},{7,9},{8,6},{9,7},{10,12... | collective-permute-start | bytes 110600 | tf_op jit(solution)/shard_map/ppermute | solution.py:574
  20.9 0.8 %collective-permute-start.9 = (f32[64,128]{1,0:T(8,128)S(1)}, f32[64,128]{1,0:T(8,128)S(1)}, u32[]{:S(2)}, u32[]{:S(2)}) collective-permute-start(f32[64,128]{1,0:T(8,128)S(1)} %get-tuple-element.58), channel_id=1, source_target_pairs={{0,2},{1,3},{2,0},{3,1},{4,6},{5,7},{6,4},{7,5},{8,10},{9,11},{10,... | collective-permute-start | bytes 98312 | tf_op jit(solution)/shard_map/ppermute | solution.py:575
  21.7 1.1 %last_inner.1 = (f32[16,64,128]{2,1,0:T(8,128)S(1)}, f32[16,64,128]{2,1,0:T(8,128)S(1)}, f32[12,64,128]{2,1,0:T(8,128)S(1)}) custom-call(f32[16,64,128]{2,1,0:T(8,128)S(1)} %get-tuple-element.48.x_ref, f32[16,64,128]{2,1,0:T(8,128)S(1)} %get-tuple-element.33.across_ref, f32[16,64,128]{2,1,0:T(8,128)S(1)} %get-tuple-element.34.down_ref, ...), custom_call_target="tpu_custom_call" | custom-call | tf_op jit(solution)/shard_map/last_inner/pallas_call | solution.py:519
  22.8 0.0 collective-permute-done.9.first_ref
  22.8 0.5 %collective-permute-done.10.second_ref = f32[72,128]{1,0:T(8,128)S(1)} collective-permute-done((f32[72,128]{1,0:T(8,128)S(1)}, f32[72,128]{1,0:T(8,128)S(1)}, u32[]{:S(2)}, u32[]{:S(2)}) %collective-permute-start.10) | collective-permute-done | bytes 36896 | tf_op jit(solution)/shard_map/ppermute | solution.py:574
  23.3 0.0 collective-permute-done.8.early_second_ref
  23.3 0.0 collective-permute-done.7.early_first_ref
  23.3 1.6 %last_outer.1 = (f32[16,8192]{1,0:T(8,128)}, f32[16,64,128]{2,1,0:T(8,128)S(1)}) custom-call(f32[16,64,128]{2,1,0:T(8,128)S(1)} %get-tuple-element.48.x_ref, f32[16,64,128]{2,1,0:T(8,128)S(1)} %get-tuple-element.33.across_ref, f32[16,64,128]{2,1,0:T(8,128)S(1)} %get-tuple-element.34.down_ref, ...), custom_call_target="tpu_custom_call", output_to_operand_aliasing={{1}: (12, {})} | custom-call | tf_op jit(solution)/shard_map/last_outer/pallas_call | solution.py:519
  (2 shorter events, 0.0 us)
Async XLA Ops:
  0.0 4.6 %copy-start = (s32[1,2,16,8192]{3,2,1,0:T(8,128)S(1)}, s32[1,2,16,8192]{3,2,1,0:T(8,128)}, u32[]{:S(2)}) copy-start(s32[1,2,16,8192]{3,2,1,0:T(8,128)} %index_ref.1) | copy-start | bytes 3145732
  0.0 5.5 %collective-permute-start = (s32[64,128]{1,0:T(8,128)}, s32[64,128]{1,0:T(8,128)S(1)}, u32[]{:S(2)}, u32[]{:S(2)}) collective-permute-start(s32[64,128]{1,0:T(8,128)} %bitcast.3), channel_id=1, source_target_pairs={{0,1},{1,0},{2,3},{3,2},{4,5},{5,4},{6,7},{7,6},{8,9},{9,8},{10,11... | collective-permute-start | bytes 98312 | tf_op jit(solution)/shard_map/ppermute | solution.py:584
  2.9 1.0 %copy-start.1 = (f32[1,16,8192]{2,1,0:T(8,128)S(1)}, f32[1,16,8192]{2,1,0:T(8,128)}, u32[]{:S(2)}) copy-start(f32[1,16,8192]{2,1,0:T(8,128)} %field_ref.2) | copy-start | bytes 1572868
  4.0 0.7 %copy-start.5 = (f32[1,16]{1,0:T(1,128)S(1)}, f32[1,16]{1,0:T(1,128)}, u32[]{:S(2)}) copy-start(f32[1,16]{1,0:T(1,128)} %param.7) | copy-start | bytes 196
  4.6 0.9 %copy-start.3 = (s32[1,8192]{1,0:T(1,128)S(1)}, s32[1,8192]{1,0:T(1,128)}, u32[]{:S(2)}) copy-start(s32[1,8192]{1,0:T(1,128)} %param.10) | copy-start | bytes 98308
  4.7 0.9 %copy-start.4 = (s32[1,8192]{1,0:T(1,128)S(1)}, s32[1,8192]{1,0:T(1,128)}, u32[]{:S(2)}) copy-start(s32[1,8192]{1,0:T(1,128)} %param.11) | copy-start | bytes 98308
  5.6 1.7 %copy-start.2 = (f32[1,16,8192]{2,1,0:T(8,128)S(1)}, f32[1,16,8192]{2,1,0:T(8,128)}, u32[]{:S(2)}) copy-start(f32[1,16,8192]{2,1,0:T(8,128)} %field_ref.3) | copy-start | bytes 1572868
  5.7 4.3 %collective-permute-start.1 = (f32[2,64,128]{2,1,0:T(8,128)S(1)}, f32[2,64,128]{2,1,0:T(8,128)S(1)}, u32[]{:S(2)}, u32[]{:S(2)}) collective-permute-start(f32[2,64,128]{2,1,0:T(8,128)S(1)} %get-tuple-element.37), channel_id=1, source_target_pairs={{0,1},{1,0},{2,3},{3,2},{4,5},{5,4},{6,7},{7,6},{8,9},{9,8},{10,11... | collective-permute-start | bytes 196616 | tf_op jit(solution)/shard_map/ppermute | solution.py:569
  7.5 5.0 %collective-permute-start.3 = (f32[256,128]{1,0:T(8,128)S(1)}, f32[256,128]{1,0:T(8,128)S(1)}, u32[]{:S(2)}, u32[]{:S(2)}) collective-permute-start(f32[256,128]{1,0:T(8,128)S(1)} %get-tuple-element.39), channel_id=1, source_target_pairs={{0,1},{1,0},{2,4},{3,5},{4,2},{5,3},{6,8},{7,9},{8,6},{9,7},{10,12... | collective-permute-start | bytes 393224 | tf_op jit(solution)/shard_map/ppermute | solution.py:574
  8.5 4.1 %collective-permute-start.2 = (f32[264,128]{1,0:T(8,128)S(1)}, f32[264,128]{1,0:T(8,128)S(1)}, u32[]{:S(2)}, u32[]{:S(2)}) collective-permute-start(f32[264,128]{1,0:T(8,128)S(1)} %get-tuple-element.38), channel_id=1, source_target_pairs={{0,2},{1,3},{2,0},{3,1},{4,6},{5,7},{6,4},{7,5},{8,10},{9,11},{10,... | collective-permute-start | bytes 405512 | tf_op jit(solution)/shard_map/ppermute | solution.py:575
  10.2 4.7 %collective-permute-start.5 = (f32[200,128]{1,0:T(8,128)S(1)}, f32[200,128]{1,0:T(8,128)S(1)}, u32[]{:S(2)}, u32[]{:S(2)}) collective-permute-start(f32[200,128]{1,0:T(8,128)S(1)} %get-tuple-element.40.after_ref), channel_id=1, source_target_pairs={{0,1},{1,0},{2,4},{3,5},{4,2},{5,3},{6,8},{7,9},{8,6},{9,7},{10,12... | collective-permute-start | bytes 307208 | tf_op jit(solution)/shard_map/ppermute | solution.py:574
  11.7 2.3 %collective-permute-start.4 = (f32[192,128]{1,0:T(8,128)S(1)}, f32[192,128]{1,0:T(8,128)S(1)}, u32[]{:S(2)}, u32[]{:S(2)}) collective-permute-start(f32[192,128]{1,0:T(8,128)S(1)} %get-tuple-element.46), channel_id=1, source_target_pairs={{0,2},{1,3},{2,0},{3,1},{4,6},{5,7},{6,4},{7,5},{8,10},{9,11},{10,... | collective-permute-start | bytes 294920 | tf_op jit(solution)/shard_map/ppermute | solution.py:575
  15.3 4.0 %collective-permute-start.6 = (f32[1,64,128]{2,1,0:T(8,128)S(1)}, f32[1,64,128]{2,1,0:T(8,128)S(1)}, u32[]{:S(2)}, u32[]{:S(2)}) collective-permute-start(f32[1,64,128]{2,1,0:T(8,128)S(1)} %get-tuple-element.49.after_ref), channel_id=1, source_target_pairs={{0,1},{1,0},{2,3},{3,2},{4,5},{5,4},{6,7},{7,6},{8,9},{9,8},{10,11... | collective-permute-start | bytes 98312 | tf_op jit(solution)/shard_map/ppermute | solution.py:569
  17.0 6.3 %collective-permute-start.8 = (f32[192,128]{1,0:T(8,128)S(1)}, f32[192,128]{1,0:T(8,128)S(1)}, u32[]{:S(2)}, u32[]{:S(2)}) collective-permute-start(f32[192,128]{1,0:T(8,128)S(1)} %get-tuple-element.57), channel_id=1, source_target_pairs={{0,1},{1,0},{2,4},{3,5},{4,2},{5,3},{6,8},{7,9},{8,6},{9,7},{10,12... | collective-permute-start | bytes 294920 | tf_op jit(solution)/shard_map/ppermute | solution.py:574
  17.6 5.7 %collective-permute-start.7 = (f32[200,128]{1,0:T(8,128)S(1)}, f32[200,128]{1,0:T(8,128)S(1)}, u32[]{:S(2)}, u32[]{:S(2)}) collective-permute-start(f32[200,128]{1,0:T(8,128)S(1)} %get-tuple-element.56), channel_id=1, source_target_pairs={{0,2},{1,3},{2,0},{3,1},{4,6},{5,7},{6,4},{7,5},{8,10},{9,11},{10,... | collective-permute-start | bytes 307208 | tf_op jit(solution)/shard_map/ppermute | solution.py:575
  19.3 4.0 %collective-permute-start.10 = (f32[72,128]{1,0:T(8,128)S(1)}, f32[72,128]{1,0:T(8,128)S(1)}, u32[]{:S(2)}, u32[]{:S(2)}) collective-permute-start(f32[72,128]{1,0:T(8,128)S(1)} %get-tuple-element.52.after_ref), channel_id=1, source_target_pairs={{0,1},{1,0},{2,4},{3,5},{4,2},{5,3},{6,8},{7,9},{8,6},{9,7},{10,12... | collective-permute-start | bytes 110600 | tf_op jit(solution)/shard_map/ppermute | solution.py:574
  20.9 1.9 %collective-permute-start.9 = (f32[64,128]{1,0:T(8,128)S(1)}, f32[64,128]{1,0:T(8,128)S(1)}, u32[]{:S(2)}, u32[]{:S(2)}) collective-permute-start(f32[64,128]{1,0:T(8,128)S(1)} %get-tuple-element.58), channel_id=1, source_target_pairs={{0,2},{1,3},{2,0},{3,1},{4,6},{5,7},{6,4},{7,5},{8,10},{9,11},{10,... | collective-permute-start | bytes 98312 | tf_op jit(solution)/shard_map/ppermute | solution.py:575

commit v7 on v6

--- a/solution.py
+++ b/solution.py
@@ -13,7 +13,7 @@
 LOWER_BOUND = 0.05
 UPPER_BOUND = 2.0
 LANES = 128
-CHUNKS = 2
+CHUNKS = 4
 FILL = 8
 
 
@@ -76,11 +76,31 @@
             out_ref[pl.ds(top, 8), start // LANES, :] = field_ref[0, pl.ds(top, 8), pl.ds(start, LANES)]
 
 
+def unpack_volts_kernel(volts_ref, class_ref, x_ref, table_ref, held, class_held, sems):
+    rows, cols = held.shape
+    chunks = chunks_of(cols, CHUNKS)
+    pairs = [(volts_ref.at[0, :, pl.ds(*chunk)], held.at[:, pl.ds(*chunk)]) for chunk in chunks]
+    pairs.append((class_ref, class_held))
+    arriving = [pltpu.make_async_copy(*pair, sems.at[number]) for number, pair in enumerate(pairs)]
+    for copy in arriving:
+        copy.start()
+    for (first, width), copy in zip(chunks, arriving):
+        copy.wait()
+        for top in range(0, rows, 8):
+            part = pl.ds(top, 8)
+            for start in range(first, first + width, LANES):
+                x_ref[part, start // LANES, :] = held[part, pl.ds(start, LANES)]
+    arriving[-1].wait()
+    table_ref[...] = jnp.zeros(table_ref.shape, jnp.float32)
+    count = class_held.shape[1]
+    table_ref[:, pl.ds(0, count)] = jnp.broadcast_to(class_held[...], (8, count))
+
+
 def unpack_index_kernel(index_ref, table_ref, across_ref, down_ref):
     rows, cols = index_ref.shape[2:]
     tile, _ = place()
     last_tile = tile == lax.axis_size("tile") - 1
-    table = jnp.broadcast_to(table_ref[...], (8, LANES))
+    table = table_ref[...]
     lane = lax.broadcasted_iota(jnp.int32, (8, LANES), 1)
     sub = lax.broadcasted_iota(jnp.int32, (8, LANES), 0)
     for top in range(0, rows, 8):
@@ -459,6 +479,45 @@
     inner_rows(rows, 1, None, *shared, scratch[:-1], scratch[-1], core_ref, keep_ref)
 
 
+def last_middle_kernel(
+    rows,
+    x_ref,
+    across_ref,
+    down_ref,
+    side_ref,
+    inverse_ref,
+    keep_ref,
+    halo_ref,
+    first_ref,
+    second_ref,
+    core_ref,
+    kept_ref,
+    next_ref,
+):
+    edge_x = taken_by_parity(first_ref, second_ref, 0, x_ref.shape[1])
+    for side in range(2):
+        outside = halo_ref[2] * edge_x[0] if side == 0 else down_ref[rows - 1] * edge_x[1]
+        further = x_ref[0 if side == 0 else rows - 1], x_ref[1 if side == 0 else rows - 2]
+        previous = None
+        for sweep in range(SWEEPS):
+            row = sweep if side == 0 else rows - 1 - sweep
+            links = (row - 1, row) if side == 0 else (row, row - 1)
+            x, within = further
+            flow = beside(x, across_ref[row]) + (outside if sweep == 0 else down_ref[links[0]] * outside)
+            flow = flow + down_ref[links[1]] * within
+            value, update = relaxed(x, flow, side_ref[row], inverse_ref[row], previous, sweep)
+            if sweep == SWEEPS - 1:
+                next_ref[row] = value
+                break
+            slot = 3 * (2 * sweep + side)
+            kept_ref[slot] = value
+            kept_ref[slot + 1] = keep_ref[slot]
+            kept_ref[slot + 2] = update
+            further = keep_ref[slot], keep_ref[slot + 1]
+            previous = keep_ref[slot + 2]
+            outside = value
+
+
 def last_outer_kernel(
     single,
     rows,
@@ -493,7 +552,7 @@
         outer = outer_rows(
             side,
             rows,
-            1,
+            0,
             (early[0][side], sides, halo_ref[side]),
             halo_ref[2] if side == 0 else down_ref[rows - 1],
             edge_ref[side],
@@ -526,7 +585,7 @@
         compiler_params=pltpu.CompilerParams(vmem_limit_bytes=40 * 1024 * 1024),
         cost_estimate=work and pl.CostEstimate(flops=work, bytes_accessed=work, transcendentals=0),
         name=name,
-    )(*(array for _, array in ins))
+    )(*(pltpu.with_memory_space_constraint(array, pltpu.HBM) if space == "hbm" else array for space, array in ins))
 
 
 def routes(tiles, layers):
@@ -582,9 +641,19 @@
     cells = via_cells.reshape(lines, LANES)
     counts = via_counts.reshape(lines, LANES)
     low = move(cells, perm=up)
-    table = jnp.pad(class_conductance, ((0, 0), (0, LANES - class_conductance.shape[1])))
+    x, table = call(
+        unpack_volts_kernel,
+        "unpack_volts",
+        [("hbm", start_volts), ("hbm", class_conductance)],
+        [field, ("vmem", (8, LANES))],
+        [
+            pltpu.VMEM((rows, cols), jnp.float32),
+            pltpu.VMEM(class_conductance.shape, jnp.float32),
+            pltpu.SemaphoreType.DMA((CHUNKS + 1,)),
+        ],
+        work=1000000000,
+    )
     across, downward = call(unpack_index_kernel, "unpack_index", vmem(class_index, table), [field] * 2)
-    (x,) = call(unpack_field_kernel, "unpack_volts", vmem(start_volts), [field])
     first_sent, second_sent, own_weight, own, *sends = call(
         functools.partial(links_kernel, single),
         "links",
@@ -652,6 +721,13 @@
         [field, field, ("vmem", rows_of(KEPT))],
         work,
     )
+    keep, core = call(
+        functools.partial(last_middle_kernel, rows),
+        "last_middle",
+        vmem(x, across, downward, side, inverse, keep, halo, *early, core),
+        [("vmem", rows_of(KEPT)), field],
+        aliases={9: 1},
+    )
     volts, _ = call(
         functools.partial(last_outer_kernel, single, rows),
         "last_outer",

time: 25.1 us -> 24.9 us (level)
  local copies, waits for them, and re-layouts: 1.43 us -> 0.02 us
  starting transfers between devices: 14 us -> 15.4 us
  waiting for transfers between devices: 2.84 us -> 1.64 us
  Pallas kernels: 6.55 us -> 7.5 us
    unnamed x12 -> x8, local copies, waits for them, and re-layouts: 1.42 us -> 0.02 us
    pallas_call x11 -> x12, Pallas kernels: 6.55 us -> 7.5 us  [call(): pl.pallas_call(kernel, out_shape=[jax.ShapeDtypeStruct(shape, *(kind or [...]
    ppermute x2, starting transfers between devices: 3.11 us -> 3.99 us  [between_layers(): got = move(sends[0], perm=up)]
    ppermute x4, waiting for transfers between devices: 1.99 us -> 1.28 us  [beside_tile(): across_chips = move(sent[1], perm=second)]
    ppermute x2, waiting for transfers between devices: 0.83 us -> 0.34 us  [between_layers(): got = move(sends[0], perm=up)]
    ppermute x4, starting transfers between devices: 3.32 us -> 3.75 us  [beside_tile(): return (move(sent[0], perm=first), across_chips)]
  transfers between devices with their start and end apart: 11 -> 11, of which waited for: 5 -> 4; matrix products, arithmetic and copies ran while one was open for 0% -> 0% of each run, Pallas kernels for 18% -> 23%
where the time goes in v7:
time: 24.9 us; the launch traced here: 24.7 us
  starting transfers between devices  15.4 us (62%)
  Pallas kernels  7.5 us (30%)
  waiting for transfers between devices  1.64 us (7%)
    pallas_call x12, Pallas kernels, call(): pl.pallas_call(kernel, out_shape=[jax.ShapeDtypeStruct(shape, *(kind or [...  7.5 us
    ppermute x4, starting transfers between devices, beside_tile(): across_chips = move(sent[1], perm=second)  4.72 us
    ppermute x2, starting transfers between devices, between_layers(): got = move(sends[0], perm=up)  3.99 us
    ppermute x4, starting transfers between devices, beside_tile(): return (move(sent[0], perm=first), across_chips)  3.75 us
    ppermute x1, starting transfers between devices, local(): low = move(cells, perm=up)  2.94 us
    ppermute x4, waiting for transfers between devices, beside_tile(): across_chips = move(sent[1], perm=second)  1.28 us
  transfers between devices with their start and end apart: 11, of which 4 were waited for; matrix products, arithmetic and copies ran while one was open for 0% of the time, Pallas kernels for 23%

profile of v7, /device:TPU:0, one launch (start us, length us, event | category | flops | bytes accessed | tf_op | source)
XLA Modules:
  0.0 24.7 jit_solution(1275582697506686153)
XLA Ops:
  0.0 0.0 copy-start
  0.0 2.9 %collective-permute-start = (s32[64,128]{1,0:T(8,128)}, s32[64,128]{1,0:T(8,128)S(1)}, u32[]{:S(2)}, u32[]{:S(2)}) collective-permute-start(s32[64,128]{1,0:T(8,128)} %bitcast.3), channel_id=1, source_target_pairs={{0,1},{1,0},{2,3},{3,2},{4,5},{5,4},{6,7},{7,6},{8,9},{9,8},{10,11... | collective-permute-start | bytes 98312 | tf_op jit(solution)/shard_map/ppermute | solution.py:643
  2.9 1.2 %unpack_volts.1 = (f32[16,64,128]{2,1,0:T(8,128)S(1)}, f32[8,128]{1,0:T(8,128)S(1)}) custom-call(f32[1,16,8192]{2,1,0:T(8,128)} %volts_ref.1, f32[1,16]{1,0:T(1,128)} %class_ref.1), custom_call_target="tpu_custom_call" | custom-call | flops 1000000000 | bytes 1000000000 | tf_op jit(solution)/shard_map/unpack_volts/pallas_call | solution.py:578
  4.2 0.0 copy-done
  4.2 0.0 copy-start.2
  4.2 0.0 copy-start.3
  4.2 0.9 %unpack_index.1 = (f32[16,64,128]{2,1,0:T(8,128)S(1)}, f32[16,64,128]{2,1,0:T(8,128)S(1)}) custom-call(s32[1,2,16,8192]{3,2,1,0:T(8,128)S(1)} %copy-done, f32[8,128]{1,0:T(8,128)S(1)} %get-tuple-element.38.table_ref), custom_call_target="tpu_custom_call" | custom-call | tf_op jit(solution)/shard_map/unpack_index/pallas_call | solution.py:578
  5.1 0.0 collective-permute-done.low_ref
  5.1 0.0 copy-done.2
  5.1 0.0 copy-done.3
  5.1 0.0 copy-start.1
  5.1 0.1 links.1
  5.2 2.0 %collective-permute-start.1 = (f32[2,64,128]{2,1,0:T(8,128)S(1)}, f32[2,64,128]{2,1,0:T(8,128)S(1)}, u32[]{:S(2)}, u32[]{:S(2)}) collective-permute-start(f32[2,64,128]{2,1,0:T(8,128)S(1)} %get-tuple-element.43), channel_id=1, source_target_pairs={{0,1},{1,0},{2,3},{3,2},{4,5},{5,4},{6,7},{7,6},{8,9},{9,8},{10,11... | collective-permute-start | bytes 196616 | tf_op jit(solution)/shard_map/ppermute | solution.py:628
  7.2 0.0 copy-done.1
  7.2 0.3 %unpack_loads.1.loads_ref = f32[16,64,128]{2,1,0:T(8,128)S(1)} custom-call(f32[1,16,8192]{2,1,0:T(8,128)S(1)} %copy-done.1), custom_call_target="tpu_custom_call" | custom-call | tf_op jit(solution)/shard_map/unpack_loads/pallas_call | solution.py:578
  7.5 1.0 %collective-permute-start.3 = (f32[256,128]{1,0:T(8,128)S(1)}, f32[256,128]{1,0:T(8,128)S(1)}, u32[]{:S(2)}, u32[]{:S(2)}) collective-permute-start(f32[256,128]{1,0:T(8,128)S(1)} %get-tuple-element.45), channel_id=1, source_target_pairs={{0,1},{1,0},{2,4},{3,5},{4,2},{5,3},{6,8},{7,9},{8,6},{9,7},{10,12... | collective-permute-start | bytes 393224 | tf_op jit(solution)/shard_map/ppermute | solution.py:633
  8.5 0.7 %collective-permute-start.2 = (f32[264,128]{1,0:T(8,128)S(1)}, f32[264,128]{1,0:T(8,128)S(1)}, u32[]{:S(2)}, u32[]{:S(2)}) collective-permute-start(f32[264,128]{1,0:T(8,128)S(1)} %get-tuple-element.44), channel_id=1, source_target_pairs={{0,2},{1,3},{2,0},{3,1},{4,6},{5,7},{6,4},{7,5},{8,10},{9,11},{10,... | collective-permute-start | bytes 405512 | tf_op jit(solution)/shard_map/ppermute | solution.py:634
  9.2 0.3 %collective-permute-done.1.above_ref.below_ref.weight_ref = f32[2,64,128]{2,1,0:T(8,128)S(1)} collective-permute-done((f32[2,64,128]{2,1,0:T(8,128)S(1)}, f32[2,64,128]{2,1,0:T(8,128)S(1)}, u32[]{:S(2)}, u32[]{:S(2)}) %collective-permute-start.1) | collective-permute-done | bytes 65568 | tf_op jit(solution)/shard_map/ppermute | solution.py:628
  9.6 0.2 first_edges.1
  9.8 2.0 %collective-permute-start.5 = (f32[200,128]{1,0:T(8,128)S(1)}, f32[200,128]{1,0:T(8,128)S(1)}, u32[]{:S(2)}, u32[]{:S(2)}) collective-permute-start(f32[200,128]{1,0:T(8,128)S(1)} %get-tuple-element.46.after_ref), channel_id=1, source_target_pairs={{0,1},{1,0},{2,4},{3,5},{4,2},{5,3},{6,8},{7,9},{8,6},{9,7},{10,12... | collective-permute-start | bytes 307208 | tf_op jit(solution)/shard_map/ppermute | solution.py:633
  11.7 0.1 collective-permute-start.4
  11.9 0.7 %collective-permute-done.3.second_ref = f32[256,128]{1,0:T(8,128)S(1)} collective-permute-done((f32[256,128]{1,0:T(8,128)S(1)}, f32[256,128]{1,0:T(8,128)S(1)}, u32[]{:S(2)}, u32[]{:S(2)}) %collective-permute-start.3) | collective-permute-done | bytes 131104 | tf_op jit(solution)/shard_map/ppermute | solution.py:633
  12.6 0.0 collective-permute-done.2.first_ref
  12.6 1.5 %first_inner.1 = (f32[16,64,128]{2,1,0:T(8,128)S(1)}, f32[16,64,128]{2,1,0:T(8,128)S(1)}, f32[16,64,128]{2,1,0:T(8,128)S(1)}, f32[12,64,128]{2,1,0:T(8,128)S(1)}...) custom-call(f32[16,64,128]{2,1,0:T(8,128)S(1)} %get-tuple-element.37.x_ref, ...), custom_call_target="tpu_custom_call" | custom-call | tf_op jit(solution)/shard_map/first_inner/pallas_call | solution.py:578
  14.1 0.0 collective-permute-done.4.first_ref
  14.1 0.4 %collective-permute-done.5.second_ref = f32[200,128]{1,0:T(8,128)S(1)} collective-permute-done((f32[200,128]{1,0:T(8,128)S(1)}, f32[200,128]{1,0:T(8,128)S(1)}, u32[]{:S(2)}, u32[]{:S(2)}) %collective-permute-start.5) | collective-permute-done | bytes 102432 | tf_op jit(solution)/shard_map/ppermute | solution.py:633
  14.5 0.4 %first_outer.1 = (f32[16,64,128]{2,1,0:T(8,128)S(1)}, f32[2,64,128]{2,1,0:T(8,128)S(1)}, f32[1,64,128]{2,1,0:T(8,128)S(1)}) custom-call(f32[16,64,128]{2,1,0:T(8,128)S(1)} %get-tuple-element.37.x_ref, f32[16,64,128]{2,1,0:T(8,128)S(1)} %get-tuple-element.39.across_ref, ...), custom_call_target="tpu_custom_call", output_to_operand_aliasing={{0}: (12, {})} | custom-call | tf_op jit(solution)/shard_map/first_outer/pallas_call | solution.py:578
  14.9 2.0 %collective-permute-start.6 = (f32[1,64,128]{2,1,0:T(8,128)S(1)}, f32[1,64,128]{2,1,0:T(8,128)S(1)}, u32[]{:S(2)}, u32[]{:S(2)}) collective-permute-start(f32[1,64,128]{2,1,0:T(8,128)S(1)} %get-tuple-element.55.after_ref), channel_id=1, source_target_pairs={{0,1},{1,0},{2,3},{3,2},{4,5},{5,4},{6,7},{7,6},{8,9},{9,8},{10,11... | collective-permute-start | bytes 98312 | tf_op jit(solution)/shard_map/ppermute | solution.py:628
  16.9 0.1 next_early.1
  17.0 0.2 collective-permute-start.8
  17.2 2.1 %collective-permute-start.7 = (f32[200,128]{1,0:T(8,128)S(1)}, f32[200,128]{1,0:T(8,128)S(1)}, u32[]{:S(2)}, u32[]{:S(2)}) collective-permute-start(f32[200,128]{1,0:T(8,128)S(1)} %get-tuple-element.61), channel_id=1, source_target_pairs={{0,2},{1,3},{2,0},{3,1},{4,6},{5,7},{6,4},{7,5},{8,10},{9,11},{10,... | collective-permute-start | bytes 307208 | tf_op jit(solution)/shard_map/ppermute | solution.py:634
  19.2 0.0 collective-permute-done.6.volts_ref.above_ref.below_ref
  19.3 1.6 %collective-permute-start.10 = (f32[72,128]{1,0:T(8,128)S(1)}, f32[72,128]{1,0:T(8,128)S(1)}, u32[]{:S(2)}, u32[]{:S(2)}) collective-permute-start(f32[72,128]{1,0:T(8,128)S(1)} %get-tuple-element.58.after_ref), channel_id=1, source_target_pairs={{0,1},{1,0},{2,4},{3,5},{4,2},{5,3},{6,8},{7,9},{8,6},{9,7},{10,12... | collective-permute-start | bytes 110600 | tf_op jit(solution)/shard_map/ppermute | solution.py:633
  20.9 0.8 %collective-permute-start.9 = (f32[64,128]{1,0:T(8,128)S(1)}, f32[64,128]{1,0:T(8,128)S(1)}, u32[]{:S(2)}, u32[]{:S(2)}) collective-permute-start(f32[64,128]{1,0:T(8,128)S(1)} %get-tuple-element.66), channel_id=1, source_target_pairs={{0,2},{1,3},{2,0},{3,1},{4,6},{5,7},{6,4},{7,5},{8,10},{9,11},{10,... | collective-permute-start | bytes 98312 | tf_op jit(solution)/shard_map/ppermute | solution.py:634
  21.7 1.1 %last_inner.1 = (f32[16,64,128]{2,1,0:T(8,128)S(1)}, f32[16,64,128]{2,1,0:T(8,128)S(1)}, f32[12,64,128]{2,1,0:T(8,128)S(1)}) custom-call(f32[16,64,128]{2,1,0:T(8,128)S(1)} %get-tuple-element.54.x_ref, f32[16,64,128]{2,1,0:T(8,128)S(1)} %get-tuple-element.39.across_ref, f32[16,64,128]{2,1,0:T(8,128)S(1)} %get-tuple-element.40.down_ref, ...), custom_call_target="tpu_custom_call" | custom-call | tf_op jit(solution)/shard_map/last_inner/pallas_call | solution.py:578
  22.8 0.0 collective-permute-done.8.second_ref.early_second_ref
  22.8 0.0 collective-permute-done.7.first_ref.early_first_ref
  22.8 0.2 last_middle.1
  23.0 0.0 collective-permute-done.9.first_ref
  23.1 0.2 collective-permute-done.10.second_ref
  23.3 1.4 %last_outer.1 = (f32[16,8192]{1,0:T(8,128)}, f32[16,64,128]{2,1,0:T(8,128)S(1)}) custom-call(f32[16,64,128]{2,1,0:T(8,128)S(1)} %get-tuple-element.54.x_ref, f32[16,64,128]{2,1,0:T(8,128)S(1)} %get-tuple-element.39.across_ref, f32[16,64,128]{2,1,0:T(8,128)S(1)} %get-tuple-element.40.down_ref, ...), custom_call_target="tpu_custom_call", output_to_operand_aliasing={{1}: (12, {})} | custom-call | tf_op jit(solution)/shard_map/last_outer/pallas_call | solution.py:578
  (1 shorter events, 0.0 us)
Async XLA Ops:
  0.0 4.2 %copy-start = (s32[1,2,16,8192]{3,2,1,0:T(8,128)S(1)}, s32[1,2,16,8192]{3,2,1,0:T(8,128)}, u32[]{:S(2)}) copy-start(s32[1,2,16,8192]{3,2,1,0:T(8,128)} %index_ref.1) | copy-start | bytes 3145732
  0.0 5.1 %collective-permute-start = (s32[64,128]{1,0:T(8,128)}, s32[64,128]{1,0:T(8,128)S(1)}, u32[]{:S(2)}, u32[]{:S(2)}) collective-permute-start(s32[64,128]{1,0:T(8,128)} %bitcast.3), channel_id=1, source_target_pairs={{0,1},{1,0},{2,3},{3,2},{4,5},{5,4},{6,7},{7,6},{8,9},{9,8},{10,11... | collective-permute-start | bytes 98312 | tf_op jit(solution)/shard_map/ppermute | solution.py:643
  4.2 0.9 %copy-start.2 = (s32[1,8192]{1,0:T(1,128)S(1)}, s32[1,8192]{1,0:T(1,128)}, u32[]{:S(2)}) copy-start(s32[1,8192]{1,0:T(1,128)} %param.10) | copy-start | bytes 98308
  4.2 0.9 %copy-start.3 = (s32[1,8192]{1,0:T(1,128)S(1)}, s32[1,8192]{1,0:T(1,128)}, u32[]{:S(2)}) copy-start(s32[1,8192]{1,0:T(1,128)} %param.11) | copy-start | bytes 98308
  5.1 2.1 %copy-start.1 = (f32[1,16,8192]{2,1,0:T(8,128)S(1)}, f32[1,16,8192]{2,1,0:T(8,128)}, u32[]{:S(2)}) copy-start(f32[1,16,8192]{2,1,0:T(8,128)} %field_ref.1) | copy-start | bytes 1572868
  5.2 4.3 %collective-permute-start.1 = (f32[2,64,128]{2,1,0:T(8,128)S(1)}, f32[2,64,128]{2,1,0:T(8,128)S(1)}, u32[]{:S(2)}, u32[]{:S(2)}) collective-permute-start(f32[2,64,128]{2,1,0:T(8,128)S(1)} %get-tuple-element.43), channel_id=1, source_target_pairs={{0,1},{1,0},{2,3},{3,2},{4,5},{5,4},{6,7},{7,6},{8,9},{9,8},{10,11... | collective-permute-start | bytes 196616 | tf_op jit(solution)/shard_map/ppermute | solution.py:628
  7.5 5.0 %collective-permute-start.3 = (f32[256,128]{1,0:T(8,128)S(1)}, f32[256,128]{1,0:T(8,128)S(1)}, u32[]{:S(2)}, u32[]{:S(2)}) collective-permute-start(f32[256,128]{1,0:T(8,128)S(1)} %get-tuple-element.45), channel_id=1, source_target_pairs={{0,1},{1,0},{2,4},{3,5},{4,2},{5,3},{6,8},{7,9},{8,6},{9,7},{10,12... | collective-permute-start | bytes 393224 | tf_op jit(solution)/shard_map/ppermute | solution.py:633
  8.5 4.1 %collective-permute-start.2 = (f32[264,128]{1,0:T(8,128)S(1)}, f32[264,128]{1,0:T(8,128)S(1)}, u32[]{:S(2)}, u32[]{:S(2)}) collective-permute-start(f32[264,128]{1,0:T(8,128)S(1)} %get-tuple-element.44), channel_id=1, source_target_pairs={{0,2},{1,3},{2,0},{3,1},{4,6},{5,7},{6,4},{7,5},{8,10},{9,11},{10,... | collective-permute-start | bytes 405512 | tf_op jit(solution)/shard_map/ppermute | solution.py:634
  9.8 4.7 %collective-permute-start.5 = (f32[200,128]{1,0:T(8,128)S(1)}, f32[200,128]{1,0:T(8,128)S(1)}, u32[]{:S(2)}, u32[]{:S(2)}) collective-permute-start(f32[200,128]{1,0:T(8,128)S(1)} %get-tuple-element.46.after_ref), channel_id=1, source_target_pairs={{0,1},{1,0},{2,4},{3,5},{4,2},{5,3},{6,8},{7,9},{8,6},{9,7},{10,12... | collective-permute-start | bytes 307208 | tf_op jit(solution)/shard_map/ppermute | solution.py:633
  11.7 2.3 %collective-permute-start.4 = (f32[192,128]{1,0:T(8,128)S(1)}, f32[192,128]{1,0:T(8,128)S(1)}, u32[]{:S(2)}, u32[]{:S(2)}) collective-permute-start(f32[192,128]{1,0:T(8,128)S(1)} %get-tuple-element.52), channel_id=1, source_target_pairs={{0,2},{1,3},{2,0},{3,1},{4,6},{5,7},{6,4},{7,5},{8,10},{9,11},{10,... | collective-permute-start | bytes 294920 | tf_op jit(solution)/shard_map/ppermute | solution.py:634
  14.9 4.4 %collective-permute-start.6 = (f32[1,64,128]{2,1,0:T(8,128)S(1)}, f32[1,64,128]{2,1,0:T(8,128)S(1)}, u32[]{:S(2)}, u32[]{:S(2)}) collective-permute-start(f32[1,64,128]{2,1,0:T(8,128)S(1)} %get-tuple-element.55.after_ref), channel_id=1, source_target_pairs={{0,1},{1,0},{2,3},{3,2},{4,5},{5,4},{6,7},{7,6},{8,9},{9,8},{10,11... | collective-permute-start | bytes 98312 | tf_op jit(solution)/shard_map/ppermute | solution.py:628
  17.0 5.8 %collective-permute-start.8 = (f32[192,128]{1,0:T(8,128)S(1)}, f32[192,128]{1,0:T(8,128)S(1)}, u32[]{:S(2)}, u32[]{:S(2)}) collective-permute-start(f32[192,128]{1,0:T(8,128)S(1)} %get-tuple-element.62), channel_id=1, source_target_pairs={{0,1},{1,0},{2,4},{3,5},{4,2},{5,3},{6,8},{7,9},{8,6},{9,7},{10,12... | collective-permute-start | bytes 294920 | tf_op jit(solution)/shard_map/ppermute | solution.py:633
  17.2 5.6 %collective-permute-start.7 = (f32[200,128]{1,0:T(8,128)S(1)}, f32[200,128]{1,0:T(8,128)S(1)}, u32[]{:S(2)}, u32[]{:S(2)}) collective-permute-start(f32[200,128]{1,0:T(8,128)S(1)} %get-tuple-element.61), channel_id=1, source_target_pairs={{0,2},{1,3},{2,0},{3,1},{4,6},{5,7},{6,4},{7,5},{8,10},{9,11},{10,... | collective-permute-start | bytes 307208 | tf_op jit(solution)/shard_map/ppermute | solution.py:634
  19.3 4.0 %collective-permute-start.10 = (f32[72,128]{1,0:T(8,128)S(1)}, f32[72,128]{1,0:T(8,128)S(1)}, u32[]{:S(2)}, u32[]{:S(2)}) collective-permute-start(f32[72,128]{1,0:T(8,128)S(1)} %get-tuple-element.58.after_ref), channel_id=1, source_target_pairs={{0,1},{1,0},{2,4},{3,5},{4,2},{5,3},{6,8},{7,9},{8,6},{9,7},{10,12... | collective-permute-start | bytes 110600 | tf_op jit(solution)/shard_map/ppermute | solution.py:633
  20.9 2.2 %collective-permute-start.9 = (f32[64,128]{1,0:T(8,128)S(1)}, f32[64,128]{1,0:T(8,128)S(1)}, u32[]{:S(2)}, u32[]{:S(2)}) collective-permute-start(f32[64,128]{1,0:T(8,128)S(1)} %get-tuple-element.66), channel_id=1, source_target_pairs={{0,2},{1,3},{2,0},{3,1},{4,6},{5,7},{6,4},{7,5},{8,10},{9,11},{10,... | collective-permute-start | bytes 98312 | tf_op jit(solution)/shard_map/ppermute | solution.py:634

commit v8 on v7

--- a/solution.py
+++ b/solution.py
@@ -13,7 +13,7 @@
 LOWER_BOUND = 0.05
 UPPER_BOUND = 2.0
 LANES = 128
-CHUNKS = 4
+CHUNKS = 2
 FILL = 8
 
 
@@ -53,6 +53,10 @@
     return lax.axis_index("tile"), lax.axis_index("layer")
 
 
+def weight_of(count_ref):
+    return VIA_UNIT * count_ref[...].astype(jnp.float32)
+
+
 def marked(cells, row, value):
     return jnp.where(cells == row, value, 0.0)
 
@@ -76,27 +80,16 @@
             out_ref[pl.ds(top, 8), start // LANES, :] = field_ref[0, pl.ds(top, 8), pl.ds(start, LANES)]
 
 
-def unpack_volts_kernel(volts_ref, class_ref, x_ref, table_ref, held, class_held, sems):
-    rows, cols = held.shape
-    chunks = chunks_of(cols, CHUNKS)
-    pairs = [(volts_ref.at[0, :, pl.ds(*chunk)], held.at[:, pl.ds(*chunk)]) for chunk in chunks]
-    pairs.append((class_ref, class_held))
-    arriving = [pltpu.make_async_copy(*pair, sems.at[number]) for number, pair in enumerate(pairs)]
-    for copy in arriving:
-        copy.start()
-    for (first, width), copy in zip(chunks, arriving):
-        copy.wait()
-        for top in range(0, rows, 8):
-            part = pl.ds(top, 8)
-            for start in range(first, first + width, LANES):
-                x_ref[part, start // LANES, :] = held[part, pl.ds(start, LANES)]
-    arriving[-1].wait()
+def table_kernel(class_ref, table_ref):
+    count = class_ref.shape[1]
     table_ref[...] = jnp.zeros(table_ref.shape, jnp.float32)
-    count = class_held.shape[1]
-    table_ref[:, pl.ds(0, count)] = jnp.broadcast_to(class_held[...], (8, count))
-
-
-def unpack_index_kernel(index_ref, table_ref, across_ref, down_ref):
+    table_ref[:, pl.ds(0, count)] = jnp.broadcast_to(class_ref[...], (8, count))
+
+
+def unpack_kernel(index_ref, volts_ref, own_ref, count_ref, table_ref, across_ref, down_ref, x_ref, cells_ref, weight_ref):
+    unpack_field_kernel(volts_ref, x_ref)
+    cells_ref[...] = own_ref[...]
+    weight_ref[...] = weight_of(count_ref)
     rows, cols = index_ref.shape[2:]
     tile, _ = place()
     last_tile = tile == lax.axis_size("tile") - 1
@@ -181,17 +174,12 @@
 
 
 def links_kernel(
-    single, x_ref, across_ref, down_ref, own_ref, count_ref, low_ref, first_ref, second_ref, weight_ref, cells_ref, *sends
+    single, x_ref, across_ref, down_ref, own_ref, low_ref, first_ref, second_ref, *sends
 ):
     rows = x_ref.shape[0]
-    own, low = own_ref[...], low_ref[...]
-    weight = VIA_UNIT * count_ref[...].astype(jnp.float32)
-    cells_ref[...] = own
-    weight_ref[...] = weight
-    links = chosen(single, own, low)
+    links = chosen(single, own_ref[...], low_ref[...])
     for send_ref, cells in zip(sends, links):
         send_ref[0] = pick(x_ref, cells, rows)
-    sends[0][1] = weight
     for slot, ref in enumerate((x_ref, across_ref, down_ref)):
         send_by_parity(first_ref, second_ref, slot, ref[0], ref[rows - 1])
     if single:
@@ -199,9 +187,21 @@
 
 
 def first_edges_kernel(
-    rows, x_ref, across_ref, down_ref, loads_ref, own_ref, own_weight_ref, low_ref, above_ref, below_ref, first_ref, second_ref
-):
-    via, fixed, moving = via_terms(own_ref, own_weight_ref, low_ref, below_ref[1], above_ref[0], below_ref[0])
+    rows,
+    x_ref,
+    across_ref,
+    down_ref,
+    loads_ref,
+    own_ref,
+    own_weight_ref,
+    low_ref,
+    low_count_ref,
+    above_ref,
+    below_ref,
+    first_ref,
+    second_ref,
+):
+    via, fixed, moving = via_terms(own_ref, own_weight_ref, low_ref, weight_of(low_count_ref), above_ref[0], below_ref[0])
 
     def right_side(row):
         return fixed(row) + moving(row) - loads_ref[row]
@@ -230,14 +230,14 @@
     own_ref,
     own_weight_ref,
     low_ref,
-    weight_ref,
+    low_count_ref,
     after_ref,
     first_ref,
     second_ref,
     *factor_refs,
 ):
     _, layer = place()
-    _, fixed, _ = via_terms(own_ref, own_weight_ref, low_ref, weight_ref[1], None, None)
+    _, fixed, _ = via_terms(own_ref, own_weight_ref, low_ref, weight_of(low_count_ref), None, None)
 
     def right_side(row):
         return fixed(row) - loads_ref[row]
@@ -248,7 +248,7 @@
         send_by_parity(first_ref, second_ref, 1 + slot, *pair)
     if single:
         cells = jnp.where(layer == 0, own_ref[...], low_ref[...])
-        weight = jnp.where(layer == 0, own_weight_ref[...], weight_ref[1])
+        weight = jnp.where(layer == 0, own_weight_ref[...], weight_of(low_count_ref))
         factors = []
         for (edge, within, link), inverse in zip(edge_ends(rows), inverses):
             share = FACTORS[0][1] * inverse * down_ref[link]
@@ -258,9 +258,9 @@
 
 
 def next_late_kernel(
-    rows, down_ref, inverse_ref, own_ref, own_weight_ref, low_ref, weight_ref, above_ref, below_ref, first_ref, second_ref
-):
-    _, _, moving = via_terms(own_ref, own_weight_ref, low_ref, weight_ref[1], above_ref[0], below_ref[0])
+    rows, down_ref, inverse_ref, own_ref, own_weight_ref, low_ref, low_count_ref, above_ref, below_ref, first_ref, second_ref
+):
+    _, _, moving = via_terms(own_ref, own_weight_ref, low_ref, weight_of(low_count_ref), above_ref[0], below_ref[0])
     found = []
     for edge, within, link in edge_ends(rows):
         change = moving(edge)
@@ -371,6 +371,7 @@
     own_ref,
     own_weight_ref,
     low_ref,
+    low_count_ref,
     above_ref,
     below_ref,
     first_ref,
@@ -385,7 +386,7 @@
     *scratch,
 ):
     tile, _ = place()
-    via, fixed, moving = via_terms(own_ref, own_weight_ref, low_ref, below_ref[1], above_ref[0], below_ref[0])
+    via, fixed, moving = via_terms(own_ref, own_weight_ref, low_ref, weight_of(low_count_ref), above_ref[0], below_ref[0])
     top_x, low_x = taken_by_parity(first_ref, second_ref, 0, x_ref.shape[1])
     top_across, low_across = taken_by_parity(first_ref, second_ref, 1, x_ref.shape[1])
     link, _ = taken_by_parity(first_ref, second_ref, 2, x_ref.shape[1])
@@ -463,7 +464,7 @@
     own_ref,
     own_weight_ref,
     low_ref,
-    weight_ref,
+    low_count_ref,
     above_ref,
     below_ref,
     after_ref,
@@ -472,7 +473,7 @@
     keep_ref,
     *scratch,
 ):
-    _, fixed, moving = via_terms(own_ref, own_weight_ref, low_ref, weight_ref[1], above_ref[0], below_ref[0])
+    _, fixed, moving = via_terms(own_ref, own_weight_ref, low_ref, weight_of(low_count_ref), above_ref[0], below_ref[0])
     for row in range(rows):
         side_ref[row] = fixed(row) + moving(row) - loads_ref[row]
     shared = (x_ref, across_ref, down_ref, side_ref, inverse_ref)
@@ -641,37 +642,29 @@
     cells = via_cells.reshape(lines, LANES)
     counts = via_counts.reshape(lines, LANES)
     low = move(cells, perm=up)
-    x, table = call(
-        unpack_volts_kernel,
-        "unpack_volts",
-        [("hbm", start_volts), ("hbm", class_conductance)],
-        [field, ("vmem", (8, LANES))],
-        [
-            pltpu.VMEM((rows, cols), jnp.float32),
-            pltpu.VMEM(class_conductance.shape, jnp.float32),
-            pltpu.SemaphoreType.DMA((CHUNKS + 1,)),
-        ],
-        work=1000000000,
-    )
-    across, downward = call(unpack_index_kernel, "unpack_index", vmem(class_index, table), [field] * 2)
-    first_sent, second_sent, own_weight, own, *sends = call(
+    low_count = move(counts, perm=up)
+    (table,) = call(table_kernel, "table", vmem(class_conductance), [("vmem", (8, LANES))], work=10**9)
+    across, downward, x, own, own_weight = call(
+        unpack_kernel,
+        "unpack",
+        vmem(class_index, start_volts, cells, counts, table),
+        [field] * 3 + [("vmem", cells.shape, cells.dtype), ("vmem", cells.shape)],
+    )
+    vias = (own, own_weight, low, low_count)
+    first_sent, second_sent, *sends = call(
         functools.partial(links_kernel, single),
         "links",
-        vmem(x, across, downward, cells, counts, low),
-        messages(4 if single else 3, 0)
-        + [("vmem", cells.shape), ("vmem", cells.shape, cells.dtype), ("vmem", rows_of(2))]
-        + ([] if single else [("vmem", rows_of(1))]),
-    )
-    vias = (own, own_weight, low)
+        vmem(x, across, downward, own, low),
+        messages(4 if single else 3, 1) + picks,
+    )
     above, below = between_layers(sends)
-    weights = below
     (load,) = call(unpack_field_kernel, "unpack_loads", vmem(loads), [field])
     early = beside_tile((first_sent, second_sent))
     sent = call(
         functools.partial(first_edges_kernel, rows),
         "first_edges",
         vmem(x, across, downward, load, *vias, above, below),
-        messages(3, 1),
+        messages(3, 0),
         work=2 * 10**10,
     )
     got = beside_tile(sent)
@@ -693,8 +686,8 @@
     sent = call(
         functools.partial(next_early_kernel, single, rows),
         "next_early",
-        vmem(x, across, downward, load, inverse, *vias, weights) + [("any", sends[0])],
-        messages(3, 0) + [("vmem", cells.shape)] * (2 if single else 0),
+        vmem(x, across, downward, load, inverse, *vias) + [("any", sends[0])],
+        messages(3, 1) + [("vmem", cells.shape)] * (2 if single else 0),
     )
     early = beside_tile(sent[:2])
     if single:
@@ -709,7 +702,7 @@
         late = call(
             functools.partial(next_late_kernel, rows),
             "next_late",
-            vmem(downward, inverse, *vias, weights, above, below),
+            vmem(downward, inverse, *vias, above, below),
             messages(2, 1),
             work=2 * 10**10,
         )
@@ -717,7 +710,7 @@
     core, side, keep = call(
         functools.partial(last_inner_kernel, rows),
         "last_inner",
-        vmem(x, across, downward, load, inverse, *vias, weights, above, below) + [("any", late[1])],
+        vmem(x, across, downward, load, inverse, *vias, above, below) + [("any", late[1])],
         [field, field, ("vmem", rows_of(KEPT))],
         work,
     )

time: 24.9 us -> 24.5 us (0.984)
  starting transfers between devices: 15.4 us -> 11.8 us
  waiting for transfers between devices: 1.64 us -> 4.58 us
  local copies, waits for them, and re-layouts: 0.02 us -> 1.27 us
  Pallas kernels: 7.5 us -> 6.52 us
    ppermute x4, starting transfers between devices: 3.75 us -> 0.69 us  [beside_tile(): return (move(sent[0], perm=first), across_chips)]
    ppermute x2, waiting for transfers between devices: 0.34 us -> 2.59 us  [between_layers(): got = move(sends[0], perm=up)]
    unnamed x8 -> x12, local copies, waits for them, and re-layouts: 0.02 us -> 1.27 us
    pallas_call x12, Pallas kernels: 7.5 us -> 6.52 us  [call(): pl.pallas_call(kernel, out_shape=[jax.ShapeDtypeStruct(shape, *(kind or [...]
    ppermute x4, waiting for transfers between devices: 1.28 us -> 1.97 us  [beside_tile(): across_chips = move(sent[1], perm=second)]
    ppermute x2, starting transfers between devices: 3.99 us -> 3.33 us  [between_layers(): got = move(sends[0], perm=up)]
  transfers between devices with their start and end apart: 11 -> 12, of which waited for: 4 -> 5; matrix products, arithmetic and copies ran while one was open for 0% -> 0% of each run, Pallas kernels for 23% -> 19%
where the time goes in v8:
time: 24.5 us; the launch traced here: 24.3 us
  starting transfers between devices  11.8 us (48%)
  Pallas kernels  6.52 us (27%)
  waiting for transfers between devices  4.58 us (19%)
  local copies, waits for them, and re-layouts  1.27 us (5%)
    pallas_call x12, Pallas kernels, call(): pl.pallas_call(kernel, out_shape=[jax.ShapeDtypeStruct(shape, *(kind or [...  6.52 us
    ppermute x4, starting transfers between devices, beside_tile(): across_chips = move(sent[1], perm=second)  4.77 us
    ppermute x2, starting transfers between devices, between_layers(): got = move(sends[0], perm=up)  3.33 us
    ppermute x1, starting transfers between devices, local(): low = move(cells, perm=up)  2.94 us
    ppermute x2, waiting for transfers between devices, between_layers(): got = move(sends[0], perm=up)  2.59 us
    ppermute x4, waiting for transfers between devices, beside_tile(): across_chips = move(sent[1], perm=second)  1.97 us
    unnamed x12, local copies, waits for them, and re-layouts  1.27 us
    ppermute x4, starting transfers between devices, beside_tile(): return (move(sent[0], perm=first), across_chips)  0.69 us
  transfers between devices with their start and end apart: 12, of which 5 were waited for; matrix products, arithmetic and copies ran while one was open for 0% of the time, Pallas kernels for 19%

profile of v8, /device:TPU:0, one launch (start us, length us, event | category | flops | bytes accessed | tf_op | source)
XLA Modules:
  0.0 24.3 jit_solution(4090261706255518709)
XLA Ops:
  0.0 0.0 copy-start.5
  0.0 2.9 %collective-permute-start = (s32[64,128]{1,0:T(8,128)}, s32[64,128]{1,0:T(8,128)S(1)}, u32[]{:S(2)}, u32[]{:S(2)}) collective-permute-start(s32[64,128]{1,0:T(8,128)} %bitcast.3), channel_id=1, source_target_pairs={{0,1},{1,0},{2,3},{3,2},{4,5},{5,4},{6,7},{7,6},{8,9},{9,8},{10,11... | collective-permute-start | bytes 98312 | tf_op jit(solution)/shard_map/ppermute | solution.py:644
  2.9 0.0 copy-start
  2.9 0.0 copy-start.1
  2.9 0.0 copy-start.3
  2.9 0.0 copy-start.4
  3.0 0.1 collective-permute-start.1
  3.0 0.0 copy-done.5
  3.1 1.1 %copy-done = s32[1,2,16,8192]{3,2,1,0:T(8,128)S(1)} copy-done((s32[1,2,16,8192]{3,2,1,0:T(8,128)S(1)}, s32[1,2,16,8192]{3,2,1,0:T(8,128)}, u32[]{:S(2)}) %copy-start) | copy-done | bytes 1048600
  4.2 0.1 copy-done.1
  4.3 0.0 copy-done.3
  4.3 0.0 copy-done.4
  4.3 1.1 %unpack.1 = (f32[16,64,128]{2,1,0:T(8,128)S(1)}, f32[16,64,128]{2,1,0:T(8,128)S(1)}, f32[16,64,128]{2,1,0:T(8,128)S(1)}, s32[64,128]{1,0:T(8,128)S(1)}, f32[64,128]{1,0:T(8,128)S(1)}) custom-call(s32[1,2,16,8192]{3,2,1,0:T(8,128)S(1)} %copy-done, f32[1,16,8192]{2,1,0:T(8,128)S(1)} %copy-done.1, s32[64,128]{1,0:T(8,128)S(1)} %bitcast.4, ...), custom_call_target="tpu_custom_call" | custom-call | tf_op jit(solution)/shard_map/unpack/pallas_call | solution.py:579
  5.4 0.0 collective-permute-done.low_ref
  5.5 0.0 copy-start.2
  5.5 0.1 links.1
  5.6 1.7 %collective-permute-start.2 = (f32[1,64,128]{2,1,0:T(8,128)S(1)}, f32[1,64,128]{2,1,0:T(8,128)S(1)}, u32[]{:S(2)}, u32[]{:S(2)}) collective-permute-start(f32[1,64,128]{2,1,0:T(8,128)S(1)} %get-tuple-element.41), channel_id=1, source_target_pairs={{0,1},{1,0},{2,3},{3,2},{4,5},{5,4},{6,7},{7,6},{8,9},{9,8},{10,11... | collective-permute-start | bytes 98312 | tf_op jit(solution)/shard_map/ppermute | solution.py:629
  7.2 0.0 copy-done.2
  7.2 0.3 %unpack_loads.1.loads_ref = f32[16,64,128]{2,1,0:T(8,128)S(1)} custom-call(f32[1,16,8192]{2,1,0:T(8,128)S(1)} %copy-done.2), custom_call_target="tpu_custom_call" | custom-call | tf_op jit(solution)/shard_map/unpack_loads/pallas_call | solution.py:579
  7.5 0.1 collective-permute-start.3
  7.6 1.0 %collective-permute-start.4 = (f32[264,128]{1,0:T(8,128)S(1)}, f32[264,128]{1,0:T(8,128)S(1)}, u32[]{:S(2)}, u32[]{:S(2)}) collective-permute-start(f32[264,128]{1,0:T(8,128)S(1)} %get-tuple-element.43), channel_id=1, source_target_pairs={{0,1},{1,0},{2,4},{3,5},{4,2},{5,3},{6,8},{7,9},{8,6},{9,7},{10,12... | collective-permute-start | bytes 405512 | tf_op jit(solution)/shard_map/ppermute | solution.py:634
  8.5 0.0 collective-permute-done.1.low_count_ref
  8.5 1.0 %collective-permute-done.2.above_ref.below_ref = f32[1,64,128]{2,1,0:T(8,128)S(1)} collective-permute-done((f32[1,64,128]{2,1,0:T(8,128)S(1)}, f32[1,64,128]{2,1,0:T(8,128)S(1)}, u32[]{:S(2)}, u32[]{:S(2)}) %collective-permute-start.2) | collective-permute-done | bytes 32800 | tf_op jit(solution)/shard_map/ppermute | solution.py:629
  9.5 0.2 first_edges.1
  9.7 0.1 collective-permute-start.5
  9.8 1.7 %collective-permute-start.6 = (f32[192,128]{1,0:T(8,128)S(1)}, f32[192,128]{1,0:T(8,128)S(1)}, u32[]{:S(2)}, u32[]{:S(2)}) collective-permute-start(f32[192,128]{1,0:T(8,128)S(1)} %get-tuple-element.44.after_ref), channel_id=1, source_target_pairs={{0,1},{1,0},{2,4},{3,5},{4,2},{5,3},{6,8},{7,9},{8,6},{9,7},{10,12... | collective-permute-start | bytes 294920 | tf_op jit(solution)/shard_map/ppermute | solution.py:634
  11.5 0.0 collective-permute-done.3.first_ref
  11.5 1.2 %collective-permute-done.4.second_ref = f32[264,128]{1,0:T(8,128)S(1)} collective-permute-done((f32[264,128]{1,0:T(8,128)S(1)}, f32[264,128]{1,0:T(8,128)S(1)}, u32[]{:S(2)}, u32[]{:S(2)}) %collective-permute-start.4) | collective-permute-done | bytes 135200 | tf_op jit(solution)/shard_map/ppermute | solution.py:634
  12.7 1.5 %first_inner.1 = (f32[16,64,128]{2,1,0:T(8,128)S(1)}, f32[16,64,128]{2,1,0:T(8,128)S(1)}, f32[16,64,128]{2,1,0:T(8,128)S(1)}, f32[12,64,128]{2,1,0:T(8,128)S(1)}...) custom-call(f32[16,64,128]{2,1,0:T(8,128)S(1)} %get-tuple-element.36.x_ref, ...), custom_call_target="tpu_custom_call" | custom-call | tf_op jit(solution)/shard_map/first_inner/pallas_call | solution.py:579
  14.2 0.3 %collective-permute-done.6.second_ref = f32[192,128]{1,0:T(8,128)S(1)} collective-permute-done((f32[192,128]{1,0:T(8,128)S(1)}, f32[192,128]{1,0:T(8,128)S(1)}, u32[]{:S(2)}, u32[]{:S(2)}) %collective-permute-start.6) | collective-permute-done | bytes 98336 | tf_op jit(solution)/shard_map/ppermute | solution.py:634
  14.5 0.0 collective-permute-done.5.first_ref
  14.5 0.4 %first_outer.1 = (f32[16,64,128]{2,1,0:T(8,128)S(1)}, f32[2,64,128]{2,1,0:T(8,128)S(1)}, f32[1,64,128]{2,1,0:T(8,128)S(1)}) custom-call(f32[16,64,128]{2,1,0:T(8,128)S(1)} %get-tuple-element.36.x_ref, f32[16,64,128]{2,1,0:T(8,128)S(1)} %get-tuple-element.37.across_ref, ...), custom_call_target="tpu_custom_call", output_to_operand_aliasing={{0}: (12, {})} | custom-call | tf_op jit(solution)/shard_map/first_outer/pallas_call | solution.py:579
  14.9 1.7 %collective-permute-start.7 = (f32[1,64,128]{2,1,0:T(8,128)S(1)}, f32[1,64,128]{2,1,0:T(8,128)S(1)}, u32[]{:S(2)}, u32[]{:S(2)}) collective-permute-start(f32[1,64,128]{2,1,0:T(8,128)S(1)} %get-tuple-element.53.after_ref), channel_id=1, source_target_pairs={{0,1},{1,0},{2,3},{3,2},{4,5},{5,4},{6,7},{7,6},{8,9},{9,8},{10,11... | collective-permute-start | bytes 98312 | tf_op jit(solution)/shard_map/ppermute | solution.py:629
  16.5 0.1 next_early.1
  16.7 0.1 collective-permute-start.8
  16.7 0.5 %collective-permute-start.9 = (f32[200,128]{1,0:T(8,128)S(1)}, f32[200,128]{1,0:T(8,128)S(1)}, u32[]{:S(2)}, u32[]{:S(2)}) collective-permute-start(f32[200,128]{1,0:T(8,128)S(1)} %get-tuple-element.60), channel_id=1, source_target_pairs={{0,1},{1,0},{2,4},{3,5},{4,2},{5,3},{6,8},{7,9},{8,6},{9,7},{10,12... | collective-permute-start | bytes 307208 | tf_op jit(solution)/shard_map/ppermute | solution.py:634
  17.2 1.6 %collective-permute-done.7.volts_ref.above_ref.below_ref = f32[1,64,128]{2,1,0:T(8,128)S(1)} collective-permute-done((f32[1,64,128]{2,1,0:T(8,128)S(1)}, f32[1,64,128]{2,1,0:T(8,128)S(1)}, u32[]{:S(2)}, u32[]{:S(2)}) %collective-permute-start.7) | collective-permute-done | bytes 32800 | tf_op jit(solution)/shard_map/ppermute | solution.py:629
  18.9 1.7 %collective-permute-start.11 = (f32[72,128]{1,0:T(8,128)S(1)}, f32[72,128]{1,0:T(8,128)S(1)}, u32[]{:S(2)}, u32[]{:S(2)}) collective-permute-start(f32[72,128]{1,0:T(8,128)S(1)} %get-tuple-element.56.after_ref), channel_id=1, source_target_pairs={{0,1},{1,0},{2,4},{3,5},{4,2},{5,3},{6,8},{7,9},{8,6},{9,7},{10,12... | collective-permute-start | bytes 110600 | tf_op jit(solution)/shard_map/ppermute | solution.py:634
  20.5 0.5 %collective-permute-start.10 = (f32[64,128]{1,0:T(8,128)S(1)}, f32[64,128]{1,0:T(8,128)S(1)}, u32[]{:S(2)}, u32[]{:S(2)}) collective-permute-start(f32[64,128]{1,0:T(8,128)S(1)} %get-tuple-element.64), channel_id=1, source_target_pairs={{0,2},{1,3},{2,0},{3,1},{4,6},{5,7},{6,4},{7,5},{8,10},{9,11},{10,... | collective-permute-start | bytes 98312 | tf_op jit(solution)/shard_map/ppermute | solution.py:635
  21.0 1.1 %last_inner.1 = (f32[16,64,128]{2,1,0:T(8,128)S(1)}, f32[16,64,128]{2,1,0:T(8,128)S(1)}, f32[12,64,128]{2,1,0:T(8,128)S(1)}) custom-call(f32[16,64,128]{2,1,0:T(8,128)S(1)} %get-tuple-element.52.x_ref, f32[16,64,128]{2,1,0:T(8,128)S(1)} %get-tuple-element.37.across_ref, f32[16,64,128]{2,1,0:T(8,128)S(1)} %get-tuple-element.38.down_ref, ...), custom_call_target="tpu_custom_call" | custom-call | tf_op jit(solution)/shard_map/last_inner/pallas_call | solution.py:579
  22.1 0.0 collective-permute-done.8.first_ref.early_first_ref
  22.1 0.0 collective-permute-done.9.second_ref.early_second_ref
  22.2 0.2 last_middle.1
  22.4 0.0 collective-permute-done.10.first_ref
  22.4 0.5 %collective-permute-done.11.second_ref = f32[72,128]{1,0:T(8,128)S(1)} collective-permute-done((f32[72,128]{1,0:T(8,128)S(1)}, f32[72,128]{1,0:T(8,128)S(1)}, u32[]{:S(2)}, u32[]{:S(2)}) %collective-permute-start.11) | collective-permute-done | bytes 36896 | tf_op jit(solution)/shard_map/ppermute | solution.py:634
  22.9 1.4 %last_outer.1 = (f32[16,8192]{1,0:T(8,128)}, f32[16,64,128]{2,1,0:T(8,128)S(1)}) custom-call(f32[16,64,128]{2,1,0:T(8,128)S(1)} %get-tuple-element.52.x_ref, f32[16,64,128]{2,1,0:T(8,128)S(1)} %get-tuple-element.37.across_ref, f32[16,64,128]{2,1,0:T(8,128)S(1)} %get-tuple-element.38.down_ref, ...), custom_call_target="tpu_custom_call", output_to_operand_aliasing={{1}: (12, {})} | custom-call | tf_op jit(solution)/shard_map/last_outer/pallas_call | solution.py:579
  (2 shorter events, 0.0 us)
Async XLA Ops:
  0.0 3.0 %copy-start.5 = (f32[1,16]{1,0:T(1,128)S(1)}, f32[1,16]{1,0:T(1,128)}, u32[]{:S(2)}) copy-start(f32[1,16]{1,0:T(1,128)} %class_ref.1) | copy-start | bytes 196
  0.0 5.4 %collective-permute-start = (s32[64,128]{1,0:T(8,128)}, s32[64,128]{1,0:T(8,128)S(1)}, u32[]{:S(2)}, u32[]{:S(2)}) collective-permute-start(s32[64,128]{1,0:T(8,128)} %bitcast.3), channel_id=1, source_target_pairs={{0,1},{1,0},{2,3},{3,2},{4,5},{5,4},{6,7},{7,6},{8,9},{9,8},{10,11... | collective-permute-start | bytes 98312 | tf_op jit(solution)/shard_map/ppermute | solution.py:644
  2.9 1.2 %copy-start = (s32[1,2,16,8192]{3,2,1,0:T(8,128)S(1)}, s32[1,2,16,8192]{3,2,1,0:T(8,128)}, u32[]{:S(2)}) copy-start(s32[1,2,16,8192]{3,2,1,0:T(8,128)} %index_ref.1) | copy-start | bytes 3145732
  2.9 1.4 %copy-start.1 = (f32[1,16,8192]{2,1,0:T(8,128)S(1)}, f32[1,16,8192]{2,1,0:T(8,128)}, u32[]{:S(2)}) copy-start(f32[1,16,8192]{2,1,0:T(8,128)} %volts_ref.1) | copy-start | bytes 1572868
  2.9 1.4 %copy-start.3 = (s32[1,8192]{1,0:T(1,128)S(1)}, s32[1,8192]{1,0:T(1,128)}, u32[]{:S(2)}) copy-start(s32[1,8192]{1,0:T(1,128)} %param.10) | copy-start | bytes 98308
  2.9 1.4 %copy-start.4 = (s32[1,8192]{1,0:T(1,128)S(1)}, s32[1,8192]{1,0:T(1,128)}, u32[]{:S(2)}) copy-start(s32[1,8192]{1,0:T(1,128)} %param.11) | copy-start | bytes 98308
  3.0 5.6 %collective-permute-start.1 = (s32[64,128]{1,0:T(8,128)}, s32[64,128]{1,0:T(8,128)S(1)}, u32[]{:S(2)}, u32[]{:S(2)}) collective-permute-start(s32[64,128]{1,0:T(8,128)} %bitcast.5), channel_id=1, source_target_pairs={{0,1},{1,0},{2,3},{3,2},{4,5},{5,4},{6,7},{7,6},{8,9},{9,8},{10,11... | collective-permute-start | bytes 98312 | tf_op jit(solution)/shard_map/ppermute | solution.py:645
  5.5 1.8 %copy-start.2 = (f32[1,16,8192]{2,1,0:T(8,128)S(1)}, f32[1,16,8192]{2,1,0:T(8,128)}, u32[]{:S(2)}) copy-start(f32[1,16,8192]{2,1,0:T(8,128)} %field_ref.1) | copy-start | bytes 1572868
  5.6 4.0 %collective-permute-start.2 = (f32[1,64,128]{2,1,0:T(8,128)S(1)}, f32[1,64,128]{2,1,0:T(8,128)S(1)}, u32[]{:S(2)}, u32[]{:S(2)}) collective-permute-start(f32[1,64,128]{2,1,0:T(8,128)S(1)} %get-tuple-element.41), channel_id=1, source_target_pairs={{0,1},{1,0},{2,3},{3,2},{4,5},{5,4},{6,7},{7,6},{8,9},{9,8},{10,11... | collective-permute-start | bytes 98312 | tf_op jit(solution)/shard_map/ppermute | solution.py:629
  7.5 4.0 %collective-permute-start.3 = (f32[256,128]{1,0:T(8,128)S(1)}, f32[256,128]{1,0:T(8,128)S(1)}, u32[]{:S(2)}, u32[]{:S(2)}) collective-permute-start(f32[256,128]{1,0:T(8,128)S(1)} %get-tuple-element.42), channel_id=1, source_target_pairs={{0,2},{1,3},{2,0},{3,1},{4,6},{5,7},{6,4},{7,5},{8,10},{9,11},{10,... | collective-permute-start | bytes 393224 | tf_op jit(solution)/shard_map/ppermute | solution.py:635
  7.6 5.1 %collective-permute-start.4 = (f32[264,128]{1,0:T(8,128)S(1)}, f32[264,128]{1,0:T(8,128)S(1)}, u32[]{:S(2)}, u32[]{:S(2)}) collective-permute-start(f32[264,128]{1,0:T(8,128)S(1)} %get-tuple-element.43), channel_id=1, source_target_pairs={{0,1},{1,0},{2,4},{3,5},{4,2},{5,3},{6,8},{7,9},{8,6},{9,7},{10,12... | collective-permute-start | bytes 405512 | tf_op jit(solution)/shard_map/ppermute | solution.py:634
  9.7 4.8 %collective-permute-start.5 = (f32[200,128]{1,0:T(8,128)S(1)}, f32[200,128]{1,0:T(8,128)S(1)}, u32[]{:S(2)}, u32[]{:S(2)}) collective-permute-start(f32[200,128]{1,0:T(8,128)S(1)} %get-tuple-element.50), channel_id=1, source_target_pairs={{0,2},{1,3},{2,0},{3,1},{4,6},{5,7},{6,4},{7,5},{8,10},{9,11},{10,... | collective-permute-start | bytes 307208 | tf_op jit(solution)/shard_map/ppermute | solution.py:635
  9.8 4.7 %collective-permute-start.6 = (f32[192,128]{1,0:T(8,128)S(1)}, f32[192,128]{1,0:T(8,128)S(1)}, u32[]{:S(2)}, u32[]{:S(2)}) collective-permute-start(f32[192,128]{1,0:T(8,128)S(1)} %get-tuple-element.44.after_ref), channel_id=1, source_target_pairs={{0,1},{1,0},{2,4},{3,5},{4,2},{5,3},{6,8},{7,9},{8,6},{9,7},{10,12... | collective-permute-start | bytes 294920 | tf_op jit(solution)/shard_map/ppermute | solution.py:634
  14.9 4.0 %collective-permute-start.7 = (f32[1,64,128]{2,1,0:T(8,128)S(1)}, f32[1,64,128]{2,1,0:T(8,128)S(1)}, u32[]{:S(2)}, u32[]{:S(2)}) collective-permute-start(f32[1,64,128]{2,1,0:T(8,128)S(1)} %get-tuple-element.53.after_ref), channel_id=1, source_target_pairs={{0,1},{1,0},{2,3},{3,2},{4,5},{5,4},{6,7},{7,6},{8,9},{9,8},{10,11... | collective-permute-start | bytes 98312 | tf_op jit(solution)/shard_map/ppermute | solution.py:629
  16.7 5.5 %collective-permute-start.8 = (f32[192,128]{1,0:T(8,128)S(1)}, f32[192,128]{1,0:T(8,128)S(1)}, u32[]{:S(2)}, u32[]{:S(2)}) collective-permute-start(f32[192,128]{1,0:T(8,128)S(1)} %get-tuple-element.59), channel_id=1, source_target_pairs={{0,2},{1,3},{2,0},{3,1},{4,6},{5,7},{6,4},{7,5},{8,10},{9,11},{10,... | collective-permute-start | bytes 294920 | tf_op jit(solution)/shard_map/ppermute | solution.py:635
  16.7 5.4 %collective-permute-start.9 = (f32[200,128]{1,0:T(8,128)S(1)}, f32[200,128]{1,0:T(8,128)S(1)}, u32[]{:S(2)}, u32[]{:S(2)}) collective-permute-start(f32[200,128]{1,0:T(8,128)S(1)} %get-tuple-element.60), channel_id=1, source_target_pairs={{0,1},{1,0},{2,4},{3,5},{4,2},{5,3},{6,8},{7,9},{8,6},{9,7},{10,12... | collective-permute-start | bytes 307208 | tf_op jit(solution)/shard_map/ppermute | solution.py:634
  18.9 4.0 %collective-permute-start.11 = (f32[72,128]{1,0:T(8,128)S(1)}, f32[72,128]{1,0:T(8,128)S(1)}, u32[]{:S(2)}, u32[]{:S(2)}) collective-permute-start(f32[72,128]{1,0:T(8,128)S(1)} %get-tuple-element.56.after_ref), channel_id=1, source_target_pairs={{0,1},{1,0},{2,4},{3,5},{4,2},{5,3},{6,8},{7,9},{8,6},{9,7},{10,12... | collective-permute-start | bytes 110600 | tf_op jit(solution)/shard_map/ppermute | solution.py:634
  20.5 1.9 %collective-permute-start.10 = (f32[64,128]{1,0:T(8,128)S(1)}, f32[64,128]{1,0:T(8,128)S(1)}, u32[]{:S(2)}, u32[]{:S(2)}) collective-permute-start(f32[64,128]{1,0:T(8,128)S(1)} %get-tuple-element.64), channel_id=1, source_target_pairs={{0,2},{1,3},{2,0},{3,1},{4,6},{5,7},{6,4},{7,5},{8,10},{9,11},{10,... | collective-permute-start | bytes 98312 | tf_op jit(solution)/shard_map/ppermute | solution.py:635

commit v9 on v8

--- a/solution.py
+++ b/solution.py
@@ -86,8 +86,11 @@
     table_ref[:, pl.ds(0, count)] = jnp.broadcast_to(class_ref[...], (8, count))
 
 
-def unpack_kernel(index_ref, volts_ref, own_ref, count_ref, table_ref, across_ref, down_ref, x_ref, cells_ref, weight_ref):
+def unpack_volts_kernel(volts_ref, after_ref, x_ref):
     unpack_field_kernel(volts_ref, x_ref)
+
+
+def unpack_kernel(index_ref, own_ref, count_ref, table_ref, across_ref, down_ref, cells_ref, weight_ref):
     cells_ref[...] = own_ref[...]
     weight_ref[...] = weight_of(count_ref)
     rows, cols = index_ref.shape[2:]
@@ -493,7 +496,8 @@
     second_ref,
     core_ref,
     kept_ref,
-    next_ref,
+    laid_ref,
+    row_ref,
 ):
     edge_x = taken_by_parity(first_ref, second_ref, 0, x_ref.shape[1])
     for side in range(2):
@@ -508,7 +512,7 @@
             flow = flow + down_ref[links[1]] * within
             value, update = relaxed(x, flow, side_ref[row], inverse_ref[row], previous, sweep)
             if sweep == SWEEPS - 1:
-                next_ref[row] = value
+                row_ref[side] = value
                 break
             slot = 3 * (2 * sweep + side)
             kept_ref[slot] = value
@@ -517,6 +521,12 @@
             further = keep_ref[slot], keep_ref[slot + 1]
             previous = keep_ref[slot + 2]
             outside = value
+    for top in range(0, rows, 8):
+        for line in range(x_ref.shape[1]):
+            laid_ref[pl.ds(top, 8), pl.ds(line * LANES, LANES)] = core_ref[pl.ds(top, 8), line, :]
+    for side, row in enumerate((SWEEPS - 1, rows - SWEEPS)):
+        for line in range(x_ref.shape[1]):
+            laid_ref[pl.ds(row, 1), pl.ds(line * LANES, LANES)] = row_ref[side, pl.ds(line, 1), :]
 
 
 def last_outer_kernel(
@@ -534,10 +544,10 @@
     early_second_ref,
     first_ref,
     second_ref,
-    core_ref,
+    laid_ref,
     out_ref,
-    next_ref,
     held,
+    rim,
     sems,
 ):
     lines = x_ref.shape[1]
@@ -559,17 +569,16 @@
             edge_ref[side],
             *(x_ref, across_ref, down_ref, side_ref, inverse_ref, keep_ref),
         )
+        count = SWEEPS - 1
+        base = 0 if side == 0 else rows - count
         for row, value in outer.items():
-            next_ref[row] = value
-        half = rows // 2
-        for first, width in chunks_of(held.shape[1], CHUNKS):
-            for top in range(side * half, side * half + half, 8):
-                for start in range(first, first + width, LANES):
-                    held[pl.ds(top, 8), pl.ds(start, LANES)] = next_ref[pl.ds(top, 8), start // LANES, :]
-            part = pl.ds(side * half, half), pl.ds(first, width)
-            copy = pltpu.make_async_copy(held.at[part], out_ref.at[part], sems.at[len(leaving)])
-            copy.start()
-            leaving.append(copy)
+            rim[side, row - base] = value
+        for line in range(lines):
+            held[pl.ds(base, count), pl.ds(line * LANES, LANES)] = rim[side, :, line, :]
+        part = pl.ds(side * (rows // 2), rows // 2)
+        copy = pltpu.make_async_copy(held.at[part], out_ref.at[part], sems.at[side])
+        copy.start()
+        leaving.append(copy)
     for copy in leaving:
         copy.wait()
 
@@ -643,13 +652,15 @@
     counts = via_counts.reshape(lines, LANES)
     low = move(cells, perm=up)
     low_count = move(counts, perm=up)
-    (table,) = call(table_kernel, "table", vmem(class_conductance), [("vmem", (8, LANES))], work=10**9)
-    across, downward, x, own, own_weight = call(
+    (table,) = call(table_kernel, "table", vmem(class_conductance), [("vmem", (8, LANES))], work=3*10**8)
+    across, downward, own, own_weight = call(
         unpack_kernel,
         "unpack",
-        vmem(class_index, start_volts, cells, counts, table),
-        [field] * 3 + [("vmem", cells.shape, cells.dtype), ("vmem", cells.shape)],
-    )
+        vmem(class_index, cells, counts, table),
+        [field] * 2 + [("vmem", cells.shape, cells.dtype), ("vmem", cells.shape)],
+        work=3*10**8,
+    )
+    (x,) = call(unpack_volts_kernel, "unpack_volts", vmem(start_volts) + [("any", across)], [field])
     vias = (own, own_weight, low, low_count)
     first_sent, second_sent, *sends = call(
         functools.partial(links_kernel, single),
@@ -714,19 +725,19 @@
         [field, field, ("vmem", rows_of(KEPT))],
         work,
     )
-    keep, core = call(
+    keep, laid = call(
         functools.partial(last_middle_kernel, rows),
         "last_middle",
         vmem(x, across, downward, side, inverse, keep, halo, *early, core),
-        [("vmem", rows_of(KEPT)), field],
-        aliases={9: 1},
+        [("vmem", rows_of(KEPT)), ("vmem", (rows, cols))],
+        [pltpu.VMEM(rows_of(2), jnp.float32)],
     )
     volts, _ = call(
         functools.partial(last_outer_kernel, single, rows),
         "last_outer",
-        vmem(x, across, downward, side, inverse, keep, halo, edge, *early, *got, core),
-        [("hbm", (rows, cols)), field],
-        [pltpu.VMEM((rows, cols), jnp.float32), pltpu.SemaphoreType.DMA((2 * CHUNKS,))],
+        vmem(x, across, downward, side, inverse, keep, halo, edge, *early, *got, laid),
+        [("hbm", (rows, cols)), ("vmem", (rows, cols))],
+        [pltpu.VMEM((2, SWEEPS - 1, lines, LANES), jnp.float32), pltpu.SemaphoreType.DMA((2,))],
         aliases={12: 1},
     )
     return volts[None]

time: 24.5 us -> 24.2 us (0.988)
  waiting for transfers between devices: 4.58 us -> 3.45 us
  starting transfers between devices: 11.8 us -> 12.9 us
  local copies, waits for them, and re-layouts: 1.27 us -> 0.89 us
    ppermute x4, waiting for transfers between devices: 1.97 us -> 1.21 us  [beside_tile(): across_chips = move(sent[1], perm=second)]
    ppermute x2, starting transfers between devices: 3.33 us -> 3.96 us  [between_layers(): got = move(sends[0], perm=up)]
    unnamed x12, local copies, waits for them, and re-layouts: 1.27 us -> 0.89 us
    ppermute x2, waiting for transfers between devices: 2.59 us -> 2.22 us  [between_layers(): got = move(sends[0], perm=up)]
    ppermute x4, starting transfers between devices: 4.77 us -> 5.02 us  [beside_tile(): across_chips = move(sent[1], perm=second)]
    pallas_call x12 -> x13, Pallas kernels: 6.52 us -> 6.58 us  [call(): pl.pallas_call(kernel, out_shape=[jax.ShapeDtypeStruct(shape, *(kind or [...]
  transfers between devices with their start and end apart: 12 -> 12, of which waited for: 5 -> 3; matrix products, arithmetic and copies ran while one was open for 0% -> 0% of each run, Pallas kernels for 19% -> 21%
where the time goes in v9:
time: 24.2 us; the launch traced here: 23.9 us
  starting transfers between devices  12.9 us (53%)
  Pallas kernels  6.58 us (27%)
  waiting for transfers between devices  3.45 us (14%)
  local copies, waits for them, and re-layouts  0.89 us (4%)
    pallas_call x13, Pallas kernels, call(): pl.pallas_call(kernel, out_shape=[jax.ShapeDtypeStruct(shape, *(kind or [...  6.58 us
    ppermute x4, starting transfers between devices, beside_tile(): across_chips = move(sent[1], perm=second)  5.02 us
    ppermute x2, starting transfers between devices, between_layers(): got = move(sends[0], perm=up)  3.96 us
    ppermute x1, starting transfers between devices, local(): low = move(cells, perm=up)  2.94 us
    ppermute x2, waiting for transfers between devices, between_layers(): got = move(sends[0], perm=up)  2.22 us
    ppermute x4, waiting for transfers between devices, beside_tile(): across_chips = move(sent[1], perm=second)  1.21 us
    ppermute x4, starting transfers between devices, beside_tile(): return (move(sent[0], perm=first), across_chips)  0.89 us
    unnamed x12, local copies, waits for them, and re-layouts  0.89 us
  transfers between devices with their start and end apart: 12, of which 3 were waited for; matrix products, arithmetic and copies ran while one was open for 0% of the time, Pallas kernels for 21%

profile of v9, /device:TPU:0, one launch (start us, length us, event | category | flops | bytes accessed | tf_op | source)
XLA Modules:
  0.0 23.9 jit_solution(18198082964493595619)
XLA Ops:
  0.0 0.0 copy-start
  0.0 2.9 %collective-permute-start = (s32[64,128]{1,0:T(8,128)}, s32[64,128]{1,0:T(8,128)S(1)}, u32[]{:S(2)}, u32[]{:S(2)}) collective-permute-start(s32[64,128]{1,0:T(8,128)} %bitcast.3), channel_id=1, source_target_pairs={{0,1},{1,0},{2,3},{3,2},{4,5},{5,4},{6,7},{7,6},{8,9},{9,8},{10,11... | collective-permute-start | bytes 98312 | tf_op jit(solution)/shard_map/ppermute | solution.py:653
  2.9 0.0 copy-start.3
  2.9 0.0 copy-start.4
  2.9 0.1 collective-permute-start.1
  3.0 0.0 copy-start.5
  3.0 0.7 %copy-done.5 = f32[1,16]{1,0:T(1,128)S(1)} copy-done((f32[1,16]{1,0:T(1,128)S(1)}, f32[1,16]{1,0:T(1,128)}, u32[]{:S(2)}) %copy-start.5) | copy-done | bytes 88
  3.7 0.0 copy-done
  3.7 0.0 copy-done.3
  3.7 0.0 copy-done.4
  3.7 0.0 copy-start.1
  3.7 0.9 %unpack.1 = (f32[16,64,128]{2,1,0:T(8,128)S(1)}, f32[16,64,128]{2,1,0:T(8,128)S(1)}, s32[64,128]{1,0:T(8,128)S(1)}, f32[64,128]{1,0:T(8,128)S(1)}) custom-call(s32[1,2,16,8192]{3,2,1,0:T(8,128)S(1)} %copy-done, s32[64,128]{1,0:T(8,128)S(1)} %bitcast.4, s32[64,128]{1,0:T(8,128)S(1)} %bitcast.6, f32[8,128]{1,0:T(8,128)S(1)} %table.1.table_ref), custom_call_target="tpu_custom_call" | custom-call | flops 300000000 | bytes 300000000 | tf_op jit(solution)/shard_map/unpack/pallas_call | solution.py:588
  4.6 0.2 copy-done.1
  4.8 0.3 %unpack_volts.1.x_ref = f32[16,64,128]{2,1,0:T(8,128)S(1)} custom-call(f32[1,16,8192]{2,1,0:T(8,128)S(1)} %copy-done.1, f32[16,64,128]{2,1,0:T(8,128)S(1)} %get-tuple-element.35.after_ref.across_ref), custom_call_target="tpu_custom_call" | custom-call | tf_op jit(solution)/shard_map/unpack_volts/pallas_call | solution.py:588
  5.1 0.0 collective-permute-done.low_ref
  5.1 0.0 copy-start.2
  5.1 0.1 links.1
  5.2 2.0 %collective-permute-start.2 = (f32[1,64,128]{2,1,0:T(8,128)S(1)}, f32[1,64,128]{2,1,0:T(8,128)S(1)}, u32[]{:S(2)}, u32[]{:S(2)}) collective-permute-start(f32[1,64,128]{2,1,0:T(8,128)S(1)} %get-tuple-element.39), channel_id=1, source_target_pairs={{0,1},{1,0},{2,3},{3,2},{4,5},{5,4},{6,7},{7,6},{8,9},{9,8},{10,11... | collective-permute-start | bytes 98312 | tf_op jit(solution)/shard_map/ppermute | solution.py:638
  7.2 0.0 copy-done.2
  7.2 0.3 %unpack_loads.1.loads_ref = f32[16,64,128]{2,1,0:T(8,128)S(1)} custom-call(f32[1,16,8192]{2,1,0:T(8,128)S(1)} %copy-done.2), custom_call_target="tpu_custom_call" | custom-call | tf_op jit(solution)/shard_map/unpack_loads/pallas_call | solution.py:588
  7.5 0.1 collective-permute-start.3
  7.6 1.0 %collective-permute-start.4 = (f32[264,128]{1,0:T(8,128)S(1)}, f32[264,128]{1,0:T(8,128)S(1)}, u32[]{:S(2)}, u32[]{:S(2)}) collective-permute-start(f32[264,128]{1,0:T(8,128)S(1)} %get-tuple-element.41), channel_id=1, source_target_pairs={{0,1},{1,0},{2,4},{3,5},{4,2},{5,3},{6,8},{7,9},{8,6},{9,7},{10,12... | collective-permute-start | bytes 405512 | tf_op jit(solution)/shard_map/ppermute | solution.py:643
  8.5 0.0 collective-permute-done.1.low_count_ref
  8.5 0.6 %collective-permute-done.2.above_ref.below_ref = f32[1,64,128]{2,1,0:T(8,128)S(1)} collective-permute-done((f32[1,64,128]{2,1,0:T(8,128)S(1)}, f32[1,64,128]{2,1,0:T(8,128)S(1)}, u32[]{:S(2)}, u32[]{:S(2)}) %collective-permute-start.2) | collective-permute-done | bytes 32800 | tf_op jit(solution)/shard_map/ppermute | solution.py:638
  9.2 0.2 first_edges.1
  9.3 0.2 collective-permute-start.5
  9.5 1.9 %collective-permute-start.6 = (f32[192,128]{1,0:T(8,128)S(1)}, f32[192,128]{1,0:T(8,128)S(1)}, u32[]{:S(2)}, u32[]{:S(2)}) collective-permute-start(f32[192,128]{1,0:T(8,128)S(1)} %get-tuple-element.42.after_ref), channel_id=1, source_target_pairs={{0,1},{1,0},{2,4},{3,5},{4,2},{5,3},{6,8},{7,9},{8,6},{9,7},{10,12... | collective-permute-start | bytes 294920 | tf_op jit(solution)/shard_map/ppermute | solution.py:643
  11.5 0.0 collective-permute-done.3.first_ref
  11.5 1.2 %collective-permute-done.4.second_ref = f32[264,128]{1,0:T(8,128)S(1)} collective-permute-done((f32[264,128]{1,0:T(8,128)S(1)}, f32[264,128]{1,0:T(8,128)S(1)}, u32[]{:S(2)}, u32[]{:S(2)}) %collective-permute-start.4) | collective-permute-done | bytes 135200 | tf_op jit(solution)/shard_map/ppermute | solution.py:643
  12.7 1.5 %first_inner.1 = (f32[16,64,128]{2,1,0:T(8,128)S(1)}, f32[16,64,128]{2,1,0:T(8,128)S(1)}, f32[16,64,128]{2,1,0:T(8,128)S(1)}, f32[12,64,128]{2,1,0:T(8,128)S(1)}...) custom-call(f32[16,64,128]{2,1,0:T(8,128)S(1)} %unpack_volts.1.x_ref, ...), custom_call_target="tpu_custom_call" | custom-call | tf_op jit(solution)/shard_map/first_inner/pallas_call | solution.py:588
  14.2 0.0 collective-permute-done.6.second_ref
  14.2 0.0 collective-permute-done.5.first_ref
  14.2 0.4 %first_outer.1 = (f32[16,64,128]{2,1,0:T(8,128)S(1)}, f32[2,64,128]{2,1,0:T(8,128)S(1)}, f32[1,64,128]{2,1,0:T(8,128)S(1)}) custom-call(f32[16,64,128]{2,1,0:T(8,128)S(1)} %unpack_volts.1.x_ref, f32[16,64,128]{2,1,0:T(8,128)S(1)} %get-tuple-element.35.after_ref.across_ref, ...), custom_call_target="tpu_custom_call", output_to_operand_aliasing={{0}: (12, {})} | custom-call | tf_op jit(solution)/shard_map/first_outer/pallas_call | solution.py:588
  14.6 1.9 %collective-permute-start.7 = (f32[1,64,128]{2,1,0:T(8,128)S(1)}, f32[1,64,128]{2,1,0:T(8,128)S(1)}, u32[]{:S(2)}, u32[]{:S(2)}) collective-permute-start(f32[1,64,128]{2,1,0:T(8,128)S(1)} %get-tuple-element.51.after_ref), channel_id=1, source_target_pairs={{0,1},{1,0},{2,3},{3,2},{4,5},{5,4},{6,7},{7,6},{8,9},{9,8},{10,11... | collective-permute-start | bytes 98312 | tf_op jit(solution)/shard_map/ppermute | solution.py:638
  16.5 0.1 next_early.1
  16.7 0.1 collective-permute-start.8
  16.7 0.2 collective-permute-start.9
  17.0 1.6 %collective-permute-done.7.volts_ref.above_ref.below_ref = f32[1,64,128]{2,1,0:T(8,128)S(1)} collective-permute-done((f32[1,64,128]{2,1,0:T(8,128)S(1)}, f32[1,64,128]{2,1,0:T(8,128)S(1)}, u32[]{:S(2)}, u32[]{:S(2)}) %collective-permute-start.7) | collective-permute-done | bytes 32800 | tf_op jit(solution)/shard_map/ppermute | solution.py:638
  18.6 1.9 %collective-permute-start.11 = (f32[72,128]{1,0:T(8,128)S(1)}, f32[72,128]{1,0:T(8,128)S(1)}, u32[]{:S(2)}, u32[]{:S(2)}) collective-permute-start(f32[72,128]{1,0:T(8,128)S(1)} %get-tuple-element.54.after_ref), channel_id=1, source_target_pairs={{0,1},{1,0},{2,4},{3,5},{4,2},{5,3},{6,8},{7,9},{8,6},{9,7},{10,12... | collective-permute-start | bytes 110600 | tf_op jit(solution)/shard_map/ppermute | solution.py:643
  20.5 0.5 %collective-permute-start.10 = (f32[64,128]{1,0:T(8,128)S(1)}, f32[64,128]{1,0:T(8,128)S(1)}, u32[]{:S(2)}, u32[]{:S(2)}) collective-permute-start(f32[64,128]{1,0:T(8,128)S(1)} %get-tuple-element.62), channel_id=1, source_target_pairs={{0,2},{1,3},{2,0},{3,1},{4,6},{5,7},{6,4},{7,5},{8,10},{9,11},{10,... | collective-permute-start | bytes 98312 | tf_op jit(solution)/shard_map/ppermute | solution.py:644
  21.1 1.1 %last_inner.1 = (f32[16,64,128]{2,1,0:T(8,128)S(1)}, f32[16,64,128]{2,1,0:T(8,128)S(1)}, f32[12,64,128]{2,1,0:T(8,128)S(1)}) custom-call(f32[16,64,128]{2,1,0:T(8,128)S(1)} %get-tuple-element.50.x_ref, f32[16,64,128]{2,1,0:T(8,128)S(1)} %get-tuple-element.35.after_ref.across_ref, f32[16,64,128]{2,1,0:T(8,128)S(1)} %get-tuple-element.36.down_ref, ...), custom_call_target="tpu_custom_call" | custom-call | tf_op jit(solution)/shard_map/last_inner/pallas_call | solution.py:588
  22.2 0.0 collective-permute-done.8.first_ref.early_first_ref
  22.2 0.0 collective-permute-done.9.second_ref.early_second_ref
  22.2 0.5 %last_middle.1 = (f32[12,64,128]{2,1,0:T(8,128)S(1)}, f32[16,8192]{1,0:T(8,128)S(1)}) custom-call(f32[16,64,128]{2,1,0:T(8,128)S(1)} %get-tuple-element.50.x_ref, f32[16,64,128]{2,1,0:T(8,128)S(1)} %get-tuple-element.35.after_ref.across_ref, f32[16,64,128]{2,1,0:T(8,128)S(1)} %get-tuple-element.36.down_ref, f32[16,64,128]{2,1,0:T(8,128)S(1)} %get-tuple-element.55.side_ref, ...), custom_call_target="tpu_custom_call" | custom-call | tf_op jit(solution)/shard_map/last_middle/pallas_call | solution.py:588
  22.8 0.0 collective-permute-done.10.first_ref
  22.8 0.0 collective-permute-done.11.second_ref
  22.8 1.1 %last_outer.1 = (f32[16,8192]{1,0:T(8,128)}, f32[16,8192]{1,0:T(8,128)S(1)}) custom-call(f32[16,64,128]{2,1,0:T(8,128)S(1)} %get-tuple-element.50.x_ref, f32[16,64,128]{2,1,0:T(8,128)S(1)} %get-tuple-element.35.after_ref.across_ref, f32[16,64,128]{2,1,0:T(8,128)S(1)} %get-tuple-element.36.down_ref, ...), custom_call_target="tpu_custom_call", output_to_operand_aliasing={{1}: (12, {})} | custom-call | tf_op jit(solution)/shard_map/last_outer/pallas_call | solution.py:588
  (2 shorter events, 0.0 us)
Async XLA Ops:
  0.0 3.7 %copy-start = (s32[1,2,16,8192]{3,2,1,0:T(8,128)S(1)}, s32[1,2,16,8192]{3,2,1,0:T(8,128)}, u32[]{:S(2)}) copy-start(s32[1,2,16,8192]{3,2,1,0:T(8,128)} %index_ref.1) | copy-start | bytes 3145732
  0.0 5.1 %collective-permute-start = (s32[64,128]{1,0:T(8,128)}, s32[64,128]{1,0:T(8,128)S(1)}, u32[]{:S(2)}, u32[]{:S(2)}) collective-permute-start(s32[64,128]{1,0:T(8,128)} %bitcast.3), channel_id=1, source_target_pairs={{0,1},{1,0},{2,3},{3,2},{4,5},{5,4},{6,7},{7,6},{8,9},{9,8},{10,11... | collective-permute-start | bytes 98312 | tf_op jit(solution)/shard_map/ppermute | solution.py:653
  2.9 0.8 %copy-start.3 = (s32[1,8192]{1,0:T(1,128)S(1)}, s32[1,8192]{1,0:T(1,128)}, u32[]{:S(2)}) copy-start(s32[1,8192]{1,0:T(1,128)} %param.10) | copy-start | bytes 98308
  2.9 0.8 %copy-start.4 = (s32[1,8192]{1,0:T(1,128)S(1)}, s32[1,8192]{1,0:T(1,128)}, u32[]{:S(2)}) copy-start(s32[1,8192]{1,0:T(1,128)} %param.11) | copy-start | bytes 98308
  2.9 5.6 %collective-permute-start.1 = (s32[64,128]{1,0:T(8,128)}, s32[64,128]{1,0:T(8,128)S(1)}, u32[]{:S(2)}, u32[]{:S(2)}) collective-permute-start(s32[64,128]{1,0:T(8,128)} %bitcast.5), channel_id=1, source_target_pairs={{0,1},{1,0},{2,3},{3,2},{4,5},{5,4},{6,7},{7,6},{8,9},{9,8},{10,11... | collective-permute-start | bytes 98312 | tf_op jit(solution)/shard_map/ppermute | solution.py:654
  3.0 0.7 %copy-start.5 = (f32[1,16]{1,0:T(1,128)S(1)}, f32[1,16]{1,0:T(1,128)}, u32[]{:S(2)}) copy-start(f32[1,16]{1,0:T(1,128)} %class_ref.1) | copy-start | bytes 196
  3.7 1.0 %copy-start.1 = (f32[1,16,8192]{2,1,0:T(8,128)S(1)}, f32[1,16,8192]{2,1,0:T(8,128)}, u32[]{:S(2)}) copy-start(f32[1,16,8192]{2,1,0:T(8,128)} %volts_ref.1) | copy-start | bytes 1572868
  5.1 2.1 %copy-start.2 = (f32[1,16,8192]{2,1,0:T(8,128)S(1)}, f32[1,16,8192]{2,1,0:T(8,128)}, u32[]{:S(2)}) copy-start(f32[1,16,8192]{2,1,0:T(8,128)} %field_ref.1) | copy-start | bytes 1572868
  5.2 4.0 %collective-permute-start.2 = (f32[1,64,128]{2,1,0:T(8,128)S(1)}, f32[1,64,128]{2,1,0:T(8,128)S(1)}, u32[]{:S(2)}, u32[]{:S(2)}) collective-permute-start(f32[1,64,128]{2,1,0:T(8,128)S(1)} %get-tuple-element.39), channel_id=1, source_target_pairs={{0,1},{1,0},{2,3},{3,2},{4,5},{5,4},{6,7},{7,6},{8,9},{9,8},{10,11... | collective-permute-start | bytes 98312 | tf_op jit(solution)/shard_map/ppermute | solution.py:638
  7.5 4.0 %collective-permute-start.3 = (f32[256,128]{1,0:T(8,128)S(1)}, f32[256,128]{1,0:T(8,128)S(1)}, u32[]{:S(2)}, u32[]{:S(2)}) collective-permute-start(f32[256,128]{1,0:T(8,128)S(1)} %get-tuple-element.40), channel_id=1, source_target_pairs={{0,2},{1,3},{2,0},{3,1},{4,6},{5,7},{6,4},{7,5},{8,10},{9,11},{10,... | collective-permute-start | bytes 393224 | tf_op jit(solution)/shard_map/ppermute | solution.py:644
  7.6 5.1 %collective-permute-start.4 = (f32[264,128]{1,0:T(8,128)S(1)}, f32[264,128]{1,0:T(8,128)S(1)}, u32[]{:S(2)}, u32[]{:S(2)}) collective-permute-start(f32[264,128]{1,0:T(8,128)S(1)} %get-tuple-element.41), channel_id=1, source_target_pairs={{0,1},{1,0},{2,4},{3,5},{4,2},{5,3},{6,8},{7,9},{8,6},{9,7},{10,12... | collective-permute-start | bytes 405512 | tf_op jit(solution)/shard_map/ppermute | solution.py:643
  9.3 4.9 %collective-permute-start.5 = (f32[200,128]{1,0:T(8,128)S(1)}, f32[200,128]{1,0:T(8,128)S(1)}, u32[]{:S(2)}, u32[]{:S(2)}) collective-permute-start(f32[200,128]{1,0:T(8,128)S(1)} %get-tuple-element.48), channel_id=1, source_target_pairs={{0,2},{1,3},{2,0},{3,1},{4,6},{5,7},{6,4},{7,5},{8,10},{9,11},{10,... | collective-permute-start | bytes 307208 | tf_op jit(solution)/shard_map/ppermute | solution.py:644
  9.5 4.7 %collective-permute-start.6 = (f32[192,128]{1,0:T(8,128)S(1)}, f32[192,128]{1,0:T(8,128)S(1)}, u32[]{:S(2)}, u32[]{:S(2)}) collective-permute-start(f32[192,128]{1,0:T(8,128)S(1)} %get-tuple-element.42.after_ref), channel_id=1, source_target_pairs={{0,1},{1,0},{2,4},{3,5},{4,2},{5,3},{6,8},{7,9},{8,6},{9,7},{10,12... | collective-permute-start | bytes 294920 | tf_op jit(solution)/shard_map/ppermute | solution.py:643
  14.6 4.0 %collective-permute-start.7 = (f32[1,64,128]{2,1,0:T(8,128)S(1)}, f32[1,64,128]{2,1,0:T(8,128)S(1)}, u32[]{:S(2)}, u32[]{:S(2)}) collective-permute-start(f32[1,64,128]{2,1,0:T(8,128)S(1)} %get-tuple-element.51.after_ref), channel_id=1, source_target_pairs={{0,1},{1,0},{2,3},{3,2},{4,5},{5,4},{6,7},{7,6},{8,9},{9,8},{10,11... | collective-permute-start | bytes 98312 | tf_op jit(solution)/shard_map/ppermute | solution.py:638
  16.7 5.5 %collective-permute-start.8 = (f32[192,128]{1,0:T(8,128)S(1)}, f32[192,128]{1,0:T(8,128)S(1)}, u32[]{:S(2)}, u32[]{:S(2)}) collective-permute-start(f32[192,128]{1,0:T(8,128)S(1)} %get-tuple-element.57), channel_id=1, source_target_pairs={{0,2},{1,3},{2,0},{3,1},{4,6},{5,7},{6,4},{7,5},{8,10},{9,11},{10,... | collective-permute-start | bytes 294920 | tf_op jit(solution)/shard_map/ppermute | solution.py:644
  16.7 5.5 %collective-permute-start.9 = (f32[200,128]{1,0:T(8,128)S(1)}, f32[200,128]{1,0:T(8,128)S(1)}, u32[]{:S(2)}, u32[]{:S(2)}) collective-permute-start(f32[200,128]{1,0:T(8,128)S(1)} %get-tuple-element.58), channel_id=1, source_target_pairs={{0,1},{1,0},{2,4},{3,5},{4,2},{5,3},{6,8},{7,9},{8,6},{9,7},{10,12... | collective-permute-start | bytes 307208 | tf_op jit(solution)/shard_map/ppermute | solution.py:643
  18.6 4.2 %collective-permute-start.11 = (f32[72,128]{1,0:T(8,128)S(1)}, f32[72,128]{1,0:T(8,128)S(1)}, u32[]{:S(2)}, u32[]{:S(2)}) collective-permute-start(f32[72,128]{1,0:T(8,128)S(1)} %get-tuple-element.54.after_ref), channel_id=1, source_target_pairs={{0,1},{1,0},{2,4},{3,5},{4,2},{5,3},{6,8},{7,9},{8,6},{9,7},{10,12... | collective-permute-start | bytes 110600 | tf_op jit(solution)/shard_map/ppermute | solution.py:643
  20.5 2.3 %collective-permute-start.10 = (f32[64,128]{1,0:T(8,128)S(1)}, f32[64,128]{1,0:T(8,128)S(1)}, u32[]{:S(2)}, u32[]{:S(2)}) collective-permute-start(f32[64,128]{1,0:T(8,128)S(1)} %get-tuple-element.62), channel_id=1, source_target_pairs={{0,2},{1,3},{2,0},{3,1},{4,6},{5,7},{6,4},{7,5},{8,10},{9,11},{10,... | collective-permute-start | bytes 98312 | tf_op jit(solution)/shard_map/ppermute | solution.py:644

commit v10 on v9

--- a/solution.py
+++ b/solution.py
@@ -84,6 +84,15 @@
     count = class_ref.shape[1]
     table_ref[...] = jnp.zeros(table_ref.shape, jnp.float32)
     table_ref[:, pl.ds(0, count)] = jnp.broadcast_to(class_ref[...], (8, count))
+
+
+def unpack_loads_kernel(loads_ref, own_ref, weight_ref, out_ref):
+    unpack_field_kernel(loads_ref, out_ref)
+    _, layer = place()
+    supplied = jnp.where(layer == lax.axis_size("layer") - 1, weight_ref[...], 0.0)
+    cells = own_ref[...]
+    for row in range(out_ref.shape[0]):
+        out_ref[row] = out_ref[row] - marked(cells, row, supplied)
 
 
 def unpack_volts_kernel(volts_ref, after_ref, x_ref):
@@ -115,27 +124,29 @@
 
 def via_terms(own_ref, own_weight_ref, low_ref, low_weight, from_above, from_below):
     _, layer = place()
-    on_top = layer == lax.axis_size("layer") - 1
+    layers = lax.axis_size("layer")
     own_weight = own_weight_ref[...]
     low_weight = jnp.where(layer == 0, 0.0, low_weight)
-    fixed_source = jnp.where(on_top, own_weight, 0.0)
     own, low = own_ref[...], low_ref[...]
 
     def via(row):
         return marked(own, row, own_weight) + marked(low, row, low_weight)
 
-    def fixed(row):
-        return marked(own, row, fixed_source)
-
-    if from_above is None:
-        return via, fixed, None
-    own_source = jnp.where(on_top, 0.0, own_weight * from_above)
+    if layers == 2:
+        cells = jnp.where(layer == 0, own, low)
+        source = jnp.where(layer == 0, own_weight, low_weight) * from_above
+
+        def moving(row):
+            return marked(cells, row, source)
+
+        return via, moving
+    own_source = jnp.where(layer == layers - 1, 0.0, own_weight * from_above)
     low_source = low_weight * from_below
 
     def moving(row):
         return marked(own, row, own_source) + marked(low, row, low_source)
 
-    return via, fixed, moving
+    return via, moving
 
 
 def send_by_parity(first_ref, second_ref, slot, top, bottom):
@@ -148,6 +159,13 @@
     if slot == 0:
         longer = first_ref if lengths[0] > lengths[1] else second_ref
         longer[pl.ds(min(lengths), FILL)] = jnp.zeros((FILL, LANES), jnp.float32)
+
+
+def by_parity(work):
+    tile, _ = place()
+    even = lax.rem(tile, 2) == 0
+    for side in range(2):
+        pl.when(even if side == 1 else jnp.logical_not(even))(functools.partial(work, side))
 
 
 def taken_by_parity(first_ref, second_ref, slot, lines):
@@ -204,10 +222,10 @@
     first_ref,
     second_ref,
 ):
-    via, fixed, moving = via_terms(own_ref, own_weight_ref, low_ref, weight_of(low_count_ref), above_ref[0], below_ref[0])
+    via, moving = via_terms(own_ref, own_weight_ref, low_ref, weight_of(low_count_ref), above_ref[0], below_ref[0])
 
     def right_side(row):
-        return fixed(row) + moving(row) - loads_ref[row]
+        return moving(row) - loads_ref[row]
 
     def diagonal(row, links):
         across = across_ref[row]
@@ -240,10 +258,9 @@
     *factor_refs,
 ):
     _, layer = place()
-    _, fixed, _ = via_terms(own_ref, own_weight_ref, low_ref, weight_of(low_count_ref), None, None)
 
     def right_side(row):
-        return fixed(row) - loads_ref[row]
+        return -loads_ref[row]
 
     send_by_parity(first_ref, second_ref, 0, x_ref[0], x_ref[rows - 1])
     inverses = inverse_ref[1], inverse_ref[rows - 2]
@@ -263,7 +280,7 @@
 def next_late_kernel(
     rows, down_ref, inverse_ref, own_ref, own_weight_ref, low_ref, low_count_ref, above_ref, below_ref, first_ref, second_ref
 ):
-    _, _, moving = via_terms(own_ref, own_weight_ref, low_ref, weight_of(low_count_ref), above_ref[0], below_ref[0])
+    _, moving = via_terms(own_ref, own_weight_ref, low_ref, weight_of(low_count_ref), above_ref[0], below_ref[0])
     found = []
     for edge, within, link in edge_ends(rows):
         change = moving(edge)
@@ -389,7 +406,7 @@
     *scratch,
 ):
     tile, _ = place()
-    via, fixed, moving = via_terms(own_ref, own_weight_ref, low_ref, weight_of(low_count_ref), above_ref[0], below_ref[0])
+    via, moving = via_terms(own_ref, own_weight_ref, low_ref, weight_of(low_count_ref), above_ref[0], below_ref[0])
     top_x, low_x = taken_by_parity(first_ref, second_ref, 0, x_ref.shape[1])
     top_across, low_across = taken_by_parity(first_ref, second_ref, 1, x_ref.shape[1])
     link, _ = taken_by_parity(first_ref, second_ref, 2, x_ref.shape[1])
@@ -400,7 +417,7 @@
     for slot, value in enumerate(held):
         halo_ref[slot] = value
     for row in range(rows):
-        side_ref[row] = fixed(row) + moving(row) - loads_ref[row]
+        side_ref[row] = moving(row) - loads_ref[row]
         across = across_ref[row]
         diagonal = across + column_left(across) + down_ref[row] + via(row)
         diagonal = diagonal + (down_ref[row - 1] if row > 0 else link)
@@ -415,9 +432,10 @@
         picked_ref[index] = total
 
 
-def first_outer_kernel(
+def first_rim(
     single,
     rows,
+    side,
     x_ref,
     across_ref,
     down_ref,
@@ -425,36 +443,48 @@
     inverse_ref,
     keep_ref,
     halo_ref,
-    picked_ref,
     own_ref,
     low_ref,
-    first_ref,
-    second_ref,
-    core_ref,
+    picked_ref,
+    late_ref,
     next_ref,
     edge_ref,
-    *sends,
-):
-    top_q0, low_q0 = taken_by_parity(first_ref, second_ref, 0, x_ref.shape[1])
-    top_q1, low_q1 = taken_by_parity(first_ref, second_ref, 1, x_ref.shape[1])
-    top_diag, low_diag = taken_by_parity(first_ref, second_ref, 2, x_ref.shape[1])
-    link, low_link = halo_ref[2], down_ref[rows - 1]
-    top_inverse = 1.0 / (top_diag + link)
-    low_inverse = 1.0 / (low_diag + low_link)
-    edge_ref[0] = top_inverse
-    edge_ref[1] = low_inverse
+    totals,
+):
+    lines = x_ref.shape[1]
+    q0, q1, diagonal = (late_ref[pl.ds(slot * lines, lines)] for slot in range(3))
+    link = halo_ref[2] if side == 0 else down_ref[rows - 1]
+    inverse = 1.0 / (diagonal + link)
+    edge_ref[side] = inverse
     shared = (x_ref, across_ref, down_ref, side_ref, inverse_ref, keep_ref)
-    outer = outer_rows(0, rows, 0, (halo_ref[3], (top_q0, top_q1), halo_ref[0]), link, top_inverse, *shared)
-    outer.update(
-        outer_rows(1, rows, 0, (halo_ref[4], (low_q0, low_q1), halo_ref[1]), low_link, low_inverse, *shared)
-    )
+    outer = outer_rows(side, rows, 0, (halo_ref[3 + side], (q0, q1), halo_ref[side]), link, inverse, *shared)
     for row, value in outer.items():
         next_ref[row] = value
     for index, cells in enumerate(chosen(single, own_ref[...], low_ref[...])):
         total = picked_ref[index]
         for row, value in outer.items():
             total = total + marked(cells, row, value)
+        totals(index, total)
+
+
+def first_near_kernel(single, rows, *refs):
+    *ins, _, next_ref, edge_ref, found_ref = refs
+
+    def found(index, total):
+        found_ref[index] = total
+
+    by_parity(lambda side: first_rim(single, rows, side, *ins, next_ref, edge_ref, found))
+
+
+def first_far_kernel(single, rows, *refs):
+    count = 1 if single else 2
+    *ins, _, _, next_ref, edge_ref = refs[:-count]
+    sends = refs[-count:]
+
+    def found(index, total):
         sends[index][0] = total
+
+    by_parity(lambda near: first_rim(single, rows, 1 - near, *ins, next_ref, edge_ref, found))
 
 
 def last_inner_kernel(
@@ -476,14 +506,15 @@
     keep_ref,
     *scratch,
 ):
-    _, fixed, moving = via_terms(own_ref, own_weight_ref, low_ref, weight_of(low_count_ref), above_ref[0], below_ref[0])
+    _, moving = via_terms(own_ref, own_weight_ref, low_ref, weight_of(low_count_ref), above_ref[0], below_ref[0])
     for row in range(rows):
-        side_ref[row] = fixed(row) + moving(row) - loads_ref[row]
+        side_ref[row] = moving(row) - loads_ref[row]
     shared = (x_ref, across_ref, down_ref, side_ref, inverse_ref)
     inner_rows(rows, 1, None, *shared, scratch[:-1], scratch[-1], core_ref, keep_ref)
 
 
 def last_middle_kernel(
+    single,
     rows,
     x_ref,
     across_ref,
@@ -492,12 +523,15 @@
     inverse_ref,
     keep_ref,
     halo_ref,
+    edge_ref,
     first_ref,
     second_ref,
+    late_ref,
     core_ref,
     kept_ref,
     laid_ref,
     row_ref,
+    rim,
 ):
     edge_x = taken_by_parity(first_ref, second_ref, 0, x_ref.shape[1])
     for side in range(2):
@@ -527,11 +561,14 @@
     for side, row in enumerate((SWEEPS - 1, rows - SWEEPS)):
         for line in range(x_ref.shape[1]):
             laid_ref[pl.ds(row, 1), pl.ds(line * LANES, LANES)] = row_ref[side, pl.ds(line, 1), :]
-
-
-def last_outer_kernel(
+    known = (x_ref, across_ref, down_ref, side_ref, inverse_ref, kept_ref, halo_ref, edge_ref)
+    by_parity(lambda near: rim_rows(single, rows, near, *known, first_ref, late_ref, laid_ref, rim))
+
+
+def rim_rows(
     single,
     rows,
+    side,
     x_ref,
     across_ref,
     down_ref,
@@ -540,47 +577,55 @@
     keep_ref,
     halo_ref,
     edge_ref,
-    early_first_ref,
-    early_second_ref,
-    first_ref,
-    second_ref,
+    early_ref,
+    late_ref,
     laid_ref,
-    out_ref,
-    held,
     rim,
-    sems,
 ):
     lines = x_ref.shape[1]
-    early = [taken_by_parity(early_first_ref, early_second_ref, slot, lines) for slot in range(3)]
-    late = [taken_by_parity(first_ref, second_ref, slot, lines) for slot in range(1 if single else 2)]
-    leaving = []
-    for side in range(2):
-        if single:
-            changes = halo_ref[5 + side] * late[0][side], late[0][side]
-        else:
-            changes = late[0][side], late[1][side]
-        sides = early[1][side] + changes[0], early[2][side] + changes[1]
-        outer = outer_rows(
-            side,
-            rows,
-            0,
-            (early[0][side], sides, halo_ref[side]),
-            halo_ref[2] if side == 0 else down_ref[rows - 1],
-            edge_ref[side],
-            *(x_ref, across_ref, down_ref, side_ref, inverse_ref, keep_ref),
-        )
-        count = SWEEPS - 1
-        base = 0 if side == 0 else rows - count
-        for row, value in outer.items():
-            rim[side, row - base] = value
-        for line in range(lines):
-            held[pl.ds(base, count), pl.ds(line * LANES, LANES)] = rim[side, :, line, :]
-        part = pl.ds(side * (rows // 2), rows // 2)
-        copy = pltpu.make_async_copy(held.at[part], out_ref.at[part], sems.at[side])
-        copy.start()
-        leaving.append(copy)
-    for copy in leaving:
-        copy.wait()
+
+    def row_of(ref, slot):
+        return ref[pl.ds(slot * lines, lines)]
+
+    if single:
+        changes = halo_ref[5 + side] * row_of(late_ref, 0), row_of(late_ref, 0)
+    else:
+        changes = row_of(late_ref, 0), row_of(late_ref, 1)
+    sides = row_of(early_ref, 1) + changes[0], row_of(early_ref, 2) + changes[1]
+    outer = outer_rows(
+        side,
+        rows,
+        0,
+        (row_of(early_ref, 0), sides, halo_ref[side]),
+        halo_ref[2] if side == 0 else down_ref[rows - 1],
+        edge_ref[side],
+        *(x_ref, across_ref, down_ref, side_ref, inverse_ref, keep_ref),
+    )
+    count = SWEEPS - 1
+    base = 0 if side == 0 else rows - count
+    for row, value in outer.items():
+        rim[row - base] = value
+    for line in range(lines):
+        laid_ref[pl.ds(base, count), pl.ds(line * LANES, LANES)] = rim[:, line, :]
+
+
+def last_far_kernel(single, rows, *refs):
+    *ins, _, out_ref, laid_ref, rim, sems = refs
+    half = rows // 2
+
+    def work(near):
+        copies = []
+        for side in (near, 1 - near):
+            if side != near:
+                rim_rows(single, rows, side, *ins, laid_ref, rim)
+            part = pl.ds(side * half, half)
+            copy = pltpu.make_async_copy(laid_ref.at[part], out_ref.at[part], sems.at[side])
+            copy.start()
+            copies.append(copy)
+        for copy in copies:
+            copy.wait()
+
+    by_parity(work)
 
 
 def call(kernel, name, ins, outs, scratch=(), aliases=None, work=None):
@@ -669,7 +714,7 @@
         messages(4 if single else 3, 1) + picks,
     )
     above, below = between_layers(sends)
-    (load,) = call(unpack_field_kernel, "unpack_loads", vmem(loads), [field])
+    (load,) = call(unpack_loads_kernel, "unpack_loads", vmem(loads, own, own_weight), [field])
     early = beside_tile((first_sent, second_sent))
     sent = call(
         functools.partial(first_edges_kernel, rows),
@@ -686,12 +731,20 @@
         [field, field, field, ("vmem", rows_of(KEPT)), ("vmem", rows_of(7 if single else 5)), ("vmem", rows_of(pick_count))],
         work,
     )
+    known = vmem(x, across, downward, side, inverse, keep, halo, own, low)
+    near_x, near_edge, near_picked = call(
+        functools.partial(first_near_kernel, single, rows),
+        "first_near",
+        known + vmem(picked, got[0], core),
+        [field, ("vmem", rows_of(2)), ("vmem", rows_of(pick_count))],
+        aliases={11: 0},
+    )
     x, edge, *sends = call(
-        functools.partial(first_outer_kernel, single, rows),
-        "first_outer",
-        vmem(x, across, downward, side, inverse, keep, halo, picked, own, low, *got, core),
+        functools.partial(first_far_kernel, single, rows),
+        "first_far",
+        known + vmem(near_picked, got[1], near_x, near_edge),
         [field, ("vmem", rows_of(2))] + picks,
-        aliases={12: 0},
+        aliases={11: 0, 12: 1},
     )
     above, below = between_layers(sends)
     sent = call(
@@ -725,20 +778,23 @@
         [field, field, ("vmem", rows_of(KEPT))],
         work,
     )
+    rim = pltpu.VMEM((SWEEPS - 1, lines, LANES), jnp.float32)
     keep, laid = call(
-        functools.partial(last_middle_kernel, rows),
+        functools.partial(last_middle_kernel, single, rows),
         "last_middle",
-        vmem(x, across, downward, side, inverse, keep, halo, *early, core),
+        vmem(x, across, downward, side, inverse, keep, halo, edge, *early, got[0], core),
         [("vmem", rows_of(KEPT)), ("vmem", (rows, cols))],
-        [pltpu.VMEM(rows_of(2), jnp.float32)],
-    )
+        [pltpu.VMEM(rows_of(2), jnp.float32), rim],
+    )
+    plane = ("vmem", (rows, cols))
+    known = vmem(x, across, downward, side, inverse, keep, halo, edge)
     volts, _ = call(
-        functools.partial(last_outer_kernel, single, rows),
-        "last_outer",
-        vmem(x, across, downward, side, inverse, keep, halo, edge, *early, *got, laid),
-        [("hbm", (rows, cols)), ("vmem", (rows, cols))],
-        [pltpu.VMEM((2, SWEEPS - 1, lines, LANES), jnp.float32), pltpu.SemaphoreType.DMA((2,))],
-        aliases={12: 1},
+        functools.partial(last_far_kernel, single, rows),
+        "last_far",
+        known + vmem(early[1], got[1], laid),
+        [("hbm", (rows, cols)), plane],
+        [rim, pltpu.SemaphoreType.DMA((2,))],
+        aliases={10: 1},
     )
     return volts[None]
 

time: 24.2 us -> 24.1 us (level)
  starting transfers between devices: 12.9 us -> 12.6 us
    ppermute x2, starting transfers between devices: 3.96 us -> 3.66 us  [between_layers(): got = move(sends[0], perm=up)]
    pallas_call x13 -> x14, Pallas kernels: 6.58 us -> 6.72 us  [call(): pl.pallas_call(kernel, out_shape=[jax.ShapeDtypeStruct(shape, *(kind or [...]
  transfers between devices with their start and end apart: 12 -> 12, of which waited for: 3 -> 3; matrix products, arithmetic and copies ran while one was open for 0% -> 0% of each run, Pallas kernels for 21% -> 23%
where the time goes in v10:
time: 24.1 us; the launch traced here: 23.8 us
  starting transfers between devices  12.6 us (52%)
  Pallas kernels  6.72 us (28%)
  waiting for transfers between devices  3.45 us (14%)
  local copies, waits for them, and re-layouts  0.89 us (4%)
    pallas_call x14, Pallas kernels, call(): pl.pallas_call(kernel, out_shape=[jax.ShapeDtypeStruct(shape, *(kind or [...  6.72 us
    ppermute x4, starting transfers between devices, beside_tile(): across_chips = move(sent[1], perm=second)  4.97 us
    ppermute x2, starting transfers between devices, between_layers(): got = move(sends[0], perm=up)  3.66 us
    ppermute x1, starting transfers between devices, local(): low = move(cells, perm=up)  2.94 us
    ppermute x2, waiting for transfers between devices, between_layers(): got = move(sends[0], perm=up)  2.17 us
    ppermute x4, waiting for transfers between devices, beside_tile(): across_chips = move(sent[1], perm=second)  1.27 us
    ppermute x4, starting transfers between devices, beside_tile(): return (move(sent[0], perm=first), across_chips)  0.95 us
    unnamed x12, local copies, waits for them, and re-layouts  0.89 us
  transfers between devices with their start and end apart: 12, of which 3 were waited for; matrix products, arithmetic and copies ran while one was open for 0% of the time, Pallas kernels for 23%

profile of v10, /device:TPU:0, one launch (start us, length us, event | category | flops | bytes accessed | tf_op | source)
XLA Modules:
  0.0 23.8 jit_solution(2164320652661918537)
XLA Ops:
  0.0 0.0 copy-start
  0.0 2.9 %collective-permute-start = (s32[64,128]{1,0:T(8,128)}, s32[64,128]{1,0:T(8,128)S(1)}, u32[]{:S(2)}, u32[]{:S(2)}) collective-permute-start(s32[64,128]{1,0:T(8,128)} %bitcast.3), channel_id=1, source_target_pairs={{0,1},{1,0},{2,3},{3,2},{4,5},{5,4},{6,7},{7,6},{8,9},{9,8},{10,11... | collective-permute-start | bytes 98312 | tf_op jit(solution)/shard_map/ppermute | solution.py:698
  2.9 0.0 copy-start.3
  2.9 0.0 copy-start.4
  2.9 0.1 collective-permute-start.1
  3.0 0.0 copy-start.5
  3.0 0.7 %copy-done.5 = f32[1,16]{1,0:T(1,128)S(1)} copy-done((f32[1,16]{1,0:T(1,128)S(1)}, f32[1,16]{1,0:T(1,128)}, u32[]{:S(2)}) %copy-start.5) | copy-done | bytes 88
  3.7 0.0 copy-done
  3.7 0.0 copy-done.3
  3.7 0.0 copy-done.4
  3.7 0.0 copy-start.1
  3.7 0.9 %unpack.1 = (f32[16,64,128]{2,1,0:T(8,128)S(1)}, f32[16,64,128]{2,1,0:T(8,128)S(1)}, s32[64,128]{1,0:T(8,128)S(1)}, f32[64,128]{1,0:T(8,128)S(1)}) custom-call(s32[1,2,16,8192]{3,2,1,0:T(8,128)S(1)} %copy-done, s32[64,128]{1,0:T(8,128)S(1)} %bitcast.4, s32[64,128]{1,0:T(8,128)S(1)} %bitcast.6, f32[8,128]{1,0:T(8,128)S(1)} %table.1.table_ref), custom_call_target="tpu_custom_call" | custom-call | flops 300000000 | bytes 300000000 | tf_op jit(solution)/shard_map/unpack/pallas_call | solution.py:633
  4.6 0.2 copy-done.1
  4.8 0.3 %unpack_volts.1.x_ref.refs_0_ = f32[16,64,128]{2,1,0:T(8,128)S(1)} custom-call(f32[1,16,8192]{2,1,0:T(8,128)S(1)} %copy-done.1, f32[16,64,128]{2,1,0:T(8,128)S(1)} %get-tuple-element.38.after_ref.across_ref.refs_1_), custom_call_target="tpu_custom_call" | custom-call | tf_op jit(solution)/shard_map/unpack_volts/pallas_call | solution.py:633
  5.1 0.0 collective-permute-done.low_ref.refs_8_
  5.1 0.0 copy-start.2
  5.1 0.1 links.1
  5.2 2.0 %collective-permute-start.2 = (f32[1,64,128]{2,1,0:T(8,128)S(1)}, f32[1,64,128]{2,1,0:T(8,128)S(1)}, u32[]{:S(2)}, u32[]{:S(2)}) collective-permute-start(f32[1,64,128]{2,1,0:T(8,128)S(1)} %get-tuple-element.42), channel_id=1, source_target_pairs={{0,1},{1,0},{2,3},{3,2},{4,5},{5,4},{6,7},{7,6},{8,9},{9,8},{10,11... | collective-permute-start | bytes 98312 | tf_op jit(solution)/shard_map/ppermute | solution.py:683
  7.2 0.0 copy-done.2
  7.2 0.3 %unpack_loads.1.loads_ref = f32[16,64,128]{2,1,0:T(8,128)S(1)} custom-call(f32[1,16,8192]{2,1,0:T(8,128)S(1)} %copy-done.2, s32[64,128]{1,0:T(8,128)S(1)} %get-tuple-element.40.own_ref.refs_7_, f32[64,128]{1,0:T(8,128)S(1)} %get-tuple-element.41.weight_ref.own_weight_ref), custom_call_target="tpu_custom_call" | custom-call | tf_op jit(solution)/shard_map/unpack_loads/pallas_call | solution.py:633
  7.6 0.1 collective-permute-start.3
  7.6 1.0 %collective-permute-start.4 = (f32[264,128]{1,0:T(8,128)S(1)}, f32[264,128]{1,0:T(8,128)S(1)}, u32[]{:S(2)}, u32[]{:S(2)}) collective-permute-start(f32[264,128]{1,0:T(8,128)S(1)} %get-tuple-element.44), channel_id=1, source_target_pairs={{0,1},{1,0},{2,4},{3,5},{4,2},{5,3},{6,8},{7,9},{8,6},{9,7},{10,12... | collective-permute-start | bytes 405512 | tf_op jit(solution)/shard_map/ppermute | solution.py:688
  8.6 0.0 collective-permute-done.1.low_count_ref
  8.6 0.6 %collective-permute-done.2.above_ref.below_ref = f32[1,64,128]{2,1,0:T(8,128)S(1)} collective-permute-done((f32[1,64,128]{2,1,0:T(8,128)S(1)}, f32[1,64,128]{2,1,0:T(8,128)S(1)}, u32[]{:S(2)}, u32[]{:S(2)}) %collective-permute-start.2) | collective-permute-done | bytes 32800 | tf_op jit(solution)/shard_map/ppermute | solution.py:683
  9.2 0.2 first_edges.1
  9.3 0.3 %collective-permute-start.5 = (f32[200,128]{1,0:T(8,128)S(1)}, f32[200,128]{1,0:T(8,128)S(1)}, u32[]{:S(2)}, u32[]{:S(2)}) collective-permute-start(f32[200,128]{1,0:T(8,128)S(1)} %get-tuple-element.51), channel_id=1, source_target_pairs={{0,2},{1,3},{2,0},{3,1},{4,6},{5,7},{6,4},{7,5},{8,10},{9,11},{10,... | collective-permute-start | bytes 307208 | tf_op jit(solution)/shard_map/ppermute | solution.py:689
  9.6 1.9 %collective-permute-start.6 = (f32[192,128]{1,0:T(8,128)S(1)}, f32[192,128]{1,0:T(8,128)S(1)}, u32[]{:S(2)}, u32[]{:S(2)}) collective-permute-start(f32[192,128]{1,0:T(8,128)S(1)} %get-tuple-element.45.after_ref), channel_id=1, source_target_pairs={{0,1},{1,0},{2,4},{3,5},{4,2},{5,3},{6,8},{7,9},{8,6},{9,7},{10,12... | collective-permute-start | bytes 294920 | tf_op jit(solution)/shard_map/ppermute | solution.py:688
  11.5 0.0 collective-permute-done.3.first_ref
  11.5 1.3 %collective-permute-done.4.second_ref = f32[264,128]{1,0:T(8,128)S(1)} collective-permute-done((f32[264,128]{1,0:T(8,128)S(1)}, f32[264,128]{1,0:T(8,128)S(1)}, u32[]{:S(2)}, u32[]{:S(2)}) %collective-permute-start.4) | collective-permute-done | bytes 135200 | tf_op jit(solution)/shard_map/ppermute | solution.py:688
  12.7 1.5 %first_inner.1 = (f32[16,64,128]{2,1,0:T(8,128)S(1)}, f32[16,64,128]{2,1,0:T(8,128)S(1)}, f32[16,64,128]{2,1,0:T(8,128)S(1)}, f32[12,64,128]{2,1,0:T(8,128)S(1)}...) custom-call(f32[16,64,128]{2,1,0:T(8,128)S(1)} %unpack_volts.1.x_ref.refs_0_, ...), custom_call_target="tpu_custom_call" | custom-call | tf_op jit(solution)/shard_map/first_inner/pallas_call | solution.py:633
  14.2 0.0 collective-permute-done.5.refs_10_
  14.2 0.3 %first_near.1 = (f32[16,64,128]{2,1,0:T(8,128)S(1)}, f32[2,64,128]{2,1,0:T(8,128)S(1)}, f32[1,64,128]{2,1,0:T(8,128)S(1)}) custom-call(f32[16,64,128]{2,1,0:T(8,128)S(1)} %unpack_volts.1.x_ref.refs_0_, f32[16,64,128]{2,1,0:T(8,128)S(1)} %get-tuple-element.38.after_ref.across_ref.refs_1_, ...), custom_call_target="tpu_custom_call", output_to_operand_aliasing={{0}: (11, {})} | custom-call | tf_op jit(solution)/shard_map/first_near/pallas_call | solution.py:633
  14.5 0.0 collective-permute-done.6.refs_10_
  14.5 0.3 %first_far.1 = (f32[16,64,128]{2,1,0:T(8,128)S(1)}, f32[2,64,128]{2,1,0:T(8,128)S(1)}, f32[1,64,128]{2,1,0:T(8,128)S(1)}) custom-call(f32[16,64,128]{2,1,0:T(8,128)S(1)} %unpack_volts.1.x_ref.refs_0_, f32[16,64,128]{2,1,0:T(8,128)S(1)} %get-tuple-element.38.after_ref.across_ref.refs_1_, ...), custom_call_target="tpu_custom_call", output_to_operand_aliasing={{0}: (11, {}), {1}: (12, {})} | custom-call | tf_op jit(solution)/shard_map/first_far/pallas_call | solution.py:633
  14.8 1.6 %collective-permute-start.7 = (f32[1,64,128]{2,1,0:T(8,128)S(1)}, f32[1,64,128]{2,1,0:T(8,128)S(1)}, u32[]{:S(2)}, u32[]{:S(2)}) collective-permute-start(f32[1,64,128]{2,1,0:T(8,128)S(1)} %get-tuple-element.57.after_ref), channel_id=1, source_target_pairs={{0,1},{1,0},{2,3},{3,2},{4,5},{5,4},{6,7},{7,6},{8,9},{9,8},{10,11... | collective-permute-start | bytes 98312 | tf_op jit(solution)/shard_map/ppermute | solution.py:683
  16.4 0.1 next_early.1
  16.5 0.1 collective-permute-start.8
  16.6 0.5 %collective-permute-start.9 = (f32[200,128]{1,0:T(8,128)S(1)}, f32[200,128]{1,0:T(8,128)S(1)}, u32[]{:S(2)}, u32[]{:S(2)}) collective-permute-start(f32[200,128]{1,0:T(8,128)S(1)} %get-tuple-element.65), channel_id=1, source_target_pairs={{0,1},{1,0},{2,4},{3,5},{4,2},{5,3},{6,8},{7,9},{8,6},{9,7},{10,12... | collective-permute-start | bytes 307208 | tf_op jit(solution)/shard_map/ppermute | solution.py:688
  17.1 1.6 %collective-permute-done.7.volts_ref.above_ref.below_ref = f32[1,64,128]{2,1,0:T(8,128)S(1)} collective-permute-done((f32[1,64,128]{2,1,0:T(8,128)S(1)}, f32[1,64,128]{2,1,0:T(8,128)S(1)}, u32[]{:S(2)}, u32[]{:S(2)}) %collective-permute-start.7) | collective-permute-done | bytes 32800 | tf_op jit(solution)/shard_map/ppermute | solution.py:683
  18.7 1.6 %collective-permute-start.11 = (f32[72,128]{1,0:T(8,128)S(1)}, f32[72,128]{1,0:T(8,128)S(1)}, u32[]{:S(2)}, u32[]{:S(2)}) collective-permute-start(f32[72,128]{1,0:T(8,128)S(1)} %get-tuple-element.60.after_ref), channel_id=1, source_target_pairs={{0,1},{1,0},{2,4},{3,5},{4,2},{5,3},{6,8},{7,9},{8,6},{9,7},{10,12... | collective-permute-start | bytes 110600 | tf_op jit(solution)/shard_map/ppermute | solution.py:688
  20.4 0.6 %collective-permute-start.10 = (f32[64,128]{1,0:T(8,128)S(1)}, f32[64,128]{1,0:T(8,128)S(1)}, u32[]{:S(2)}, u32[]{:S(2)}) collective-permute-start(f32[64,128]{1,0:T(8,128)S(1)} %get-tuple-element.66), channel_id=1, source_target_pairs={{0,2},{1,3},{2,0},{3,1},{4,6},{5,7},{6,4},{7,5},{8,10},{9,11},{10,... | collective-permute-start | bytes 98312 | tf_op jit(solution)/shard_map/ppermute | solution.py:689
  20.9 1.0 %last_inner.1 = (f32[16,64,128]{2,1,0:T(8,128)S(1)}, f32[16,64,128]{2,1,0:T(8,128)S(1)}, f32[12,64,128]{2,1,0:T(8,128)S(1)}) custom-call(f32[16,64,128]{2,1,0:T(8,128)S(1)} %get-tuple-element.56.x_ref.refs_0_, f32[16,64,128]{2,1,0:T(8,128)S(1)} %get-tuple-element.38.after_ref.across_ref.refs_1_, f32[16,64,128]{2,1,0:T(8,128)S(1)} %get-tuple-element.39.down_ref.refs_2_, ...), custom_call_target="tpu_custom_call" | custom-call | tf_op jit(solution)/shard_map/last_inner/pallas_call | solution.py:633
  21.9 0.0 collective-permute-done.10.late_ref
  22.0 0.0 collective-permute-done.8.first_ref
  22.0 0.0 collective-permute-done.9.second_ref.refs_8_
  22.0 0.8 %last_middle.1 = (f32[12,64,128]{2,1,0:T(8,128)S(1)}, f32[16,8192]{1,0:T(8,128)S(1)}) custom-call(f32[16,64,128]{2,1,0:T(8,128)S(1)} %get-tuple-element.56.x_ref.refs_0_, f32[16,64,128]{2,1,0:T(8,128)S(1)} %get-tuple-element.38.after_ref.across_ref.refs_1_, f32[16,64,128]{2,1,0:T(8,128)S(1)} %get-tuple-element.39.down_ref.refs_2_, ...), custom_call_target="tpu_custom_call" | custom-call | tf_op jit(solution)/shard_map/last_middle/pallas_call | solution.py:633
  22.8 0.0 collective-permute-done.11.refs_9_
  22.8 1.0 %last_far.1 = (f32[16,8192]{1,0:T(8,128)}, f32[16,8192]{1,0:T(8,128)S(1)}) custom-call(f32[16,64,128]{2,1,0:T(8,128)S(1)} %get-tuple-element.56.x_ref.refs_0_, f32[16,64,128]{2,1,0:T(8,128)S(1)} %get-tuple-element.38.after_ref.across_ref.refs_1_, f32[16,64,128]{2,1,0:T(8,128)S(1)} %get-tuple-element.39.down_ref.refs_2_, ...), custom_call_target="tpu_custom_call", output_to_operand_aliasing={{1}: (10, {})} | custom-call | tf_op jit(solution)/shard_map/last_far/pallas_call | solution.py:633
  (2 shorter events, 0.0 us)
Async XLA Ops:
  0.0 3.7 %copy-start = (s32[1,2,16,8192]{3,2,1,0:T(8,128)S(1)}, s32[1,2,16,8192]{3,2,1,0:T(8,128)}, u32[]{:S(2)}) copy-start(s32[1,2,16,8192]{3,2,1,0:T(8,128)} %index_ref.1) | copy-start | bytes 3145732
  0.0 5.1 %collective-permute-start = (s32[64,128]{1,0:T(8,128)}, s32[64,128]{1,0:T(8,128)S(1)}, u32[]{:S(2)}, u32[]{:S(2)}) collective-permute-start(s32[64,128]{1,0:T(8,128)} %bitcast.3), channel_id=1, source_target_pairs={{0,1},{1,0},{2,3},{3,2},{4,5},{5,4},{6,7},{7,6},{8,9},{9,8},{10,11... | collective-permute-start | bytes 98312 | tf_op jit(solution)/shard_map/ppermute | solution.py:698
  2.9 0.8 %copy-start.3 = (s32[1,8192]{1,0:T(1,128)S(1)}, s32[1,8192]{1,0:T(1,128)}, u32[]{:S(2)}) copy-start(s32[1,8192]{1,0:T(1,128)} %param.10) | copy-start | bytes 98308
  2.9 0.8 %copy-start.4 = (s32[1,8192]{1,0:T(1,128)S(1)}, s32[1,8192]{1,0:T(1,128)}, u32[]{:S(2)}) copy-start(s32[1,8192]{1,0:T(1,128)} %param.11) | copy-start | bytes 98308
  2.9 5.7 %collective-permute-start.1 = (s32[64,128]{1,0:T(8,128)}, s32[64,128]{1,0:T(8,128)S(1)}, u32[]{:S(2)}, u32[]{:S(2)}) collective-permute-start(s32[64,128]{1,0:T(8,128)} %bitcast.5), channel_id=1, source_target_pairs={{0,1},{1,0},{2,3},{3,2},{4,5},{5,4},{6,7},{7,6},{8,9},{9,8},{10,11... | collective-permute-start | bytes 98312 | tf_op jit(solution)/shard_map/ppermute | solution.py:699
  3.0 0.7 %copy-start.5 = (f32[1,16]{1,0:T(1,128)S(1)}, f32[1,16]{1,0:T(1,128)}, u32[]{:S(2)}) copy-start(f32[1,16]{1,0:T(1,128)} %class_ref.1) | copy-start | bytes 196
  3.7 1.0 %copy-start.1 = (f32[1,16,8192]{2,1,0:T(8,128)S(1)}, f32[1,16,8192]{2,1,0:T(8,128)}, u32[]{:S(2)}) copy-start(f32[1,16,8192]{2,1,0:T(8,128)} %volts_ref.1) | copy-start | bytes 1572868
  5.1 2.1 %copy-start.2 = (f32[1,16,8192]{2,1,0:T(8,128)S(1)}, f32[1,16,8192]{2,1,0:T(8,128)}, u32[]{:S(2)}) copy-start(f32[1,16,8192]{2,1,0:T(8,128)} %loads_ref.1) | copy-start | bytes 1572868
  5.2 4.0 %collective-permute-start.2 = (f32[1,64,128]{2,1,0:T(8,128)S(1)}, f32[1,64,128]{2,1,0:T(8,128)S(1)}, u32[]{:S(2)}, u32[]{:S(2)}) collective-permute-start(f32[1,64,128]{2,1,0:T(8,128)S(1)} %get-tuple-element.42), channel_id=1, source_target_pairs={{0,1},{1,0},{2,3},{3,2},{4,5},{5,4},{6,7},{7,6},{8,9},{9,8},{10,11... | collective-permute-start | bytes 98312 | tf_op jit(solution)/shard_map/ppermute | solution.py:683
  7.6 3.9 %collective-permute-start.3 = (f32[256,128]{1,0:T(8,128)S(1)}, f32[256,128]{1,0:T(8,128)S(1)}, u32[]{:S(2)}, u32[]{:S(2)}) collective-permute-start(f32[256,128]{1,0:T(8,128)S(1)} %get-tuple-element.43), channel_id=1, source_target_pairs={{0,2},{1,3},{2,0},{3,1},{4,6},{5,7},{6,4},{7,5},{8,10},{9,11},{10,... | collective-permute-start | bytes 393224 | tf_op jit(solution)/shard_map/ppermute | solution.py:689
  7.6 5.1 %collective-permute-start.4 = (f32[264,128]{1,0:T(8,128)S(1)}, f32[264,128]{1,0:T(8,128)S(1)}, u32[]{:S(2)}, u32[]{:S(2)}) collective-permute-start(f32[264,128]{1,0:T(8,128)S(1)} %get-tuple-element.44), channel_id=1, source_target_pairs={{0,1},{1,0},{2,4},{3,5},{4,2},{5,3},{6,8},{7,9},{8,6},{9,7},{10,12... | collective-permute-start | bytes 405512 | tf_op jit(solution)/shard_map/ppermute | solution.py:688
  9.3 4.9 %collective-permute-start.5 = (f32[200,128]{1,0:T(8,128)S(1)}, f32[200,128]{1,0:T(8,128)S(1)}, u32[]{:S(2)}, u32[]{:S(2)}) collective-permute-start(f32[200,128]{1,0:T(8,128)S(1)} %get-tuple-element.51), channel_id=1, source_target_pairs={{0,2},{1,3},{2,0},{3,1},{4,6},{5,7},{6,4},{7,5},{8,10},{9,11},{10,... | collective-permute-start | bytes 307208 | tf_op jit(solution)/shard_map/ppermute | solution.py:689
  9.6 4.9 %collective-permute-start.6 = (f32[192,128]{1,0:T(8,128)S(1)}, f32[192,128]{1,0:T(8,128)S(1)}, u32[]{:S(2)}, u32[]{:S(2)}) collective-permute-start(f32[192,128]{1,0:T(8,128)S(1)} %get-tuple-element.45.after_ref), channel_id=1, source_target_pairs={{0,1},{1,0},{2,4},{3,5},{4,2},{5,3},{6,8},{7,9},{8,6},{9,7},{10,12... | collective-permute-start | bytes 294920 | tf_op jit(solution)/shard_map/ppermute | solution.py:688
  14.8 4.0 %collective-permute-start.7 = (f32[1,64,128]{2,1,0:T(8,128)S(1)}, f32[1,64,128]{2,1,0:T(8,128)S(1)}, u32[]{:S(2)}, u32[]{:S(2)}) collective-permute-start(f32[1,64,128]{2,1,0:T(8,128)S(1)} %get-tuple-element.57.after_ref), channel_id=1, source_target_pairs={{0,1},{1,0},{2,3},{3,2},{4,5},{5,4},{6,7},{7,6},{8,9},{9,8},{10,11... | collective-permute-start | bytes 98312 | tf_op jit(solution)/shard_map/ppermute | solution.py:683
  16.5 5.5 %collective-permute-start.8 = (f32[192,128]{1,0:T(8,128)S(1)}, f32[192,128]{1,0:T(8,128)S(1)}, u32[]{:S(2)}, u32[]{:S(2)}) collective-permute-start(f32[192,128]{1,0:T(8,128)S(1)} %get-tuple-element.64), channel_id=1, source_target_pairs={{0,2},{1,3},{2,0},{3,1},{4,6},{5,7},{6,4},{7,5},{8,10},{9,11},{10,... | collective-permute-start | bytes 294920 | tf_op jit(solution)/shard_map/ppermute | solution.py:689
  16.6 5.4 %collective-permute-start.9 = (f32[200,128]{1,0:T(8,128)S(1)}, f32[200,128]{1,0:T(8,128)S(1)}, u32[]{:S(2)}, u32[]{:S(2)}) collective-permute-start(f32[200,128]{1,0:T(8,128)S(1)} %get-tuple-element.65), channel_id=1, source_target_pairs={{0,1},{1,0},{2,4},{3,5},{4,2},{5,3},{6,8},{7,9},{8,6},{9,7},{10,12... | collective-permute-start | bytes 307208 | tf_op jit(solution)/shard_map/ppermute | solution.py:688
  18.7 4.1 %collective-permute-start.11 = (f32[72,128]{1,0:T(8,128)S(1)}, f32[72,128]{1,0:T(8,128)S(1)}, u32[]{:S(2)}, u32[]{:S(2)}) collective-permute-start(f32[72,128]{1,0:T(8,128)S(1)} %get-tuple-element.60.after_ref), channel_id=1, source_target_pairs={{0,1},{1,0},{2,4},{3,5},{4,2},{5,3},{6,8},{7,9},{8,6},{9,7},{10,12... | collective-permute-start | bytes 110600 | tf_op jit(solution)/shard_map/ppermute | solution.py:688
  20.4 1.6 %collective-permute-start.10 = (f32[64,128]{1,0:T(8,128)S(1)}, f32[64,128]{1,0:T(8,128)S(1)}, u32[]{:S(2)}, u32[]{:S(2)}) collective-permute-start(f32[64,128]{1,0:T(8,128)S(1)} %get-tuple-element.66), channel_id=1, source_target_pairs={{0,2},{1,3},{2,0},{3,1},{4,6},{5,7},{6,4},{7,5},{8,10},{9,11},{10,... | collective-permute-start | bytes 98312 | tf_op jit(solution)/shard_map/ppermute | solution.py:689

commit v11 on v10

--- a/solution.py
+++ b/solution.py
@@ -751,7 +751,7 @@
         functools.partial(next_early_kernel, single, rows),
         "next_early",
         vmem(x, across, downward, load, inverse, *vias) + [("any", sends[0])],
-        messages(3, 1) + [("vmem", cells.shape)] * (2 if single else 0),
+        messages(3, 0) + [("vmem", cells.shape)] * (2 if single else 0),
     )
     early = beside_tile(sent[:2])
     if single:

time: 24.1 us -> 24.1 us (level)
  waiting for transfers between devices: 3.45 us -> 2.84 us
  starting transfers between devices: 12.6 us -> 13.2 us
    ppermute x4, starting transfers between devices: 0.95 us -> 1.58 us  [beside_tile(): return (move(sent[0], perm=first), across_chips)]
    ppermute x2, waiting for transfers between devices: 2.17 us -> 1.55 us  [between_layers(): got = move(sends[0], perm=up)]
where the time goes in v11:
time: 24.1 us; the launch traced here: 23.8 us
  starting transfers between devices  13.2 us (55%)
  Pallas kernels  6.72 us (28%)
  waiting for transfers between devices  2.84 us (12%)
  local copies, waits for them, and re-layouts  0.89 us (4%)
    pallas_call x14, Pallas kernels, call(): pl.pallas_call(kernel, out_shape=[jax.ShapeDtypeStruct(shape, *(kind or [...  6.72 us
    ppermute x4, starting transfers between devices, beside_tile(): across_chips = move(sent[1], perm=second)  4.97 us
    ppermute x2, starting transfers between devices, between_layers(): got = move(sends[0], perm=up)  3.66 us
    ppermute x1, starting transfers between devices, local(): low = move(cells, perm=up)  2.94 us
    ppermute x4, starting transfers between devices, beside_tile(): return (move(sent[0], perm=first), across_chips)  1.58 us
    ppermute x2, waiting for transfers between devices, between_layers(): got = move(sends[0], perm=up)  1.55 us
    ppermute x4, waiting for transfers between devices, beside_tile(): across_chips = move(sent[1], perm=second)  1.27 us
    unnamed x12, local copies, waits for them, and re-layouts  0.89 us
  transfers between devices with their start and end apart: 12, of which 3 were waited for; matrix products, arithmetic and copies ran while one was open for 0% of the time, Pallas kernels for 23%

profile of v11, /device:TPU:0, one launch (start us, length us, event | category | flops | bytes accessed | tf_op | source)
XLA Modules:
  0.0 23.8 jit_solution(1555110779207161946)
XLA Ops:
  0.0 0.0 copy-start
  0.0 2.9 %collective-permute-start = (s32[64,128]{1,0:T(8,128)}, s32[64,128]{1,0:T(8,128)S(1)}, u32[]{:S(2)}, u32[]{:S(2)}) collective-permute-start(s32[64,128]{1,0:T(8,128)} %bitcast.3), channel_id=1, source_target_pairs={{0,1},{1,0},{2,3},{3,2},{4,5},{5,4},{6,7},{7,6},{8,9},{9,8},{10,11... | collective-permute-start | bytes 98312 | tf_op jit(solution)/shard_map/ppermute | solution.py:698
  2.9 0.0 copy-start.3
  2.9 0.0 copy-start.4
  2.9 0.1 collective-permute-start.1
  3.0 0.0 copy-start.5
  3.0 0.7 %copy-done.5 = f32[1,16]{1,0:T(1,128)S(1)} copy-done((f32[1,16]{1,0:T(1,128)S(1)}, f32[1,16]{1,0:T(1,128)}, u32[]{:S(2)}) %copy-start.5) | copy-done | bytes 88
  3.7 0.0 copy-done
  3.7 0.0 copy-done.3
  3.7 0.0 copy-done.4
  3.7 0.0 copy-start.1
  3.7 0.9 %unpack.1 = (f32[16,64,128]{2,1,0:T(8,128)S(1)}, f32[16,64,128]{2,1,0:T(8,128)S(1)}, s32[64,128]{1,0:T(8,128)S(1)}, f32[64,128]{1,0:T(8,128)S(1)}) custom-call(s32[1,2,16,8192]{3,2,1,0:T(8,128)S(1)} %copy-done, s32[64,128]{1,0:T(8,128)S(1)} %bitcast.4, s32[64,128]{1,0:T(8,128)S(1)} %bitcast.6, f32[8,128]{1,0:T(8,128)S(1)} %table.1.table_ref), custom_call_target="tpu_custom_call" | custom-call | flops 300000000 | bytes 300000000 | tf_op jit(solution)/shard_map/unpack/pallas_call | solution.py:633
  4.6 0.2 copy-done.1
  4.8 0.3 %unpack_volts.1.x_ref.refs_0_ = f32[16,64,128]{2,1,0:T(8,128)S(1)} custom-call(f32[1,16,8192]{2,1,0:T(8,128)S(1)} %copy-done.1, f32[16,64,128]{2,1,0:T(8,128)S(1)} %get-tuple-element.38.after_ref.across_ref.refs_1_), custom_call_target="tpu_custom_call" | custom-call | tf_op jit(solution)/shard_map/unpack_volts/pallas_call | solution.py:633
  5.1 0.0 collective-permute-done.low_ref.refs_8_
  5.1 0.0 copy-start.2
  5.1 0.1 links.1
  5.2 2.0 %collective-permute-start.2 = (f32[1,64,128]{2,1,0:T(8,128)S(1)}, f32[1,64,128]{2,1,0:T(8,128)S(1)}, u32[]{:S(2)}, u32[]{:S(2)}) collective-permute-start(f32[1,64,128]{2,1,0:T(8,128)S(1)} %get-tuple-element.42), channel_id=1, source_target_pairs={{0,1},{1,0},{2,3},{3,2},{4,5},{5,4},{6,7},{7,6},{8,9},{9,8},{10,11... | collective-permute-start | bytes 98312 | tf_op jit(solution)/shard_map/ppermute | solution.py:683
  7.2 0.0 copy-done.2
  7.2 0.3 %unpack_loads.1.loads_ref = f32[16,64,128]{2,1,0:T(8,128)S(1)} custom-call(f32[1,16,8192]{2,1,0:T(8,128)S(1)} %copy-done.2, s32[64,128]{1,0:T(8,128)S(1)} %get-tuple-element.40.own_ref.refs_7_, f32[64,128]{1,0:T(8,128)S(1)} %get-tuple-element.41.weight_ref.own_weight_ref), custom_call_target="tpu_custom_call" | custom-call | tf_op jit(solution)/shard_map/unpack_loads/pallas_call | solution.py:633
  7.6 0.1 collective-permute-start.3
  7.6 1.0 %collective-permute-start.4 = (f32[264,128]{1,0:T(8,128)S(1)}, f32[264,128]{1,0:T(8,128)S(1)}, u32[]{:S(2)}, u32[]{:S(2)}) collective-permute-start(f32[264,128]{1,0:T(8,128)S(1)} %get-tuple-element.44), channel_id=1, source_target_pairs={{0,1},{1,0},{2,4},{3,5},{4,2},{5,3},{6,8},{7,9},{8,6},{9,7},{10,12... | collective-permute-start | bytes 405512 | tf_op jit(solution)/shard_map/ppermute | solution.py:688
  8.6 0.0 collective-permute-done.1.low_count_ref
  8.6 0.6 %collective-permute-done.2.above_ref.below_ref = f32[1,64,128]{2,1,0:T(8,128)S(1)} collective-permute-done((f32[1,64,128]{2,1,0:T(8,128)S(1)}, f32[1,64,128]{2,1,0:T(8,128)S(1)}, u32[]{:S(2)}, u32[]{:S(2)}) %collective-permute-start.2) | collective-permute-done | bytes 32800 | tf_op jit(solution)/shard_map/ppermute | solution.py:683
  9.2 0.2 first_edges.1
  9.3 0.3 %collective-permute-start.5 = (f32[200,128]{1,0:T(8,128)S(1)}, f32[200,128]{1,0:T(8,128)S(1)}, u32[]{:S(2)}, u32[]{:S(2)}) collective-permute-start(f32[200,128]{1,0:T(8,128)S(1)} %get-tuple-element.51), channel_id=1, source_target_pairs={{0,2},{1,3},{2,0},{3,1},{4,6},{5,7},{6,4},{7,5},{8,10},{9,11},{10,... | collective-permute-start | bytes 307208 | tf_op jit(solution)/shard_map/ppermute | solution.py:689
  9.6 1.9 %collective-permute-start.6 = (f32[192,128]{1,0:T(8,128)S(1)}, f32[192,128]{1,0:T(8,128)S(1)}, u32[]{:S(2)}, u32[]{:S(2)}) collective-permute-start(f32[192,128]{1,0:T(8,128)S(1)} %get-tuple-element.45.after_ref), channel_id=1, source_target_pairs={{0,1},{1,0},{2,4},{3,5},{4,2},{5,3},{6,8},{7,9},{8,6},{9,7},{10,12... | collective-permute-start | bytes 294920 | tf_op jit(solution)/shard_map/ppermute | solution.py:688
  11.5 0.0 collective-permute-done.3.first_ref
  11.5 1.3 %collective-permute-done.4.second_ref = f32[264,128]{1,0:T(8,128)S(1)} collective-permute-done((f32[264,128]{1,0:T(8,128)S(1)}, f32[264,128]{1,0:T(8,128)S(1)}, u32[]{:S(2)}, u32[]{:S(2)}) %collective-permute-start.4) | collective-permute-done | bytes 135200 | tf_op jit(solution)/shard_map/ppermute | solution.py:688
  12.7 1.5 %first_inner.1 = (f32[16,64,128]{2,1,0:T(8,128)S(1)}, f32[16,64,128]{2,1,0:T(8,128)S(1)}, f32[16,64,128]{2,1,0:T(8,128)S(1)}, f32[12,64,128]{2,1,0:T(8,128)S(1)}...) custom-call(f32[16,64,128]{2,1,0:T(8,128)S(1)} %unpack_volts.1.x_ref.refs_0_, ...), custom_call_target="tpu_custom_call" | custom-call | tf_op jit(solution)/shard_map/first_inner/pallas_call | solution.py:633
  14.2 0.0 collective-permute-done.5.refs_10_
  14.2 0.3 %first_near.1 = (f32[16,64,128]{2,1,0:T(8,128)S(1)}, f32[2,64,128]{2,1,0:T(8,128)S(1)}, f32[1,64,128]{2,1,0:T(8,128)S(1)}) custom-call(f32[16,64,128]{2,1,0:T(8,128)S(1)} %unpack_volts.1.x_ref.refs_0_, f32[16,64,128]{2,1,0:T(8,128)S(1)} %get-tuple-element.38.after_ref.across_ref.refs_1_, ...), custom_call_target="tpu_custom_call", output_to_operand_aliasing={{0}: (11, {})} | custom-call | tf_op jit(solution)/shard_map/first_near/pallas_call | solution.py:633
  14.5 0.0 collective-permute-done.6.refs_10_
  14.5 0.3 %first_far.1 = (f32[16,64,128]{2,1,0:T(8,128)S(1)}, f32[2,64,128]{2,1,0:T(8,128)S(1)}, f32[1,64,128]{2,1,0:T(8,128)S(1)}) custom-call(f32[16,64,128]{2,1,0:T(8,128)S(1)} %unpack_volts.1.x_ref.refs_0_, f32[16,64,128]{2,1,0:T(8,128)S(1)} %get-tuple-element.38.after_ref.across_ref.refs_1_, ...), custom_call_target="tpu_custom_call", output_to_operand_aliasing={{0}: (11, {}), {1}: (12, {})} | custom-call | tf_op jit(solution)/shard_map/first_far/pallas_call | solution.py:633
  14.8 1.6 %collective-permute-start.7 = (f32[1,64,128]{2,1,0:T(8,128)S(1)}, f32[1,64,128]{2,1,0:T(8,128)S(1)}, u32[]{:S(2)}, u32[]{:S(2)}) collective-permute-start(f32[1,64,128]{2,1,0:T(8,128)S(1)} %get-tuple-element.57.after_ref), channel_id=1, source_target_pairs={{0,1},{1,0},{2,3},{3,2},{4,5},{5,4},{6,7},{7,6},{8,9},{9,8},{10,11... | collective-permute-start | bytes 98312 | tf_op jit(solution)/shard_map/ppermute | solution.py:683
  16.4 0.1 next_early.1
  16.5 0.5 %collective-permute-start.9 = (f32[192,128]{1,0:T(8,128)S(1)}, f32[192,128]{1,0:T(8,128)S(1)}, u32[]{:S(2)}, u32[]{:S(2)}) collective-permute-start(f32[192,128]{1,0:T(8,128)S(1)} %get-tuple-element.65), channel_id=1, source_target_pairs={{0,1},{1,0},{2,4},{3,5},{4,2},{5,3},{6,8},{7,9},{8,6},{9,7},{10,12... | collective-permute-start | bytes 294920 | tf_op jit(solution)/shard_map/ppermute | solution.py:688
  17.0 0.7 %collective-permute-start.8 = (f32[200,128]{1,0:T(8,128)S(1)}, f32[200,128]{1,0:T(8,128)S(1)}, u32[]{:S(2)}, u32[]{:S(2)}) collective-permute-start(f32[200,128]{1,0:T(8,128)S(1)} %get-tuple-element.64), channel_id=1, source_target_pairs={{0,2},{1,3},{2,0},{3,1},{4,6},{5,7},{6,4},{7,5},{8,10},{9,11},{10,... | collective-permute-start | bytes 307208 | tf_op jit(solution)/shard_map/ppermute | solution.py:689
  17.7 1.0 %collective-permute-done.7.volts_ref.above_ref.below_ref = f32[1,64,128]{2,1,0:T(8,128)S(1)} collective-permute-done((f32[1,64,128]{2,1,0:T(8,128)S(1)}, f32[1,64,128]{2,1,0:T(8,128)S(1)}, u32[]{:S(2)}, u32[]{:S(2)}) %collective-permute-start.7) | collective-permute-done | bytes 32800 | tf_op jit(solution)/shard_map/ppermute | solution.py:683
  18.7 1.6 %collective-permute-start.11 = (f32[72,128]{1,0:T(8,128)S(1)}, f32[72,128]{1,0:T(8,128)S(1)}, u32[]{:S(2)}, u32[]{:S(2)}) collective-permute-start(f32[72,128]{1,0:T(8,128)S(1)} %get-tuple-element.60.after_ref), channel_id=1, source_target_pairs={{0,1},{1,0},{2,4},{3,5},{4,2},{5,3},{6,8},{7,9},{8,6},{9,7},{10,12... | collective-permute-start | bytes 110600 | tf_op jit(solution)/shard_map/ppermute | solution.py:688
  20.4 0.6 %collective-permute-start.10 = (f32[64,128]{1,0:T(8,128)S(1)}, f32[64,128]{1,0:T(8,128)S(1)}, u32[]{:S(2)}, u32[]{:S(2)}) collective-permute-start(f32[64,128]{1,0:T(8,128)S(1)} %get-tuple-element.66), channel_id=1, source_target_pairs={{0,2},{1,3},{2,0},{3,1},{4,6},{5,7},{6,4},{7,5},{8,10},{9,11},{10,... | collective-permute-start | bytes 98312 | tf_op jit(solution)/shard_map/ppermute | solution.py:689
  20.9 1.0 %last_inner.1 = (f32[16,64,128]{2,1,0:T(8,128)S(1)}, f32[16,64,128]{2,1,0:T(8,128)S(1)}, f32[12,64,128]{2,1,0:T(8,128)S(1)}) custom-call(f32[16,64,128]{2,1,0:T(8,128)S(1)} %get-tuple-element.56.x_ref.refs_0_, f32[16,64,128]{2,1,0:T(8,128)S(1)} %get-tuple-element.38.after_ref.across_ref.refs_1_, f32[16,64,128]{2,1,0:T(8,128)S(1)} %get-tuple-element.39.down_ref.refs_2_, ...), custom_call_target="tpu_custom_call" | custom-call | tf_op jit(solution)/shard_map/last_inner/pallas_call | solution.py:633
  21.9 0.0 collective-permute-done.10.late_ref
  22.0 0.0 collective-permute-done.9.second_ref.refs_8_
  22.0 0.0 collective-permute-done.8.first_ref
  22.0 0.8 %last_middle.1 = (f32[12,64,128]{2,1,0:T(8,128)S(1)}, f32[16,8192]{1,0:T(8,128)S(1)}) custom-call(f32[16,64,128]{2,1,0:T(8,128)S(1)} %get-tuple-element.56.x_ref.refs_0_, f32[16,64,128]{2,1,0:T(8,128)S(1)} %get-tuple-element.38.after_ref.across_ref.refs_1_, f32[16,64,128]{2,1,0:T(8,128)S(1)} %get-tuple-element.39.down_ref.refs_2_, ...), custom_call_target="tpu_custom_call" | custom-call | tf_op jit(solution)/shard_map/last_middle/pallas_call | solution.py:633
  22.8 0.0 collective-permute-done.11.refs_9_
  22.8 1.0 %last_far.1 = (f32[16,8192]{1,0:T(8,128)}, f32[16,8192]{1,0:T(8,128)S(1)}) custom-call(f32[16,64,128]{2,1,0:T(8,128)S(1)} %get-tuple-element.56.x_ref.refs_0_, f32[16,64,128]{2,1,0:T(8,128)S(1)} %get-tuple-element.38.after_ref.across_ref.refs_1_, f32[16,64,128]{2,1,0:T(8,128)S(1)} %get-tuple-element.39.down_ref.refs_2_, ...), custom_call_target="tpu_custom_call", output_to_operand_aliasing={{1}: (10, {})} | custom-call | tf_op jit(solution)/shard_map/last_far/pallas_call | solution.py:633
  (2 shorter events, 0.0 us)
Async XLA Ops:
  0.0 3.7 %copy-start = (s32[1,2,16,8192]{3,2,1,0:T(8,128)S(1)}, s32[1,2,16,8192]{3,2,1,0:T(8,128)}, u32[]{:S(2)}) copy-start(s32[1,2,16,8192]{3,2,1,0:T(8,128)} %index_ref.1) | copy-start | bytes 3145732
  0.0 5.1 %collective-permute-start = (s32[64,128]{1,0:T(8,128)}, s32[64,128]{1,0:T(8,128)S(1)}, u32[]{:S(2)}, u32[]{:S(2)}) collective-permute-start(s32[64,128]{1,0:T(8,128)} %bitcast.3), channel_id=1, source_target_pairs={{0,1},{1,0},{2,3},{3,2},{4,5},{5,4},{6,7},{7,6},{8,9},{9,8},{10,11... | collective-permute-start | bytes 98312 | tf_op jit(solution)/shard_map/ppermute | solution.py:698
  2.9 0.8 %copy-start.3 = (s32[1,8192]{1,0:T(1,128)S(1)}, s32[1,8192]{1,0:T(1,128)}, u32[]{:S(2)}) copy-start(s32[1,8192]{1,0:T(1,128)} %param.10) | copy-start | bytes 98308
  2.9 0.8 %copy-start.4 = (s32[1,8192]{1,0:T(1,128)S(1)}, s32[1,8192]{1,0:T(1,128)}, u32[]{:S(2)}) copy-start(s32[1,8192]{1,0:T(1,128)} %param.11) | copy-start | bytes 98308
  2.9 5.7 %collective-permute-start.1 = (s32[64,128]{1,0:T(8,128)}, s32[64,128]{1,0:T(8,128)S(1)}, u32[]{:S(2)}, u32[]{:S(2)}) collective-permute-start(s32[64,128]{1,0:T(8,128)} %bitcast.5), channel_id=1, source_target_pairs={{0,1},{1,0},{2,3},{3,2},{4,5},{5,4},{6,7},{7,6},{8,9},{9,8},{10,11... | collective-permute-start | bytes 98312 | tf_op jit(solution)/shard_map/ppermute | solution.py:699
  3.0 0.7 %copy-start.5 = (f32[1,16]{1,0:T(1,128)S(1)}, f32[1,16]{1,0:T(1,128)}, u32[]{:S(2)}) copy-start(f32[1,16]{1,0:T(1,128)} %class_ref.1) | copy-start | bytes 196
  3.7 1.0 %copy-start.1 = (f32[1,16,8192]{2,1,0:T(8,128)S(1)}, f32[1,16,8192]{2,1,0:T(8,128)}, u32[]{:S(2)}) copy-start(f32[1,16,8192]{2,1,0:T(8,128)} %volts_ref.1) | copy-start | bytes 1572868
  5.1 2.1 %copy-start.2 = (f32[1,16,8192]{2,1,0:T(8,128)S(1)}, f32[1,16,8192]{2,1,0:T(8,128)}, u32[]{:S(2)}) copy-start(f32[1,16,8192]{2,1,0:T(8,128)} %loads_ref.1) | copy-start | bytes 1572868
  5.2 4.0 %collective-permute-start.2 = (f32[1,64,128]{2,1,0:T(8,128)S(1)}, f32[1,64,128]{2,1,0:T(8,128)S(1)}, u32[]{:S(2)}, u32[]{:S(2)}) collective-permute-start(f32[1,64,128]{2,1,0:T(8,128)S(1)} %get-tuple-element.42), channel_id=1, source_target_pairs={{0,1},{1,0},{2,3},{3,2},{4,5},{5,4},{6,7},{7,6},{8,9},{9,8},{10,11... | collective-permute-start | bytes 98312 | tf_op jit(solution)/shard_map/ppermute | solution.py:683
  7.6 3.9 %collective-permute-start.3 = (f32[256,128]{1,0:T(8,128)S(1)}, f32[256,128]{1,0:T(8,128)S(1)}, u32[]{:S(2)}, u32[]{:S(2)}) collective-permute-start(f32[256,128]{1,0:T(8,128)S(1)} %get-tuple-element.43), channel_id=1, source_target_pairs={{0,2},{1,3},{2,0},{3,1},{4,6},{5,7},{6,4},{7,5},{8,10},{9,11},{10,... | collective-permute-start | bytes 393224 | tf_op jit(solution)/shard_map/ppermute | solution.py:689
  7.6 5.1 %collective-permute-start.4 = (f32[264,128]{1,0:T(8,128)S(1)}, f32[264,128]{1,0:T(8,128)S(1)}, u32[]{:S(2)}, u32[]{:S(2)}) collective-permute-start(f32[264,128]{1,0:T(8,128)S(1)} %get-tuple-element.44), channel_id=1, source_target_pairs={{0,1},{1,0},{2,4},{3,5},{4,2},{5,3},{6,8},{7,9},{8,6},{9,7},{10,12... | collective-permute-start | bytes 405512 | tf_op jit(solution)/shard_map/ppermute | solution.py:688
  9.3 4.9 %collective-permute-start.5 = (f32[200,128]{1,0:T(8,128)S(1)}, f32[200,128]{1,0:T(8,128)S(1)}, u32[]{:S(2)}, u32[]{:S(2)}) collective-permute-start(f32[200,128]{1,0:T(8,128)S(1)} %get-tuple-element.51), channel_id=1, source_target_pairs={{0,2},{1,3},{2,0},{3,1},{4,6},{5,7},{6,4},{7,5},{8,10},{9,11},{10,... | collective-permute-start | bytes 307208 | tf_op jit(solution)/shard_map/ppermute | solution.py:689
  9.6 4.9 %collective-permute-start.6 = (f32[192,128]{1,0:T(8,128)S(1)}, f32[192,128]{1,0:T(8,128)S(1)}, u32[]{:S(2)}, u32[]{:S(2)}) collective-permute-start(f32[192,128]{1,0:T(8,128)S(1)} %get-tuple-element.45.after_ref), channel_id=1, source_target_pairs={{0,1},{1,0},{2,4},{3,5},{4,2},{5,3},{6,8},{7,9},{8,6},{9,7},{10,12... | collective-permute-start | bytes 294920 | tf_op jit(solution)/shard_map/ppermute | solution.py:688
  14.8 4.0 %collective-permute-start.7 = (f32[1,64,128]{2,1,0:T(8,128)S(1)}, f32[1,64,128]{2,1,0:T(8,128)S(1)}, u32[]{:S(2)}, u32[]{:S(2)}) collective-permute-start(f32[1,64,128]{2,1,0:T(8,128)S(1)} %get-tuple-element.57.after_ref), channel_id=1, source_target_pairs={{0,1},{1,0},{2,3},{3,2},{4,5},{5,4},{6,7},{7,6},{8,9},{9,8},{10,11... | collective-permute-start | bytes 98312 | tf_op jit(solution)/shard_map/ppermute | solution.py:683
  16.5 5.5 %collective-permute-start.9 = (f32[192,128]{1,0:T(8,128)S(1)}, f32[192,128]{1,0:T(8,128)S(1)}, u32[]{:S(2)}, u32[]{:S(2)}) collective-permute-start(f32[192,128]{1,0:T(8,128)S(1)} %get-tuple-element.65), channel_id=1, source_target_pairs={{0,1},{1,0},{2,4},{3,5},{4,2},{5,3},{6,8},{7,9},{8,6},{9,7},{10,12... | collective-permute-start | bytes 294920 | tf_op jit(solution)/shard_map/ppermute | solution.py:688
  17.0 4.9 %collective-permute-start.8 = (f32[200,128]{1,0:T(8,128)S(1)}, f32[200,128]{1,0:T(8,128)S(1)}, u32[]{:S(2)}, u32[]{:S(2)}) collective-permute-start(f32[200,128]{1,0:T(8,128)S(1)} %get-tuple-element.64), channel_id=1, source_target_pairs={{0,2},{1,3},{2,0},{3,1},{4,6},{5,7},{6,4},{7,5},{8,10},{9,11},{10,... | collective-permute-start | bytes 307208 | tf_op jit(solution)/shard_map/ppermute | solution.py:689
  18.7 4.1 %collective-permute-start.11 = (f32[72,128]{1,0:T(8,128)S(1)}, f32[72,128]{1,0:T(8,128)S(1)}, u32[]{:S(2)}, u32[]{:S(2)}) collective-permute-start(f32[72,128]{1,0:T(8,128)S(1)} %get-tuple-element.60.after_ref), channel_id=1, source_target_pairs={{0,1},{1,0},{2,4},{3,5},{4,2},{5,3},{6,8},{7,9},{8,6},{9,7},{10,12... | collective-permute-start | bytes 110600 | tf_op jit(solution)/shard_map/ppermute | solution.py:688
  20.4 1.6 %collective-permute-start.10 = (f32[64,128]{1,0:T(8,128)S(1)}, f32[64,128]{1,0:T(8,128)S(1)}, u32[]{:S(2)}, u32[]{:S(2)}) collective-permute-start(f32[64,128]{1,0:T(8,128)S(1)} %get-tuple-element.66), channel_id=1, source_target_pairs={{0,2},{1,3},{2,0},{3,1},{4,6},{5,7},{6,4},{7,5},{8,10},{9,11},{10,... | collective-permute-start | bytes 98312 | tf_op jit(solution)/shard_map/ppermute | solution.py:689
